TPU v7x, 128 devices: a whole 4x4x4 slice. The times are simulated.
128 devices in a mesh: dp: 4 (over z), expert: 32 (over x, y, core).
Axes of the slice: x: 4, y: 4, z: 4, core: 2. Of those that a mesh axis runs over, the one named last changes fastest.
Arguments:
- ids: int32 [4, 4096], P('dp'), may hold values from 0 to 32063
- targets: int32 [4, 4096], P('dp'), may hold values from 0 to 32063
- documents: int32 [128, 128], P(('dp', 'expert')), may hold values from 0 to 3, never falling along the last dimension, each value on 1 to 64 neighbouring positions
- domains: int32 [4, 4096], replicated, may hold values from 0 to 5
- loss_rows: int32 [4, 2048], replicated, may hold values from 0 to 127, as said below
- routes: int32 [16384, 6], P(('dp', 'expert')), may hold values from 0 to 31, all different within a row; in each aligned block of 128 rows (0 to 127, 128 to 255, ...) at most 32 rows name the same one
- dense_rows: float32 [1024, 6944], P(('dp', 'expert'))
- shared_down: float32 [1408, 1024], P(('dp', 'expert')), may hold values from -0.15625 to 0.15625
- gains: float32 [3, 1024], P(None, ('dp', 'expert'))
- tables: float32 [2, 32064, 1024], P(None, 'expert', 'dp')
- expert_up: float32 [32, 2, 1024, 704], P('expert', None, None, 'dp'), may hold values from -0.1875 to 0.1875
- expert_down: float32 [32, 704, 1024], P('expert', 'dp'), may hold values from -1.75 to 1.75
- dense_m: float32 [1024, 6944], P(('dp', 'expert')), may hold values from -1.1920929e-06 to 1.1920929e-06
- shared_m: float32 [1408, 1024], P(('dp', 'expert')), may hold values from -1.1920929e-06 to 1.1920929e-06
- gains_m: float32 [3, 1024], P(None, ('dp', 'expert')), may hold values from -1.1920929e-06 to 1.1920929e-06
- tables_m: float32 [2, 32064, 1024], P(None, 'expert', 'dp'), may hold values from -1.1920929e-06 to 1.1920929e-06
- up_m: float32 [32, 2, 1024, 704], P('expert', None, None, 'dp'), may hold values from -1.1920929e-06 to 1.1920929e-06
- down_m: float32 [32, 704, 1024], P('expert', 'dp'), may hold values from -2.3841858e-07 to 2.3841858e-07
- dense_v: float32 [1024, 6944], P(('dp', 'expert')), may hold values from 1.4641431e-13 to 5.8565723e-13
- shared_v: float32 [1408, 1024], P(('dp', 'expert')), may hold values from 1.4641431e-13 to 5.8565723e-13
- gains_v: float32 [3, 1024], P(None, ('dp', 'expert')), may hold values from 6.97211e-12 to 4.183266e-11
- tables_v: float32 [2, 32064, 1024], P(None, 'expert', 'dp'), may hold values from 1.4641431e-13 to 5.8565723e-13
- up_v: float32 [32, 2, 1024, 704], P('expert', None, None, 'dp'), may hold values from 1.4641431e-13 to 5.8565723e-13
- down_v: float32 [32, 704, 1024], P('expert', 'dp'), may hold values from 7.320715e-15 to 2.928286e-14
- expert_bias: float32 [32], replicated, may hold values from -1.25 to 1.25
Outputs:
- dense_new: float32 [1024, 6944], P(('dp', 'expert'))
- shared_new: float32 [1408, 1024], P(('dp', 'expert'))
- gains_new: float32 [3, 1024], P(None, ('dp', 'expert'))
- tables_new: float32 [2, 32064, 1024], P(None, 'expert', 'dp')
- up_new: float32 [32, 2, 1024, 704], P('expert', None, None, 'dp')
- down_new: float32 [32, 704, 1024], P('expert', 'dp')
- dense_m_new: float32 [1024, 6944], P(('dp', 'expert'))
- shared_m_new: float32 [1408, 1024], P(('dp', 'expert'))
- gains_m_new: float32 [3, 1024], P(None, ('dp', 'expert'))
- tables_m_new: float32 [2, 32064, 1024], P(None, 'expert', 'dp')
- up_m_new: float32 [32, 2, 1024, 704], P('expert', None, None, 'dp')
- down_m_new: float32 [32, 704, 1024], P('expert', 'dp')
- dense_v_new: float32 [1024, 6944], P(('dp', 'expert'))
- shared_v_new: float32 [1408, 1024], P(('dp', 'expert'))
- gains_v_new: float32 [3, 1024], P(None, ('dp', 'expert'))
- tables_v_new: float32 [2, 32064, 1024], P(None, 'expert', 'dp')
- up_v_new: float32 [32, 2, 1024, 704], P('expert', None, None, 'dp')
- down_v_new: float32 [32, 704, 1024], P('expert', 'dp')
- bias_new: float32 [32], replicated
- grad_norm: float32 [], replicated
- loss_sum: float32 [], replicated
- weight_sum: float32 [], replicated
Inputs may be any that keep to these rules, and one draw needn't show every extreme that they name: `routes`: in each aligned block of 128 rows (the tokens of one device) no expert is named by more than 32 rows, a bound that some block reaches. `documents`: within each row the document numbers never fall. `loss_rows`: each device's 64 entries are distinct and ascending and include its first and last position.
All inputs are finite; a program needn't handle non-finite values.
Results may differ from a plain program's by a relative error of at most 0.02.
The roundings to bfloat16 on the way count: a program that leaves them out, or rounds other values in their place, can miss the bound.
Values may be sent and summed in bfloat16 or wider, within the bound.
No kernel may reach another device: no remote copies, remote signals or barrier semaphores. Data moves between devices by JAX's collectives and lax.ppermute only.
A program may use at most 256 MiB of HBM per device.

v0:
```python
import math

import jax
import jax.numpy as jnp
from jax import lax
from jax.sharding import PartitionSpec as P

HD = 128
TOP = 6
STEP = 10


NORM_EPS = 1e-06
HIGH = lax.Precision.HIGHEST
BETA_ONE = 0.9
BETA_TWO = 0.95
ADAM_EPS = 1e-08
DECAY = 0.1
CLIP_NORM = 0.02
BIAS_RATE = 0.05
ROPE_BASE = 10000.0
RATES = (0.03, 0.03, 0.5, 0.4, 0.03, 0.5)
MASKED = -1e30
LOW = jnp.bfloat16
BOTH = ("dp", "expert")
STREAMS = 4


def product(left, right):
    return jnp.dot(left, right, preferred_element_type=jnp.float32)


def inner_rows(left, right, precision=None):
    return lax.dot_general(
        left,
        right,
        (((0,), (0,)), ((), ())),
        precision=precision,
        preferred_element_type=jnp.float32,
    )


def inner_cols(left, right, precision=None):
    return lax.dot_general(
        left,
        right,
        (((1,), (1,)), ((), ())),
        precision=precision,
        preferred_element_type=jnp.float32,
    )


def split_three(values):
    high = values.astype(LOW)
    rest = values - high.astype(jnp.float32)
    middle = rest.astype(LOW)
    last = (rest - middle.astype(jnp.float32)).astype(LOW)
    return high, middle, last


def pick_exact(choice, values):
    return sum(product(choice, part) for part in split_three(values))


def norm_apply(values, gain_row):
    return (
        values * lax.rsqrt(jnp.mean(values * values, axis=-1, keepdims=True) + NORM_EPS) * gain_row
    )


def swiglu(gate_act, up_act):
    return jax.nn.silu(gate_act) * up_act


def rope_tables(length, head_size):
    positions = jnp.arange(length, dtype=jnp.float32)
    frequency = ROPE_BASE ** (-2.0 * jnp.arange(head_size // 2, dtype=jnp.float32) / head_size)
    angles = positions[:, None] * frequency[None, :]
    return (jnp.cos(angles)[:, None, :], jnp.sin(angles)[:, None, :])


def rotate(values, cosine, sine):
    half_size = values.shape[-1] // 2
    first_half = values[..., :half_size]
    second_half = values[..., half_size:]
    return jnp.concatenate(
        [first_half * cosine - second_half * sine, second_half * cosine + first_half * sine],
        axis=-1,
    )


def adam_update(weight, grad, first, second, rate, clip_scale):
    grad = grad * clip_scale
    first = BETA_ONE * first + (1.0 - BETA_ONE) * grad
    second = BETA_TWO * second + (1.0 - BETA_TWO) * grad * grad
    first_fix = first / (1.0 - BETA_ONE**STEP)
    second_fix = second / (1.0 - BETA_TWO**STEP)
    weight = weight - rate * (first_fix / (jnp.sqrt(second_fix) + ADAM_EPS) + DECAY * weight)
    return (weight, first, second)


def swap(value, number):
    return lax.ppermute(value, "expert", [(i, i ^ number) for i in range(32)])


def by_distance(values, index):
    rest = values.shape[1:]
    for bit in range(5):
        halves = values.reshape((32 >> (bit + 1), 2, 1 << bit) + rest)
        values = jnp.where(((index >> bit) & 1) == 1, halves[:, ::-1], halves)
    return values.reshape((32,) + rest)


def add_low(left, right):
    return (left.astype(jnp.float32) + right.astype(jnp.float32)).astype(LOW)


def ring_sum(blocks, shift, other_way):
    near, far = (3, 1) if other_way else (1, 3)
    if other_way:
        sent = jnp.stack([blocks[3], blocks[2]])
        kept = blocks[0:2]
    else:
        sent = blocks[1:3]
        kept = jnp.stack([blocks[0], blocks[3]])
    kept = add_low(kept, swap(sent, near << shift))
    return add_low(kept[0], swap(kept[1], far << shift))


def ring_gather(block, shift, other_way):
    near, far = (3, 1) if other_way else (1, 3)
    pair = jnp.stack([block, swap(block, far << shift)])
    met = swap(pair, near << shift)
    if other_way:
        return jnp.stack([pair[0], pair[1], met[1], met[0]])
    return jnp.stack([pair[0], met[0], met[1], pair[1]])


def plane_sum(blocks, stream):
    other_way = stream % 2 == 1
    if stream // 2 == 0:
        return ring_sum(ring_sum(blocks, 3, other_way), 1, other_way)
    turned = jnp.swapaxes(blocks, 0, 1)
    return ring_sum(ring_sum(turned, 1, other_way), 3, other_way)


def plane_gather(block, stream):
    other_way = stream % 2 == 1
    if stream // 2 == 0:
        return ring_gather(ring_gather(block, 1, other_way), 3, other_way)
    return jnp.swapaxes(
        ring_gather(ring_gather(block, 3, other_way), 1, other_way), 0, 1
    )


def expert_sum(blocks):
    _, rows, width = blocks.shape
    blocks = blocks.reshape(4, 4, 2, STREAMS, rows // STREAMS, width)
    mine = add_low(blocks[:, :, 0], swap(blocks[:, :, 1], 1))
    return jnp.concatenate([plane_sum(mine[:, :, s], s) for s in range(STREAMS)], axis=0)


def expert_gather(block):
    rows, width = block.shape
    part = rows // STREAMS
    mine = jnp.stack(
        [plane_gather(block[s * part : (s + 1) * part], s) for s in range(STREAMS)], axis=2
    )
    return jnp.stack([mine, swap(mine, 1)], axis=2).reshape(32, rows, width)


def merge_stats(first_part, second_part):
    top_value = jnp.maximum(first_part[0], second_part[0])
    total_exp = first_part[1] * jnp.exp(first_part[0] - top_value) + second_part[1] * jnp.exp(
        second_part[0] - top_value
    )
    return jnp.stack([top_value, total_exp, first_part[2] + second_part[2]])


def flip_blocks(stats, number):
    rows = stats.shape[-1]
    stats = stats.reshape(3, 2, 2, 2, 2, 2, rows)
    axes = [5 - bit for bit in range(5) if (number >> bit) & 1]
    return jnp.flip(stats, axes).reshape(3, 32, rows)


def meet_stats(stats):
    for shift in (3, 1):
        others = [flip_blocks(swap(stats, k << shift), k << shift) for k in (1, 2, 3)]
        for other in others:
            stats = merge_stats(stats, other)
    return merge_stats(stats, flip_blocks(swap(stats, 1), 1))


def hot(indices, count):
    return (indices[..., None] == jnp.arange(count, dtype=jnp.int32)).astype(LOW)


def attention_scores(query, key_rot, mask):
    scores = jnp.einsum("qhd,khd->hqk", query, key_rot, preferred_element_type=jnp.float32) * (
        1.0 / math.sqrt(HD)
    )
    return jnp.where(mask[None], scores, MASKED)


def body(
    ids,
    targets,
    documents,
    domains,
    loss_rows,
    routes,
    dense_rows,
    shared_down,
    gains,
    tables,
    expert_up,
    expert_down,
    dense_m,
    shared_m,
    gains_m,
    tables_m,
    up_m,
    down_m,
    dense_v,
    shared_v,
    gains_v,
    tables_v,
    up_v,
    down_v,
    expert_bias,
):
    f32 = jnp.float32
    groups = lax.axis_size("dp")
    axis_width = lax.axis_size("expert")
    expert_index = lax.axis_index("expert")
    group_index = lax.axis_index("dp")
    devices = groups * axis_width
    rows_dev = routes.shape[0]
    own_rows, dense_width = dense_rows.shape
    own_down, width_model = shared_down.shape
    hidden_shared = own_down * devices
    heads_count = width_model // HD
    experts = expert_bias.shape[0]
    slot_cap = min(rows_dev, rows_dev * TOP * 4 // (3 * experts))
    slots_all = experts * slot_cap
    vocab_part = tables.shape[1]
    part_width = tables.shape[2]
    vocab_start = expert_index * vocab_part
    hidden = expert_down.shape[1] * groups

    gap = -(dense_width + gains.shape[0]) % 128
    down_low = shared_down.astype(LOW)
    packed = jnp.concatenate(
        [
            dense_rows.astype(LOW),
            gains.astype(LOW).T,
            jnp.zeros((own_rows, gap), LOW),
            down_low[:own_rows],
            jnp.pad(down_low[own_rows:], ((0, 2 * own_rows - own_down), (0, 0))),
        ],
        axis=1,
    )
    packed_all = lax.all_gather(packed, BOTH, axis=0, tiled=True)
    start = dense_width + gains.shape[0] + gap
    router_start = 4 * width_model + 2 * hidden_shared
    w_qkv = packed_all[:, : 3 * width_model]
    w_out = packed_all[:, 3 * width_model : 4 * width_model]
    w_shared = packed_all[:, 4 * width_model : router_start]
    w_router = packed_all[:, router_start:dense_width]
    gain_full = packed_all[:, dense_width : dense_width + gains.shape[0]].T.astype(f32)
    down_first = packed_all[:, start : start + width_model]
    down_second = packed_all[:, start + width_model :]

    ids_all = lax.all_to_all(
        jnp.broadcast_to(ids, (groups,) + ids.shape[1:]), "dp", split_axis=0, concat_axis=0, tiled=True
    )
    ids_near = by_distance(
        ids_all.reshape(groups, axis_width, rows_dev).swapaxes(0, 1), expert_index
    )
    local_ids = (ids_near - vocab_start).reshape(4, 4, 2, groups, rows_dev)
    table_words = tables[0].astype(LOW)
    looked_up = []
    for core in (1, 0):
        found = product(hot(local_ids[:, :, core].reshape(-1), vocab_part), table_words)
        looked_up.append(found.astype(LOW).reshape(4, 4, groups, rows_dev, part_width))
    looked_up = add_low(looked_up[1], swap(looked_up[0], 1))
    x_first = jnp.stack([plane_sum(looked_up[:, :, s], s) for s in range(groups)])
    x_first = lax.all_to_all(x_first, "dp", split_axis=0, concat_axis=0, tiled=True)
    x_first = x_first.swapaxes(0, 1).reshape(rows_dev, width_model).astype(f32)

    expert_part = jnp.concatenate(
        [expert_up[0].astype(LOW).swapaxes(1, 2), expert_down.astype(LOW)], axis=0
    )
    expert_all = lax.all_gather(expert_part, "dp", axis=1, tiled=True)
    w_gate, w_up, w_down = expert_all[0], expert_all[1], expert_all[2]
    head = lax.all_gather(tables[1].astype(LOW), "dp", axis=1, tiled=True)

    positions = jnp.arange(rows_dev)
    experts_range = jnp.arange(experts, dtype=jnp.int32)
    chosen = jnp.any(routes[:, :, None] == experts_range[None, None, :], axis=1)
    earlier = product(
        (positions[:, None] > positions[None, :]).astype(LOW), chosen.astype(LOW)
    ).astype(jnp.int32)
    place = jnp.where(chosen, earlier, slot_cap)
    token_slots = hot(place, slot_cap).reshape(rows_dev, slots_all)
    slot_tokens = token_slots.T
    slot_experts = (
        jnp.arange(slots_all, dtype=jnp.int32)[:, None] // slot_cap == experts_range[None, :]
    )
    spread = slot_experts.T.astype(LOW)

    per_device = loss_rows.shape[1] // axis_width
    loss_places = loss_rows.reshape(groups, axis_width, per_device)
    at_place = loss_places[..., None] == jnp.arange(rows_dev, dtype=jnp.int32)
    counted_domains = jnp.sum(
        jnp.where(at_place, domains.reshape(groups, axis_width, 1, rows_dev), 0), axis=-1
    )
    all_weights = jnp.exp2(counted_domains.astype(f32) - 2.0)
    weight_total = jnp.sum(all_weights)
    group_weights = by_distance(lax.dynamic_index_in_dim(all_weights, group_index, 0, False), expert_index)
    group_places = lax.dynamic_index_in_dim(loss_places, group_index, 0, False)
    group_targets = jnp.sum(
        jnp.where(
            group_places[..., None] == jnp.arange(rows_dev, dtype=jnp.int32),
            targets.reshape(axis_width, 1, rows_dev),
            0,
        ),
        axis=-1,
    )
    target_local = (by_distance(group_targets, expert_index) - vocab_start).reshape(-1)
    own_choice = hot(by_distance(group_places, expert_index)[0], rows_dev)
    grad_weights = group_weights.reshape(-1) / weight_total

    docs_row = documents[0]
    mask = (positions[:, None] >= positions[None, :]) & (docs_row[:, None] == docs_row[None, :])
    cosine, sine = rope_tables(rows_dev, HD)
    h_first_low = norm_apply(x_first, gain_full[0]).astype(LOW)
    qkv_all = product(h_first_low, w_qkv)
    query = rotate(
        qkv_all[:, :width_model].reshape(rows_dev, heads_count, HD), cosine, sine
    ).astype(LOW)
    key_rot = rotate(
        qkv_all[:, width_model : 2 * width_model].reshape(rows_dev, heads_count, HD), cosine, sine
    ).astype(LOW)
    value_low = qkv_all[:, 2 * width_model :].reshape(rows_dev, heads_count, HD).astype(LOW)
    scores = attention_scores(query, key_rot, mask)
    top_score = jnp.max(scores, axis=-1, keepdims=True)
    expo = jnp.exp(scores - top_score)
    probs = expo / jnp.sum(expo, axis=-1, keepdims=True)
    attended = jnp.einsum(
        "hqk,khd->qhd", probs.astype(LOW), value_low, preferred_element_type=f32
    )
    attended = attended.reshape(rows_dev, width_model).astype(LOW)
    x_mid = x_first + product(attended, w_out)
    h_low = norm_apply(x_mid, gain_full[1]).astype(LOW)

    buffer = product(slot_tokens, h_low).astype(LOW)
    expert_rows = lax.all_to_all(buffer, "expert", split_axis=0, concat_axis=0, tiled=True)

    gate_scores = jnp.where(chosen, jax.nn.sigmoid(product(h_low, w_router)), 0.0)
    gate_total = jnp.sum(gate_scores, axis=1, keepdims=True)
    gates = gate_scores / gate_total
    gate_slots = jnp.concatenate(
        [token_slots * product(part, spread).astype(LOW) for part in split_three(gates)], axis=0
    )
    slot_gates = jnp.sum(
        jnp.where(slot_experts, pick_exact(slot_tokens, gates), 0.0), axis=1, keepdims=True
    )
    down_rows = jnp.arange(hidden_shared, dtype=jnp.int32)
    down_place = (down_rows // own_down) * own_rows + down_rows % own_down
    down_spot = jnp.where(
        down_rows % own_down < own_rows,
        down_place,
        down_place + (devices - 1) * own_rows,
    )
    down_choice = hot(down_spot, 2 * devices * own_rows)
    w_sdown = (
        product(down_choice[:, : devices * own_rows], down_first)
        + product(down_choice[:, devices * own_rows :], down_second)
    ).astype(LOW)
    shared_in = product(h_low, w_shared)
    shared_hidden = swiglu(shared_in[:, :hidden_shared], shared_in[:, hidden_shared:]).astype(LOW)
    shared_out = product(shared_hidden, w_sdown)

    gate_act = inner_cols(expert_rows, w_gate)
    up_act = inner_cols(expert_rows, w_up)
    expert_hidden = swiglu(gate_act, up_act).astype(LOW)
    expert_out = product(expert_hidden, w_down).astype(LOW)
    returned = lax.all_to_all(expert_out, "expert", split_axis=0, concat_axis=0, tiled=True)
    routed = product(gate_slots, returned).reshape(3, rows_dev, width_model)
    x_last = x_mid + shared_out + (routed[0] + routed[1] + routed[2])

    chosen_rows = product(own_choice, norm_apply(x_last, gain_full[2]).astype(LOW)).astype(LOW)
    gathered = expert_gather(chosen_rows).reshape(axis_width * per_device, width_model)
    logits = inner_cols(gathered, head)
    is_target = target_local[:, None] == jnp.arange(vocab_part, dtype=jnp.int32)[None, :]
    row_top = jnp.max(logits, axis=1)
    expos = jnp.exp(logits - row_top[:, None])
    row_total = jnp.sum(expos, axis=1)
    row_target = jnp.sum(jnp.where(is_target, logits, 0.0), axis=1)
    rest_low = jnp.where(is_target, 0.0, expos).astype(LOW)
    stats = meet_stats(
        jnp.stack([row_top, row_total, row_target]).reshape(3, axis_width, per_device)
    )
    log_norm = (stats[0] + jnp.log(stats[1])).reshape(-1)
    entropy = log_norm.reshape(axis_width, per_device)[0] - stats[2, 0]
    own_loss = jnp.sum(group_weights[0] * entropy)
    rest_scale = jnp.exp(row_top - log_norm) * grad_weights
    target_grad = (jnp.exp(stats[2].reshape(-1) - log_norm) - 1.0) * grad_weights
    target_head = product(is_target.astype(LOW), head)
    d_rows_all = product(rest_low, head) * rest_scale[:, None] + target_grad[:, None] * target_head
    d_chosen = expert_sum(
        d_rows_all.astype(LOW).reshape(axis_width, per_device, width_model)
    ).astype(f32)
    d_logits = jnp.where(
        is_target, target_grad[:, None], rest_low.astype(f32) * rest_scale[:, None]
    ).astype(LOW)
    d_head = inner_rows(d_logits, gathered).astype(LOW)
    d_head = d_head.reshape(vocab_part, groups, part_width).swapaxes(0, 1)
    d_head_part = lax.psum_scatter(d_head, "dp", scatter_dimension=0, tiled=True)[0].astype(f32)

    _, final_back = jax.vjp(norm_apply, x_last, gain_full[2])
    d_last, d_gain_last = final_back(pick_exact(own_choice.T, d_chosen))
    d_branch = d_last.astype(LOW)
    d_last_parts = split_three(d_last)

    d_buffer = (sum(product(slot_tokens, part) for part in d_last_parts) * slot_gates).astype(LOW)
    d_rows = lax.all_to_all(d_buffer, "expert", split_axis=0, concat_axis=0, tiled=True)

    d_slots = inner_cols(jnp.concatenate(d_last_parts, axis=0), returned)
    d_slots = jnp.sum(d_slots.reshape(3, rows_dev, slots_all), axis=0) * token_slots.astype(f32)
    d_gates = sum(inner_cols(part, spread) for part in split_three(d_slots))
    d_scores = (d_gates - jnp.sum(gates * d_gates, axis=1, keepdims=True)) / gate_total
    d_router_logits = jnp.where(chosen, d_scores * gate_scores * (1.0 - gate_scores), 0.0)
    d_hmid = inner_cols(d_router_logits, w_router.astype(f32), HIGH)

    _, shared_back = jax.vjp(swiglu, shared_in[:, :hidden_shared], shared_in[:, hidden_shared:])
    d_gate_shared, d_up_shared = shared_back(inner_cols(d_branch, w_sdown))
    d_shared_in = jnp.concatenate([d_gate_shared, d_up_shared], axis=1).astype(LOW)
    d_hmid = d_hmid + inner_cols(d_shared_in, w_shared)

    features = jnp.arange(width_model, dtype=jnp.int32)
    owner, row = features // own_rows, features % own_rows
    turned = (owner % axis_width) * groups + owner // axis_width
    turn_choice = hot(turned * own_rows + row, width_model)
    downs = down_rows // own_down
    down_turned = (downs % axis_width) * groups + downs // axis_width
    down_turn = hot(down_turned * (2 * own_rows) + down_rows % own_down, 2 * devices * own_rows)
    h_mid_turned = product(h_low, turn_choice).astype(LOW)
    attended_turned = product(attended, turn_choice).astype(LOW)
    h_first_turned = product(h_first_low, turn_choice).astype(LOW)
    hidden_turned = product(shared_hidden, down_turn).astype(LOW)
    d_wshared = inner_rows(h_mid_turned, d_shared_in).astype(LOW)
    d_wrouter = sum(
        inner_rows(h_mid_turned, part) for part in split_three(d_router_logits)
    ).astype(LOW)
    d_sdown = inner_rows(hidden_turned, d_branch).astype(LOW)

    d_expert_hidden = inner_cols(d_rows, w_down)
    _, expert_back = jax.vjp(swiglu, gate_act, up_act)
    d_gate_expert, d_up_expert = expert_back(d_expert_hidden)
    d_gate_expert = d_gate_expert.astype(LOW)
    d_up_expert = d_up_expert.astype(LOW)
    d_sent = (product(d_gate_expert, w_gate) + product(d_up_expert, w_up)).astype(LOW)
    d_returned = lax.all_to_all(d_sent, "expert", split_axis=0, concat_axis=0, tiled=True)
    d_experts = jnp.stack(
        [
            inner_rows(d_gate_expert, expert_rows).astype(LOW),
            inner_rows(d_up_expert, expert_rows).astype(LOW),
            inner_rows(expert_hidden, d_rows).astype(LOW),
        ]
    )
    experts_part = lax.psum_scatter(d_experts, "dp", scatter_dimension=1, tiled=True).astype(f32)

    d_hmid = d_hmid + product(token_slots, d_returned)
    _, mid_back = jax.vjp(norm_apply, x_mid, gain_full[1])
    d_mid_part, d_gain_mid = mid_back(d_hmid)
    d_mid = d_last + d_mid_part
    d_att_in = d_mid.astype(LOW)
    d_wout = inner_rows(attended_turned, d_att_in).astype(LOW)
    d_attended = inner_cols(d_att_in, w_out).astype(LOW).reshape(rows_dev, heads_count, HD)
    d_value = jnp.einsum("hqk,qhd->khd", probs.astype(LOW), d_attended, preferred_element_type=f32)
    d_probs = jnp.einsum("qhd,khd->hqk", d_attended, value_low, preferred_element_type=f32)
    d_scores = (probs * (d_probs - jnp.sum(probs * d_probs, axis=-1, keepdims=True))).astype(LOW)
    scale_query = 1.0 / math.sqrt(HD)
    d_query = (
        jnp.einsum("hqk,khd->qhd", d_scores, key_rot, preferred_element_type=f32) * scale_query
    )
    d_key = jnp.einsum("hqk,qhd->khd", d_scores, query, preferred_element_type=f32) * scale_query
    d_qkv = jnp.concatenate(
        [
            rotate(d_query, cosine, -sine).reshape(rows_dev, width_model),
            rotate(d_key, cosine, -sine).reshape(rows_dev, width_model),
            d_value.reshape(rows_dev, width_model),
        ],
        axis=1,
    ).astype(LOW)
    d_wqkv = inner_rows(h_first_turned, d_qkv).astype(LOW)
    _, first_back = jax.vjp(norm_apply, x_first, gain_full[0])
    d_first_part, d_gain_first = first_back(inner_cols(d_qkv, w_qkv))
    d_first = (d_mid + d_first_part).astype(LOW)

    d_first = d_first.reshape(rows_dev, groups, part_width).swapaxes(0, 1)
    d_first = lax.all_to_all(d_first, "dp", split_axis=0, concat_axis=0, tiled=True)
    d_tokens = jnp.stack([plane_gather(d_first[s], s) for s in range(groups)], axis=2)
    d_embed = 0.0
    for core, tokens in ((0, d_tokens), (1, swap(d_tokens, 1))):
        words = hot(local_ids[:, :, core].reshape(-1), vocab_part)
        d_embed = d_embed + inner_rows(words, tokens.reshape(-1, part_width))

    gain_grad = jnp.stack([d_gain_first, d_gain_mid, d_gain_last], axis=1)
    gain_grad = gain_grad.reshape(groups, axis_width, own_rows, -1).swapaxes(0, 1)
    gain_grad = gain_grad.reshape(width_model, -1).astype(LOW)
    early = jnp.concatenate(
        [
            d_wshared,
            d_wrouter,
            jnp.zeros((width_model, -d_wrouter.shape[1] % 128), LOW),
            d_sdown.reshape(devices, 2, own_rows, width_model)[:, 0].reshape(width_model, -1),
            d_sdown.reshape(devices, 2, own_rows, width_model)[:, 1].reshape(width_model, -1),
            d_wout,
        ],
        axis=1,
    )
    late = jnp.concatenate([d_wqkv, jnp.pad(gain_grad, ((0, 0), (0, 128 - gain_grad.shape[1])))], axis=1)
    parts = []
    for grad in (early, late):
        part = lax.psum_scatter(grad, "expert", scatter_dimension=0, tiled=True)
        part = lax.all_to_all(part, "dp", split_axis=0, concat_axis=0, tiled=True)
        parts.append(jnp.sum(part.reshape(groups, own_rows, -1).astype(f32), axis=0))
    early, late = parts
    wide = 2 * hidden_shared + -(-d_wrouter.shape[1] // 128) * 128
    dense_part = jnp.concatenate(
        [
            late[:, : 3 * width_model],
            early[:, wide + 2 * width_model :],
            early[:, : 2 * hidden_shared + d_wrouter.shape[1]],
        ],
        axis=1,
    )
    shared_part = jnp.concatenate(
        [
            early[:, wide : wide + width_model],
            early[: own_down - own_rows, wide + width_model : wide + 2 * width_model],
        ],
        axis=0,
    )
    gains_part = late[:, 3 * width_model : 3 * width_model + gains.shape[0]].T
    up_part = experts_part[:2].swapaxes(1, 2)[None]
    down_part = experts_part[2:]

    grads = (dense_part, shared_part, gains_part, d_embed, d_head_part, up_part, down_part)
    squares = sum(jnp.sum(grad_part * grad_part) for grad_part in grads)
    counts = jnp.sum(chosen.astype(f32), axis=0)
    sums = jnp.concatenate([squares[None], own_loss[None], counts, jnp.zeros((126 - experts,), f32)])
    sums = lax.all_to_all(
        jnp.broadcast_to(sums[None], (devices, 128)), BOTH, split_axis=0, concat_axis=0, tiled=True
    )
    sums = jnp.sum(sums, axis=0)
    total_squares, loss_total, counts_all = sums[0], sums[1], sums[2 : 2 + experts]
    norm_value = jnp.sqrt(total_squares)
    clip_scale = jnp.minimum(1.0, CLIP_NORM / (norm_value + 1e-06))
    tables_part = jnp.stack([d_embed, d_head_part])
    grads = (dense_part, shared_part, gains_part, tables_part, up_part, down_part)
    masters = (dense_rows, shared_down, gains, tables, expert_up, expert_down)
    firsts = (dense_m, shared_m, gains_m, tables_m, up_m, down_m)
    seconds = (dense_v, shared_v, gains_v, tables_v, up_v, down_v)
    updated = [
        adam_update(
            masters[index], grads[index], firsts[index], seconds[index], RATES[index], clip_scale
        )
        for index in range(6)
    ]
    mean_load = jnp.sum(counts_all) / experts
    bias_new = expert_bias + BIAS_RATE * jnp.sign(mean_load - counts_all)
    return (
        *(new[0] for new in updated),
        *(new[1] for new in updated),
        *(new[2] for new in updated),
        bias_new,
        norm_value,
        loss_total,
        weight_total,
    )


def solution(mesh):
    in_specs = (
        P("dp", None),
        P("dp", None),
        P(("dp", "expert"), None),
        P(),
        P(),
        P(("dp", "expert"), None),
        P(("dp", "expert"), None),
        P(("dp", "expert"), None),
        P(None, ("dp", "expert")),
        P(None, "expert", "dp"),
        P("expert", None, None, "dp"),
        P("expert", "dp", None),
        P(("dp", "expert"), None),
        P(("dp", "expert"), None),
        P(None, ("dp", "expert")),
        P(None, "expert", "dp"),
        P("expert", None, None, "dp"),
        P("expert", "dp", None),
        P(("dp", "expert"), None),
        P(("dp", "expert"), None),
        P(None, ("dp", "expert")),
        P(None, "expert", "dp"),
        P("expert", None, None, "dp"),
        P("expert", "dp", None),
        P(),
    )
    out_specs = (
        P(("dp", "expert"), None),
        P(("dp", "expert"), None),
        P(None, ("dp", "expert")),
        P(None, "expert", "dp"),
        P("expert", None, None, "dp"),
        P("expert", "dp", None),
        P(("dp", "expert"), None),
        P(("dp", "expert"), None),
        P(None, ("dp", "expert")),
        P(None, "expert", "dp"),
        P("expert", None, None, "dp"),
        P("expert", "dp", None),
        P(("dp", "expert"), None),
        P(("dp", "expert"), None),
        P(None, ("dp", "expert")),
        P(None, "expert", "dp"),
        P("expert", None, None, "dp"),
        P("expert", "dp", None),
        P(),
        P(),
        P(),
        P(),
    )
    return jax.shard_map(body, mesh=mesh, in_specs=in_specs, out_specs=out_specs, check_vma=False)
```

profile of v0, /device:TPU:1, one launch (start us, length us, event | category | flops | bytes accessed | tf_op | source)
XLA Modules:
  0.0 768.0 jit_solution(18246156138058081026)
XLA Ops:
  12.2 5.9 all-to-all-start
  23.8 9.6 %fusion.12 = bf16[8192,256]{1,0:T(8,128)(2,1)} fusion(s32[8192]{0:T(1024)S(1)} %bitcast.785, bf16[2,1002,256]{2,1,0:T(8,128)(2,1)} %copy.762), kind=kOutput, calls=%fused_computation.17 | convolution fusion | flops 4212998144 | bytes 4743168 | tf_op jit(solution)/shard_map/dot_general | solution.py:30
  44.7 7.4 fusion.11
  62.7 9.7 %collective-permute-done.1 = bf16[2,4,128,256]{3,2,1,0:T(8,128)(2,1)S(1)} collective-permute-done((bf16[2,4,128,256]{3,2,1,0:T(8,128)(2,1)S(1)}, bf16[2,4,128,256]{3,2,1,0:T(8,128)(2,1)S(1)}, u32[]{:S(2)}, u32[]{:S(2)}) %collective-permute-start.1) | collective-permute-done | bytes 524320 | tf_op jit(solution)/shard_map/ppermute | solution.py:103
  83.1 4.4 collective-permute-done.2
  94.5 4.3 collective-permute-done.3
  111.2 5.4 all-to-all-done.1
  119.6 4.3 fusion.24
  132.4 11.7 %all-to-all-start.2 = ((bf16[32,32,1024]{2,1,0:T(8,128)(2,1)}), bf16[32,32,1024]{2,1,0:T(8,128)(2,1)S(1)}, u32[]{:S(2)}, u32[]{:S(2)}) async-start(bf16[32,32,1024]{2,1,0:T(8,128)(2,1)} %bitcast.67), calls=%async_computation.2 | async-start | bytes 4194304 | tf_op jit(solution)/shard_map/all_to_all | solution.py:359
  152.5 7.8 %all-gather.7.cloned.1.call-done = bf16[3,704,1024]{2,1,0:T(8,128)(2,1)} async-done(((bf16[3,176,1024]{2,1,0:T(8,128)(2,1)}), bf16[3,704,1024]{2,1,0:T(8,128)(2,1)}) %all-gather.7.cloned.1.call-update) | async-done | bytes 4325392 | tf_op jit(solution)/shard_map/all_gather | solution.py:295
  160.3 11.9 %all-to-all-done.2 = bf16[32,32,1024]{2,1,0:T(8,128)(2,1)S(1)} async-done(((bf16[32,32,1024]{2,1,0:T(8,128)(2,1)}), bf16[32,32,1024]{2,1,0:T(8,128)(2,1)S(1)}, u32[]{:S(2)}, u32[]{:S(2)}) %all-to-all-start.2) | async-done | bytes 2097184 | tf_op jit(solution)/shard_map/all_to_all | solution.py:359
  182.9 5.5 all-to-all-start.3
  191.9 5.3 fusion.18
  197.2 6.4 add_convert_fusion.1
  203.6 13.2 %all-to-all-done.3 = bf16[32,32,1024]{2,1,0:T(8,128)(2,1)} async-done(((bf16[32,32,1024]{2,1,0:T(8,128)(2,1)}), bf16[32,32,1024]{2,1,0:T(8,128)(2,1)}, u32[]{:S(2)}, u32[]{:S(2)}) %all-to-all-start.3) | async-done | bytes 2097184 | tf_op jit(solution)/shard_map/all_to_all | solution.py:390
  247.5 6.9 collective-permute-start.33
  264.1 10.6 %fusion.342 = (f32[2048]{0:T(1024)S(1)}, f32[2048,1002]{0,1:T(8,128)}) fusion(bf16[2048,1024]{1,0:T(8,128)(2,1)} %bitcast.630, bf16[1,1002,1024]{2,1,0:T(8,128)(2,1)} %all-gather.9.cloned.1.call-done), kind=kOutput, calls=%fused_computation.718 | convolution fusion | flops 4204742656 | bytes 14462976 | tf_op jit(solution)/shard_map/dot_general | solution.py:44
  274.8 4.6 select_reduce_fusion
  295.2 8.5 %fusion.14 = f32[2048,1024]{1,0:T(8,128)} fusion(s32[2048]{0:T(1024)S(1)} %sub.536, bf16[1,1002,1024]{2,1,0:T(8,128)(2,1)} %all-gather.9.cloned.1.call-done), kind=kOutput, calls=%fused_computation.26 | convolution fusion | flops 4204744704 | bytes 10448896 | tf_op jit(solution)/shard_map/dot_general | solution.py:30
  305.8 9.4 %add_convert_fusion = bf16[2048,1024]{1,0:T(8,128)(2,1)S(1)} fusion(f32[2048,1024]{1,0:T(8,128)} %fusion.14, f32[2048]{0:T(1024)S(1)} %add_multiply_fusion, f32[2048]{0:T(1024)S(1)} %get-tuple-element.229, bf16[1,1002,1024]{2,1,0:T(8,128)(2,1)} %all-gather.9.cloned.1.call-done, f32[2048,1002]{0,1:T(8,128)} %get-tuple-element.408, ...), kind=kOutput, calls=%fused_computation.20 | convolution fusion | flops 4219289600 | bytes 22876160 | tf_op jit(solution)/shard_map/dot_general | solution.py:30
  354.3 11.0 %all-to-all-start.4 = ((bf16[32,32,1024]{2,1,0:T(8,128)(2,1)}), bf16[32,32,1024]{2,1,0:T(8,128)(2,1)}, u32[]{:S(2)}, u32[]{:S(2)}) async-start(bf16[32,32,1024]{2,1,0:T(8,128)(2,1)} %bitcast.181), calls=%async_computation.4 | async-start | bytes 4194304 | tf_op jit(solution)/shard_map/all_to_all | solution.py:429
  365.5 10.5 %fusion.57 = bf16[1002,1024]{1,0:T(8,128)(2,1)} fusion(bf16[2048,1024]{1,0:T(8,128)(2,1)} %bitcast.631, f32[2048]{0:T(1024)S(1)} %copy-done.122, f32[2048]{0:T(1024)S(1)} %copy-done.125, s32[2048]{0:T(1024)S(1)} %copy-done.116, f32[2048,1002]{0,1:T(8,128)} %get-tuple-element.408, f32[2048]{0:T(1024)S(1)} %copy-done.83), kind=kOutput, calls=%fused_computation.99 | convolution fusion | flops 4218083328 | bytes 14487552 | tf_op jit(solution)/shard_map/dot_general | solution.py:34
  381.9 11.9 %all-to-all-done.4 = bf16[32,32,1024]{2,1,0:T(8,128)(2,1)} async-done(((bf16[32,32,1024]{2,1,0:T(8,128)(2,1)}), bf16[32,32,1024]{2,1,0:T(8,128)(2,1)}, u32[]{:S(2)}, u32[]{:S(2)}) %all-to-all-start.4) | async-done | bytes 2097184 | tf_op jit(solution)/shard_map/all_to_all | solution.py:429
  397.6 4.8 multiply_convert_fusion.1
  413.9 4.7 add_convert_fusion.2
  418.6 4.5 all-to-all-start.5
  429.9 5.5 fusion.26
  435.4 16.1 %all-to-all-done.5 = bf16[32,32,1024]{2,1,0:T(8,128)(2,1)S(1)} async-done(((bf16[32,32,1024]{2,1,0:T(8,128)(2,1)}), bf16[32,32,1024]{2,1,0:T(8,128)(2,1)S(1)}, u32[]{:S(2)}, u32[]{:S(2)}) %all-to-all-start.5) | async-done | bytes 2097184 | tf_op jit(solution)/shard_map/all_to_all | solution.py:466
  467.1 6.0 multiply_reduce_fusion.4
  473.8 8.7 %convolution_convert_fusion.1 = bf16[1024,3072]{1,0:T(8,128)(2,1)} fusion(s32[1024]{0:T(1024)S(1)} %copy-done.102, bf16[128,1024]{0,1:T(8,128)(2,1)S(1)} %bitcast.697, bf16[128,1024]{0,1:T(8,128)(2,1)S(1)} %bitcast.649, bf16[128,1024]{0,1:T(8,128)(2,1)S(1)} %bitcast.647, f32[128,1024]{1,0:T(8,128)S(1)} %bitcast.621, f32[1024]{0:T(1024)S(1)} %copy-done.101, ...), kind=kOutput, calls=%fused_computation.36 | convolution fusion | flops 1080819712 | bytes 7610880 | tf_op jit(solution)/shard_map/dot_general | solution.py:34
  482.5 6.0 fusion.16
  491.2 5.8 convolution_convert_fusion.2
  497.0 4.3 convolution_convert_fusion
  507.0 19.1 %concatenate.69 = bf16[1024,6016]{1,0:T(8,128)(2,1)} concatenate(bf16[1024,2816]{1,0:T(8,128)(2,1)} %convolution_convert_fusion, bf16[1024,32]{1,0:T(8,128)(2,1)S(1)} %copy.671, bf16[1024,96]{1,0:T(8,128)(2,1)} %broadcast_in_dim.166, bf16[1024,1024]{1,0:T(8,128)(2,1)} %get-tuple-element.251, bf16[1024,1024]{1,0:T(8,128)(2,1)} %get-tuple-element.250, ...), dimensions={1} | concatenate | bytes 24641536 | tf_op jit(solution)/shard_map/concatenate | solution.py:515
  527.3 8.0 %all_to_all.85 = bf16[4,128,256]{2,1,0:T(8,128)(2,1)S(1)} all-to-all(bf16[4,128,256]{2,1,0:T(8,128)(2,1)S(1)} %bitcast.654), channel_id=1, replica_groups=mesh['dp'=4,'expert'=32] {'dp'}, dimensions={0} | all-to-all | bytes 524288 | tf_op jit(solution)/shard_map/all_to_all | solution.py:505
  545.2 4.7 collective-permute-done.63
  561.2 11.2 %collective-permute-done.60 = bf16[4,128,256]{2,1,0:T(8,128)(2,1)S(1)} collective-permute-done((bf16[4,128,256]{2,1,0:T(8,128)(2,1)S(1)}, bf16[4,128,256]{2,1,0:T(8,128)(2,1)S(1)}, u32[]{:S(2)}, u32[]{:S(2)}) %collective-permute-start.60) | collective-permute-done | bytes 262176 | tf_op jit(solution)/shard_map/ppermute | solution.py:103
  576.6 5.1 collective-permute-done.61
  584.2 7.6 collective-permute-start.74
  598.4 9.9 %fusion.3 = f32[1002,256]{1,0:T(8,128)S(1)} fusion(bf16[8192,256]{1,0:T(8,128)(2,1)S(1)} %bitcast.634, s32[8192]{0:T(1024)S(1)} %bitcast.788), kind=kOutput, calls=%fused_computation.5 | convolution fusion | flops 4210900992 | bytes 5253120 | tf_op jit(solution)/shard_map/dot_general | solution.py:34
  611.2 12.0 %multiply_reduce_fusion.2 = (f32[]{:T(128)}, f32[1002,256]{1,0:T(8,128)}) fusion(f32[1002,256]{1,0:T(8,128)S(1)} %fusion.3, bf16[8192,256]{1,0:T(8,128)(2,1)S(1)} %bitcast.633, s32[8192]{0:T(1024)S(1)} %bitcast.786), kind=kOutput, calls=%fused_computation.188 | convolution fusion | flops 4211670528 | bytes 6279172 | tf_op jit(solution)/shard_map/dot_general | solution.py:34
  624.8 6.7 all-to-all-start.6
  632.5 4.4 all-to-all-done.6
  636.9 52.3 %reduce-scatter.7.cloned.1.call-done = bf16[32,6016]{1,0:T(8,128)(2,1)} async-done(((bf16[1024,6016]{1,0:T(8,128)(2,1)}), bf16[32,6016]{1,0:T(8,128)(2,1)}) %reduce-scatter.7.cloned.1.call-update) | async-done | bytes 385040 | tf_op jit(solution)/shard_map/reduce_scatter | solution.py:529
  694.8 4.8 all-to-all-done.7
  706.9 9.0 %all-to-all-start.9 = ((f32[128,1,128]{2,1,0:T(1,128)}), f32[128,1,128]{2,1,0:T(1,128)}, u32[]{:S(2)}, u32[]{:S(2)}) async-start(f32[128,1,128]{2,1,0:T(1,128)} %broadcast_in_dim.172), calls=%async_computation.13 | async-start | bytes 131072 | tf_op jit(solution)/shard_map/all_to_all | solution.py:557
  719.0 6.3 all-to-all-done.9
  735.5 4.7 multiply_subtract_fusion
  (874 shorter events, 324.8 us)
Async XLA Ops:
  7.2 109.6 %all-gather.5.cloned.1.call-start = ((), (), s32[]{:S(2)}) async-start(), calls=%async_computation.14 | async-start | bytes 18757632 | tf_op jit(solution)/shard_map/all_gather | solution.py:264
  12.2 10.4 %all-to-all-start = ((s32[4,1,4096]{2,1,0:T(1,128)}), s32[4,1,4096]{2,1,0:T(1,128)}, u32[]{:S(2)}, u32[]{:S(2)}) async-start(s32[4,1,4096]{2,1,0:T(1,128)} %broadcast_in_dim.87), calls=%async_computation | async-start | bytes 131072 | tf_op jit(solution)/shard_map/all_to_all | solution.py:275
  18.1 142.3 %all-gather.7.cloned.1.call-start = ((), (), s32[]{:S(2)}) async-start(), calls=%async_computation.15 | async-start | bytes 5406720 | tf_op jit(solution)/shard_map/all_gather | solution.py:295
  33.4 18.7 %collective-permute-start = (bf16[4,4,4,128,256]{4,3,2,1,0:T(8,128)(2,1)}, bf16[4,4,4,128,256]{4,3,2,1,0:T(8,128)(2,1)}, u32[]{:S(2)}, u32[]{:S(2)}) collective-permute-start(bf16[4,4,4,128,256]{4,3,2,1,0:T(8,128)(2,1)} %bitcast.13), channel_id=1, source_target_pairs={{0,1},{1,0},{2,3},{3,2},{4,5},{5,4},{6,7},{7,6},{8,9},{9,8},{10,11... | collective-permute-start | bytes 12582920 | tf_op jit(solution)/shard_map/ppermute | solution.py:103
  56.3 16.1 %collective-permute-start.1 = (bf16[2,4,128,256]{3,2,1,0:T(8,128)(2,1)S(1)}, bf16[2,4,128,256]{3,2,1,0:T(8,128)(2,1)S(1)}, u32[]{:S(2)}, u32[]{:S(2)}) collective-permute-start(bf16[2,4,128,256]{3,2,1,0:T(8,128)(2,1)S(1)} %slice_bitcast_fusion.18), channel_id=1, source_target_pairs={{0,8},{1,9},{2,10},{3,11},{4,12},{5,13},{6,14},{7,15},{8,0},{9,1},... | collective-permute-start | bytes 1572872 | tf_op jit(solution)/shard_map/ppermute | solution.py:103
  57.7 17.2 %collective-permute-start.5 = (bf16[2,4,128,256]{3,2,1,0:T(8,128)(2,1)S(1)}, bf16[2,4,128,256]{3,2,1,0:T(8,128)(2,1)S(1)}, u32[]{:S(2)}, u32[]{:S(2)}) collective-permute-start(bf16[2,4,128,256]{3,2,1,0:T(8,128)(2,1)S(1)} %pad_maximum_fusion.8), channel_id=1, source_target_pairs={{0,24},{1,25},{2,26},{3,27},{4,28},{5,29},{6,30},{7,31},{8,16},{9,... | collective-permute-start | bytes 1572872 | tf_op jit(solution)/shard_map/ppermute | solution.py:103
  59.9 19.2 %collective-permute-start.13 = (bf16[2,4,128,256]{3,2,0,1:T(8,128)(2,1)S(1)}, bf16[2,4,128,256]{3,2,0,1:T(8,128)(2,1)S(1)}, u32[]{:S(2)}, u32[]{:S(2)}) collective-permute-start(bf16[2,4,128,256]{3,2,0,1:T(8,128)(2,1)S(1)} %pad_maximum_fusion.9), channel_id=1, source_target_pairs={{0,6},{1,7},{2,4},{3,5},{4,2},{5,3},{6,0},{7,1},{8,14},{9,15},{10,... | collective-permute-start | bytes 1572872 | tf_op jit(solution)/shard_map/ppermute | solution.py:103
  62.7 18.0 %collective-permute-start.9 = (bf16[2,4,128,256]{3,2,1,0:T(8,128)(2,1)S(1)}, bf16[2,4,128,256]{3,2,1,0:T(8,128)(2,1)S(1)}, u32[]{:S(2)}, u32[]{:S(2)}) collective-permute-start(bf16[2,4,128,256]{3,2,1,0:T(8,128)(2,1)S(1)} %slice.1064), channel_id=1, source_target_pairs={{0,2},{1,3},{2,0},{3,1},{4,6},{5,7},{6,4},{7,5},{8,10},{9,11},{10,... | collective-permute-start | bytes 1572872 | tf_op jit(solution)/shard_map/ppermute | solution.py:103
  72.6 14.9 %collective-permute-start.2 = (bf16[4,128,256]{2,1,0:T(8,128)(2,1)S(1)}, bf16[4,128,256]{2,1,0:T(8,128)(2,1)S(1)}, u32[]{:S(2)}, u32[]{:S(2)}) collective-permute-start(bf16[4,128,256]{2,1,0:T(8,128)(2,1)S(1)} %slice_bitcast_fusion.32), channel_id=1, source_target_pairs={{0,24},{1,25},{2,26},{3,27},{4,28},{5,29},{6,30},{7,31},{8,16},{9,... | collective-permute-start | bytes 786440 | tf_op jit(solution)/shard_map/ppermute | solution.py:103
  75.1 14.0 %collective-permute-start.6 = (bf16[4,128,256]{2,1,0:T(8,128)(2,1)S(1)}, bf16[4,128,256]{2,1,0:T(8,128)(2,1)S(1)}, u32[]{:S(2)}, u32[]{:S(2)}) collective-permute-start(bf16[4,128,256]{2,1,0:T(8,128)(2,1)S(1)} %slice_bitcast_fusion.28), channel_id=1, source_target_pairs={{0,8},{1,9},{2,10},{3,11},{4,12},{5,13},{6,14},{7,15},{8,0},{9,1},... | collective-permute-start | bytes 786440 | tf_op jit(solution)/shard_map/ppermute | solution.py:103
  79.2 14.0 %collective-permute-start.14 = (bf16[4,128,256]{2,1,0:T(8,128)(2,1)S(1)}, bf16[4,128,256]{2,1,0:T(8,128)(2,1)S(1)}, u32[]{:S(2)}, u32[]{:S(2)}) collective-permute-start(bf16[4,128,256]{2,1,0:T(8,128)(2,1)S(1)} %slice_bitcast_fusion.24), channel_id=1, source_target_pairs={{0,2},{1,3},{2,0},{3,1},{4,6},{5,7},{6,4},{7,5},{8,10},{9,11},{10,... | collective-permute-start | bytes 786440 | tf_op jit(solution)/shard_map/ppermute | solution.py:103
  80.9 13.4 %collective-permute-start.10 = (bf16[4,128,256]{2,1,0:T(8,128)(2,1)S(1)}, bf16[4,128,256]{2,1,0:T(8,128)(2,1)S(1)}, u32[]{:S(2)}, u32[]{:S(2)}) collective-permute-start(bf16[4,128,256]{2,1,0:T(8,128)(2,1)S(1)} %slice_bitcast_fusion.26), channel_id=1, source_target_pairs={{0,6},{1,7},{2,4},{3,5},{4,2},{5,3},{6,0},{7,1},{8,14},{9,15},{10,... | collective-permute-start | bytes 786440 | tf_op jit(solution)/shard_map/ppermute | solution.py:103
  87.5 11.2 %collective-permute-start.3 = (bf16[2,128,256]{2,1,0:T(8,128)(2,1)S(1)}, bf16[2,128,256]{2,1,0:T(8,128)(2,1)S(1)}, u32[]{:S(2)}, u32[]{:S(2)}) collective-permute-start(bf16[2,128,256]{2,1,0:T(8,128)(2,1)S(1)} %slice.1048), channel_id=1, source_target_pairs={{0,2},{1,3},{2,0},{3,1},{4,6},{5,7},{6,4},{7,5},{8,10},{9,11},{10,... | collective-permute-start | bytes 393224 | tf_op jit(solution)/shard_map/ppermute | solution.py:103
  89.2 12.1 %collective-permute-start.7 = (bf16[2,128,256]{2,1,0:T(8,128)(2,1)S(1)}, bf16[2,128,256]{2,1,0:T(8,128)(2,1)S(1)}, u32[]{:S(2)}, u32[]{:S(2)}) collective-permute-start(bf16[2,128,256]{2,1,0:T(8,128)(2,1)S(1)} %pad_maximum_fusion.34), channel_id=1, source_target_pairs={{0,6},{1,7},{2,4},{3,5},{4,2},{5,3},{6,0},{7,1},{8,14},{9,15},{10,... | collective-permute-start | bytes 393224 | tf_op jit(solution)/shard_map/ppermute | solution.py:103
  93.3 8.3 %collective-permute-start.15 = (bf16[2,128,256]{2,1,0:T(8,128)(2,1)S(1)}, bf16[2,128,256]{2,1,0:T(8,128)(2,1)S(1)}, u32[]{:S(2)}, u32[]{:S(2)}) collective-permute-start(bf16[2,128,256]{2,1,0:T(8,128)(2,1)S(1)} %pad_maximum_fusion.35), channel_id=1, source_target_pairs={{0,24},{1,25},{2,26},{3,27},{4,28},{5,29},{6,30},{7,31},{8,16},{9,... | collective-permute-start | bytes 393224 | tf_op jit(solution)/shard_map/ppermute | solution.py:103
  107.7 8.9 %all-to-all-start.1 = ((bf16[4,128,256]{2,1,0:T(8,128)(2,1)}), bf16[4,128,256]{2,1,0:T(8,128)(2,1)S(1)}, u32[]{:S(2)}, u32[]{:S(2)}) async-start(bf16[4,128,256]{2,1,0:T(8,128)(2,1)} %pad_maximum_fusion.18), calls=%async_computation.1 | async-start | bytes 524288 | tf_op jit(solution)/shard_map/all_to_all | solution.py:289
  132.4 39.8 %all-to-all-start.2 = ((bf16[32,32,1024]{2,1,0:T(8,128)(2,1)}), bf16[32,32,1024]{2,1,0:T(8,128)(2,1)S(1)}, u32[]{:S(2)}, u32[]{:S(2)}) async-start(bf16[32,32,1024]{2,1,0:T(8,128)(2,1)} %bitcast.67), calls=%async_computation.2 | async-start | bytes 4194304 | tf_op jit(solution)/shard_map/all_to_all | solution.py:359
  182.9 33.9 %all-to-all-start.3 = ((bf16[32,32,1024]{2,1,0:T(8,128)(2,1)}), bf16[32,32,1024]{2,1,0:T(8,128)(2,1)}, u32[]{:S(2)}, u32[]{:S(2)}) async-start(bf16[32,32,1024]{2,1,0:T(8,128)(2,1)} %bitcast.642), calls=%async_computation.3 | async-start | bytes 4194304 | tf_op jit(solution)/shard_map/all_to_all | solution.py:390
  188.4 75.7 %all-gather.9.cloned.1.call-start = ((), (), s32[]{:S(2)}) async-start(), calls=%async_computation.20 | async-start | bytes 2580480 | tf_op jit(solution)/shard_map/all_gather | solution.py:297
  233.8 8.1 %collective-permute-start.32 = (bf16[2,4,16,1024]{3,2,1,0:T(8,128)(2,1)S(1)}, bf16[2,4,16,1024]{3,2,1,0:T(8,128)(2,1)S(1)}, u32[]{:S(2)}, u32[]{:S(2)}) collective-permute-start(bf16[2,4,16,1024]{3,2,1,0:T(8,128)(2,1)S(1)} %pad_maximum_fusion.24), channel_id=1, source_target_pairs={{0,6},{1,7},{2,4},{3,5},{4,2},{5,3},{6,0},{7,1},{8,14},{9,15},{10,... | collective-permute-start | bytes 786440 | tf_op jit(solution)/shard_map/ppermute | solution.py:103
  236.3 8.6 %collective-permute-start.28 = (bf16[2,4,16,1024]{3,2,1,0:T(8,128)(2,1)S(1)}, bf16[2,4,16,1024]{3,2,1,0:T(8,128)(2,1)S(1)}, u32[]{:S(2)}, u32[]{:S(2)}) collective-permute-start(bf16[2,4,16,1024]{3,2,1,0:T(8,128)(2,1)S(1)} %pad_maximum_fusion.23), channel_id=1, source_target_pairs={{0,2},{1,3},{2,0},{3,1},{4,6},{5,7},{6,4},{7,5},{8,10},{9,11},{10,... | collective-permute-start | bytes 786440 | tf_op jit(solution)/shard_map/ppermute | solution.py:103
  236.5 8.3 %collective-permute-start.24 = (bf16[2,4,16,1024]{3,2,0,1:T(8,128)(2,1)S(1)}, bf16[2,4,16,1024]{3,2,0,1:T(8,128)(2,1)S(1)}, u32[]{:S(2)}, u32[]{:S(2)}) collective-permute-start(bf16[2,4,16,1024]{3,2,0,1:T(8,128)(2,1)S(1)} %pad_maximum_fusion.22), channel_id=1, source_target_pairs={{0,24},{1,25},{2,26},{3,27},{4,28},{5,29},{6,30},{7,31},{8,16},{9,... | collective-permute-start | bytes 786440 | tf_op jit(solution)/shard_map/ppermute | solution.py:103
  247.5 11.5 %collective-permute-start.33 = (bf16[4,4,4,16,1024]{4,3,0,1,2:T(8,128)(2,1)}, bf16[4,4,4,16,1024]{4,3,0,1,2:T(8,128)(2,1)}, u32[]{:S(2)}, u32[]{:S(2)}) collective-permute-start(bf16[4,4,4,16,1024]{4,3,0,1,2:T(8,128)(2,1)} %get-tuple-element.267), channel_id=1, source_target_pairs={{0,1},{1,0},{2,3},{3,2},{4,5},{5,4},{6,7},{7,6},{8,9},{9,8},{10,11... | collective-permute-start | bytes 6291464 | tf_op jit(solution)/shard_map/ppermute | solution.py:103
  292.5 12.8 %collective-permute-start.40 = (f32[3,32,64]{2,1,0:T(8,128)S(1)}, f32[3,32,64]{2,1,0:T(8,128)S(1)}, u32[]{:S(2)}, u32[]{:S(2)}) collective-permute-start(f32[3,32,64]{2,1,0:T(8,128)S(1)} %pad_maximum_fusion.53), channel_id=1, source_target_pairs={{0,1},{1,0},{2,3},{3,2},{4,5},{5,4},{6,7},{7,6},{8,9},{9,8},{10,11... | collective-permute-start | bytes 73736 | tf_op jit(solution)/shard_map/ppermute | solution.py:103
  321.0 7.8 %collective-permute-start.42 = (bf16[2,4,16,1024]{3,2,1,0:T(8,128)(2,1)S(1)}, bf16[2,4,16,1024]{3,2,1,0:T(8,128)(2,1)S(1)}, u32[]{:S(2)}, u32[]{:S(2)}) collective-permute-start(bf16[2,4,16,1024]{3,2,1,0:T(8,128)(2,1)S(1)} %slice_bitcast_fusion.23), channel_id=1, source_target_pairs={{0,8},{1,9},{2,10},{3,11},{4,12},{5,13},{6,14},{7,15},{8,0},{9,1},... | collective-permute-start | bytes 786440 | tf_op jit(solution)/shard_map/ppermute | solution.py:103
  322.1 9.0 %collective-permute-start.46 = (bf16[2,4,16,1024]{3,2,1,0:T(8,128)(2,1)S(1)}, bf16[2,4,16,1024]{3,2,1,0:T(8,128)(2,1)S(1)}, u32[]{:S(2)}, u32[]{:S(2)}) collective-permute-start(bf16[2,4,16,1024]{3,2,1,0:T(8,128)(2,1)S(1)} %pad_maximum_fusion.25), channel_id=1, source_target_pairs={{0,24},{1,25},{2,26},{3,27},{4,28},{5,29},{6,30},{7,31},{8,16},{9,... | collective-permute-start | bytes 786440 | tf_op jit(solution)/shard_map/ppermute | solution.py:103
  323.4 8.7 %collective-permute-start.54 = (bf16[2,4,16,1024]{3,2,0,1:T(8,128)(2,1)S(1)}, bf16[2,4,16,1024]{3,2,0,1:T(8,128)(2,1)S(1)}, u32[]{:S(2)}, u32[]{:S(2)}) collective-permute-start(bf16[2,4,16,1024]{3,2,0,1:T(8,128)(2,1)S(1)} %pad_maximum_fusion.26), channel_id=1, source_target_pairs={{0,6},{1,7},{2,4},{3,5},{4,2},{5,3},{6,0},{7,1},{8,14},{9,15},{10,... | collective-permute-start | bytes 786440 | tf_op jit(solution)/shard_map/ppermute | solution.py:103
  354.3 39.4 %all-to-all-start.4 = ((bf16[32,32,1024]{2,1,0:T(8,128)(2,1)}), bf16[32,32,1024]{2,1,0:T(8,128)(2,1)}, u32[]{:S(2)}, u32[]{:S(2)}) async-start(bf16[32,32,1024]{2,1,0:T(8,128)(2,1)} %bitcast.181), calls=%async_computation.4 | async-start | bytes 4194304 | tf_op jit(solution)/shard_map/all_to_all | solution.py:429
  365.4 228.1 %reduce-scatter.9.cloned.1.call-start = ((), (), s32[]{:S(2)}) async-start(), calls=%async_computation.18 | async-start | bytes 2580480 | tf_op jit(solution)/shard_map/reduce_scatter | solution.py:421
  381.4 241.7 %reduce-scatter.11.cloned.1.call-start = ((), (), s32[]{:S(2)}) async-start(), calls=%async_computation.19 | async-start | bytes 5406720 | tf_op jit(solution)/shard_map/reduce_scatter | solution.py:474
  418.6 32.9 %all-to-all-start.5 = ((bf16[32,32,1024]{2,1,0:T(8,128)(2,1)}), bf16[32,32,1024]{2,1,0:T(8,128)(2,1)S(1)}, u32[]{:S(2)}, u32[]{:S(2)}) async-start(bf16[32,32,1024]{2,1,0:T(8,128)(2,1)} %bitcast.641), calls=%async_computation.5 | async-start | bytes 4194304 | tf_op jit(solution)/shard_map/all_to_all | solution.py:466
  423.1 201.7 %reduce-scatter.5.cloned.1.call-start = ((), (), s32[]{:S(2)}) async-start(), calls=%async_computation.16 | async-start | bytes 6758400 | tf_op jit(solution)/shard_map/reduce_scatter | solution.py:529
  488.6 200.7 %reduce-scatter.7.cloned.1.call-start = ((), (), s32[]{:S(2)}) async-start(), calls=%async_computation.17 | async-start | bytes 12705792 | tf_op jit(solution)/shard_map/reduce_scatter | solution.py:529
  540.9 16.4 %collective-permute-start.59 = (bf16[2,128,256]{2,1,0:T(8,128)(2,1)S(1)}, bf16[2,128,256]{2,1,0:T(8,128)(2,1)S(1)}, u32[]{:S(2)}, u32[]{:S(2)}) collective-permute-start(bf16[2,128,256]{2,1,0:T(8,128)(2,1)S(1)} %pad_maximum_fusion.41), channel_id=1, source_target_pairs={{0,2},{1,3},{2,0},{3,1},{4,6},{5,7},{6,4},{7,5},{8,10},{9,11},{10,... | collective-permute-start | bytes 393224 | tf_op jit(solution)/shard_map/ppermute | solution.py:103
  541.2 8.6 %collective-permute-start.63 = (bf16[2,128,256]{2,1,0:T(8,128)(2,1)S(1)}, bf16[2,128,256]{2,1,0:T(8,128)(2,1)S(1)}, u32[]{:S(2)}, u32[]{:S(2)}) collective-permute-start(bf16[2,128,256]{2,1,0:T(8,128)(2,1)S(1)} %pad_maximum_fusion.42), channel_id=1, source_target_pairs={{0,6},{1,7},{2,4},{3,5},{4,2},{5,3},{6,0},{7,1},{8,14},{9,15},{10,... | collective-permute-start | bytes 393224 | tf_op jit(solution)/shard_map/ppermute | solution.py:103
  542.3 15.9 %collective-permute-start.67 = (bf16[2,128,256]{2,1,0:T(8,128)(2,1)S(1)}, bf16[2,128,256]{2,1,0:T(8,128)(2,1)S(1)}, u32[]{:S(2)}, u32[]{:S(2)}) collective-permute-start(bf16[2,128,256]{2,1,0:T(8,128)(2,1)S(1)} %pad_maximum_fusion.43), channel_id=1, source_target_pairs={{0,8},{1,9},{2,10},{3,11},{4,12},{5,13},{6,14},{7,15},{8,0},{9,1},... | collective-permute-start | bytes 393224 | tf_op jit(solution)/shard_map/ppermute | solution.py:103
  543.3 8.3 %collective-permute-start.71 = (bf16[2,128,256]{2,1,0:T(8,128)(2,1)S(1)}, bf16[2,128,256]{2,1,0:T(8,128)(2,1)S(1)}, u32[]{:S(2)}, u32[]{:S(2)}) collective-permute-start(bf16[2,128,256]{2,1,0:T(8,128)(2,1)S(1)} %pad_maximum_fusion.44), channel_id=1, source_target_pairs={{0,24},{1,25},{2,26},{3,27},{4,28},{5,29},{6,30},{7,31},{8,16},{9,... | collective-permute-start | bytes 393224 | tf_op jit(solution)/shard_map/ppermute | solution.py:103
  551.6 8.3 %collective-permute-start.72 = (bf16[4,128,256]{2,1,0:T(8,128)(2,1)S(1)}, bf16[4,128,256]{2,1,0:T(8,128)(2,1)S(1)}, u32[]{:S(2)}, u32[]{:S(2)}) collective-permute-start(bf16[4,128,256]{2,1,0:T(8,128)(2,1)S(1)} %get-tuple-element.311), channel_id=1, source_target_pairs={{0,2},{1,3},{2,0},{3,1},{4,6},{5,7},{6,4},{7,5},{8,10},{9,11},{10,... | collective-permute-start | bytes 786440 | tf_op jit(solution)/shard_map/ppermute | solution.py:103
  555.4 18.4 %collective-permute-start.65 = (bf16[2,4,128,256]{3,2,1,0:T(8,128)(2,1)S(1)}, bf16[2,4,128,256]{3,2,1,0:T(8,128)(2,1)S(1)}, u32[]{:S(2)}, u32[]{:S(2)}) collective-permute-start(bf16[2,4,128,256]{3,2,1,0:T(8,128)(2,1)S(1)} %pad_maximum_fusion.11), channel_id=1, source_target_pairs={{0,24},{1,25},{2,26},{3,27},{4,28},{5,29},{6,30},{7,31},{8,16},{9,... | collective-permute-start | bytes 1572872 | tf_op jit(solution)/shard_map/ppermute | solution.py:103
  557.4 15.0 %collective-permute-start.60 = (bf16[4,128,256]{2,1,0:T(8,128)(2,1)S(1)}, bf16[4,128,256]{2,1,0:T(8,128)(2,1)S(1)}, u32[]{:S(2)}, u32[]{:S(2)}) collective-permute-start(bf16[4,128,256]{2,1,0:T(8,128)(2,1)S(1)} %get-tuple-element.297), channel_id=1, source_target_pairs={{0,24},{1,25},{2,26},{3,27},{4,28},{5,29},{6,30},{7,31},{8,16},{9,... | collective-permute-start | bytes 786440 | tf_op jit(solution)/shard_map/ppermute | solution.py:103
  558.3 14.8 %collective-permute-start.68 = (bf16[4,128,256]{2,1,0:T(8,128)(2,1)S(1)}, bf16[4,128,256]{2,1,0:T(8,128)(2,1)S(1)}, u32[]{:S(2)}, u32[]{:S(2)}) collective-permute-start(bf16[4,128,256]{2,1,0:T(8,128)(2,1)S(1)} %get-tuple-element.309), channel_id=1, source_target_pairs={{0,6},{1,7},{2,4},{3,5},{4,2},{5,3},{6,0},{7,1},{8,14},{9,15},{10,... | collective-permute-start | bytes 786440 | tf_op jit(solution)/shard_map/ppermute | solution.py:103
  560.0 16.5 %collective-permute-start.73 = (bf16[2,4,128,256]{3,2,0,1:T(8,128)(2,1)S(1)}, bf16[2,4,128,256]{3,2,0,1:T(8,128)(2,1)S(1)}, u32[]{:S(2)}, u32[]{:S(2)}) collective-permute-start(bf16[2,4,128,256]{3,2,0,1:T(8,128)(2,1)S(1)} %pad_maximum_fusion.13), channel_id=1, source_target_pairs={{0,6},{1,7},{2,4},{3,5},{4,2},{5,3},{6,0},{7,1},{8,14},{9,15},{10,... | collective-permute-start | bytes 1572872 | tf_op jit(solution)/shard_map/ppermute | solution.py:103
  572.5 9.3 %collective-permute-start.61 = (bf16[2,4,128,256]{3,2,1,0:T(8,128)(2,1)S(1)}, bf16[2,4,128,256]{3,2,1,0:T(8,128)(2,1)S(1)}, u32[]{:S(2)}, u32[]{:S(2)}) collective-permute-start(bf16[2,4,128,256]{3,2,1,0:T(8,128)(2,1)S(1)} %pad_maximum_fusion.10), channel_id=1, source_target_pairs={{0,8},{1,9},{2,10},{3,11},{4,12},{5,13},{6,14},{7,15},{8,0},{9,1},... | collective-permute-start | bytes 1572872 | tf_op jit(solution)/shard_map/ppermute | solution.py:103
  573.1 9.0 %collective-permute-start.69 = (bf16[2,4,128,256]{3,2,1,0:T(8,128)(2,1)S(1)}, bf16[2,4,128,256]{3,2,1,0:T(8,128)(2,1)S(1)}, u32[]{:S(2)}, u32[]{:S(2)}) collective-permute-start(bf16[2,4,128,256]{3,2,1,0:T(8,128)(2,1)S(1)} %pad_maximum_fusion.12), channel_id=1, source_target_pairs={{0,2},{1,3},{2,0},{3,1},{4,6},{5,7},{6,4},{7,5},{8,10},{9,11},{10,... | collective-permute-start | bytes 1572872 | tf_op jit(solution)/shard_map/ppermute | solution.py:103
  584.2 24.2 %collective-permute-start.74 = (bf16[4,4,4,128,256]{4,3,1,0,2:T(8,128)(2,1)}, bf16[4,4,4,128,256]{4,3,1,0,2:T(8,128)(2,1)}, u32[]{:S(2)}, u32[]{:S(2)}) collective-permute-start(bf16[4,4,4,128,256]{4,3,1,0,2:T(8,128)(2,1)} %pad_maximum_fusion.2), channel_id=1, source_target_pairs={{0,1},{1,0},{2,3},{3,2},{4,5},{5,4},{6,7},{7,6},{8,9},{9,8},{10,11... | collective-permute-start | bytes 12582920 | tf_op jit(solution)/shard_map/ppermute | solution.py:103
  624.8 12.1 %all-to-all-start.6 = ((bf16[4,8,3200]{2,1,0:T(8,128)(2,1)}), bf16[4,8,3200]{2,1,0:T(8,128)(2,1)S(1)}, u32[]{:S(2)}, u32[]{:S(2)}) async-start(bf16[4,8,3200]{2,1,0:T(8,128)(2,1)} %bitcast.724), calls=%async_computation.7 | async-start | bytes 409600 | tf_op jit(solution)/shard_map/all_to_all | solution.py:530
  689.2 10.3 %all-to-all-start.7 = ((bf16[4,8,6016]{2,1,0:T(8,128)(2,1)}), bf16[4,8,6016]{2,1,0:T(8,128)(2,1)S(1)}, u32[]{:S(2)}, u32[]{:S(2)}) async-start(bf16[4,8,6016]{2,1,0:T(8,128)(2,1)} %bitcast.695), calls=%async_computation.9 | async-start | bytes 770048 | tf_op jit(solution)/shard_map/all_to_all | solution.py:530
  706.9 18.5 %all-to-all-start.9 = ((f32[128,1,128]{2,1,0:T(1,128)}), f32[128,1,128]{2,1,0:T(1,128)}, u32[]{:S(2)}, u32[]{:S(2)}) async-start(f32[128,1,128]{2,1,0:T(1,128)} %broadcast_in_dim.172), calls=%async_computation.13 | async-start | bytes 131072 | tf_op jit(solution)/shard_map/all_to_all | solution.py:557
  (200 other events, 1845.9 us)
Sparse Core Ops, SparseCore 0:
  11.8 100.9 all-gather.4
  114.9 45.3 all-gather.6
  222.5 30.8 all-gather.8
  381.5 29.0 reduce-scatter.8
  413.0 47.6 reduce-scatter.10
  488.7 89.0 reduce-scatter.4
  582.2 106.9 reduce-scatter.6
where the time goes:
time: 780 us; the launch traced here: 768 us
  waiting for transfers between devices  220 us (28%)
  matrix products  199 us (26%)
  starting transfers between devices  155 us (20%)
  other arithmetic  85.6 us (11%)
  local copies, waits for them, and re-layouts  76.1 us (10%)
  between operations  25.1 us (3%)
  blocking collectives  7.95 us (1%)
    ppermute x75, starting transfers between devices, swap(): return lax.ppermute(value, 'expert', [(i, i ^ number) for i in range(32)])  91.9 us
    dot_general x32, matrix products, product(): return jnp.dot(left, right, preferred_element_type=jnp.float32)  87.2 us
    ppermute x75, waiting for transfers between devices, swap(): return lax.ppermute(value, 'expert', [(i, i ^ number) for i in range(32)])  84.3 us
    dot_general x13, matrix products, inner_rows(): lax.dot_general(left, right, (((0,), (0,)), ((), ())), precision=precisio...  61.4 us
    reduce_scatter x2, waiting for transfers between devices, body(): part = lax.psum_scatter(grad, 'expert', scatter_dimension=0, tiled=True)  52.3 us
    dot_general x13, matrix products, inner_cols(): lax.dot_general(left, right, (((1,), (1,)), ((), ())), precision=precisio...  43.2 us
    unnamed x332, local copies, waits for them, and re-layouts  22.6 us
    concatenate x1, local copies, waits for them, and re-layouts, body(): jnp.concatenate([d_wshared, d_wrouter, jnp.zeros((width_model, -d_wrouter...  19.1 us
  transfers between devices with their start and end apart: 91, of which 48 were waited for; matrix products, arithmetic and copies ran while one was open for 35% of the time, Pallas kernels for 0%

commit v1 on v0

--- a/solution.py
+++ b/solution.py
@@ -103,12 +103,21 @@
     return lax.ppermute(value, "expert", [(i, i ^ number) for i in range(32)])
 
 
+def swap_group(value, number):
+    return lax.ppermute(value, "dp", [(i, i ^ number) for i in range(4)])
+
+
 def by_distance(values, index):
-    rest = values.shape[1:]
-    for bit in range(5):
-        halves = values.reshape((32 >> (bit + 1), 2, 1 << bit) + rest)
+    shape = values.shape
+    rest = shape[1:]
+    for bit in range(shape[0].bit_length() - 1):
+        halves = values.reshape((shape[0] >> (bit + 1), 2, 1 << bit) + rest)
         values = jnp.where(((index >> bit) & 1) == 1, halves[:, ::-1], halves)
-    return values.reshape((32,) + rest)
+    return values.reshape(shape)
+
+
+def after(values, trigger):
+    return lax.optimization_barrier((values, trigger))[0]
 
 
 def add_low(left, right):
@@ -136,6 +145,45 @@
     return jnp.stack([pair[0], met[0], met[1], pair[1]])
 
 
+ORDERS = ((0, 3, 1, 2), (0, 1, 3, 2))
+
+
+def in_order(values, stream):
+    order = ORDERS[stream % 2]
+    if stream >= 2:
+        values = jnp.swapaxes(values, 0, 1)
+    values = jnp.stack([values[i] for i in order])
+    return jnp.stack([values[:, i] for i in order], axis=1)
+
+
+def rank_in_order(distance, stream):
+    return sum(
+        jnp.where(distance == number, spot, 0) for spot, number in enumerate(ORDERS[stream % 2])
+    )
+
+
+def steps_of(stream):
+    near, far = (3, 1) if stream % 2 == 1 else (1, 3)
+    shifts = (3, 1) if stream < 2 else (1, 3)
+    return [number << shift for shift in shifts for number in (near, far)]
+
+
+def ordered_sum(blocks, stream):
+    shape = blocks.shape[2:]
+    blocks = blocks.reshape((16,) + shape)
+    for number in steps_of(stream):
+        half = blocks.shape[0] // 2
+        blocks = add_low(blocks[:half], swap(blocks[half:], number))
+    return blocks[0]
+
+
+def ordered_gather(block, stream):
+    blocks = block[None]
+    for number in reversed(steps_of(stream)):
+        blocks = jnp.concatenate([blocks, swap(blocks, number)], axis=0)
+    return blocks
+
+
 def plane_sum(blocks, stream):
     other_way = stream % 2 == 1
     if stream // 2 == 0:
@@ -184,12 +232,13 @@
     return jnp.flip(stats, axes).reshape(3, 32, rows)
 
 
-def meet_stats(stats):
+def meet_stats(stats, beside):
     for shift in (3, 1):
         others = [flip_blocks(swap(stats, k << shift), k << shift) for k in (1, 2, 3)]
         for other in others:
             stats = merge_stats(stats, other)
-    return merge_stats(stats, flip_blocks(swap(stats, 1), 1))
+    other, beside = lax.optimization_barrier((swap(stats, 1), beside))
+    return merge_stats(stats, flip_blocks(other, 1)), beside
 
 
 def hot(indices, count):
@@ -272,27 +321,35 @@
     down_first = packed_all[:, start : start + width_model]
     down_second = packed_all[:, start + width_model :]
 
-    ids_all = lax.all_to_all(
-        jnp.broadcast_to(ids, (groups,) + ids.shape[1:]), "dp", split_axis=0, concat_axis=0, tiled=True
-    )
-    ids_near = by_distance(
-        ids_all.reshape(groups, axis_width, rows_dev).swapaxes(0, 1), expert_index
-    )
-    local_ids = (ids_near - vocab_start).reshape(4, 4, 2, groups, rows_dev)
+    local_ids = []
+    for k in range(groups):
+        group_ids = ids[0] if k == 0 else swap_group(ids, k)[0]
+        group_ids = by_distance(group_ids.reshape(axis_width, rows_dev), expert_index)
+        local_ids.append(in_order(group_ids.reshape(4, 4, 2, rows_dev) - vocab_start, k))
     table_words = tables[0].astype(LOW)
-    looked_up = []
-    for core in (1, 0):
-        found = product(hot(local_ids[:, :, core].reshape(-1), vocab_part), table_words)
-        looked_up.append(found.astype(LOW).reshape(4, 4, groups, rows_dev, part_width))
-    looked_up = add_low(looked_up[1], swap(looked_up[0], 1))
-    x_first = jnp.stack([plane_sum(looked_up[:, :, s], s) for s in range(groups)])
-    x_first = lax.all_to_all(x_first, "dp", split_axis=0, concat_axis=0, tiled=True)
+    per_half = 16 * rows_dev
+
+    def look_up(streams, core):
+        wanted = jnp.concatenate([local_ids[k][:, :, core].reshape(-1) for k in streams])
+        found = product(hot(wanted, vocab_part), table_words).astype(LOW)
+        return found.reshape(len(streams), per_half, part_width)
+
+    x_first = []
+    for streams in ((0,), (1, 2, 3)):
+        sent = swap(look_up(streams, 1), 1)
+        summed = add_low(look_up(streams, 0), sent)
+        for place, k in enumerate(streams):
+            block = ordered_sum(summed[place].reshape(4, 4, rows_dev, part_width), k)
+            x_first.append(block if k == 0 else swap_group(block, k))
+    x_first = by_distance(jnp.stack(x_first), group_index)
     x_first = x_first.swapaxes(0, 1).reshape(rows_dev, width_model).astype(f32)
 
     expert_part = jnp.concatenate(
         [expert_up[0].astype(LOW).swapaxes(1, 2), expert_down.astype(LOW)], axis=0
     )
-    expert_all = lax.all_gather(expert_part, "dp", axis=1, tiled=True)
+    expert_all = jnp.concatenate(
+        [expert_part] + [swap_group(expert_part, k) for k in range(1, groups)], axis=1
+    )
     w_gate, w_up, w_down = expert_all[0], expert_all[1], expert_all[2]
     head = lax.all_gather(tables[1].astype(LOW), "dp", axis=1, tiled=True)
 
@@ -388,37 +445,44 @@
     expert_hidden = swiglu(gate_act, up_act).astype(LOW)
     expert_out = product(expert_hidden, w_down).astype(LOW)
     returned = lax.all_to_all(expert_out, "expert", split_axis=0, concat_axis=0, tiled=True)
+    is_target = target_local[:, None] == jnp.arange(vocab_part, dtype=jnp.int32)[None, :]
+    target_head = product(is_target.astype(LOW), head).astype(LOW)
+    returned, target_head = lax.optimization_barrier((returned, target_head))
     routed = product(gate_slots, returned).reshape(3, rows_dev, width_model)
     x_last = x_mid + shared_out + (routed[0] + routed[1] + routed[2])
 
     chosen_rows = product(own_choice, norm_apply(x_last, gain_full[2]).astype(LOW)).astype(LOW)
     gathered = expert_gather(chosen_rows).reshape(axis_width * per_device, width_model)
     logits = inner_cols(gathered, head)
-    is_target = target_local[:, None] == jnp.arange(vocab_part, dtype=jnp.int32)[None, :]
     row_top = jnp.max(logits, axis=1)
     expos = jnp.exp(logits - row_top[:, None])
     row_total = jnp.sum(expos, axis=1)
     row_target = jnp.sum(jnp.where(is_target, logits, 0.0), axis=1)
     rest_low = jnp.where(is_target, 0.0, expos).astype(LOW)
-    stats = meet_stats(
-        jnp.stack([row_top, row_total, row_target]).reshape(3, axis_width, per_device)
+    d_rest = product(rest_low, head)
+    stats, d_rest = meet_stats(
+        jnp.stack([row_top, row_total, row_target]).reshape(3, axis_width, per_device), d_rest
     )
     log_norm = (stats[0] + jnp.log(stats[1])).reshape(-1)
     entropy = log_norm.reshape(axis_width, per_device)[0] - stats[2, 0]
     own_loss = jnp.sum(group_weights[0] * entropy)
     rest_scale = jnp.exp(row_top - log_norm) * grad_weights
     target_grad = (jnp.exp(stats[2].reshape(-1) - log_norm) - 1.0) * grad_weights
-    target_head = product(is_target.astype(LOW), head)
-    d_rows_all = product(rest_low, head) * rest_scale[:, None] + target_grad[:, None] * target_head
+    d_rows_all = d_rest * rest_scale[:, None] + target_grad[:, None] * target_head.astype(f32)
     d_chosen = expert_sum(
         d_rows_all.astype(LOW).reshape(axis_width, per_device, width_model)
     ).astype(f32)
     d_logits = jnp.where(
         is_target, target_grad[:, None], rest_low.astype(f32) * rest_scale[:, None]
     ).astype(LOW)
-    d_head = inner_rows(d_logits, gathered).astype(LOW)
-    d_head = d_head.reshape(vocab_part, groups, part_width).swapaxes(0, 1)
-    d_head_part = lax.psum_scatter(d_head, "dp", scatter_dimension=0, tiled=True)[0].astype(f32)
+    d_head_part = 0.0
+    for k in range(groups):
+        columns = lax.dynamic_slice_in_dim(
+            gathered, (group_index ^ k) * part_width, part_width, axis=1
+        )
+        d_columns = inner_rows(d_logits, columns).astype(LOW)
+        d_columns = d_columns if k == 0 else swap_group(d_columns, k)
+        d_head_part = d_head_part + d_columns.astype(f32)
 
     _, final_back = jax.vjp(norm_apply, x_last, gain_full[2])
     d_last, d_gain_last = final_back(pick_exact(own_choice.T, d_chosen))
@@ -444,18 +508,27 @@
     owner, row = features // own_rows, features % own_rows
     turned = (owner % axis_width) * groups + owner // axis_width
     turn_choice = hot(turned * own_rows + row, width_model)
-    downs = down_rows // own_down
-    down_turned = (downs % axis_width) * groups + downs // axis_width
-    down_turn = hot(down_turned * (2 * own_rows) + down_rows % own_down, 2 * devices * own_rows)
+    downs, down_row = down_rows // own_down, down_rows % own_down
+    down_turned = ((downs % axis_width) * groups + downs // axis_width) * own_rows
+    down_firsts = hot(jnp.where(down_row < own_rows, down_turned + down_row, -1), width_model)
+    down_seconds = hot(
+        jnp.where(down_row < own_rows, -1, down_turned + down_row - own_rows), width_model
+    )
     h_mid_turned = product(h_low, turn_choice).astype(LOW)
-    attended_turned = product(attended, turn_choice).astype(LOW)
-    h_first_turned = product(h_first_low, turn_choice).astype(LOW)
-    hidden_turned = product(shared_hidden, down_turn).astype(LOW)
-    d_wshared = inner_rows(h_mid_turned, d_shared_in).astype(LOW)
     d_wrouter = sum(
         inner_rows(h_mid_turned, part) for part in split_three(d_router_logits)
     ).astype(LOW)
-    d_sdown = inner_rows(hidden_turned, d_branch).astype(LOW)
+    early = jnp.concatenate(
+        [
+            inner_rows(product(shared_hidden, down_firsts).astype(LOW), d_branch).astype(LOW),
+            inner_rows(product(shared_hidden, down_seconds).astype(LOW), d_branch).astype(LOW),
+            inner_rows(h_mid_turned, d_shared_in).astype(LOW),
+            jnp.pad(d_wrouter, ((0, 0), (0, -experts % 128))),
+        ],
+        axis=1,
+    )
+    d_rows, early = lax.optimization_barrier((d_rows, early))
+    early = lax.psum_scatter(early, "expert", scatter_dimension=0, tiled=True)
 
     d_expert_hidden = inner_cols(d_rows, w_down)
     _, expert_back = jax.vjp(swiglu, gate_act, up_act)
@@ -464,6 +537,7 @@
     d_up_expert = d_up_expert.astype(LOW)
     d_sent = (product(d_gate_expert, w_gate) + product(d_up_expert, w_up)).astype(LOW)
     d_returned = lax.all_to_all(d_sent, "expert", split_axis=0, concat_axis=0, tiled=True)
+    expert_rows, expert_hidden, d_rows = after((expert_rows, expert_hidden, d_rows), d_sent)
     d_experts = jnp.stack(
         [
             inner_rows(d_gate_expert, expert_rows).astype(LOW),
@@ -471,14 +545,18 @@
             inner_rows(expert_hidden, d_rows).astype(LOW),
         ]
     )
-    experts_part = lax.psum_scatter(d_experts, "dp", scatter_dimension=1, tiled=True).astype(f32)
+    d_returned, d_experts = lax.optimization_barrier((d_returned, d_experts))
+    own_hidden = hidden // groups
+    experts_part = d_experts[:, :own_hidden].astype(f32)
+    for k in range(1, groups):
+        part = swap_group(d_experts[:, k * own_hidden : (k + 1) * own_hidden], k)
+        experts_part = experts_part + part.astype(f32)
 
     d_hmid = d_hmid + product(token_slots, d_returned)
     _, mid_back = jax.vjp(norm_apply, x_mid, gain_full[1])
     d_mid_part, d_gain_mid = mid_back(d_hmid)
     d_mid = d_last + d_mid_part
     d_att_in = d_mid.astype(LOW)
-    d_wout = inner_rows(attended_turned, d_att_in).astype(LOW)
     d_attended = inner_cols(d_att_in, w_out).astype(LOW).reshape(rows_dev, heads_count, HD)
     d_value = jnp.einsum("hqk,qhd->khd", probs.astype(LOW), d_attended, preferred_element_type=f32)
     d_probs = jnp.einsum("qhd,khd->hqk", d_attended, value_low, preferred_element_type=f32)
@@ -496,58 +574,72 @@
         ],
         axis=1,
     ).astype(LOW)
-    d_wqkv = inner_rows(h_first_turned, d_qkv).astype(LOW)
     _, first_back = jax.vjp(norm_apply, x_first, gain_full[0])
     d_first_part, d_gain_first = first_back(inner_cols(d_qkv, w_qkv))
     d_first = (d_mid + d_first_part).astype(LOW)
 
-    d_first = d_first.reshape(rows_dev, groups, part_width).swapaxes(0, 1)
-    d_first = lax.all_to_all(d_first, "dp", split_axis=0, concat_axis=0, tiled=True)
-    d_tokens = jnp.stack([plane_gather(d_first[s], s) for s in range(groups)], axis=2)
+    d_first_blocks = by_distance(
+        d_first.reshape(rows_dev, groups, part_width).swapaxes(0, 1), group_index
+    )
     d_embed = 0.0
-    for core, tokens in ((0, d_tokens), (1, swap(d_tokens, 1))):
-        words = hot(local_ids[:, :, core].reshape(-1), vocab_part)
-        d_embed = d_embed + inner_rows(words, tokens.reshape(-1, part_width))
-
+    for k in range(groups):
+        block = d_first_blocks[k] if k == 0 else swap_group(d_first_blocks[k], k)
+        tokens = ordered_gather(block, k)
+        for core in (0, 1):
+            words = hot(local_ids[k][:, :, core].reshape(-1), vocab_part)
+            part = tokens if core == 0 else swap(tokens, 1)
+            d_embed = d_embed + inner_rows(words, part.reshape(-1, part_width))
+
+    d_qkv, d_att_in = after((d_qkv, d_att_in), d_first_blocks)
     gain_grad = jnp.stack([d_gain_first, d_gain_mid, d_gain_last], axis=1)
-    gain_grad = gain_grad.reshape(groups, axis_width, own_rows, -1).swapaxes(0, 1)
-    gain_grad = gain_grad.reshape(width_model, -1).astype(LOW)
-    early = jnp.concatenate(
-        [
-            d_wshared,
-            d_wrouter,
-            jnp.zeros((width_model, -d_wrouter.shape[1] % 128), LOW),
-            d_sdown.reshape(devices, 2, own_rows, width_model)[:, 0].reshape(width_model, -1),
-            d_sdown.reshape(devices, 2, own_rows, width_model)[:, 1].reshape(width_model, -1),
-            d_wout,
-        ],
-        axis=1,
-    )
-    late = jnp.concatenate([d_wqkv, jnp.pad(gain_grad, ((0, 0), (0, 128 - gain_grad.shape[1])))], axis=1)
+    gain_grad = jnp.pad(gain_grad, ((0, 0), (0, 128 - gain_grad.shape[1])))
+    late = []
+    for stream, (left, right) in enumerate(
+        (
+            (h_first_low, d_qkv[:, 2 * width_model :]),
+            (h_first_low, d_qkv[:, width_model : 2 * width_model]),
+            (h_first_low, d_qkv[:, :width_model]),
+            (attended, d_att_in),
+        )
+    ):
+        distance = (owner % axis_width) ^ expert_index
+        axes = [rank_in_order(distance >> 3, stream), rank_in_order((distance >> 1) & 3, stream)]
+        first_axis, second_axis = axes if stream < 2 else axes[::-1]
+        spot = ((distance & 1) * 16 + first_axis * 4 + second_axis) * groups + owner // axis_width
+        choice = hot(spot * own_rows + row, width_model)
+        left = product(left, choice).astype(LOW)
+        half = width_model // 2
+        grad = inner_rows(left, right)
+        if stream == 2:
+            high, middle, _ = split_three(gain_grad)
+            gain_turned = inner_rows(choice, high) + inner_rows(choice, middle)
+            grad = jnp.concatenate([grad, gain_turned], axis=1)
+        grad = grad.astype(LOW)
+        grad = add_low(grad[:half], swap(grad[half:], 1))
+        grad = ordered_sum(grad.reshape(4, 4, groups * own_rows, -1), stream)
+        late.append(grad)
+    late = jnp.concatenate(late[:2] + [late[3], late[2]], axis=1)
     parts = []
-    for grad in (early, late):
-        part = lax.psum_scatter(grad, "expert", scatter_dimension=0, tiled=True)
+    for part in (early, late):
         part = lax.all_to_all(part, "dp", split_axis=0, concat_axis=0, tiled=True)
         parts.append(jnp.sum(part.reshape(groups, own_rows, -1).astype(f32), axis=0))
     early, late = parts
-    wide = 2 * hidden_shared + -(-d_wrouter.shape[1] // 128) * 128
     dense_part = jnp.concatenate(
         [
-            late[:, : 3 * width_model],
-            early[:, wide + 2 * width_model :],
-            early[:, : 2 * hidden_shared + d_wrouter.shape[1]],
+            late[:, 3 * width_model : 4 * width_model],
+            late[:, width_model : 2 * width_model],
+            late[:, :width_model],
+            late[:, 2 * width_model : 3 * width_model],
+            early[:, 2 * width_model : 2 * width_model + 2 * hidden_shared + experts],
         ],
         axis=1,
     )
     shared_part = jnp.concatenate(
-        [
-            early[:, wide : wide + width_model],
-            early[: own_down - own_rows, wide + width_model : wide + 2 * width_model],
-        ],
+        [early[:, :width_model], early[: own_down - own_rows, width_model : 2 * width_model]],
         axis=0,
     )
-    gains_part = late[:, 3 * width_model : 3 * width_model + gains.shape[0]].T
-    up_part = experts_part[:2].swapaxes(1, 2)[None]
+    gains_part = late[:, 4 * width_model : 4 * width_model + gains.shape[0]].T
+    up_part = experts_part[:2]
     down_part = experts_part[2:]
 
     grads = (dense_part, shared_part, gains_part, d_embed, d_head_part, up_part, down_part)
@@ -561,17 +653,27 @@
     total_squares, loss_total, counts_all = sums[0], sums[1], sums[2 : 2 + experts]
     norm_value = jnp.sqrt(total_squares)
     clip_scale = jnp.minimum(1.0, CLIP_NORM / (norm_value + 1e-06))
-    tables_part = jnp.stack([d_embed, d_head_part])
+    tables_part = jnp.stack([d_embed, d_head_part], axis=1)
     grads = (dense_part, shared_part, gains_part, tables_part, up_part, down_part)
     masters = (dense_rows, shared_down, gains, tables, expert_up, expert_down)
     firsts = (dense_m, shared_m, gains_m, tables_m, up_m, down_m)
     seconds = (dense_v, shared_v, gains_v, tables_v, up_v, down_v)
-    updated = [
-        adam_update(
-            masters[index], grads[index], firsts[index], seconds[index], RATES[index], clip_scale
-        )
-        for index in range(6)
-    ]
+
+    def turn(index, value):
+        if index == 3:
+            return value.swapaxes(0, 1)
+        return value[0].swapaxes(1, 2) if index == 4 else value
+
+    def turn_back(index, value):
+        if index == 3:
+            return value.swapaxes(0, 1)
+        return value.swapaxes(1, 2)[None] if index == 4 else value
+
+    updated = []
+    for index in range(6):
+        state = [turn(index, value[index]) for value in (masters, firsts, seconds)]
+        new = adam_update(state[0], grads[index], *state[1:], RATES[index], clip_scale)
+        updated.append(tuple(turn_back(index, value) for value in new))
     mean_load = jnp.sum(counts_all) / experts
     bias_new = expert_bias + BIAS_RATE * jnp.sign(mean_load - counts_all)
     return (

time: 780 us -> 868 us (1.11)
  matrix products: 199 us -> 237 us
  starting transfers between devices: 155 us -> 185 us
  waiting for transfers between devices: 220 us -> 245 us
  other arithmetic: 85.6 us -> 98.6 us
  local copies, waits for them, and re-layouts: 76.1 us -> 65.1 us
    reduce_scatter x4 -> x1, waiting for transfers between devices: 52.3 us -> 0.02 us  [body(): early = lax.psum_scatter(early, 'expert', scatter_dimension=0, tiled=True)]
    ppermute x0 -> x18, waiting for transfers between devices: none -> 48.4 us  [swap_group(): return lax.ppermute(value, 'dp', [(i, i ^ number) for i in range(4)])]
    ppermute x75 -> x99, waiting for transfers between devices: 84.3 us -> 129 us  [swap(): return lax.ppermute(value, 'expert', [(i, i ^ number) for i in range(32)])]
    ppermute x0 -> x18, starting transfers between devices: none -> 24.6 us  [swap_group(): return lax.ppermute(value, 'dp', [(i, i ^ number) for i in range(4)])]
    concatenate x1 -> x5, local copies, waits for them, and re-layouts: 19.1 us -> 1.73 us  [the longest x4 1.72 us: ordered_gather(): blocks = jnp.concatenate([blocks, swap(blocks, number)], axis=0)]
    dot_general x13 -> x27, matrix products: 61.4 us -> 77.4 us  [inner_rows(): lax.dot_general(left, right, (((0,), (0,)), ((), ())), precision=precisio...]
    dot_general x32 -> x34, matrix products: 87.2 us -> 103 us  [product(): return jnp.dot(left, right, preferred_element_type=jnp.float32)]
    sub x6 -> x4, other arithmetic: 15.7 us -> 4.87 us  [adam_update(): weight - rate * (first_fix / (jnp.sqrt(second_fix) + ADAM_EPS) + DECAY *...]
  transfers between devices with their start and end apart: 91 -> 127, of which waited for: 48 -> 50; matrix products, arithmetic and copies ran while one was open for 35% -> 30% of each run, Pallas kernels for 0% -> 0%
where the time goes in v1:
time: 868 us; the launch traced here: 857 us
  waiting for transfers between devices  245 us (28%)
  matrix products  237 us (27%)
  starting transfers between devices  185 us (21%)
  other arithmetic  98.6 us (11%)
  local copies, waits for them, and re-layouts  65.1 us (7%)
  between operations  25.8 us (3%)
    ppermute x99, waiting for transfers between devices, swap(): return lax.ppermute(value, 'expert', [(i, i ^ number) for i in range(32)])  129 us
    dot_general x34, matrix products, product(): return jnp.dot(left, right, preferred_element_type=jnp.float32)  103 us
    ppermute x99, starting transfers between devices, swap(): return lax.ppermute(value, 'expert', [(i, i ^ number) for i in range(32)])  100 us
    dot_general x27, matrix products, inner_rows(): lax.dot_general(left, right, (((0,), (0,)), ((), ())), precision=precisio...  77.4 us
    dot_general x13, matrix products, inner_cols(): lax.dot_general(left, right, (((1,), (1,)), ((), ())), precision=precisio...  49.3 us
    ppermute x18, waiting for transfers between devices, swap_group(): return lax.ppermute(value, 'dp', [(i, i ^ number) for i in range(4)])  48.4 us
    unnamed x382, local copies, waits for them, and re-layouts  29 us
    ppermute x18, starting transfers between devices, swap_group(): return lax.ppermute(value, 'dp', [(i, i ^ number) for i in range(4)])  24.6 us
  transfers between devices with their start and end apart: 127, of which 50 were waited for; matrix products, arithmetic and copies ran while one was open for 30% of the time, Pallas kernels for 0%

profile of v1, /device:TPU:1, one launch (start us, length us, event | category | flops | bytes accessed | tf_op | source)
XLA Modules:
  0.0 856.8 jit_solution(1097862543507027691)
XLA Ops:
  39.6 6.6 fusion.18
  55.8 12.8 %collective-permute-done.1 = bf16[8,128,256]{2,1,0:T(8,128)(2,1)S(1)} collective-permute-done((bf16[8,128,256]{2,1,0:T(8,128)(2,1)S(1)}, bf16[8,128,256]{2,1,0:T(8,128)(2,1)S(1)}, u32[]{:S(2)}, u32[]{:S(2)}) %collective-permute-start.1) | collective-permute-done | bytes 524320 | tf_op jit(solution)/shard_map/ppermute | solution.py:103
  71.0 5.5 fusion.19
  83.9 4.8 collective-permute-done.26
  98.7 22.0 %collective-permute-done.19 = bf16[8,128,256]{2,1,0:T(8,128)(2,1)S(1)} collective-permute-done((bf16[8,128,256]{2,1,0:T(8,128)(2,1)S(1)}, bf16[8,128,256]{2,1,0:T(8,128)(2,1)S(1)}, u32[]{:S(2)}, u32[]{:S(2)}) %collective-permute-start.19) | collective-permute-done | bytes 524320 | tf_op jit(solution)/shard_map/ppermute | solution.py:103
  123.1 8.8 %collective-permute-done.15 = bf16[4,128,256]{2,1,0:T(8,128)(2,1)S(1)} collective-permute-done((bf16[4,128,256]{2,1,0:T(8,128)(2,1)S(1)}, bf16[4,128,256]{2,1,0:T(8,128)(2,1)S(1)}, u32[]{:S(2)}, u32[]{:S(2)}) %collective-permute-start.15) | collective-permute-done | bytes 262176 | tf_op jit(solution)/shard_map/ppermute | solution.py:103
  164.6 13.1 %all-to-all-start = ((bf16[32,32,1024]{2,1,0:T(8,128)(2,1)}), bf16[32,32,1024]{2,1,0:T(8,128)(2,1)S(1)}, u32[]{:S(2)}, u32[]{:S(2)}) async-start(bf16[32,32,1024]{2,1,0:T(8,128)(2,1)} %bitcast.73), calls=%async_computation | async-start | bytes 4194304 | tf_op jit(solution)/shard_map/all_to_all | solution.py:416
  177.7 7.8 fusion.55
  193.3 12.5 %all-to-all-done = bf16[32,32,1024]{2,1,0:T(8,128)(2,1)S(1)} async-done(((bf16[32,32,1024]{2,1,0:T(8,128)(2,1)}), bf16[32,32,1024]{2,1,0:T(8,128)(2,1)S(1)}, u32[]{:S(2)}, u32[]{:S(2)}) %all-to-all-start) | async-done | bytes 2097184 | tf_op jit(solution)/shard_map/all_to_all | solution.py:416
  209.6 5.9 multiply_convert_fusion.2
  215.6 5.1 convolution_convert_fusion.8
  220.7 5.8 all-to-all-start.1
  229.9 5.3 fusion.22
  235.2 6.4 add_convert_fusion.1
  241.6 13.2 %all-to-all-done.1 = bf16[32,32,1024]{2,1,0:T(8,128)(2,1)} async-done(((bf16[32,32,1024]{2,1,0:T(8,128)(2,1)}), bf16[32,32,1024]{2,1,0:T(8,128)(2,1)}, u32[]{:S(2)}, u32[]{:S(2)}) %all-to-all-start.1) | async-done | bytes 2097184 | tf_op jit(solution)/shard_map/all_to_all | solution.py:447
  284.7 6.2 collective-permute-start.43
  301.7 6.9 fusion.424
  308.7 4.6 select_reduce_fusion
  332.7 11.9 %fusion.82 = f32[2048,1024]{1,0:T(8,128)} fusion(bf16[1,1002,1024]{2,1,0:T(8,128)(2,1)} %all-gather.6.cloned.1.call-done, f32[2048,1002]{0,1:T(8,128)} %get-tuple-element.413, f32[2048]{0:T(1024)S(1)} %get-tuple-element.412, s32[2048]{0:T(1024)S(1)} %copy-done.91), kind=kOutput, calls=%fused_computation.137 | convolution fusion | flops 4210900992 | bytes 18665472 | tf_op jit(solution)/shard_map/dot_general | solution.py:30
  348.5 5.0 select_convert_fusion
  368.8 5.0 collective-permute-done.111
  373.7 12.0 %collective-permute-done.112 = bf16[1002,256]{1,0:T(8,128)(2,1)S(1)} collective-permute-done((bf16[1002,256]{1,0:T(8,128)(2,1)S(1)}, bf16[1002,256]{1,0:T(8,128)(2,1)S(1)}, u32[]{:S(2)}, u32[]{:S(2)}) %collective-permute-start.112) | collective-permute-done | bytes 513056 | tf_op jit(solution)/shard_map/ppermute | solution.py:107
  385.8 5.0 collective-permute-done.113
  432.9 4.4 convolution_convert_fusion.5
  455.2 5.8 multiply_convert_fusion
  460.9 13.0 %all-to-all-start.2 = ((bf16[32,32,1024]{2,1,0:T(8,128)(2,1)}), bf16[32,32,1024]{2,1,0:T(8,128)(2,1)}, u32[]{:S(2)}, u32[]{:S(2)}) async-start(bf16[32,32,1024]{2,1,0:T(8,128)(2,1)} %bitcast.647), calls=%async_computation.2 | async-start | bytes 4194304 | tf_op jit(solution)/shard_map/all_to_all | solution.py:493
  479.2 4.8 fusion.6
  484.0 18.1 %all-to-all-done.2 = bf16[32,32,1024]{2,1,0:T(8,128)(2,1)} async-done(((bf16[32,32,1024]{2,1,0:T(8,128)(2,1)}), bf16[32,32,1024]{2,1,0:T(8,128)(2,1)}, u32[]{:S(2)}, u32[]{:S(2)}) %all-to-all-start.2) | async-done | bytes 2097184 | tf_op jit(solution)/shard_map/all_to_all | solution.py:493
  502.1 6.3 fusion.60
  508.4 4.2 fusion.108
  512.7 4.7 add_convert_fusion.2
  517.3 4.5 all-to-all-start.3
  522.1 4.8 fusion.32
  540.4 9.8 %all-to-all-done.3 = bf16[32,32,1024]{2,1,0:T(8,128)(2,1)S(1)} async-done(((bf16[32,32,1024]{2,1,0:T(8,128)(2,1)}), bf16[32,32,1024]{2,1,0:T(8,128)(2,1)S(1)}, u32[]{:S(2)}, u32[]{:S(2)}) %all-to-all-start.3) | async-done | bytes 2097184 | tf_op jit(solution)/shard_map/all_to_all | solution.py:539
  566.3 5.5 multiply_reduce_fusion.7
  601.1 4.9 collective-permute-done.94
  628.7 10.0 %collective-permute-done.91 = bf16[8,128,256]{2,1,0:T(8,128)(2,1)S(1)} collective-permute-done((bf16[8,128,256]{2,1,0:T(8,128)(2,1)S(1)}, bf16[8,128,256]{2,1,0:T(8,128)(2,1)S(1)}, u32[]{:S(2)}, u32[]{:S(2)}) %collective-permute-start.91) | collective-permute-done | bytes 524320 | tf_op jit(solution)/shard_map/ppermute | solution.py:103
  643.6 5.2 fusion.11
  648.8 6.8 collective-permute-done.109
  671.8 19.0 %collective-permute-done.116 = bf16[3,176,1024]{2,1,0:T(8,128)(2,1)S(1)} collective-permute-done((bf16[3,176,1024]{2,1,0:T(8,128)(2,1)S(1)}, bf16[3,176,1024]{2,1,0:T(8,128)(2,1)S(1)}, u32[]{:S(2)}, u32[]{:S(2)}) %collective-permute-start.116) | collective-permute-done | bytes 1081376 | tf_op jit(solution)/shard_map/ppermute | solution.py:107
  741.0 4.9 fusion.7
  752.9 4.9 fusion.12
  771.1 7.7 multiply_reduce_fusion.2
  778.9 4.2 all-to-all-start.5
  783.8 5.2 all-to-all-done.5
  796.2 15.8 %all-to-all-start.6 = ((f32[128,1,128]{2,1,0:T(1,128)}), f32[128,1,128]{2,1,0:T(1,128)S(1)}, u32[]{:S(2)}, u32[]{:S(2)}) async-start(f32[128,1,128]{2,1,0:T(1,128)} %broadcast_in_dim.275), calls=%async_computation.7 | async-start | bytes 131072 | tf_op jit(solution)/shard_map/all_to_all | solution.py:649
  812.3 9.3 %all-to-all-done.6 = f32[128,1,128]{2,1,0:T(1,128)S(1)} async-done(((f32[128,1,128]{2,1,0:T(1,128)}), f32[128,1,128]{2,1,0:T(1,128)S(1)}, u32[]{:S(2)}, u32[]{:S(2)}) %all-to-all-start.6) | async-done | bytes 65568 | tf_op jit(solution)/shard_map/all_to_all | solution.py:649
  823.6 5.1 fusion.348
  (1077 shorter events, 449.9 us)
Async XLA Ops:
  7.2 141.6 %all-gather.4.cloned.1.call-start = ((), (), s32[]{:S(2)}) async-start(), calls=%async_computation.8 | async-start | bytes 18757632 | tf_op jit(solution)/shard_map/all_gather | solution.py:313
  10.7 166.9 %all-gather.6.cloned.1.call-start = ((), (), s32[]{:S(2)}) async-start(), calls=%async_computation.10 | async-start | bytes 2580480 | tf_op jit(solution)/shard_map/all_gather | solution.py:354
  10.8 22.8 %collective-permute-start.5 = (s32[1,4096]{1,0:T(1,128)}, s32[1,4096]{1,0:T(1,128)S(1)}, u32[]{:S(2)}, u32[]{:S(2)}) collective-permute-start(s32[1,4096]{1,0:T(1,128)} %param.25), channel_id=1, source_target_pairs={{0,32},{32,0},{64,96},{96,64},{1,33},{33,1},{65,97},{97,65},{2,34}... | collective-permute-start | bytes 49160 | tf_op jit(solution)/shard_map/ppermute | solution.py:107
  13.3 21.1 %collective-permute-start.7 = (s32[1,4096]{1,0:T(1,128)}, s32[1,4096]{1,0:T(1,128)S(1)}, u32[]{:S(2)}, u32[]{:S(2)}) collective-permute-start(s32[1,4096]{1,0:T(1,128)} %param.25), channel_id=1, source_target_pairs={{0,96},{32,64},{64,32},{96,0},{1,97},{33,65},{65,33},{97,1},{2,98}... | collective-permute-start | bytes 49160 | tf_op jit(solution)/shard_map/ppermute | solution.py:107
  15.6 18.9 %collective-permute-start.6 = (s32[1,4096]{1,0:T(1,128)}, s32[1,4096]{1,0:T(1,128)S(1)}, u32[]{:S(2)}, u32[]{:S(2)}) collective-permute-start(s32[1,4096]{1,0:T(1,128)} %param.25), channel_id=1, source_target_pairs={{0,64},{32,96},{64,0},{96,32},{1,65},{33,97},{65,1},{97,33},{2,66}... | collective-permute-start | bytes 49160 | tf_op jit(solution)/shard_map/ppermute | solution.py:107
  19.0 64.1 %collective-permute-start.24 = (bf16[3,176,1024]{2,1,0:T(8,128)(2,1)}, bf16[3,176,1024]{2,1,0:T(8,128)(2,1)}, u32[]{:S(2)}, u32[]{:S(2)}) collective-permute-start(bf16[3,176,1024]{2,1,0:T(8,128)(2,1)} %pad_maximum_fusion.5), channel_id=1, source_target_pairs={{0,32},{32,0},{64,96},{96,64},{1,33},{33,1},{65,97},{97,65},{2,34}... | collective-permute-start | bytes 3244040 | tf_op jit(solution)/shard_map/ppermute | solution.py:107
  19.1 64.7 %collective-permute-start.25 = (bf16[3,176,1024]{2,1,0:T(8,128)(2,1)}, bf16[3,176,1024]{2,1,0:T(8,128)(2,1)}, u32[]{:S(2)}, u32[]{:S(2)}) collective-permute-start(bf16[3,176,1024]{2,1,0:T(8,128)(2,1)} %pad_maximum_fusion.5), channel_id=1, source_target_pairs={{0,64},{32,96},{64,0},{96,32},{1,65},{33,97},{65,1},{97,33},{2,66}... | collective-permute-start | bytes 3244040 | tf_op jit(solution)/shard_map/ppermute | solution.py:107
  33.6 55.1 %collective-permute-start.26 = (bf16[3,176,1024]{2,1,0:T(8,128)(2,1)}, bf16[3,176,1024]{2,1,0:T(8,128)(2,1)}, u32[]{:S(2)}, u32[]{:S(2)}) collective-permute-start(bf16[3,176,1024]{2,1,0:T(8,128)(2,1)} %pad_maximum_fusion.5), channel_id=1, source_target_pairs={{0,96},{32,64},{64,32},{96,0},{1,97},{33,65},{65,33},{97,1},{2,98}... | collective-permute-start | bytes 3244040 | tf_op jit(solution)/shard_map/ppermute | solution.py:107
  46.3 32.9 %collective-permute-start.8 = (bf16[3,2048,256]{2,1,0:T(8,128)(2,1)}, bf16[3,2048,256]{2,1,0:T(8,128)(2,1)}, u32[]{:S(2)}, u32[]{:S(2)}) collective-permute-start(bf16[3,2048,256]{2,1,0:T(8,128)(2,1)} %bitcast.43), channel_id=1, source_target_pairs={{0,1},{1,0},{2,3},{3,2},{4,5},{5,4},{6,7},{7,6},{8,9},{9,8},{10,11... | collective-permute-start | bytes 9437192 | tf_op jit(solution)/shard_map/ppermute | solution.py:103
  53.8 14.8 %collective-permute-start.1 = (bf16[8,128,256]{2,1,0:T(8,128)(2,1)S(1)}, bf16[8,128,256]{2,1,0:T(8,128)(2,1)S(1)}, u32[]{:S(2)}, u32[]{:S(2)}) collective-permute-start(bf16[8,128,256]{2,1,0:T(8,128)(2,1)S(1)} %bitcast.721), channel_id=1, source_target_pairs={{0,8},{1,9},{2,10},{3,11},{4,12},{5,13},{6,14},{7,15},{8,0},{9,1},... | collective-permute-start | bytes 1572872 | tf_op jit(solution)/shard_map/ppermute | solution.py:103
  77.6 14.7 %collective-permute-start.3 = (bf16[2,128,256]{2,1,0:T(8,128)(2,1)S(1)}, bf16[2,128,256]{2,1,0:T(8,128)(2,1)S(1)}, u32[]{:S(2)}, u32[]{:S(2)}) collective-permute-start(bf16[2,128,256]{2,1,0:T(8,128)(2,1)S(1)} %slice.1319), channel_id=1, source_target_pairs={{0,2},{1,3},{2,0},{3,1},{4,6},{5,7},{6,4},{7,5},{8,10},{9,11},{10,... | collective-permute-start | bytes 393224 | tf_op jit(solution)/shard_map/ppermute | solution.py:103
  92.4 53.1 %collective-permute-start.4 = (bf16[1,128,256]{2,1,0:T(8,128)(2,1)S(1)}, bf16[1,128,256]{2,1,0:T(8,128)(2,1)S(1)}, u32[]{:S(2)}, u32[]{:S(2)}) collective-permute-start(bf16[1,128,256]{2,1,0:T(8,128)(2,1)S(1)} %slice.1321), channel_id=1, source_target_pairs={{0,6},{1,7},{2,4},{3,5},{4,2},{5,3},{6,0},{7,1},{8,14},{9,15},{10,... | collective-permute-start | bytes 196616 | tf_op jit(solution)/shard_map/ppermute | solution.py:103
  94.6 26.1 %collective-permute-start.19 = (bf16[8,128,256]{2,1,0:T(8,128)(2,1)S(1)}, bf16[8,128,256]{2,1,0:T(8,128)(2,1)S(1)}, u32[]{:S(2)}, u32[]{:S(2)}) collective-permute-start(bf16[8,128,256]{2,1,0:T(8,128)(2,1)S(1)} %bitcast.718), channel_id=1, source_target_pairs={{0,6},{1,7},{2,4},{3,5},{4,2},{5,3},{6,0},{7,1},{8,14},{9,15},{10,... | collective-permute-start | bytes 1572872 | tf_op jit(solution)/shard_map/ppermute | solution.py:103
  95.5 25.5 %collective-permute-start.10 = (bf16[4,128,256]{2,1,0:T(8,128)(2,1)S(1)}, bf16[4,128,256]{2,1,0:T(8,128)(2,1)S(1)}, u32[]{:S(2)}, u32[]{:S(2)}) collective-permute-start(bf16[4,128,256]{2,1,0:T(8,128)(2,1)S(1)} %slice.1342), channel_id=1, source_target_pairs={{0,8},{1,9},{2,10},{3,11},{4,12},{5,13},{6,14},{7,15},{8,0},{9,1},... | collective-permute-start | bytes 786440 | tf_op jit(solution)/shard_map/ppermute | solution.py:103
  96.3 35.6 %collective-permute-start.15 = (bf16[4,128,256]{2,1,0:T(8,128)(2,1)S(1)}, bf16[4,128,256]{2,1,0:T(8,128)(2,1)S(1)}, u32[]{:S(2)}, u32[]{:S(2)}) collective-permute-start(bf16[4,128,256]{2,1,0:T(8,128)(2,1)S(1)} %slice.1350), channel_id=1, source_target_pairs={{0,6},{1,7},{2,4},{3,5},{4,2},{5,3},{6,0},{7,1},{8,14},{9,15},{10,... | collective-permute-start | bytes 786440 | tf_op jit(solution)/shard_map/ppermute | solution.py:103
  121.1 16.5 %collective-permute-start.11 = (bf16[2,128,256]{2,1,0:T(8,128)(2,1)S(1)}, bf16[2,128,256]{2,1,0:T(8,128)(2,1)S(1)}, u32[]{:S(2)}, u32[]{:S(2)}) collective-permute-start(bf16[2,128,256]{2,1,0:T(8,128)(2,1)S(1)} %slice.1344), channel_id=1, source_target_pairs={{0,6},{1,7},{2,4},{3,5},{4,2},{5,3},{6,0},{7,1},{8,14},{9,15},{10,... | collective-permute-start | bytes 393224 | tf_op jit(solution)/shard_map/ppermute | solution.py:103
  164.6 41.2 %all-to-all-start = ((bf16[32,32,1024]{2,1,0:T(8,128)(2,1)}), bf16[32,32,1024]{2,1,0:T(8,128)(2,1)S(1)}, u32[]{:S(2)}, u32[]{:S(2)}) async-start(bf16[32,32,1024]{2,1,0:T(8,128)(2,1)} %bitcast.73), calls=%async_computation | async-start | bytes 4194304 | tf_op jit(solution)/shard_map/all_to_all | solution.py:416
  220.7 34.1 %all-to-all-start.1 = ((bf16[32,32,1024]{2,1,0:T(8,128)(2,1)}), bf16[32,32,1024]{2,1,0:T(8,128)(2,1)}, u32[]{:S(2)}, u32[]{:S(2)}) async-start(bf16[32,32,1024]{2,1,0:T(8,128)(2,1)} %bitcast.670), calls=%async_computation.1 | async-start | bytes 4194304 | tf_op jit(solution)/shard_map/all_to_all | solution.py:447
  329.6 17.9 %collective-permute-start.50 = (f32[3,32,64]{2,1,0:T(8,128)S(1)}, f32[3,32,64]{2,1,0:T(8,128)S(1)}, u32[]{:S(2)}, u32[]{:S(2)}) collective-permute-start(f32[3,32,64]{2,1,0:T(8,128)S(1)} %pad_maximum_fusion.47), channel_id=1, source_target_pairs={{0,1},{1,0},{2,3},{3,2},{4,5},{5,4},{6,7},{7,6},{8,9},{9,8},{10,11... | collective-permute-start | bytes 73736 | tf_op jit(solution)/shard_map/ppermute | solution.py:103
  357.1 36.7 %collective-permute-start.51 = (bf16[4,4,4,16,1024]{4,3,2,1,0:T(8,128)(2,1)S(1)}, bf16[4,4,4,16,1024]{4,3,2,1,0:T(8,128)(2,1)S(1)}, u32[]{:S(2)}, u32[]{:S(2)}) collective-permute-start(bf16[4,4,4,16,1024]{4,3,2,1,0:T(8,128)(2,1)S(1)} %slice_bitcast_fusion), channel_id=1, source_target_pairs={{0,1},{1,0},{2,3},{3,2},{4,5},{5,4},{6,7},{7,6},{8,9},{9,8},{10,11... | collective-permute-start | bytes 6291464 | tf_op jit(solution)/shard_map/ppermute | solution.py:103
  361.8 24.0 %collective-permute-start.112 = (bf16[1002,256]{1,0:T(8,128)(2,1)S(1)}, bf16[1002,256]{1,0:T(8,128)(2,1)S(1)}, u32[]{:S(2)}, u32[]{:S(2)}) collective-permute-start(bf16[1002,256]{1,0:T(8,128)(2,1)S(1)} %convolution_convert_fusion.13), channel_id=1, source_target_pairs={{0,64},{32,96},{64,0},{96,32},{1,65},{33,97},{65,1},{97,33},{2,66}... | collective-permute-start | bytes 1539080 | tf_op jit(solution)/shard_map/ppermute | solution.py:107
  365.7 25.1 %collective-permute-start.113 = (bf16[1002,256]{1,0:T(8,128)(2,1)S(1)}, bf16[1002,256]{1,0:T(8,128)(2,1)S(1)}, u32[]{:S(2)}, u32[]{:S(2)}) collective-permute-start(bf16[1002,256]{1,0:T(8,128)(2,1)S(1)} %convolution_convert_fusion.12), channel_id=1, source_target_pairs={{0,96},{32,64},{64,32},{96,0},{1,97},{33,65},{65,33},{97,1},{2,98}... | collective-permute-start | bytes 1539080 | tf_op jit(solution)/shard_map/ppermute | solution.py:107
  460.9 41.1 %all-to-all-start.2 = ((bf16[32,32,1024]{2,1,0:T(8,128)(2,1)}), bf16[32,32,1024]{2,1,0:T(8,128)(2,1)}, u32[]{:S(2)}, u32[]{:S(2)}) async-start(bf16[32,32,1024]{2,1,0:T(8,128)(2,1)} %bitcast.647), calls=%async_computation.2 | async-start | bytes 4194304 | tf_op jit(solution)/shard_map/all_to_all | solution.py:493
  517.3 32.9 %all-to-all-start.3 = ((bf16[32,32,1024]{2,1,0:T(8,128)(2,1)}), bf16[32,32,1024]{2,1,0:T(8,128)(2,1)S(1)}, u32[]{:S(2)}, u32[]{:S(2)}) async-start(bf16[32,32,1024]{2,1,0:T(8,128)(2,1)} %bitcast.669), calls=%async_computation.3 | async-start | bytes 4194304 | tf_op jit(solution)/shard_map/all_to_all | solution.py:539
  521.9 257.1 %reduce-scatter.2.cloned.1.call-start = ((), (), s32[]{:S(2)}) async-start(), calls=%async_computation.9 | async-start | bytes 10543104 | tf_op jit(solution)/shard_map/reduce_scatter | solution.py:531
  563.2 108.1 %collective-permute-start.114 = (bf16[3,176,1024]{2,1,0:T(8,128)(2,1)}, bf16[3,176,1024]{2,1,0:T(8,128)(2,1)S(1)}, u32[]{:S(2)}, u32[]{:S(2)}) collective-permute-start(bf16[3,176,1024]{2,1,0:T(8,128)(2,1)} %get-tuple-element.251), channel_id=1, source_target_pairs={{0,32},{32,0},{64,96},{96,64},{1,33},{33,1},{65,97},{97,65},{2,34}... | collective-permute-start | bytes 3244040 | tf_op jit(solution)/shard_map/ppermute | solution.py:107
  573.0 22.3 %collective-permute-start.88 = (bf16[1,128,256]{2,1,0:T(8,128)(2,1)S(1)}, bf16[1,128,256]{2,1,0:T(8,128)(2,1)S(1)}, u32[]{:S(2)}, u32[]{:S(2)}) collective-permute-start(bf16[1,128,256]{2,1,0:T(8,128)(2,1)S(1)} %get-tuple-element.304), channel_id=1, source_target_pairs={{0,6},{1,7},{2,4},{3,5},{4,2},{5,3},{6,0},{7,1},{8,14},{9,15},{10,... | collective-permute-start | bytes 196616 | tf_op jit(solution)/shard_map/ppermute | solution.py:103
  574.2 21.9 %collective-permute-start.93 = (bf16[128,256]{1,0:T(8,128)(2,1)}, bf16[128,256]{1,0:T(8,128)(2,1)}, u32[]{:S(2)}, u32[]{:S(2)}) collective-permute-start(bf16[128,256]{1,0:T(8,128)(2,1)} %get-tuple-element.308), channel_id=1, source_target_pairs={{0,32},{32,0},{64,96},{96,64},{1,33},{33,1},{65,97},{97,65},{2,34}... | collective-permute-start | bytes 196616 | tf_op jit(solution)/shard_map/ppermute | solution.py:107
  575.7 21.9 %collective-permute-start.99 = (bf16[128,256]{1,0:T(8,128)(2,1)}, bf16[128,256]{1,0:T(8,128)(2,1)S(1)}, u32[]{:S(2)}, u32[]{:S(2)}) collective-permute-start(bf16[128,256]{1,0:T(8,128)(2,1)} %get-tuple-element.307), channel_id=1, source_target_pairs={{0,64},{32,96},{64,0},{96,32},{1,65},{33,97},{65,1},{97,33},{2,66}... | collective-permute-start | bytes 196616 | tf_op jit(solution)/shard_map/ppermute | solution.py:107
  576.9 21.2 %collective-permute-start.105 = (bf16[128,256]{1,0:T(8,128)(2,1)}, bf16[128,256]{1,0:T(8,128)(2,1)S(1)}, u32[]{:S(2)}, u32[]{:S(2)}) collective-permute-start(bf16[128,256]{1,0:T(8,128)(2,1)} %get-tuple-element.306), channel_id=1, source_target_pairs={{0,96},{32,64},{64,32},{96,0},{1,97},{33,65},{65,33},{97,1},{2,98}... | collective-permute-start | bytes 196616 | tf_op jit(solution)/shard_map/ppermute | solution.py:107
  596.0 15.4 %collective-permute-start.89 = (bf16[2,128,256]{2,1,0:T(8,128)(2,1)S(1)}, bf16[2,128,256]{2,1,0:T(8,128)(2,1)S(1)}, u32[]{:S(2)}, u32[]{:S(2)}) collective-permute-start(bf16[2,128,256]{2,1,0:T(8,128)(2,1)S(1)} %pad_maximum_fusion.35), channel_id=1, source_target_pairs={{0,2},{1,3},{2,0},{3,1},{4,6},{5,7},{6,4},{7,5},{8,10},{9,11},{10,... | collective-permute-start | bytes 393224 | tf_op jit(solution)/shard_map/ppermute | solution.py:103
  621.3 17.4 %collective-permute-start.91 = (bf16[8,128,256]{2,1,0:T(8,128)(2,1)S(1)}, bf16[8,128,256]{2,1,0:T(8,128)(2,1)S(1)}, u32[]{:S(2)}, u32[]{:S(2)}) collective-permute-start(bf16[8,128,256]{2,1,0:T(8,128)(2,1)S(1)} %pad_maximum_fusion.8), channel_id=1, source_target_pairs={{0,8},{1,9},{2,10},{3,11},{4,12},{5,13},{6,14},{7,15},{8,0},{9,1},... | collective-permute-start | bytes 1572872 | tf_op jit(solution)/shard_map/ppermute | solution.py:103
  624.1 17.0 %collective-permute-start.97 = (bf16[8,128,256]{2,1,0:T(8,128)(2,1)S(1)}, bf16[8,128,256]{2,1,0:T(8,128)(2,1)S(1)}, u32[]{:S(2)}, u32[]{:S(2)}) collective-permute-start(bf16[8,128,256]{2,1,0:T(8,128)(2,1)S(1)} %pad_maximum_fusion.9), channel_id=1, source_target_pairs={{0,24},{1,25},{2,26},{3,27},{4,28},{5,29},{6,30},{7,31},{8,16},{9,... | collective-permute-start | bytes 1572872 | tf_op jit(solution)/shard_map/ppermute | solution.py:103
  626.4 16.9 %collective-permute-start.103 = (bf16[8,128,256]{2,1,0:T(8,128)(2,1)S(1)}, bf16[8,128,256]{2,1,0:T(8,128)(2,1)S(1)}, u32[]{:S(2)}, u32[]{:S(2)}) collective-permute-start(bf16[8,128,256]{2,1,0:T(8,128)(2,1)S(1)} %pad_maximum_fusion.10), channel_id=1, source_target_pairs={{0,2},{1,3},{2,0},{3,1},{4,6},{5,7},{6,4},{7,5},{8,10},{9,11},{10,... | collective-permute-start | bytes 1572872 | tf_op jit(solution)/shard_map/ppermute | solution.py:103
  627.2 44.3 %collective-permute-start.115 = (bf16[3,176,1024]{2,1,0:T(8,128)(2,1)S(1)}, bf16[3,176,1024]{2,1,0:T(8,128)(2,1)S(1)}, u32[]{:S(2)}, u32[]{:S(2)}) collective-permute-start(bf16[3,176,1024]{2,1,0:T(8,128)(2,1)S(1)} %copy-done.28), channel_id=1, source_target_pairs={{0,64},{32,96},{64,0},{96,32},{1,65},{33,97},{65,1},{97,33},{2,66}... | collective-permute-start | bytes 3244040 | tf_op jit(solution)/shard_map/ppermute | solution.py:107
  638.7 25.3 %collective-permute-start.68 = (bf16[512,1024]{1,0:T(8,128)(2,1)S(1)}, bf16[512,1024]{1,0:T(8,128)(2,1)S(1)}, u32[]{:S(2)}, u32[]{:S(2)}) collective-permute-start(bf16[512,1024]{1,0:T(8,128)(2,1)S(1)} %slice.1473), channel_id=1, source_target_pairs={{0,1},{1,0},{2,3},{3,2},{4,5},{5,4},{6,7},{7,6},{8,9},{9,8},{10,11... | collective-permute-start | bytes 3145736 | tf_op jit(solution)/shard_map/ppermute | solution.py:103
  641.0 14.6 %collective-permute-start.109 = (bf16[8,128,256]{2,1,0:T(8,128)(2,1)S(1)}, bf16[8,128,256]{2,1,0:T(8,128)(2,1)S(1)}, u32[]{:S(2)}, u32[]{:S(2)}) collective-permute-start(bf16[8,128,256]{2,1,0:T(8,128)(2,1)S(1)} %pad_maximum_fusion.11), channel_id=1, source_target_pairs={{0,6},{1,7},{2,4},{3,5},{4,2},{5,3},{6,0},{7,1},{8,14},{9,15},{10,... | collective-permute-start | bytes 1572872 | tf_op jit(solution)/shard_map/ppermute | solution.py:103
  643.3 23.2 %collective-permute-start.73 = (bf16[512,1024]{1,0:T(8,128)(2,1)S(1)}, bf16[512,1024]{1,0:T(8,128)(2,1)S(1)}, u32[]{:S(2)}, u32[]{:S(2)}) collective-permute-start(bf16[512,1024]{1,0:T(8,128)(2,1)S(1)} %slice.1483), channel_id=1, source_target_pairs={{0,1},{1,0},{2,3},{3,2},{4,5},{5,4},{6,7},{7,6},{8,9},{9,8},{10,11... | collective-permute-start | bytes 3145736 | tf_op jit(solution)/shard_map/ppermute | solution.py:103
  664.1 26.7 %collective-permute-start.116 = (bf16[3,176,1024]{2,1,0:T(8,128)(2,1)S(1)}, bf16[3,176,1024]{2,1,0:T(8,128)(2,1)S(1)}, u32[]{:S(2)}, u32[]{:S(2)}) collective-permute-start(bf16[3,176,1024]{2,1,0:T(8,128)(2,1)S(1)} %copy-done.27), channel_id=1, source_target_pairs={{0,96},{32,64},{64,32},{96,0},{1,97},{33,65},{65,33},{97,1},{2,98}... | collective-permute-start | bytes 3244040 | tf_op jit(solution)/shard_map/ppermute | solution.py:107
  666.5 29.8 %collective-permute-start.83 = (bf16[512,1152]{0,1:T(8,128)(2,1)S(1)}, bf16[512,1152]{0,1:T(8,128)(2,1)S(1)}, u32[]{:S(2)}, u32[]{:S(2)}) collective-permute-start(bf16[512,1152]{0,1:T(8,128)(2,1)S(1)} %pad_maximum_fusion.4), channel_id=1, source_target_pairs={{0,1},{1,0},{2,3},{3,2},{4,5},{5,4},{6,7},{7,6},{8,9},{9,8},{10,11... | collective-permute-start | bytes 3538952 | tf_op jit(solution)/shard_map/ppermute | solution.py:103
  668.6 71.3 %collective-permute-start.92 = (bf16[16,128,256]{2,1,0:T(8,128)(2,1)}, bf16[16,128,256]{2,1,0:T(8,128)(2,1)}, u32[]{:S(2)}, u32[]{:S(2)}) collective-permute-start(bf16[16,128,256]{2,1,0:T(8,128)(2,1)} %constant_dynamic-update-slice_fusion.7), channel_id=1, source_target_pairs={{0,1},{1,0},{2,3},{3,2},{4,5},{5,4},{6,7},{7,6},{8,9},{9,8},{10,11... | collective-permute-start | bytes 3145736 | tf_op jit(solution)/shard_map/ppermute | solution.py:103
  671.3 81.6 %collective-permute-start.98 = (bf16[16,128,256]{2,1,0:T(8,128)(2,1)}, bf16[16,128,256]{2,1,0:T(8,128)(2,1)}, u32[]{:S(2)}, u32[]{:S(2)}) collective-permute-start(bf16[16,128,256]{2,1,0:T(8,128)(2,1)} %constant_dynamic-update-slice_fusion.12), channel_id=1, source_target_pairs={{0,1},{1,0},{2,3},{3,2},{4,5},{5,4},{6,7},{7,6},{8,9},{9,8},{10,11... | collective-permute-start | bytes 3145736 | tf_op jit(solution)/shard_map/ppermute | solution.py:103
  671.6 30.1 %collective-permute-start.69 = (bf16[8,32,1024]{2,1,0:T(8,128)(2,1)}, bf16[8,32,1024]{2,1,0:T(8,128)(2,1)}, u32[]{:S(2)}, u32[]{:S(2)}) collective-permute-start(bf16[8,32,1024]{2,1,0:T(8,128)(2,1)} %bitcast.210), channel_id=1, source_target_pairs={{0,8},{1,9},{2,10},{3,11},{4,12},{5,13},{6,14},{7,15},{8,0},{9,1},... | collective-permute-start | bytes 1572872 | tf_op jit(solution)/shard_map/ppermute | solution.py:103
  690.8 14.2 %collective-permute-start.74 = (bf16[8,32,1024]{2,1,0:T(8,128)(2,1)}, bf16[8,32,1024]{2,1,0:T(8,128)(2,1)}, u32[]{:S(2)}, u32[]{:S(2)}) collective-permute-start(bf16[8,32,1024]{2,1,0:T(8,128)(2,1)} %bitcast.213), channel_id=1, source_target_pairs={{0,24},{1,25},{2,26},{3,27},{4,28},{5,29},{6,30},{7,31},{8,16},{9,... | collective-permute-start | bytes 1572872 | tf_op jit(solution)/shard_map/ppermute | solution.py:103
  705.0 52.8 %collective-permute-start.104 = (bf16[16,128,256]{2,1,0:T(8,128)(2,1)S(1)}, bf16[16,128,256]{2,1,0:T(8,128)(2,1)S(1)}, u32[]{:S(2)}, u32[]{:S(2)}) collective-permute-start(bf16[16,128,256]{2,1,0:T(8,128)(2,1)S(1)} %copy-done.147), channel_id=1, source_target_pairs={{0,1},{1,0},{2,3},{3,2},{4,5},{5,4},{6,7},{7,6},{8,9},{9,8},{10,11... | collective-permute-start | bytes 3145736 | tf_op jit(solution)/shard_map/ppermute | solution.py:103
  721.0 42.0 %collective-permute-start.110 = (bf16[16,128,256]{2,1,0:T(8,128)(2,1)S(1)}, bf16[16,128,256]{2,1,0:T(8,128)(2,1)S(1)}, u32[]{:S(2)}, u32[]{:S(2)}) collective-permute-start(bf16[16,128,256]{2,1,0:T(8,128)(2,1)S(1)} %copy-done.145), channel_id=1, source_target_pairs={{0,1},{1,0},{2,3},{3,2},{4,5},{5,4},{6,7},{7,6},{8,9},{9,8},{10,11... | collective-permute-start | bytes 3145736 | tf_op jit(solution)/shard_map/ppermute | solution.py:103
  738.2 14.4 %collective-permute-start.85 = (bf16[4,32,1152]{2,1,0:T(8,128)(2,1)S(1)}, bf16[4,32,1152]{2,1,0:T(8,128)(2,1)S(1)}, u32[]{:S(2)}, u32[]{:S(2)}) collective-permute-start(bf16[4,32,1152]{2,1,0:T(8,128)(2,1)S(1)} %slice.1507), channel_id=1, source_target_pairs={{0,6},{1,7},{2,4},{3,5},{4,2},{5,3},{6,0},{7,1},{8,14},{9,15},{10,... | collective-permute-start | bytes 884744 | tf_op jit(solution)/shard_map/ppermute | solution.py:103
  796.2 25.3 %all-to-all-start.6 = ((f32[128,1,128]{2,1,0:T(1,128)}), f32[128,1,128]{2,1,0:T(1,128)S(1)}, u32[]{:S(2)}, u32[]{:S(2)}) async-start(f32[128,1,128]{2,1,0:T(1,128)} %broadcast_in_dim.275), calls=%async_computation.7 | async-start | bytes 131072 | tf_op jit(solution)/shard_map/all_to_all | solution.py:649
  (251 other events, 1950.4 us)
Sparse Core Ops, SparseCore 0:
  11.7 131.5 all-gather.3
  145.6 31.6 all-gather.5
  529.3 102.1 reduce-scatter.1

commit v2 on v1

--- a/solution.py
+++ b/solution.py
@@ -1,8 +1,11 @@
+import functools
 import math
 
 import jax
 import jax.numpy as jnp
 from jax import lax
+from jax.experimental import pallas as pl
+from jax.experimental.pallas import tpu as pltpu
 from jax.sharding import PartitionSpec as P
 
 HD = 128
@@ -99,6 +102,26 @@
     return (weight, first, second)
 
 
+def tables_kernel(rate, clip, weight, grad, first, second, weight_out, first_out, second_out):
+    new = adam_update(weight[...], grad[...], first[...], second[...], rate, clip[0, 0])
+    weight_out[...], first_out[...], second_out[...] = new
+
+
+def tables_update(weight, grad, first, second, rate, clip_scale):
+    words, pair, width = weight.shape
+    rows = max(count for count in range(1, 257) if words % count == 0)
+    block = pl.BlockSpec((rows, pair, width), lambda i: (i, 0, 0))
+    return pl.pallas_call(
+        functools.partial(tables_kernel, rate),
+        grid=(words // rows,),
+        in_specs=[pl.BlockSpec(memory_space=pltpu.SMEM)] + [block] * 4,
+        out_specs=[block] * 3,
+        out_shape=[jax.ShapeDtypeStruct(weight.shape, jnp.float32)] * 3,
+        compiler_params=pltpu.CompilerParams(vmem_limit_bytes=48 * 1024 * 1024),
+        name="tables_update",
+    )(clip_scale.reshape(1, 1), weight, grad, first, second)
+
+
 def swap(value, number):
     return lax.ppermute(value, "expert", [(i, i ^ number) for i in range(32)])
 
@@ -234,11 +257,12 @@
 
 def meet_stats(stats, beside):
     for shift in (3, 1):
-        others = [flip_blocks(swap(stats, k << shift), k << shift) for k in (1, 2, 3)]
-        for other in others:
-            stats = merge_stats(stats, other)
-    other, beside = lax.optimization_barrier((swap(stats, 1), beside))
-    return merge_stats(stats, flip_blocks(other, 1)), beside
+        others = [swap(stats, k << shift) for k in (1, 2, 3)]
+        if shift == 3:
+            others = after(others, beside)
+        for k, other in enumerate(others, 1):
+            stats = merge_stats(stats, flip_blocks(other, k << shift))
+    return merge_stats(stats, flip_blocks(swap(stats, 1), 1))
 
 
 def hot(indices, count):
@@ -321,37 +345,35 @@
     down_first = packed_all[:, start : start + width_model]
     down_second = packed_all[:, start + width_model :]
 
-    local_ids = []
-    for k in range(groups):
-        group_ids = ids[0] if k == 0 else swap_group(ids, k)[0]
-        group_ids = by_distance(group_ids.reshape(axis_width, rows_dev), expert_index)
-        local_ids.append(in_order(group_ids.reshape(4, 4, 2, rows_dev) - vocab_start, k))
+    ids_all = lax.all_to_all(
+        jnp.broadcast_to(ids, (groups,) + ids.shape[1:]), "dp", split_axis=0, concat_axis=0, tiled=True
+    ).reshape(groups, axis_width, rows_dev)
+    ids_near = by_distance(ids_all.swapaxes(0, 1), expert_index) - vocab_start
+    ids_near = ids_near.reshape(4, 4, 2, groups, rows_dev)
+    ids_near = jnp.stack([in_order(ids_near[:, :, :, s], s) for s in range(groups)])
     table_words = tables[0].astype(LOW)
-    per_half = 16 * rows_dev
-
-    def look_up(streams, core):
-        wanted = jnp.concatenate([local_ids[k][:, :, core].reshape(-1) for k in streams])
-        found = product(hot(wanted, vocab_part), table_words).astype(LOW)
-        return found.reshape(len(streams), per_half, part_width)
-
-    x_first = []
-    for streams in ((0,), (1, 2, 3)):
-        sent = swap(look_up(streams, 1), 1)
-        summed = add_low(look_up(streams, 0), sent)
-        for place, k in enumerate(streams):
-            block = ordered_sum(summed[place].reshape(4, 4, rows_dev, part_width), k)
-            x_first.append(block if k == 0 else swap_group(block, k))
-    x_first = by_distance(jnp.stack(x_first), group_index)
+    looked_up = []
+    for core in (1, 0):
+        found = product(hot(ids_near[:, :, :, core].reshape(-1), vocab_part), table_words)
+        looked_up.append(found.astype(LOW).reshape(groups, 16 * rows_dev, part_width))
+    looked_up = add_low(looked_up[1], swap(looked_up[0], 1))
+    routes, loss_rows, domains, targets, documents = after(
+        (routes, loss_rows, domains, targets, documents), looked_up
+    )
+    x_first = jnp.stack(
+        [
+            ordered_sum(looked_up[s].reshape(4, 4, rows_dev, part_width), s)
+            for s in range(groups)
+        ]
+    )
+    x_first = lax.all_to_all(x_first, "dp", split_axis=0, concat_axis=0, tiled=True)
     x_first = x_first.swapaxes(0, 1).reshape(rows_dev, width_model).astype(f32)
 
     expert_part = jnp.concatenate(
         [expert_up[0].astype(LOW).swapaxes(1, 2), expert_down.astype(LOW)], axis=0
     )
-    expert_all = jnp.concatenate(
-        [expert_part] + [swap_group(expert_part, k) for k in range(1, groups)], axis=1
-    )
+    expert_all = lax.all_gather(expert_part, "dp", axis=1, tiled=True)
     w_gate, w_up, w_down = expert_all[0], expert_all[1], expert_all[2]
-    head = lax.all_gather(tables[1].astype(LOW), "dp", axis=1, tiled=True)
 
     positions = jnp.arange(rows_dev)
     experts_range = jnp.arange(experts, dtype=jnp.int32)
@@ -409,6 +431,7 @@
         "hqk,khd->qhd", probs.astype(LOW), value_low, preferred_element_type=f32
     )
     attended = attended.reshape(rows_dev, width_model).astype(LOW)
+    head = lax.all_gather(after(tables[1].astype(LOW), attended), "dp", axis=1, tiled=True)
     x_mid = x_first + product(attended, w_out)
     h_low = norm_apply(x_mid, gain_full[1]).astype(LOW)
 
@@ -424,7 +447,7 @@
     slot_gates = jnp.sum(
         jnp.where(slot_experts, pick_exact(slot_tokens, gates), 0.0), axis=1, keepdims=True
     )
-    down_rows = jnp.arange(hidden_shared, dtype=jnp.int32)
+    down_rows = after(jnp.arange(hidden_shared, dtype=jnp.int32), buffer)
     down_place = (down_rows // own_down) * own_rows + down_rows % own_down
     down_spot = jnp.where(
         down_rows % own_down < own_rows,
@@ -447,7 +470,7 @@
     returned = lax.all_to_all(expert_out, "expert", split_axis=0, concat_axis=0, tiled=True)
     is_target = target_local[:, None] == jnp.arange(vocab_part, dtype=jnp.int32)[None, :]
     target_head = product(is_target.astype(LOW), head).astype(LOW)
-    returned, target_head = lax.optimization_barrier((returned, target_head))
+    returned = after(returned, target_head)
     routed = product(gate_slots, returned).reshape(3, rows_dev, width_model)
     x_last = x_mid + shared_out + (routed[0] + routed[1] + routed[2])
 
@@ -460,7 +483,7 @@
     row_target = jnp.sum(jnp.where(is_target, logits, 0.0), axis=1)
     rest_low = jnp.where(is_target, 0.0, expos).astype(LOW)
     d_rest = product(rest_low, head)
-    stats, d_rest = meet_stats(
+    stats = meet_stats(
         jnp.stack([row_top, row_total, row_target]).reshape(3, axis_width, per_device), d_rest
     )
     log_norm = (stats[0] + jnp.log(stats[1])).reshape(-1)
@@ -469,20 +492,11 @@
     rest_scale = jnp.exp(row_top - log_norm) * grad_weights
     target_grad = (jnp.exp(stats[2].reshape(-1) - log_norm) - 1.0) * grad_weights
     d_rows_all = d_rest * rest_scale[:, None] + target_grad[:, None] * target_head.astype(f32)
-    d_chosen = expert_sum(
-        d_rows_all.astype(LOW).reshape(axis_width, per_device, width_model)
-    ).astype(f32)
+    d_rows_all = d_rows_all.astype(LOW)
     d_logits = jnp.where(
         is_target, target_grad[:, None], rest_low.astype(f32) * rest_scale[:, None]
     ).astype(LOW)
-    d_head_part = 0.0
-    for k in range(groups):
-        columns = lax.dynamic_slice_in_dim(
-            gathered, (group_index ^ k) * part_width, part_width, axis=1
-        )
-        d_columns = inner_rows(d_logits, columns).astype(LOW)
-        d_columns = d_columns if k == 0 else swap_group(d_columns, k)
-        d_head_part = d_head_part + d_columns.astype(f32)
+    d_chosen = expert_sum(d_rows_all.reshape(axis_width, per_device, width_model)).astype(f32)
 
     _, final_back = jax.vjp(norm_apply, x_last, gain_full[2])
     d_last, d_gain_last = final_back(pick_exact(own_choice.T, d_chosen))
@@ -492,17 +506,10 @@
     d_buffer = (sum(product(slot_tokens, part) for part in d_last_parts) * slot_gates).astype(LOW)
     d_rows = lax.all_to_all(d_buffer, "expert", split_axis=0, concat_axis=0, tiled=True)
 
-    d_slots = inner_cols(jnp.concatenate(d_last_parts, axis=0), returned)
-    d_slots = jnp.sum(d_slots.reshape(3, rows_dev, slots_all), axis=0) * token_slots.astype(f32)
-    d_gates = sum(inner_cols(part, spread) for part in split_three(d_slots))
-    d_scores = (d_gates - jnp.sum(gates * d_gates, axis=1, keepdims=True)) / gate_total
-    d_router_logits = jnp.where(chosen, d_scores * gate_scores * (1.0 - gate_scores), 0.0)
-    d_hmid = inner_cols(d_router_logits, w_router.astype(f32), HIGH)
-
     _, shared_back = jax.vjp(swiglu, shared_in[:, :hidden_shared], shared_in[:, hidden_shared:])
     d_gate_shared, d_up_shared = shared_back(inner_cols(d_branch, w_sdown))
     d_shared_in = jnp.concatenate([d_gate_shared, d_up_shared], axis=1).astype(LOW)
-    d_hmid = d_hmid + inner_cols(d_shared_in, w_shared)
+    d_hmid = inner_cols(d_shared_in, w_shared)
 
     features = jnp.arange(width_model, dtype=jnp.int32)
     owner, row = features // own_rows, features % own_rows
@@ -514,20 +521,39 @@
     down_seconds = hot(
         jnp.where(down_row < own_rows, -1, down_turned + down_row - own_rows), width_model
     )
-    h_mid_turned = product(h_low, turn_choice).astype(LOW)
-    d_wrouter = sum(
-        inner_rows(h_mid_turned, part) for part in split_three(d_router_logits)
-    ).astype(LOW)
-    early = jnp.concatenate(
+    early_left = after((h_low, shared_hidden), d_buffer)
+    h_mid_turned = product(early_left[0], turn_choice).astype(LOW)
+    left = jnp.concatenate(
         [
-            inner_rows(product(shared_hidden, down_firsts).astype(LOW), d_branch).astype(LOW),
-            inner_rows(product(shared_hidden, down_seconds).astype(LOW), d_branch).astype(LOW),
-            inner_rows(h_mid_turned, d_shared_in).astype(LOW),
-            jnp.pad(d_wrouter, ((0, 0), (0, -experts % 128))),
+            h_mid_turned,
+            product(early_left[1], down_firsts).astype(LOW),
+            product(early_left[1], down_seconds).astype(LOW),
         ],
-        axis=1,
-    )
-    d_rows, early = lax.optimization_barrier((d_rows, early))
+        axis=0,
+    )
+
+    def spread_out(before, value, behind):
+        return jnp.pad(value, ((0, 0), (before, behind)))
+
+    right = jnp.concatenate(
+        [
+            spread_out(0, d_shared_in, 2 * width_model),
+            spread_out(2 * hidden_shared, d_branch, width_model),
+            spread_out(2 * hidden_shared + width_model, d_branch, 0),
+        ],
+        axis=0,
+    )
+    early = inner_rows(left, right).astype(LOW)
+    d_logits, gathered = after((d_logits, gathered), d_buffer)
+    d_head = inner_rows(d_logits, gathered).astype(LOW)
+
+    def head_block(k):
+        return lax.dynamic_slice_in_dim(
+            d_head, (group_index ^ k) * part_width, part_width, axis=1
+        )
+
+    head_parts = [head_block(0), swap_group(head_block(1), 1), swap_group(head_block(3), 3)]
+    d_rows = after(d_rows, (early, head_parts[1:]))
     early = lax.psum_scatter(early, "expert", scatter_dimension=0, tiled=True)
 
     d_expert_hidden = inner_cols(d_rows, w_down)
@@ -537,6 +563,14 @@
     d_up_expert = d_up_expert.astype(LOW)
     d_sent = (product(d_gate_expert, w_gate) + product(d_up_expert, w_up)).astype(LOW)
     d_returned = lax.all_to_all(d_sent, "expert", split_axis=0, concat_axis=0, tiled=True)
+    d_last_late, returned = after((d_last_parts, returned), d_sent)
+    d_slots = inner_cols(jnp.concatenate(d_last_late, axis=0), returned)
+    d_slots = jnp.sum(d_slots.reshape(3, rows_dev, slots_all), axis=0) * token_slots.astype(f32)
+    d_gates = sum(inner_cols(part, spread) for part in split_three(d_slots))
+    d_scores = (d_gates - jnp.sum(gates * d_gates, axis=1, keepdims=True)) / gate_total
+    d_router_logits = jnp.where(chosen, d_scores * gate_scores * (1.0 - gate_scores), 0.0)
+    d_hmid = d_hmid + inner_cols(d_router_logits, w_router.astype(f32), HIGH)
+
     expert_rows, expert_hidden, d_rows = after((expert_rows, expert_hidden, d_rows), d_sent)
     d_experts = jnp.stack(
         [
@@ -545,12 +579,15 @@
             inner_rows(expert_hidden, d_rows).astype(LOW),
         ]
     )
-    d_returned, d_experts = lax.optimization_barrier((d_returned, d_experts))
-    own_hidden = hidden // groups
-    experts_part = d_experts[:, :own_hidden].astype(f32)
-    for k in range(1, groups):
-        part = swap_group(d_experts[:, k * own_hidden : (k + 1) * own_hidden], k)
-        experts_part = experts_part + part.astype(f32)
+    d_experts = d_experts.reshape(3, groups, hidden // groups, width_model)
+
+    def experts_block(k):
+        return lax.dynamic_index_in_dim(d_experts, group_index ^ k, 1, False)
+
+    expert_parts = [
+        experts_block(0), swap_group(experts_block(1), 1), swap_group(experts_block(3), 3)
+    ]
+    d_returned = after(d_returned, expert_parts[1:])
 
     d_hmid = d_hmid + product(token_slots, d_returned)
     _, mid_back = jax.vjp(norm_apply, x_mid, gain_full[1])
@@ -578,28 +615,27 @@
     d_first_part, d_gain_first = first_back(inner_cols(d_qkv, w_qkv))
     d_first = (d_mid + d_first_part).astype(LOW)
 
-    d_first_blocks = by_distance(
-        d_first.reshape(rows_dev, groups, part_width).swapaxes(0, 1), group_index
-    )
-    d_embed = 0.0
-    for k in range(groups):
-        block = d_first_blocks[k] if k == 0 else swap_group(d_first_blocks[k], k)
-        tokens = ordered_gather(block, k)
-        for core in (0, 1):
-            words = hot(local_ids[k][:, :, core].reshape(-1), vocab_part)
-            part = tokens if core == 0 else swap(tokens, 1)
-            d_embed = d_embed + inner_rows(words, part.reshape(-1, part_width))
-
-    d_qkv, d_att_in = after((d_qkv, d_att_in), d_first_blocks)
-    gain_grad = jnp.stack([d_gain_first, d_gain_mid, d_gain_last], axis=1)
-    gain_grad = jnp.pad(gain_grad, ((0, 0), (0, 128 - gain_grad.shape[1])))
+    d_first = d_first.reshape(rows_dev, groups, part_width).swapaxes(0, 1)
+    d_qkv, d_att_in = after((d_qkv, d_att_in), d_first)
+    d_first = lax.all_to_all(d_first, "dp", split_axis=0, concat_axis=0, tiled=True)
+    d_first = after(d_first, early)
+    d_tokens = lax.all_gather(
+        d_first.reshape(groups * rows_dev, part_width), "expert", axis=0, tiled=True
+    )
+    token_words = (ids_all.swapaxes(0, 1) - vocab_start).reshape(1, -1)
+    words = (token_words == jnp.arange(vocab_part, dtype=jnp.int32)[:, None]).astype(LOW)
+    d_embed = product(words, d_tokens)
+
+    gain_grad = split_three(jnp.stack([d_gain_first, d_gain_mid, d_gain_last]))
+    router_parts = split_three(d_router_logits)
+    units = jnp.eye(gains.shape[0], 128, dtype=LOW)
     late = []
     for stream, (left, right) in enumerate(
         (
+            (attended, d_att_in),
             (h_first_low, d_qkv[:, 2 * width_model :]),
             (h_first_low, d_qkv[:, width_model : 2 * width_model]),
             (h_first_low, d_qkv[:, :width_model]),
-            (attended, d_att_in),
         )
     ):
         distance = (owner % axis_width) ^ expert_index
@@ -607,38 +643,72 @@
         first_axis, second_axis = axes if stream < 2 else axes[::-1]
         spot = ((distance & 1) * 16 + first_axis * 4 + second_axis) * groups + owner // axis_width
         choice = hot(spot * own_rows + row, width_model)
+        if stream == 0:
+            left = jnp.concatenate([left, h_low, h_low], axis=0)
+            right = jnp.concatenate(
+                [
+                    spread_out(0, right, 128),
+                    spread_out(width_model, router_parts[0], 128 - experts),
+                    spread_out(width_model, router_parts[1], 128 - experts),
+                ],
+                axis=0,
+            )
+        if stream == 3:
+            left = jnp.concatenate([left, *gain_grad], axis=0)
+            right = jnp.concatenate(
+                [jnp.pad(right, ((0, 0), (0, 128)))]
+                + [jnp.pad(units, ((0, 0), (width_model, 0)))] * 3,
+                axis=0,
+            )
         left = product(left, choice).astype(LOW)
         half = width_model // 2
-        grad = inner_rows(left, right)
-        if stream == 2:
-            high, middle, _ = split_three(gain_grad)
-            gain_turned = inner_rows(choice, high) + inner_rows(choice, middle)
-            grad = jnp.concatenate([grad, gain_turned], axis=1)
-        grad = grad.astype(LOW)
-        grad = add_low(grad[:half], swap(grad[half:], 1))
-        grad = ordered_sum(grad.reshape(4, 4, groups * own_rows, -1), stream)
-        late.append(grad)
-    late = jnp.concatenate(late[:2] + [late[3], late[2]], axis=1)
-    parts = []
-    for part in (early, late):
-        part = lax.all_to_all(part, "dp", split_axis=0, concat_axis=0, tiled=True)
-        parts.append(jnp.sum(part.reshape(groups, own_rows, -1).astype(f32), axis=0))
-    early, late = parts
+        sent = swap(inner_rows(left[:, half:], right).astype(LOW), 1)
+        grad = (inner_rows(left[:, :half], right) + sent.astype(f32)).astype(LOW)
+        late.append(grad.reshape(4, 4, groups * own_rows, -1))
+    late = [grad.reshape((16,) + grad.shape[2:]) for grad in late]
+    for step in range(4):
+        if step == 1:
+            far = after((head_block(2), experts_block(2)), late)
+            far = [swap_group(part, 2) for part in far]
+        if step == 3:
+            late = after(late, far)
+        half = late[0].shape[0] // 2
+        late = [
+            add_low(grad[:half], swap(grad[half:], steps_of(stream)[step]))
+            for stream, grad in enumerate(late)
+        ]
+    late = [grad[0] for grad in late]
+    d_head_part = sum(part.astype(f32) for part in head_parts + far[:1])
+    experts_part = sum(part.astype(f32) for part in expert_parts + far[1:])
+    late_width = sum(part.shape[1] for part in late)
+    parts = lax.all_to_all(
+        jnp.concatenate(late + [early], axis=1), "dp", split_axis=0, concat_axis=0, tiled=True
+    )
+    parts = after(parts, d_embed)
+    parts = jnp.sum(parts.reshape(groups, own_rows, -1).astype(f32), axis=0)
+    late, early = parts[:, :late_width], parts[:, late_width:]
+    behind = width_model + 128
     dense_part = jnp.concatenate(
         [
-            late[:, 3 * width_model : 4 * width_model],
-            late[:, width_model : 2 * width_model],
+            late[:, 2 * width_model + behind : 3 * width_model + behind],
+            late[:, width_model + behind : 2 * width_model + behind],
+            late[:, behind : width_model + behind],
             late[:, :width_model],
-            late[:, 2 * width_model : 3 * width_model],
-            early[:, 2 * width_model : 2 * width_model + 2 * hidden_shared + experts],
+            early[:, : 2 * hidden_shared],
+            late[:, width_model : width_model + experts],
         ],
         axis=1,
     )
+    start = 2 * hidden_shared
     shared_part = jnp.concatenate(
-        [early[:, :width_model], early[: own_down - own_rows, width_model : 2 * width_model]],
+        [
+            early[:, start : start + width_model],
+            early[: own_down - own_rows, start + width_model :],
+        ],
         axis=0,
     )
-    gains_part = late[:, 4 * width_model : 4 * width_model + gains.shape[0]].T
+    start = 3 * width_model + behind
+    gains_part = late[:, start : start + gains.shape[0]].T
     up_part = experts_part[:2]
     down_part = experts_part[2:]
 
@@ -672,7 +742,8 @@
     updated = []
     for index in range(6):
         state = [turn(index, value[index]) for value in (masters, firsts, seconds)]
-        new = adam_update(state[0], grads[index], *state[1:], RATES[index], clip_scale)
+        update = tables_update if index == 3 else adam_update
+        new = update(state[0], grads[index], *state[1:], RATES[index], clip_scale)
         updated.append(tuple(turn_back(index, value) for value in new))
     mean_load = jnp.sum(counts_all) / experts
     bias_new = expert_bias + BIAS_RATE * jnp.sign(mean_load - counts_all)

time: 868 us -> 678 us (0.78)
  waiting for transfers between devices: 245 us -> 146 us
  matrix products: 237 us -> 195 us
  starting transfers between devices: 185 us -> 155 us
  local copies, waits for them, and re-layouts: 65.1 us -> 40.4 us
  other arithmetic: 98.6 us -> 88.6 us
  blocking collectives: 0 us -> 8.77 us
    dot_general x27 -> x13, matrix products: 77.4 us -> 28.2 us  [inner_rows(): lax.dot_general(left, right, (((0,), (0,)), ((), ())), precision=precisio...]
    ppermute x99 -> x78, waiting for transfers between devices: 129 us -> 83 us  [swap(): return lax.ppermute(value, 'expert', [(i, i ^ number) for i in range(32)])]
    ppermute x18 -> x6, starting transfers between devices: 24.6 us -> 3.87 us  [swap_group(): return lax.ppermute(value, 'dp', [(i, i ^ number) for i in range(4)])]
    ppermute x18 -> x6, waiting for transfers between devices: 48.4 us -> 28.7 us  [swap_group(): return lax.ppermute(value, 'dp', [(i, i ^ number) for i in range(4)])]
    all_to_all x1, waiting for transfers between devices: 18.1 us -> 1.36 us  [body(): lax.all_to_all(d_buffer, 'expert', split_axis=0, concat_axis=0, tiled=True)]
    concatenate x22 -> x1, other arithmetic: 14.6 us -> 0.05 us  [body(): jnp.concatenate([d_gate_shared, d_up_shared], axis=1).astype(LOW)]
    dot_general x34 -> x39, matrix products: 103 us -> 115 us  [product(): return jnp.dot(left, right, preferred_element_type=jnp.float32)]
    ppermute x99 -> x78, starting transfers between devices: 100 us -> 88.8 us  [swap(): return lax.ppermute(value, 'expert', [(i, i ^ number) for i in range(32)])]
  transfers between devices with their start and end apart: 127 -> 97, of which waited for: 50 -> 49; matrix products, arithmetic and copies ran while one was open for 30% -> 36% of each run, Pallas kernels for 0% -> 0%
where the time goes in v2:
time: 678 us; the launch traced here: 667 us
  matrix products  195 us (29%)
  starting transfers between devices  155 us (23%)
  waiting for transfers between devices  146 us (22%)
  other arithmetic  88.6 us (13%)
  local copies, waits for them, and re-layouts  40.4 us (6%)
  between operations  25.7 us (4%)
  blocking collectives  8.77 us (1%)
  Pallas kernels  7.03 us (1%)
    dot_general x39, matrix products, product(): return jnp.dot(left, right, preferred_element_type=jnp.float32)  115 us
    ppermute x78, starting transfers between devices, swap(): return lax.ppermute(value, 'expert', [(i, i ^ number) for i in range(32)])  88.8 us
    ppermute x78, waiting for transfers between devices, swap(): return lax.ppermute(value, 'expert', [(i, i ^ number) for i in range(32)])  83 us
    dot_general x13, matrix products, inner_cols(): lax.dot_general(left, right, (((1,), (1,)), ((), ())), precision=precisio...  44.5 us
    ppermute x6, waiting for transfers between devices, swap_group(): return lax.ppermute(value, 'dp', [(i, i ^ number) for i in range(4)])  28.7 us
    dot_general x13, matrix products, inner_rows(): lax.dot_general(left, right, (((0,), (0,)), ((), ())), precision=precisio...  28.2 us
    unnamed x358, local copies, waits for them, and re-layouts  19.2 us
    all_to_all x1, starting transfers between devices, body(): lax.all_to_all(jnp.broadcast_to(sums[None], (devices, 128)), BOTH, split_...  14.5 us
  transfers between devices with their start and end apart: 97, of which 49 were waited for; matrix products, arithmetic and copies ran while one was open for 36% of the time, Pallas kernels for 0%

profile of v2, /device:TPU:1, one launch (start us, length us, event | category | flops | bytes accessed | tf_op | source)
XLA Modules:
  0.0 666.5 jit_solution(3586861279131184240)
XLA Ops:
  12.0 5.9 all-to-all-start
  23.0 8.4 %fusion.7 = bf16[8192,256]{1,0:T(8,128)(2,1)} fusion(s32[8192]{0:T(1024)S(1)} %bitcast.760, bf16[2,1002,256]{2,1,0:T(8,128)(2,1)S(1)} %copy.547), kind=kOutput, calls=%fused_computation.13 | convolution fusion | flops 4212998144 | bytes 4743168 | tf_op jit(solution)/shard_map/dot_general | solution.py:33
  37.2 7.4 %fusion.8 = bf16[8192,256]{1,0:T(8,128)(2,1)S(1)} fusion(s32[8192]{0:T(1024)S(1)} %bitcast.759, bf16[2,1002,256]{2,1,0:T(8,128)(2,1)S(1)} %copy.547), kind=kOutput, calls=%fused_computation.14 | convolution fusion | flops 4212998144 | bytes 4743168 | tf_op jit(solution)/shard_map/dot_general | solution.py:33
  58.2 10.8 %collective-permute-done.13 = bf16[8,128,256]{2,1,0:T(8,128)(2,1)} collective-permute-done((bf16[8,128,256]{2,1,0:T(8,128)(2,1)}, bf16[8,128,256]{2,1,0:T(8,128)(2,1)}, u32[]{:S(2)}, u32[]{:S(2)}) %collective-permute-start.13) | collective-permute-done | bytes 524320 | tf_op jit(solution)/shard_map/ppermute | solution.py:126
  78.4 5.2 collective-permute-done.14
  91.7 5.2 collective-permute-done.15
  106.1 4.2 all-to-all-start.1
  110.9 5.0 all-to-all-done.1
  118.2 4.1 fusion.24
  132.0 9.0 %all-to-all-start.2 = ((bf16[32,32,1024]{2,1,0:T(8,128)(2,1)}), bf16[32,32,1024]{2,1,0:T(8,128)(2,1)}, u32[]{:S(2)}, u32[]{:S(2)}) async-start(bf16[32,32,1024]{2,1,0:T(8,128)(2,1)} %bitcast.62), calls=%async_computation.2 | async-start | bytes 4194304 | tf_op jit(solution)/shard_map/all_to_all | solution.py:439
  153.1 6.8 %fusion.16 = f32[1408,1024]{1,0:T(8,128)} fusion(pred[1408,2048]{1,0:T(32,128)(4,1)S(1)} %iota_compare_fusion.6, bf16[1024,9088]{1,0:T(8,128)(2,1)} %all-gather.5.cloned.1.call-done), kind=kOutput, calls=%fused_computation.35 | convolution fusion | flops 2952790016 | bytes 9306112 | tf_op jit(solution)/shard_map/dot_general | solution.py:33
  161.2 8.3 %all-to-all-done.2 = bf16[32,32,1024]{2,1,0:T(8,128)(2,1)} async-done(((bf16[32,32,1024]{2,1,0:T(8,128)(2,1)}), bf16[32,32,1024]{2,1,0:T(8,128)(2,1)}, u32[]{:S(2)}, u32[]{:S(2)}) %all-to-all-start.2) | async-done | bytes 2097184 | tf_op jit(solution)/shard_map/all_to_all | solution.py:439
  169.4 3.8 fusion.81
  173.3 6.1 multiply_convert_fusion.2
  182.7 5.2 all-to-all-start.3
  190.0 7.2 %add_convert_fusion.1 = bf16[1408,1024]{1,0:T(8,128)(2,1)} fusion(f32[1408,1024]{1,0:T(8,128)} %fusion.16, pred[1408,2048]{1,0:T(32,128)(4,1)S(1)} %iota_compare_fusion.6, bf16[1024,9088]{1,0:T(8,128)(2,1)} %all-gather.5.cloned.1.call-done), kind=kOutput, calls=%fused_computation.34 | convolution fusion | flops 2955673600 | bytes 12189696 | tf_op jit(solution)/shard_map/dot_general | solution.py:33
  197.2 7.8 %fusion.37 = bf16[2048,1024]{1,0:T(8,128)(2,1)} fusion(bf16[1002,1024]{1,0:T(8,128)(2,1)} %all-gather.9.cloned.1.call-done, s32[2048]{0:T(1024)S(1)} %sub.559), kind=kOutput, calls=%fused_computation.69 | convolution fusion | flops 4206841856 | bytes 6254592 | tf_op jit(solution)/shard_map/dot_general | solution.py:33
  205.0 11.3 %all-to-all-done.3 = bf16[32,32,1024]{2,1,0:T(8,128)(2,1)} async-done(((bf16[32,32,1024]{2,1,0:T(8,128)(2,1)}), bf16[32,32,1024]{2,1,0:T(8,128)(2,1)}, u32[]{:S(2)}, u32[]{:S(2)}) %all-to-all-start.3) | async-done | bytes 2097184 | tf_op jit(solution)/shard_map/all_to_all | solution.py:470
  244.0 7.1 %collective-permute-start.33 = (bf16[4,4,4,16,1024]{4,3,0,1,2:T(8,128)(2,1)}, bf16[4,4,4,16,1024]{4,3,0,1,2:T(8,128)(2,1)}, u32[]{:S(2)}, u32[]{:S(2)}) collective-permute-start(bf16[4,4,4,16,1024]{4,3,0,1,2:T(8,128)(2,1)} %get-tuple-element.305), channel_id=1, source_target_pairs={{0,1},{1,0},{2,3},{3,2},{4,5},{5,4},{6,7},{7,6},{8,9},{9,8},{10,11... | collective-permute-start | bytes 6291464 | tf_op jit(solution)/shard_map/ppermute | solution.py:126
  259.1 6.8 %fusion.395 = (f32[2048]{0:T(1024)S(1)}, f32[2048,1002]{0,1:T(8,128)}) fusion(bf16[2048,1024]{1,0:T(8,128)(2,1)S(1)} %bitcast.606, bf16[1002,1024]{1,0:T(8,128)(2,1)S(1)} %copy-done.158), kind=kOutput, calls=%fused_computation.797 | convolution fusion | flops 4204742656 | bytes 14462976 | tf_op jit(solution)/shard_map/dot_general | solution.py:47
  265.9 4.6 select_reduce_fusion
  274.5 11.9 %fusion.213 = f32[2048,1024]{1,0:T(8,128)} fusion(bf16[1002,1024]{1,0:T(8,128)(2,1)} %all-gather.9.cloned.1.call-done, f32[2048,1002]{0,1:T(8,128)} %get-tuple-element.445, f32[2048]{0:T(1024)S(1)} %get-tuple-element.444, s32[2048]{0:T(1024)S(1)} %sub.559), kind=kOutput, calls=%fused_computation.439 | convolution fusion | flops 4210900992 | bytes 18665472 | tf_op jit(solution)/shard_map/dot_general | solution.py:33
  299.7 5.3 add_convert_fusion
  314.7 5.3 collective-permute-done.54
  350.2 8.2 %convolution_convert_fusion = bf16[1024,4864]{1,0:T(8,128)(2,1)} fusion(bf16[128,1024]{1,0:T(8,128)(2,1)S(1)} %get-tuple-element.75, bf16[128,2816]{1,0:T(8,128)(2,1)S(1)} %pad_maximum_fusion.6, bf16[128,1024]{1,0:T(8,128)(2,1)S(1)} %fusion.99, bf16[128,1024]{1,0:T(8,128)(2,1)S(1)} %fusion.100, bf16[128,1024]{1,0:T(8,128)(2,1)S(1)} %fusion.98), kind=kOutput, calls=%fused_computation.15 | convolution fusion | flops 3858694144 | bytes 11730944 | tf_op jit(solution)/shard_map/dot_general | solution.py:37
  358.4 10.4 %all-to-all-start.4 = ((bf16[32,32,1024]{2,1,0:T(8,128)(2,1)}), bf16[32,32,1024]{2,1,0:T(8,128)(2,1)}, u32[]{:S(2)}, u32[]{:S(2)}) async-start(bf16[32,32,1024]{2,1,0:T(8,128)(2,1)} %bitcast.598), calls=%async_computation.4 | async-start | bytes 4194304 | tf_op jit(solution)/shard_map/all_to_all | solution.py:507
  368.9 5.4 select_convert_fusion
  374.3 4.6 convolution_convert_fusion.5
  382.1 6.0 fusion.26
  388.1 6.6 collective-permute-done.58
  397.0 6.6 multiply_convert_fusion.1
  403.7 4.3 fusion.80
  408.0 4.7 add_convert_fusion.2
  412.7 7.2 %all-to-all-start.5 = ((bf16[32,32,1024]{2,1,0:T(8,128)(2,1)}), bf16[32,32,1024]{2,1,0:T(8,128)(2,1)}, u32[]{:S(2)}, u32[]{:S(2)}) async-start(bf16[32,32,1024]{2,1,0:T(8,128)(2,1)} %bitcast.614), calls=%async_computation.5 | async-start | bytes 4194304 | tf_op jit(solution)/shard_map/all_to_all | solution.py:565
  420.4 3.8 convolution_convert_fusion.7
  442.3 17.5 %collective-permute-done.60 = bf16[3,176,1024]{2,1,0:T(8,128)(2,1)} collective-permute-done((bf16[3,176,1024]{2,1,0:T(8,128)(2,1)}, bf16[3,176,1024]{2,1,0:T(8,128)(2,1)}, u32[]{:S(2)}, u32[]{:S(2)}) %collective-permute-start.60) | collective-permute-done | bytes 1081376 | tf_op jit(solution)/shard_map/ppermute | solution.py:130
  473.3 5.8 multiply_reduce_fusion.6
  479.4 8.8 %all_to_all.79 = bf16[4,128,256]{2,1,0:T(8,128)(2,1)} all-to-all(bf16[4,128,256]{2,1,0:T(8,128)(2,1)S(1)} %bitcast.633), channel_id=1, replica_groups=mesh['dp'=4,'expert'=32] {'dp'}, dimensions={0} | all-to-all | bytes 524288 | tf_op jit(solution)/shard_map/all_to_all | solution.py:620
  513.2 8.4 %collective-permute-done.67 = bf16[8,32,1024]{2,1,0:T(8,128)(2,1)S(1)} collective-permute-done((bf16[8,32,1024]{2,1,0:T(8,128)(2,1)S(1)}, bf16[8,32,1024]{2,1,0:T(8,128)(2,1)S(1)}, u32[]{:S(2)}, u32[]{:S(2)}) %collective-permute-start.67) | collective-permute-done | bytes 524320 | tf_op jit(solution)/shard_map/ppermute | solution.py:126
  529.0 6.7 %collective-permute-done.68 = bf16[4,32,1024]{2,1,0:T(8,128)(2,1)S(1)} collective-permute-done((bf16[4,32,1024]{2,1,0:T(8,128)(2,1)S(1)}, bf16[4,32,1024]{2,1,0:T(8,128)(2,1)S(1)}, u32[]{:S(2)}, u32[]{:S(2)}) %collective-permute-start.68) | collective-permute-done | bytes 262176 | tf_op jit(solution)/shard_map/ppermute | solution.py:126
  542.2 5.4 collective-permute-done.69
  575.3 4.4 all-to-all-start.6
  579.7 14.5 %multiply_reduce_fusion.2 = (f32[]{:T(128)}, f32[1002,256]{1,0:T(8,128)}) fusion(bf16[16384,256]{1,0:T(8,128)(2,1)} %all-gather.11.cloned.1.call-done, s32[16384]{0:T(1024)S(1)} %bitcast.723), kind=kOutput, calls=%fused_computation.218 | convolution fusion | flops 8422315008 | bytes 9480196 | tf_op jit(solution)/shard_map/dot_general | solution.py:33
  606.2 14.5 %all-to-all-start.8 = ((f32[128,1,128]{2,1,0:T(1,128)}), f32[128,1,128]{2,1,0:T(1,128)S(1)}, u32[]{:S(2)}, u32[]{:S(2)}) async-start(f32[128,1,128]{2,1,0:T(1,128)} %broadcast_in_dim.258), calls=%async_computation.9 | async-start | bytes 131072 | tf_op jit(solution)/shard_map/all_to_all | solution.py:719
  620.8 4.4 pad_maximum_fusion.3.grad
  625.1 5.1 all-to-all-done.8
  638.8 5.1 fusion.200
  651.4 7.0 %tables_update.1 = (f32[1002,2,256]{2,1,0:T(2,128)}, f32[1002,2,256]{2,1,0:T(2,128)}, f32[1002,2,256]{2,1,0:T(2,128)}) custom-call(f32[1,1]{1,0:T(1,128)} %bitcast.241.clip, f32[1002,2,256]{2,1,0:T(2,128)S(1)} %bitcast.594, f32[1002,2,256]{2,1,0:T(2,128)S(1)} %copy-done.1, f32[1002,2,256]{2,1,0:T(2,128)S(1)} %bitcast.595, f32[1002,2,256]{2,1,0:T(2,128)} %bitcast.621), custom_call_target="tpu_custom_call" | custom-call | tf_op jit(solution)/shard_map/tables_update/pallas_call | solution.py:114
  (943 shorter events, 302.5 us)
Async XLA Ops:
  7.2 109.0 %all-gather.5.cloned.1.call-start = ((), (), s32[]{:S(2)}) async-start(), calls=%async_computation.10 | async-start | bytes 18757632 | tf_op jit(solution)/shard_map/all_gather | solution.py:337
  12.0 10.3 %all-to-all-start = ((s32[4,1,4096]{2,1,0:T(1,128)}), s32[4,1,4096]{2,1,0:T(1,128)S(1)}, u32[]{:S(2)}, u32[]{:S(2)}) async-start(s32[4,1,4096]{2,1,0:T(1,128)} %broadcast_in_dim.236), calls=%async_computation | async-start | bytes 131072 | tf_op jit(solution)/shard_map/all_to_all | solution.py:348
  17.9 143.3 %all-gather.7.cloned.1.call-start = ((), (), s32[]{:S(2)}) async-start(), calls=%async_computation.11 | async-start | bytes 5406720 | tf_op jit(solution)/shard_map/all_gather | solution.py:375
  31.4 13.2 %collective-permute-start = (bf16[4,2048,256]{2,1,0:T(8,128)(2,1)}, bf16[4,2048,256]{2,1,0:T(8,128)(2,1)}, u32[]{:S(2)}, u32[]{:S(2)}) collective-permute-start(bf16[4,2048,256]{2,1,0:T(8,128)(2,1)} %bitcast.31), channel_id=1, source_target_pairs={{0,1},{1,0},{2,3},{3,2},{4,5},{5,4},{6,7},{7,6},{8,9},{9,8},{10,11... | collective-permute-start | bytes 12582920 | tf_op jit(solution)/shard_map/ppermute | solution.py:126
  49.7 19.2 %collective-permute-start.13 = (bf16[8,128,256]{2,1,0:T(8,128)(2,1)}, bf16[8,128,256]{2,1,0:T(8,128)(2,1)}, u32[]{:S(2)}, u32[]{:S(2)}) collective-permute-start(bf16[8,128,256]{2,1,0:T(8,128)(2,1)} %bitcast.39), channel_id=1, source_target_pairs={{0,6},{1,7},{2,4},{3,5},{4,2},{5,3},{6,0},{7,1},{8,14},{9,15},{10,... | collective-permute-start | bytes 1572872 | tf_op jit(solution)/shard_map/ppermute | solution.py:126
  52.6 17.7 %collective-permute-start.9 = (bf16[8,128,256]{2,1,0:T(8,128)(2,1)}, bf16[8,128,256]{2,1,0:T(8,128)(2,1)}, u32[]{:S(2)}, u32[]{:S(2)}) collective-permute-start(bf16[8,128,256]{2,1,0:T(8,128)(2,1)} %bitcast.37), channel_id=1, source_target_pairs={{0,2},{1,3},{2,0},{3,1},{4,6},{5,7},{6,4},{7,5},{8,10},{9,11},{10,... | collective-permute-start | bytes 1572872 | tf_op jit(solution)/shard_map/ppermute | solution.py:126
  52.6 20.3 %collective-permute-start.5 = (bf16[8,128,256]{2,1,0:T(8,128)(2,1)}, bf16[8,128,256]{2,1,0:T(8,128)(2,1)}, u32[]{:S(2)}, u32[]{:S(2)}) collective-permute-start(bf16[8,128,256]{2,1,0:T(8,128)(2,1)} %bitcast.35), channel_id=1, source_target_pairs={{0,24},{1,25},{2,26},{3,27},{4,28},{5,29},{6,30},{7,31},{8,16},{9,... | collective-permute-start | bytes 1572872 | tf_op jit(solution)/shard_map/ppermute | solution.py:126
  55.0 20.3 %collective-permute-start.1 = (bf16[8,128,256]{2,1,0:T(8,128)(2,1)}, bf16[8,128,256]{2,1,0:T(8,128)(2,1)}, u32[]{:S(2)}, u32[]{:S(2)}) collective-permute-start(bf16[8,128,256]{2,1,0:T(8,128)(2,1)} %bitcast.33), channel_id=1, source_target_pairs={{0,8},{1,9},{2,10},{3,11},{4,12},{5,13},{6,14},{7,15},{8,0},{9,1},... | collective-permute-start | bytes 1572872 | tf_op jit(solution)/shard_map/ppermute | solution.py:126
  70.2 13.4 %collective-permute-start.14 = (bf16[4,128,256]{2,1,0:T(8,128)(2,1)S(1)}, bf16[4,128,256]{2,1,0:T(8,128)(2,1)S(1)}, u32[]{:S(2)}, u32[]{:S(2)}) collective-permute-start(bf16[4,128,256]{2,1,0:T(8,128)(2,1)S(1)} %slice.1361), channel_id=1, source_target_pairs={{0,2},{1,3},{2,0},{3,1},{4,6},{5,7},{6,4},{7,5},{8,10},{9,11},{10,... | collective-permute-start | bytes 786440 | tf_op jit(solution)/shard_map/ppermute | solution.py:126
  71.7 14.9 %collective-permute-start.10 = (bf16[4,128,256]{2,1,0:T(8,128)(2,1)S(1)}, bf16[4,128,256]{2,1,0:T(8,128)(2,1)S(1)}, u32[]{:S(2)}, u32[]{:S(2)}) collective-permute-start(bf16[4,128,256]{2,1,0:T(8,128)(2,1)S(1)} %slice.1353), channel_id=1, source_target_pairs={{0,6},{1,7},{2,4},{3,5},{4,2},{5,3},{6,0},{7,1},{8,14},{9,15},{10,... | collective-permute-start | bytes 786440 | tf_op jit(solution)/shard_map/ppermute | solution.py:126
  74.1 13.6 %collective-permute-start.6 = (bf16[4,128,256]{2,1,0:T(8,128)(2,1)S(1)}, bf16[4,128,256]{2,1,0:T(8,128)(2,1)S(1)}, u32[]{:S(2)}, u32[]{:S(2)}) collective-permute-start(bf16[4,128,256]{2,1,0:T(8,128)(2,1)S(1)} %slice.1345), channel_id=1, source_target_pairs={{0,8},{1,9},{2,10},{3,11},{4,12},{5,13},{6,14},{7,15},{8,0},{9,1},... | collective-permute-start | bytes 786440 | tf_op jit(solution)/shard_map/ppermute | solution.py:126
  76.5 14.7 %collective-permute-start.2 = (bf16[4,128,256]{2,1,0:T(8,128)(2,1)S(1)}, bf16[4,128,256]{2,1,0:T(8,128)(2,1)S(1)}, u32[]{:S(2)}, u32[]{:S(2)}) collective-permute-start(bf16[4,128,256]{2,1,0:T(8,128)(2,1)S(1)} %slice.1337), channel_id=1, source_target_pairs={{0,24},{1,25},{2,26},{3,27},{4,28},{5,29},{6,30},{7,31},{8,16},{9,... | collective-permute-start | bytes 786440 | tf_op jit(solution)/shard_map/ppermute | solution.py:126
  83.7 13.2 %collective-permute-start.15 = (bf16[2,128,256]{2,1,0:T(8,128)(2,1)S(1)}, bf16[2,128,256]{2,1,0:T(8,128)(2,1)S(1)}, u32[]{:S(2)}, u32[]{:S(2)}) collective-permute-start(bf16[2,128,256]{2,1,0:T(8,128)(2,1)S(1)} %slice.1363), channel_id=1, source_target_pairs={{0,24},{1,25},{2,26},{3,27},{4,28},{5,29},{6,30},{7,31},{8,16},{9,... | collective-permute-start | bytes 393224 | tf_op jit(solution)/shard_map/ppermute | solution.py:126
  86.7 10.3 %collective-permute-start.11 = (bf16[2,128,256]{2,1,0:T(8,128)(2,1)S(1)}, bf16[2,128,256]{2,1,0:T(8,128)(2,1)S(1)}, u32[]{:S(2)}, u32[]{:S(2)}) collective-permute-start(bf16[2,128,256]{2,1,0:T(8,128)(2,1)S(1)} %slice.1355), channel_id=1, source_target_pairs={{0,8},{1,9},{2,10},{3,11},{4,12},{5,13},{6,14},{7,15},{8,0},{9,1},... | collective-permute-start | bytes 393224 | tf_op jit(solution)/shard_map/ppermute | solution.py:126
  87.8 11.2 %collective-permute-start.7 = (bf16[2,128,256]{2,1,0:T(8,128)(2,1)S(1)}, bf16[2,128,256]{2,1,0:T(8,128)(2,1)S(1)}, u32[]{:S(2)}, u32[]{:S(2)}) collective-permute-start(bf16[2,128,256]{2,1,0:T(8,128)(2,1)S(1)} %slice.1347), channel_id=1, source_target_pairs={{0,6},{1,7},{2,4},{3,5},{4,2},{5,3},{6,0},{7,1},{8,14},{9,15},{10,... | collective-permute-start | bytes 393224 | tf_op jit(solution)/shard_map/ppermute | solution.py:126
  106.1 9.8 %all-to-all-start.1 = ((bf16[4,128,256]{2,1,0:T(8,128)(2,1)}), bf16[4,128,256]{2,1,0:T(8,128)(2,1)S(1)}, u32[]{:S(2)}, u32[]{:S(2)}) async-start(bf16[4,128,256]{2,1,0:T(8,128)(2,1)} %pad_maximum_fusion.8), calls=%async_computation.1 | async-start | bytes 524288 | tf_op jit(solution)/shard_map/all_to_all | solution.py:369
  132.0 37.4 %all-to-all-start.2 = ((bf16[32,32,1024]{2,1,0:T(8,128)(2,1)}), bf16[32,32,1024]{2,1,0:T(8,128)(2,1)}, u32[]{:S(2)}, u32[]{:S(2)}) async-start(bf16[32,32,1024]{2,1,0:T(8,128)(2,1)} %bitcast.62), calls=%async_computation.2 | async-start | bytes 4194304 | tf_op jit(solution)/shard_map/all_to_all | solution.py:439
  141.1 56.2 %all-gather.9.cloned.1.call-start = ((), (), s32[]{:S(2)}) async-start(), calls=%async_computation.12 | async-start | bytes 2580480 | tf_op jit(solution)/shard_map/all_gather | solution.py:434
  182.7 33.6 %all-to-all-start.3 = ((bf16[32,32,1024]{2,1,0:T(8,128)(2,1)}), bf16[32,32,1024]{2,1,0:T(8,128)(2,1)}, u32[]{:S(2)}, u32[]{:S(2)}) async-start(bf16[32,32,1024]{2,1,0:T(8,128)(2,1)} %bitcast.615), calls=%async_computation.3 | async-start | bytes 4194304 | tf_op jit(solution)/shard_map/all_to_all | solution.py:470
  187.9 300.3 %reduce-scatter.2.cloned.1.call-start = ((), (), s32[]{:S(2)}) async-start(), calls=%async_computation.13 | async-start | bytes 10272768 | tf_op jit(solution)/shard_map/reduce_scatter | solution.py:557
  244.0 11.5 %collective-permute-start.33 = (bf16[4,4,4,16,1024]{4,3,0,1,2:T(8,128)(2,1)}, bf16[4,4,4,16,1024]{4,3,0,1,2:T(8,128)(2,1)}, u32[]{:S(2)}, u32[]{:S(2)}) collective-permute-start(bf16[4,4,4,16,1024]{4,3,0,1,2:T(8,128)(2,1)} %get-tuple-element.305), channel_id=1, source_target_pairs={{0,1},{1,0},{2,3},{3,2},{4,5},{5,4},{6,7},{7,6},{8,9},{9,8},{10,11... | collective-permute-start | bytes 6291464 | tf_op jit(solution)/shard_map/ppermute | solution.py:126
  270.6 15.8 %collective-permute-start.34 = (f32[3,32,64]{2,1,0:T(8,128)S(1)}, f32[3,32,64]{2,1,0:T(8,128)S(1)}, u32[]{:S(2)}, u32[]{:S(2)}) collective-permute-start(f32[3,32,64]{2,1,0:T(8,128)S(1)} %constant_dynamic-update-slice_fusion), channel_id=1, source_target_pairs={{0,8},{1,9},{2,10},{3,11},{4,12},{5,13},{6,14},{7,15},{8,0},{9,1},... | collective-permute-start | bytes 73736 | tf_op jit(solution)/shard_map/ppermute | solution.py:126
  270.7 15.8 %collective-permute-start.35 = (f32[3,32,64]{2,1,0:T(8,128)S(1)}, f32[3,32,64]{2,1,0:T(8,128)S(1)}, u32[]{:S(2)}, u32[]{:S(2)}) collective-permute-start(f32[3,32,64]{2,1,0:T(8,128)S(1)} %constant_dynamic-update-slice_fusion), channel_id=1, source_target_pairs={{0,16},{1,17},{2,18},{3,19},{4,20},{5,21},{6,22},{7,23},{8,24},{9,... | collective-permute-start | bytes 73736 | tf_op jit(solution)/shard_map/ppermute | solution.py:126
  273.4 13.0 %collective-permute-start.36 = (f32[3,32,64]{2,1,0:T(8,128)S(1)}, f32[3,32,64]{2,1,0:T(8,128)S(1)}, u32[]{:S(2)}, u32[]{:S(2)}) collective-permute-start(f32[3,32,64]{2,1,0:T(8,128)S(1)} %constant_dynamic-update-slice_fusion), channel_id=1, source_target_pairs={{0,24},{1,25},{2,26},{3,27},{4,28},{5,29},{6,30},{7,31},{8,16},{9,... | collective-permute-start | bytes 73736 | tf_op jit(solution)/shard_map/ppermute | solution.py:126
  310.9 9.1 %collective-permute-start.54 = (bf16[2,4,16,1024]{3,2,0,1:T(8,128)(2,1)S(1)}, bf16[2,4,16,1024]{3,2,0,1:T(8,128)(2,1)S(1)}, u32[]{:S(2)}, u32[]{:S(2)}) collective-permute-start(bf16[2,4,16,1024]{3,2,0,1:T(8,128)(2,1)S(1)} %pad_maximum_fusion.16), channel_id=1, source_target_pairs={{0,6},{1,7},{2,4},{3,5},{4,2},{5,3},{6,0},{7,1},{8,14},{9,15},{10,... | collective-permute-start | bytes 786440 | tf_op jit(solution)/shard_map/ppermute | solution.py:126
  313.0 9.1 %collective-permute-start.46 = (bf16[2,4,16,1024]{3,2,1,0:T(8,128)(2,1)S(1)}, bf16[2,4,16,1024]{3,2,1,0:T(8,128)(2,1)S(1)}, u32[]{:S(2)}, u32[]{:S(2)}) collective-permute-start(bf16[2,4,16,1024]{3,2,1,0:T(8,128)(2,1)S(1)} %pad_maximum_fusion.15), channel_id=1, source_target_pairs={{0,24},{1,25},{2,26},{3,27},{4,28},{5,29},{6,30},{7,31},{8,16},{9,... | collective-permute-start | bytes 786440 | tf_op jit(solution)/shard_map/ppermute | solution.py:126
  358.4 38.5 %all-to-all-start.4 = ((bf16[32,32,1024]{2,1,0:T(8,128)(2,1)}), bf16[32,32,1024]{2,1,0:T(8,128)(2,1)}, u32[]{:S(2)}, u32[]{:S(2)}) async-start(bf16[32,32,1024]{2,1,0:T(8,128)(2,1)} %bitcast.598), calls=%async_computation.4 | async-start | bytes 4194304 | tf_op jit(solution)/shard_map/all_to_all | solution.py:507
  381.2 13.4 %collective-permute-start.58 = (bf16[1002,256]{1,0:T(8,128)(2,1)S(1)}, bf16[1002,256]{1,0:T(8,128)(2,1)S(1)}, u32[]{:S(2)}, u32[]{:S(2)}) collective-permute-start(bf16[1002,256]{1,0:T(8,128)(2,1)S(1)} %get-tuple-element.308), channel_id=1, source_target_pairs={{0,32},{32,0},{64,96},{96,64},{1,33},{33,1},{65,97},{97,65},{2,34}... | collective-permute-start | bytes 1539080 | tf_op jit(solution)/shard_map/ppermute | solution.py:130
  381.5 14.1 %collective-permute-start.59 = (bf16[1002,256]{1,0:T(8,128)(2,1)S(1)}, bf16[1002,256]{1,0:T(8,128)(2,1)S(1)}, u32[]{:S(2)}, u32[]{:S(2)}) collective-permute-start(bf16[1002,256]{1,0:T(8,128)(2,1)S(1)} %get-tuple-element.307), channel_id=1, source_target_pairs={{0,96},{32,64},{64,32},{96,0},{1,97},{33,65},{65,33},{97,1},{2,98}... | collective-permute-start | bytes 1539080 | tf_op jit(solution)/shard_map/ppermute | solution.py:130
  412.7 48.3 %all-to-all-start.5 = ((bf16[32,32,1024]{2,1,0:T(8,128)(2,1)}), bf16[32,32,1024]{2,1,0:T(8,128)(2,1)}, u32[]{:S(2)}, u32[]{:S(2)}) async-start(bf16[32,32,1024]{2,1,0:T(8,128)(2,1)} %bitcast.614), calls=%async_computation.5 | async-start | bytes 4194304 | tf_op jit(solution)/shard_map/all_to_all | solution.py:565
  419.9 159.8 %all-gather.11.cloned.1.call-start = ((), (), s32[]{:S(2)}) async-start(), calls=%async_computation.14 | async-start | bytes 8650752 | tf_op jit(solution)/shard_map/all_gather | solution.py:622
  434.3 25.5 %collective-permute-start.60 = (bf16[3,176,1024]{2,1,0:T(8,128)(2,1)}, bf16[3,176,1024]{2,1,0:T(8,128)(2,1)}, u32[]{:S(2)}, u32[]{:S(2)}) collective-permute-start(bf16[3,176,1024]{2,1,0:T(8,128)(2,1)} %get-tuple-element.284), channel_id=1, source_target_pairs={{0,32},{32,0},{64,96},{96,64},{1,33},{33,1},{65,97},{97,65},{2,34}... | collective-permute-start | bytes 3244040 | tf_op jit(solution)/shard_map/ppermute | solution.py:130
  434.5 26.5 %collective-permute-start.61 = (bf16[3,176,1024]{2,1,0:T(8,128)(2,1)}, bf16[3,176,1024]{2,1,0:T(8,128)(2,1)}, u32[]{:S(2)}, u32[]{:S(2)}) collective-permute-start(bf16[3,176,1024]{2,1,0:T(8,128)(2,1)} %get-tuple-element.283), channel_id=1, source_target_pairs={{0,96},{32,64},{64,32},{96,0},{1,97},{33,65},{65,33},{97,1},{2,98}... | collective-permute-start | bytes 3244040 | tf_op jit(solution)/shard_map/ppermute | solution.py:130
  498.1 11.4 %collective-permute-start.62 = (bf16[512,1152]{1,0:T(8,128)(2,1)S(1)}, bf16[512,1152]{1,0:T(8,128)(2,1)S(1)}, u32[]{:S(2)}, u32[]{:S(2)}) collective-permute-start(bf16[512,1152]{1,0:T(8,128)(2,1)S(1)} %convolution_convert_fusion.1), channel_id=1, source_target_pairs={{0,1},{1,0},{2,3},{3,2},{4,5},{5,4},{6,7},{7,6},{8,9},{9,8},{10,11... | collective-permute-start | bytes 3538952 | tf_op jit(solution)/shard_map/ppermute | solution.py:126
  505.0 16.7 %collective-permute-start.67 = (bf16[8,32,1024]{2,1,0:T(8,128)(2,1)S(1)}, bf16[8,32,1024]{2,1,0:T(8,128)(2,1)S(1)}, u32[]{:S(2)}, u32[]{:S(2)}) collective-permute-start(bf16[8,32,1024]{2,1,0:T(8,128)(2,1)S(1)} %bitcast.656), channel_id=1, source_target_pairs={{0,24},{1,25},{2,26},{3,27},{4,28},{5,29},{6,30},{7,31},{8,16},{9,... | collective-permute-start | bytes 1572872 | tf_op jit(solution)/shard_map/ppermute | solution.py:126
  508.2 14.3 %collective-permute-start.71 = (bf16[8,32,1024]{2,1,0:T(8,128)(2,1)S(1)}, bf16[8,32,1024]{2,1,0:T(8,128)(2,1)S(1)}, u32[]{:S(2)}, u32[]{:S(2)}) collective-permute-start(bf16[8,32,1024]{2,1,0:T(8,128)(2,1)S(1)} %bitcast.657), channel_id=1, source_target_pairs={{0,2},{1,3},{2,0},{3,1},{4,6},{5,7},{6,4},{7,5},{8,10},{9,11},{10,... | collective-permute-start | bytes 1572872 | tf_op jit(solution)/shard_map/ppermute | solution.py:126
  510.4 14.0 %collective-permute-start.63 = (bf16[8,32,1152]{2,1,0:T(8,128)(2,1)S(1)}, bf16[8,32,1152]{2,1,0:T(8,128)(2,1)S(1)}, u32[]{:S(2)}, u32[]{:S(2)}) collective-permute-start(bf16[8,32,1152]{2,1,0:T(8,128)(2,1)S(1)} %bitcast.638), channel_id=1, source_target_pairs={{0,8},{1,9},{2,10},{3,11},{4,12},{5,13},{6,14},{7,15},{8,0},{9,1},... | collective-permute-start | bytes 1769480 | tf_op jit(solution)/shard_map/ppermute | solution.py:126
  511.4 16.0 %collective-permute-start.75 = (bf16[8,32,1152]{2,1,0:T(8,128)(2,1)S(1)}, bf16[8,32,1152]{2,1,0:T(8,128)(2,1)S(1)}, u32[]{:S(2)}, u32[]{:S(2)}) collective-permute-start(bf16[8,32,1152]{2,1,0:T(8,128)(2,1)S(1)} %bitcast.639), channel_id=1, source_target_pairs={{0,6},{1,7},{2,4},{3,5},{4,2},{5,3},{6,0},{7,1},{8,14},{9,15},{10,... | collective-permute-start | bytes 1769480 | tf_op jit(solution)/shard_map/ppermute | solution.py:126
  521.9 13.8 %collective-permute-start.68 = (bf16[4,32,1024]{2,1,0:T(8,128)(2,1)S(1)}, bf16[4,32,1024]{2,1,0:T(8,128)(2,1)S(1)}, u32[]{:S(2)}, u32[]{:S(2)}) collective-permute-start(bf16[4,32,1024]{2,1,0:T(8,128)(2,1)S(1)} %slice.1482), channel_id=1, source_target_pairs={{0,8},{1,9},{2,10},{3,11},{4,12},{5,13},{6,14},{7,15},{8,0},{9,1},... | collective-permute-start | bytes 786440 | tf_op jit(solution)/shard_map/ppermute | solution.py:126
  522.7 16.0 %collective-permute-start.72 = (bf16[4,32,1024]{2,1,0:T(8,128)(2,1)S(1)}, bf16[4,32,1024]{2,1,0:T(8,128)(2,1)S(1)}, u32[]{:S(2)}, u32[]{:S(2)}) collective-permute-start(bf16[4,32,1024]{2,1,0:T(8,128)(2,1)S(1)} %slice.1490), channel_id=1, source_target_pairs={{0,6},{1,7},{2,4},{3,5},{4,2},{5,3},{6,0},{7,1},{8,14},{9,15},{10,... | collective-permute-start | bytes 786440 | tf_op jit(solution)/shard_map/ppermute | solution.py:126
  524.7 27.2 %collective-permute-start.64 = (bf16[4,32,1152]{2,1,0:T(8,128)(2,1)S(1)}, bf16[4,32,1152]{2,1,0:T(8,128)(2,1)S(1)}, u32[]{:S(2)}, u32[]{:S(2)}) collective-permute-start(bf16[4,32,1152]{2,1,0:T(8,128)(2,1)S(1)} %slice.1474), channel_id=1, source_target_pairs={{0,24},{1,25},{2,26},{3,27},{4,28},{5,29},{6,30},{7,31},{8,16},{9,... | collective-permute-start | bytes 884744 | tf_op jit(solution)/shard_map/ppermute | solution.py:126
  527.6 24.5 %collective-permute-start.76 = (bf16[4,32,1152]{2,1,0:T(8,128)(2,1)S(1)}, bf16[4,32,1152]{2,1,0:T(8,128)(2,1)S(1)}, u32[]{:S(2)}, u32[]{:S(2)}) collective-permute-start(bf16[4,32,1152]{2,1,0:T(8,128)(2,1)S(1)} %slice.1498), channel_id=1, source_target_pairs={{0,2},{1,3},{2,0},{3,1},{4,6},{5,7},{6,4},{7,5},{8,10},{9,11},{10,... | collective-permute-start | bytes 884744 | tf_op jit(solution)/shard_map/ppermute | solution.py:126
  527.7 30.2 %collective-permute-start.78 = (bf16[1002,256]{1,0:T(8,128)(2,1)S(1)}, bf16[1002,256]{1,0:T(8,128)(2,1)S(1)}, u32[]{:S(2)}, u32[]{:S(2)}) collective-permute-start(bf16[1002,256]{1,0:T(8,128)(2,1)S(1)} %copy-done.53), channel_id=1, source_target_pairs={{0,64},{32,96},{64,0},{96,32},{1,65},{33,97},{65,1},{97,33},{2,66}... | collective-permute-start | bytes 1539080 | tf_op jit(solution)/shard_map/ppermute | solution.py:130
  535.7 27.3 %collective-permute-start.79 = (bf16[3,176,1024]{2,1,0:T(8,128)(2,1)S(1)}, bf16[3,176,1024]{2,1,0:T(8,128)(2,1)S(1)}, u32[]{:S(2)}, u32[]{:S(2)}) collective-permute-start(bf16[3,176,1024]{2,1,0:T(8,128)(2,1)S(1)} %copy-done.21), channel_id=1, source_target_pairs={{0,64},{32,96},{64,0},{96,32},{1,65},{33,97},{65,1},{97,33},{2,66}... | collective-permute-start | bytes 3244040 | tf_op jit(solution)/shard_map/ppermute | solution.py:130
  538.7 9.0 %collective-permute-start.69 = (bf16[2,32,1024]{2,1,0:T(8,128)(2,1)S(1)}, bf16[2,32,1024]{2,1,0:T(8,128)(2,1)S(1)}, u32[]{:S(2)}, u32[]{:S(2)}) collective-permute-start(bf16[2,32,1024]{2,1,0:T(8,128)(2,1)S(1)} %slice.1484), channel_id=1, source_target_pairs={{0,6},{1,7},{2,4},{3,5},{4,2},{5,3},{6,0},{7,1},{8,14},{9,15},{10,... | collective-permute-start | bytes 393224 | tf_op jit(solution)/shard_map/ppermute | solution.py:126
  563.0 8.9 %collective-permute-start.80 = (bf16[1,32,1152]{2,1,0:T(8,128)(2,1)S(1)}, bf16[1,32,1152]{2,1,0:T(8,128)(2,1)S(1)}, u32[]{:S(2)}, u32[]{:S(2)}) collective-permute-start(bf16[1,32,1152]{2,1,0:T(8,128)(2,1)S(1)} %slice.1289), channel_id=1, source_target_pairs={{0,6},{1,7},{2,4},{3,5},{4,2},{5,3},{6,0},{7,1},{8,14},{9,15},{10,... | collective-permute-start | bytes 221192 | tf_op jit(solution)/shard_map/ppermute | solution.py:126
  575.3 19.0 %all-to-all-start.6 = ((bf16[4,8,9216]{2,1,0:T(8,128)(2,1)}), bf16[4,8,9216]{2,1,0:T(8,128)(2,1)}, u32[]{:S(2)}, u32[]{:S(2)}) async-start(bf16[4,8,9216]{2,1,0:T(8,128)(2,1)} %bitcast_dynamic-update-slice_fusion), calls=%async_computation.7 | async-start | bytes 1179648 | tf_op jit(solution)/shard_map/all_to_all | solution.py:684
  606.2 24.0 %all-to-all-start.8 = ((f32[128,1,128]{2,1,0:T(1,128)}), f32[128,1,128]{2,1,0:T(1,128)S(1)}, u32[]{:S(2)}, u32[]{:S(2)}) async-start(f32[128,1,128]{2,1,0:T(1,128)} %broadcast_in_dim.258), calls=%async_computation.9 | async-start | bytes 131072 | tf_op jit(solution)/shard_map/all_to_all | solution.py:719
  (219 other events, 1757.4 us)
Sparse Core Ops, SparseCore 0:
  11.7 98.3 all-gather.4
  112.4 48.7 all-gather.6
  163.4 33.8 all-gather.8
  358.5 119.4 reduce-scatter.1
  488.3 66.9 all-gather.10

commit v3 on v2

--- a/solution.py
+++ b/solution.py
@@ -102,6 +102,11 @@
     return (weight, first, second)
 
 
+def lane_squares(values):
+    sums = jnp.sum(values * values, axis=tuple(range(values.ndim - 1)))
+    return jnp.sum(jnp.pad(sums, (0, -sums.shape[0] % 128)).reshape(-1, 128), axis=0)
+
+
 def tables_kernel(rate, clip, weight, grad, first, second, weight_out, first_out, second_out):
     new = adam_update(weight[...], grad[...], first[...], second[...], rate, clip[0, 0])
     weight_out[...], first_out[...], second_out[...] = new
@@ -117,7 +122,7 @@
         in_specs=[pl.BlockSpec(memory_space=pltpu.SMEM)] + [block] * 4,
         out_specs=[block] * 3,
         out_shape=[jax.ShapeDtypeStruct(weight.shape, jnp.float32)] * 3,
-        compiler_params=pltpu.CompilerParams(vmem_limit_bytes=48 * 1024 * 1024),
+        compiler_params=pltpu.CompilerParams(vmem_limit_bytes=56 * 1024 * 1024),
         name="tables_update",
     )(clip_scale.reshape(1, 1), weight, grad, first, second)
 
@@ -172,97 +177,130 @@
 
 
 def in_order(values, stream):
-    order = ORDERS[stream % 2]
     if stream >= 2:
         values = jnp.swapaxes(values, 0, 1)
-    values = jnp.stack([values[i] for i in order])
-    return jnp.stack([values[:, i] for i in order], axis=1)
-
-
-def rank_in_order(distance, stream):
-    return sum(
-        jnp.where(distance == number, spot, 0) for spot, number in enumerate(ORDERS[stream % 2])
-    )
-
-
-def steps_of(stream):
-    near, far = (3, 1) if stream % 2 == 1 else (1, 3)
-    shifts = (3, 1) if stream < 2 else (1, 3)
-    return [number << shift for shift in shifts for number in (near, far)]
-
-
-def ordered_sum(blocks, stream):
-    shape = blocks.shape[2:]
-    blocks = blocks.reshape((16,) + shape)
-    for number in steps_of(stream):
-        half = blocks.shape[0] // 2
-        blocks = add_low(blocks[:half], swap(blocks[half:], number))
-    return blocks[0]
-
-
-def ordered_gather(block, stream):
-    blocks = block[None]
-    for number in reversed(steps_of(stream)):
-        blocks = jnp.concatenate([blocks, swap(blocks, number)], axis=0)
-    return blocks
-
-
-def plane_sum(blocks, stream):
-    other_way = stream % 2 == 1
-    if stream // 2 == 0:
-        return ring_sum(ring_sum(blocks, 3, other_way), 1, other_way)
-    turned = jnp.swapaxes(blocks, 0, 1)
-    return ring_sum(ring_sum(turned, 1, other_way), 3, other_way)
-
-
-def plane_gather(block, stream):
-    other_way = stream % 2 == 1
-    if stream // 2 == 0:
-        return ring_gather(ring_gather(block, 1, other_way), 3, other_way)
-    return jnp.swapaxes(
-        ring_gather(ring_gather(block, 3, other_way), 1, other_way), 0, 1
-    )
+    values = jnp.stack([values[i] for i in ORDERS[stream % 2]])
+    return jnp.stack([values[:, i] for i in ORDERS[stream // 2]], axis=1)
+
+
+def rank_in_order(distance, way):
+    return sum(jnp.where(distance == number, spot, 0) for spot, number in enumerate(ORDERS[way]))
+
+
+def ring_steps(shift, way):
+    return [number << shift for number in ((1, 3), (3, 1))[way]]
+
+
+def halve(blocks, number):
+    half = blocks.shape[0] // 2
+    return add_low(blocks[:half], swap(blocks[half:], number))
+
+
+def streams_sum(streams, between=lambda step, streams: streams, joined=True):
+    streams = list(streams)
+    for step in (0, 1):
+        streams = between(step, streams)
+        streams = [
+            halve(blocks, ring_steps(3 if stream < 2 else 1, stream % 2)[step])
+            for stream, blocks in enumerate(streams)
+        ]
+    if not joined:
+        for step in (0, 1):
+            streams = [
+                halve(blocks, ring_steps(1 if stream < 2 else 3, stream // 2)[step])
+                for stream, blocks in enumerate(streams)
+            ]
+        return [blocks[0] for blocks in streams]
+    widths = [blocks.shape[-1] for blocks in streams]
+    pairs = [jnp.concatenate(streams[pair : pair + 2], axis=-1) for pair in (0, 2)]
+    for step in (0, 1):
+        pairs = between(2 + step, pairs)
+        pairs = [
+            halve(blocks, ring_steps(1 if pair == 0 else 3, pair)[step])
+            for pair, blocks in enumerate(pairs)
+        ]
+    return [
+        part
+        for pair, blocks in enumerate(pairs)
+        for part in jnp.split(blocks[0], [widths[2 * pair]], axis=-1)
+    ]
+
+
+def planes_sum(streams):
+    sums = []
+    for pair, shifts in enumerate(((3, 1), (1, 3))):
+        firsts = []
+        for way in (0, 1):
+            blocks = streams[2 * pair + way]
+            blocks = blocks if pair == 0 else jnp.swapaxes(blocks, 0, 1)
+            firsts.append(ring_sum(blocks, shifts[0], way == 1))
+        sums.append(ring_sum(jnp.concatenate(firsts, axis=1), shifts[1], pair == 1))
+    return jnp.concatenate(sums, axis=0)
+
+
+def planes_gather(block):
+    rows, width = block.shape
+    halves = block.reshape(2, rows // 2, width)
+    streams = []
+    for pair, shifts in enumerate(((1, 3), (3, 1))):
+        joined = ring_gather(halves[pair], shifts[0], pair == 1).reshape(4, 2, rows // 4, width)
+        for way in (0, 1):
+            met = ring_gather(joined[:, way], shifts[1], way == 1)
+            streams.append(met if pair == 0 else jnp.swapaxes(met, 0, 1))
+    return jnp.stack(streams, axis=2)
 
 
 def expert_sum(blocks):
     _, rows, width = blocks.shape
-    blocks = blocks.reshape(4, 4, 2, STREAMS, rows // STREAMS, width)
-    mine = add_low(blocks[:, :, 0], swap(blocks[:, :, 1], 1))
-    return jnp.concatenate([plane_sum(mine[:, :, s], s) for s in range(STREAMS)], axis=0)
+    blocks = blocks.reshape(2, 4, 4, STREAMS, rows // STREAMS, width)
+    mine = add_low(blocks[0], swap(blocks[1], 1))
+    return planes_sum([mine[:, :, s] for s in range(STREAMS)])
 
 
 def expert_gather(block):
     rows, width = block.shape
-    part = rows // STREAMS
-    mine = jnp.stack(
-        [plane_gather(block[s * part : (s + 1) * part], s) for s in range(STREAMS)], axis=2
-    )
-    return jnp.stack([mine, swap(mine, 1)], axis=2).reshape(32, rows, width)
-
-
-def merge_stats(first_part, second_part):
-    top_value = jnp.maximum(first_part[0], second_part[0])
-    total_exp = first_part[1] * jnp.exp(first_part[0] - top_value) + second_part[1] * jnp.exp(
-        second_part[0] - top_value
-    )
-    return jnp.stack([top_value, total_exp, first_part[2] + second_part[2]])
-
-
-def flip_blocks(stats, number):
-    rows = stats.shape[-1]
-    stats = stats.reshape(3, 2, 2, 2, 2, 2, rows)
-    axes = [5 - bit for bit in range(5) if (number >> bit) & 1]
-    return jnp.flip(stats, axes).reshape(3, 32, rows)
+    mine = planes_gather(block).reshape(16, rows, width)
+    return jnp.concatenate([mine, swap(mine, 1)], axis=0)
+
+
+def core_first(values):
+    return jnp.moveaxis(values.reshape((16, 2) + values.shape[1:]), 1, 0).reshape(values.shape)
+
+
+def merge_kernel(numbers, rows, stats, *refs):
+    others, merged = refs[:-1], refs[-1]
+    top, total, target = stats[0:1, :], stats[1:2, :], stats[2:3, :]
+    for number, other in zip(numbers, others, strict=True):
+        values = other[...]
+        kc, kx, ky = number & 1, number >> 3, (number >> 1) & 3
+        pieces = []
+        for block in range(32):
+            source = ((block >> 4) ^ kc) * 16 + (((block >> 2) & 3) ^ kx) * 4 + ((block & 3) ^ ky)
+            pieces.append(values[:, source * rows : (source + 1) * rows])
+        values = jnp.concatenate(pieces, axis=1)
+        other_top, other_total = values[0:1, :], values[1:2, :]
+        new_top = jnp.maximum(top, other_top)
+        total = total * jnp.exp(top - new_top) + other_total * jnp.exp(other_top - new_top)
+        top, target = new_top, target + values[2:3, :]
+    merged[...] = jnp.concatenate([top, total, target], axis=0)
+
+
+def merge_stats(stats, others, numbers):
+    return pl.pallas_call(
+        functools.partial(merge_kernel, numbers, stats.shape[1] // 32),
+        out_shape=jax.ShapeDtypeStruct(stats.shape, stats.dtype),
+        name="merge_stats",
+    )(stats, *others)
 
 
 def meet_stats(stats, beside):
     for shift in (3, 1):
-        others = [swap(stats, k << shift) for k in (1, 2, 3)]
+        numbers = [k << shift for k in (1, 2, 3)]
+        others = [swap(stats, number) for number in numbers]
         if shift == 3:
             others = after(others, beside)
-        for k, other in enumerate(others, 1):
-            stats = merge_stats(stats, flip_blocks(other, k << shift))
-    return merge_stats(stats, flip_blocks(swap(stats, 1), 1))
+        stats = merge_stats(stats, others, numbers)
+    return merge_stats(stats, [swap(stats, 1)], [1])
 
 
 def hot(indices, count):
@@ -345,8 +383,8 @@
     down_first = packed_all[:, start : start + width_model]
     down_second = packed_all[:, start + width_model :]
 
-    ids_all = lax.all_to_all(
-        jnp.broadcast_to(ids, (groups,) + ids.shape[1:]), "dp", split_axis=0, concat_axis=0, tiled=True
+    ids_all = by_distance(
+        jnp.concatenate([ids] + [swap_group(ids, k) for k in range(1, groups)], axis=0), group_index
     ).reshape(groups, axis_width, rows_dev)
     ids_near = by_distance(ids_all.swapaxes(0, 1), expert_index) - vocab_start
     ids_near = ids_near.reshape(4, 4, 2, groups, rows_dev)
@@ -357,14 +395,22 @@
         found = product(hot(ids_near[:, :, :, core].reshape(-1), vocab_part), table_words)
         looked_up.append(found.astype(LOW).reshape(groups, 16 * rows_dev, part_width))
     looked_up = add_low(looked_up[1], swap(looked_up[0], 1))
+    summed = []
+
+    def note(step, streams):
+        if step == 1:
+            summed.append(streams[0])
+        return streams
+
+    x_first = jnp.stack(
+        streams_sum(
+            (looked_up[s].reshape(16, rows_dev, part_width) for s in range(groups)),
+            note,
+            joined=False,
+        )
+    )
     routes, loss_rows, domains, targets, documents = after(
-        (routes, loss_rows, domains, targets, documents), looked_up
-    )
-    x_first = jnp.stack(
-        [
-            ordered_sum(looked_up[s].reshape(4, 4, rows_dev, part_width), s)
-            for s in range(groups)
-        ]
+        (routes, loss_rows, domains, targets, documents), summed
     )
     x_first = lax.all_to_all(x_first, "dp", split_axis=0, concat_axis=0, tiled=True)
     x_first = x_first.swapaxes(0, 1).reshape(rows_dev, width_model).astype(f32)
@@ -397,7 +443,9 @@
     )
     all_weights = jnp.exp2(counted_domains.astype(f32) - 2.0)
     weight_total = jnp.sum(all_weights)
-    group_weights = by_distance(lax.dynamic_index_in_dim(all_weights, group_index, 0, False), expert_index)
+    group_weights = core_first(
+        by_distance(lax.dynamic_index_in_dim(all_weights, group_index, 0, False), expert_index)
+    )
     group_places = lax.dynamic_index_in_dim(loss_places, group_index, 0, False)
     group_targets = jnp.sum(
         jnp.where(
@@ -407,7 +455,7 @@
         ),
         axis=-1,
     )
-    target_local = (by_distance(group_targets, expert_index) - vocab_start).reshape(-1)
+    target_local = core_first(by_distance(group_targets, expert_index)).reshape(-1) - vocab_start
     own_choice = hot(by_distance(group_places, expert_index)[0], rows_dev)
     grad_weights = group_weights.reshape(-1) / weight_total
 
@@ -463,6 +511,38 @@
     shared_hidden = swiglu(shared_in[:, :hidden_shared], shared_in[:, hidden_shared:]).astype(LOW)
     shared_out = product(shared_hidden, w_sdown)
 
+    features = jnp.arange(width_model, dtype=jnp.int32)
+    owner, row = features // own_rows, features % own_rows
+    turned = (owner % axis_width) * groups + owner // axis_width
+    turn_choice = hot(turned * own_rows + row, width_model)
+    downs, down_row = down_rows // own_down, down_rows % own_down
+    down_turned = ((downs % axis_width) * groups + downs // axis_width) * own_rows
+    down_firsts = hot(jnp.where(down_row < own_rows, down_turned + down_row, -1), width_model)
+    down_seconds = hot(
+        jnp.where(down_row < own_rows, -1, down_turned + down_row - own_rows), width_model
+    )
+    early_left = jnp.concatenate(
+        [
+            product(h_low, turn_choice).astype(LOW),
+            product(shared_hidden, down_firsts).astype(LOW),
+            product(shared_hidden, down_seconds).astype(LOW),
+        ],
+        axis=0,
+    )
+    late_left, late_choice = [], []
+    for stream, left in enumerate((attended, h_first_low, h_first_low, h_first_low)):
+        distance = (owner % axis_width) ^ expert_index
+        axes = [distance >> 3, (distance >> 1) & 3]
+        first_axis, second_axis = axes if stream < 2 else axes[::-1]
+        first_axis = rank_in_order(first_axis, stream % 2)
+        second_axis = rank_in_order(second_axis, stream // 2)
+        spot = ((distance & 1) * 16 + first_axis * 4 + second_axis) * groups + owner // axis_width
+        choice = hot(spot * own_rows + row, width_model)
+        if stream == 0:
+            left = jnp.concatenate([left, h_low, h_low], axis=0)
+        late_left.append(product(left, choice).astype(LOW))
+        late_choice.append(choice)
+
     gate_act = inner_cols(expert_rows, w_gate)
     up_act = inner_cols(expert_rows, w_up)
     expert_hidden = swiglu(gate_act, up_act).astype(LOW)
@@ -470,7 +550,7 @@
     returned = lax.all_to_all(expert_out, "expert", split_axis=0, concat_axis=0, tiled=True)
     is_target = target_local[:, None] == jnp.arange(vocab_part, dtype=jnp.int32)[None, :]
     target_head = product(is_target.astype(LOW), head).astype(LOW)
-    returned = after(returned, target_head)
+    returned = after(returned, (target_head, early_left, late_left))
     routed = product(gate_slots, returned).reshape(3, rows_dev, width_model)
     x_last = x_mid + shared_out + (routed[0] + routed[1] + routed[2])
 
@@ -483,14 +563,14 @@
     row_target = jnp.sum(jnp.where(is_target, logits, 0.0), axis=1)
     rest_low = jnp.where(is_target, 0.0, expos).astype(LOW)
     d_rest = product(rest_low, head)
-    stats = meet_stats(
-        jnp.stack([row_top, row_total, row_target]).reshape(3, axis_width, per_device), d_rest
-    )
-    log_norm = (stats[0] + jnp.log(stats[1])).reshape(-1)
-    entropy = log_norm.reshape(axis_width, per_device)[0] - stats[2, 0]
+    stats = meet_stats(jnp.stack([row_top, row_total, row_target]), d_rest)
+    log_norm = stats[0] + jnp.log(stats[1])
+    entropy = log_norm[:per_device] - stats[2, :per_device]
     own_loss = jnp.sum(group_weights[0] * entropy)
+    counts = jnp.sum(chosen.astype(f32), axis=0)
+    terms = jnp.concatenate([own_loss[None], counts, jnp.zeros((127 - experts,), f32)])
     rest_scale = jnp.exp(row_top - log_norm) * grad_weights
-    target_grad = (jnp.exp(stats[2].reshape(-1) - log_norm) - 1.0) * grad_weights
+    target_grad = (jnp.exp(stats[2] - log_norm) - 1.0) * grad_weights
     d_rows_all = d_rest * rest_scale[:, None] + target_grad[:, None] * target_head.astype(f32)
     d_rows_all = d_rows_all.astype(LOW)
     d_logits = jnp.where(
@@ -510,27 +590,6 @@
     d_gate_shared, d_up_shared = shared_back(inner_cols(d_branch, w_sdown))
     d_shared_in = jnp.concatenate([d_gate_shared, d_up_shared], axis=1).astype(LOW)
     d_hmid = inner_cols(d_shared_in, w_shared)
-
-    features = jnp.arange(width_model, dtype=jnp.int32)
-    owner, row = features // own_rows, features % own_rows
-    turned = (owner % axis_width) * groups + owner // axis_width
-    turn_choice = hot(turned * own_rows + row, width_model)
-    downs, down_row = down_rows // own_down, down_rows % own_down
-    down_turned = ((downs % axis_width) * groups + downs // axis_width) * own_rows
-    down_firsts = hot(jnp.where(down_row < own_rows, down_turned + down_row, -1), width_model)
-    down_seconds = hot(
-        jnp.where(down_row < own_rows, -1, down_turned + down_row - own_rows), width_model
-    )
-    early_left = after((h_low, shared_hidden), d_buffer)
-    h_mid_turned = product(early_left[0], turn_choice).astype(LOW)
-    left = jnp.concatenate(
-        [
-            h_mid_turned,
-            product(early_left[1], down_firsts).astype(LOW),
-            product(early_left[1], down_seconds).astype(LOW),
-        ],
-        axis=0,
-    )
 
     def spread_out(before, value, behind):
         return jnp.pad(value, ((0, 0), (before, behind)))
@@ -543,7 +602,7 @@
         ],
         axis=0,
     )
-    early = inner_rows(left, right).astype(LOW)
+    early = inner_rows(early_left, right).astype(LOW)
     d_logits, gathered = after((d_logits, gathered), d_buffer)
     d_head = inner_rows(d_logits, gathered).astype(LOW)
 
@@ -587,7 +646,6 @@
     expert_parts = [
         experts_block(0), swap_group(experts_block(1), 1), swap_group(experts_block(3), 3)
     ]
-    d_returned = after(d_returned, expert_parts[1:])
 
     d_hmid = d_hmid + product(token_slots, d_returned)
     _, mid_back = jax.vjp(norm_apply, x_mid, gain_full[1])
@@ -595,6 +653,7 @@
     d_mid = d_last + d_mid_part
     d_att_in = d_mid.astype(LOW)
     d_attended = inner_cols(d_att_in, w_out).astype(LOW).reshape(rows_dev, heads_count, HD)
+    d_attended = after(d_attended, expert_parts[1:])
     d_value = jnp.einsum("hqk,qhd->khd", probs.astype(LOW), d_attended, preferred_element_type=f32)
     d_probs = jnp.einsum("qhd,khd->hqk", d_attended, value_low, preferred_element_type=f32)
     d_scores = (probs * (d_probs - jnp.sum(probs * d_probs, axis=-1, keepdims=True))).astype(LOW)
@@ -618,7 +677,6 @@
     d_first = d_first.reshape(rows_dev, groups, part_width).swapaxes(0, 1)
     d_qkv, d_att_in = after((d_qkv, d_att_in), d_first)
     d_first = lax.all_to_all(d_first, "dp", split_axis=0, concat_axis=0, tiled=True)
-    d_first = after(d_first, early)
     d_tokens = lax.all_gather(
         d_first.reshape(groups * rows_dev, part_width), "expert", axis=0, tiled=True
     )
@@ -630,21 +688,16 @@
     router_parts = split_three(d_router_logits)
     units = jnp.eye(gains.shape[0], 128, dtype=LOW)
     late = []
-    for stream, (left, right) in enumerate(
+    for stream, right in enumerate(
         (
-            (attended, d_att_in),
-            (h_first_low, d_qkv[:, 2 * width_model :]),
-            (h_first_low, d_qkv[:, width_model : 2 * width_model]),
-            (h_first_low, d_qkv[:, :width_model]),
+            d_att_in,
+            d_qkv[:, 2 * width_model :],
+            d_qkv[:, width_model : 2 * width_model],
+            d_qkv[:, :width_model],
         )
     ):
-        distance = (owner % axis_width) ^ expert_index
-        axes = [rank_in_order(distance >> 3, stream), rank_in_order((distance >> 1) & 3, stream)]
-        first_axis, second_axis = axes if stream < 2 else axes[::-1]
-        spot = ((distance & 1) * 16 + first_axis * 4 + second_axis) * groups + owner // axis_width
-        choice = hot(spot * own_rows + row, width_model)
+        left = late_left[stream]
         if stream == 0:
-            left = jnp.concatenate([left, h_low, h_low], axis=0)
             right = jnp.concatenate(
                 [
                     spread_out(0, right, 128),
@@ -654,37 +707,32 @@
                 axis=0,
             )
         if stream == 3:
-            left = jnp.concatenate([left, *gain_grad], axis=0)
+            gain_left = product(jnp.concatenate(gain_grad, axis=0), late_choice[3]).astype(LOW)
+            left = jnp.concatenate([left, gain_left], axis=0)
             right = jnp.concatenate(
-                [jnp.pad(right, ((0, 0), (0, 128)))]
-                + [jnp.pad(units, ((0, 0), (width_model, 0)))] * 3,
-                axis=0,
+                [spread_out(0, right, 128)] + [spread_out(width_model, units, 0)] * 3, axis=0
             )
-        left = product(left, choice).astype(LOW)
         half = width_model // 2
         sent = swap(inner_rows(left[:, half:], right).astype(LOW), 1)
         grad = (inner_rows(left[:, :half], right) + sent.astype(f32)).astype(LOW)
-        late.append(grad.reshape(4, 4, groups * own_rows, -1))
-    late = [grad.reshape((16,) + grad.shape[2:]) for grad in late]
-    for step in range(4):
+        late.append(grad.reshape(16, groups * own_rows, -1))
+    far = []
+
+    def between(step, streams):
+        if step == 0:
+            streams = after(streams, early)
         if step == 1:
-            far = after((head_block(2), experts_block(2)), late)
-            far = [swap_group(part, 2) for part in far]
-        if step == 3:
-            late = after(late, far)
-        half = late[0].shape[0] // 2
-        late = [
-            add_low(grad[:half], swap(grad[half:], steps_of(stream)[step]))
-            for stream, grad in enumerate(late)
-        ]
-    late = [grad[0] for grad in late]
+            parts = after((head_block(2), experts_block(2)), streams)
+            far.extend(swap_group(part, 2) for part in parts)
+        return after(streams, (far, d_embed)) if step == 3 else streams
+
+    late = streams_sum(late, between)
     d_head_part = sum(part.astype(f32) for part in head_parts + far[:1])
     experts_part = sum(part.astype(f32) for part in expert_parts + far[1:])
     late_width = sum(part.shape[1] for part in late)
     parts = lax.all_to_all(
         jnp.concatenate(late + [early], axis=1), "dp", split_axis=0, concat_axis=0, tiled=True
     )
-    parts = after(parts, d_embed)
     parts = jnp.sum(parts.reshape(groups, own_rows, -1).astype(f32), axis=0)
     late, early = parts[:, :late_width], parts[:, late_width:]
     behind = width_model + 128
@@ -712,15 +760,16 @@
     up_part = experts_part[:2]
     down_part = experts_part[2:]
 
-    grads = (dense_part, shared_part, gains_part, d_embed, d_head_part, up_part, down_part)
-    squares = sum(jnp.sum(grad_part * grad_part) for grad_part in grads)
-    counts = jnp.sum(chosen.astype(f32), axis=0)
-    sums = jnp.concatenate([squares[None], own_loss[None], counts, jnp.zeros((126 - experts,), f32)])
+    grads = (parts, d_embed, d_head_part, experts_part)
+    squares = sum(lane_squares(grad) for grad in grads)
+    sums = jnp.stack([squares, terms])
+    d_embed, d_head_part, gains_part = after((d_embed, d_head_part, gains_part), sums)
     sums = lax.all_to_all(
-        jnp.broadcast_to(sums[None], (devices, 128)), BOTH, split_axis=0, concat_axis=0, tiled=True
+        jnp.broadcast_to(sums[None], (devices, 2, 128)), BOTH, split_axis=0, concat_axis=0, tiled=True
     )
     sums = jnp.sum(sums, axis=0)
-    total_squares, loss_total, counts_all = sums[0], sums[1], sums[2 : 2 + experts]
+    total_squares = jnp.sum(sums[0])
+    loss_total, counts_all = sums[1, 0], sums[1, 1 : 1 + experts]
     norm_value = jnp.sqrt(total_squares)
     clip_scale = jnp.minimum(1.0, CLIP_NORM / (norm_value + 1e-06))
     tables_part = jnp.stack([d_embed, d_head_part], axis=1)

time: 678 us -> 655 us (0.966)
  starting transfers between devices: 155 us -> 134 us
  other arithmetic: 88.6 us -> 76.4 us
    ppermute x78 -> x66, waiting for transfers between devices: 83 us -> 103 us  [swap(): return lax.ppermute(value, 'expert', [(i, i ^ number) for i in range(32)])]
    ppermute x6 -> x9, waiting for transfers between devices: 28.7 us -> 10.2 us  [swap_group(): return lax.ppermute(value, 'dp', [(i, i ^ number) for i in range(4)])]
    ppermute x78 -> x66, starting transfers between devices: 88.8 us -> 71.1 us  [swap(): return lax.ppermute(value, 'expert', [(i, i ^ number) for i in range(32)])]
    all_to_all x1, waiting for transfers between devices: 0.01 us -> 14 us  [body(): lax.all_to_all(d_sent, 'expert', split_axis=0, concat_axis=0, tiled=True)]
    dot_general x13, matrix products: 28.2 us -> 39 us  [inner_rows(): lax.dot_general(left, right, (((0,), (0,)), ((), ())), precision=precisio...]
    all_to_all x2 -> x1, waiting for transfers between devices: 7.91 us -> 0.8 us  [body(): lax.all_to_all(jnp.broadcast_to(sums[None], (devices, 2, 128)), BOTH, spl...]
    all_to_all x2 -> x1, starting transfers between devices: 20.4 us -> 13.8 us  [body(): lax.all_to_all(jnp.broadcast_to(sums[None], (devices, 2, 128)), BOTH, spl...]
    dot_general x39 -> x40, matrix products: 115 us -> 113 us  [product(): return jnp.dot(left, right, preferred_element_type=jnp.float32)]
  transfers between devices with their start and end apart: 97 -> 87, of which waited for: 49 -> 52; matrix products, arithmetic and copies ran while one was open for 36% -> 39% of each run, Pallas kernels for 0% -> 0%
where the time goes in v3:
time: 655 us; the launch traced here: 644 us
  matrix products  200 us (31%)
  waiting for transfers between devices  152 us (23%)
  starting transfers between devices  134 us (20%)
  other arithmetic  76.4 us (12%)
  local copies, waits for them, and re-layouts  39.3 us (6%)
  between operations  20.3 us (3%)
  Pallas kernels  12.7 us (2%)
  blocking collectives  9.47 us (1%)
    dot_general x40, matrix products, product(): return jnp.dot(left, right, preferred_element_type=jnp.float32)  113 us
    ppermute x66, waiting for transfers between devices, swap(): return lax.ppermute(value, 'expert', [(i, i ^ number) for i in range(32)])  103 us
    ppermute x66, starting transfers between devices, swap(): return lax.ppermute(value, 'expert', [(i, i ^ number) for i in range(32)])  71.1 us
    dot_general x13, matrix products, inner_cols(): lax.dot_general(left, right, (((1,), (1,)), ((), ())), precision=precisio...  40.7 us
    dot_general x13, matrix products, inner_rows(): lax.dot_general(left, right, (((0,), (0,)), ((), ())), precision=precisio...  39 us
    unnamed x331, local copies, waits for them, and re-layouts  19.3 us
    all_to_all x1, waiting for transfers between devices, body(): lax.all_to_all(d_sent, 'expert', split_axis=0, concat_axis=0, tiled=True)  14 us
    all_to_all x1, starting transfers between devices, body(): lax.all_to_all(jnp.broadcast_to(sums[None], (devices, 2, 128)), BOTH, spl...  13.8 us
  transfers between devices with their start and end apart: 87, of which 52 were waited for; matrix products, arithmetic and copies ran while one was open for 39% of the time, Pallas kernels for 0%

profile of v3, /device:TPU:1, one launch (start us, length us, event | category | flops | bytes accessed | tf_op | source)
XLA Modules:
  0.0 643.8 jit_solution(14820098335580968312)
XLA Ops:
  10.7 4.5 collective-permute-start.1
  21.8 8.5 %fusion.7 = bf16[8192,256]{1,0:T(8,128)(2,1)} fusion(s32[8192]{0:T(1024)S(1)} %bitcast.628, bf16[2,1002,256]{2,1,0:T(8,128)(2,1)S(1)} %copy.775), kind=kOutput, calls=%fused_computation.13 | convolution fusion | flops 4212998144 | bytes 4743168 | tf_op jit(solution)/shard_map/dot_general | solution.py:33
  35.7 7.4 %fusion.8 = bf16[8192,256]{1,0:T(8,128)(2,1)S(1)} fusion(s32[8192]{0:T(1024)S(1)} %bitcast.629, bf16[2,1002,256]{2,1,0:T(8,128)(2,1)S(1)} %copy.775), kind=kOutput, calls=%fused_computation.14 | convolution fusion | flops 4212998144 | bytes 4743168 | tf_op jit(solution)/shard_map/dot_general | solution.py:33
  43.1 3.4 fusion.9
  55.5 10.4 %collective-permute-done.4 = bf16[8,128,256]{2,1,0:T(8,128)(2,1)} collective-permute-done((bf16[8,128,256]{2,1,0:T(8,128)(2,1)}, bf16[8,128,256]{2,1,0:T(8,128)(2,1)}, u32[]{:S(2)}, u32[]{:S(2)}) %collective-permute-start.4) | collective-permute-done | bytes 524320 | tf_op jit(solution)/shard_map/ppermute | solution.py:131
  109.8 3.4 all-to-all-start
  113.8 5.0 all-to-all-done
  121.6 4.3 fusion.24
  136.0 10.2 %all-to-all-start.1 = ((bf16[32,32,1024]{2,1,0:T(8,128)(2,1)}), bf16[32,32,1024]{2,1,0:T(8,128)(2,1)}, u32[]{:S(2)}, u32[]{:S(2)}) async-start(bf16[32,32,1024]{2,1,0:T(8,128)(2,1)} %bitcast.63), calls=%async_computation.1 | async-start | bytes 4194304 | tf_op jit(solution)/shard_map/all_to_all | solution.py:487
  152.8 3.6 fusion.28
  164.5 7.1 %fusion.16 = f32[1408,1024]{1,0:T(8,128)} fusion(pred[1408,2048]{1,0:T(32,128)(4,1)S(1)} %iota_compare_fusion.6, bf16[1024,9088]{1,0:T(8,128)(2,1)} %all-gather.5.cloned.1.call-done), kind=kOutput, calls=%fused_computation.35 | convolution fusion | flops 2952790016 | bytes 9306112 | tf_op jit(solution)/shard_map/dot_general | solution.py:33
  174.5 3.9 fusion.83
  178.5 6.2 multiply_convert_fusion.2
  187.8 5.6 all-to-all-start.2
  195.4 7.6 %add_convert_fusion.1 = bf16[1408,1024]{1,0:T(8,128)(2,1)} fusion(f32[1408,1024]{1,0:T(8,128)} %fusion.16, pred[1408,2048]{1,0:T(32,128)(4,1)S(1)} %iota_compare_fusion.6, bf16[1024,9088]{1,0:T(8,128)(2,1)} %all-gather.5.cloned.1.call-done), kind=kOutput, calls=%fused_computation.34 | convolution fusion | flops 2955673600 | bytes 12189696 | tf_op jit(solution)/shard_map/dot_general | solution.py:33
  203.0 7.8 %fusion.38 = bf16[2048,1024]{1,0:T(8,128)(2,1)} fusion(bf16[1002,1024]{1,0:T(8,128)(2,1)} %all-gather.9.cloned.1.call-done, s32[2048]{0:T(1024)S(1)} %sub.255), kind=kOutput, calls=%fused_computation.70 | convolution fusion | flops 4206841856 | bytes 6254592 | tf_op jit(solution)/shard_map/dot_general | solution.py:33
  210.8 11.0 %all-to-all-done.2 = bf16[32,32,1024]{2,1,0:T(8,128)(2,1)} async-done(((bf16[32,32,1024]{2,1,0:T(8,128)(2,1)}), bf16[32,32,1024]{2,1,0:T(8,128)(2,1)}, u32[]{:S(2)}, u32[]{:S(2)}) %all-to-all-start.2) | async-done | bytes 2097184 | tf_op jit(solution)/shard_map/all_to_all | solution.py:550
  249.1 6.2 collective-permute-start.32
  255.3 3.8 select_reduce_fusion.1
  262.1 4.5 fusion.369
  272.3 7.0 %fusion.224 = f32[2048,1024]{1,0:T(8,128)} fusion(bf16[1002,1024]{1,0:T(8,128)(2,1)S(1)} %copy-done.141, f32[2048,1002]{0,1:T(8,128)S(1)} %get-tuple-element.430, f32[2048]{0:T(1024)S(1)} %get-tuple-element.429, s32[2048]{0:T(1024)S(1)} %sub.255), kind=kOutput, calls=%fused_computation.466 | convolution fusion | flops 4210900992 | bytes 18665472 | tf_op jit(solution)/shard_map/dot_general | solution.py:33
  297.3 5.3 add_convert_fusion
  339.2 8.2 %convolution_convert_fusion = bf16[1024,4864]{1,0:T(8,128)(2,1)} fusion(bf16[128,1024]{1,0:T(8,128)(2,1)S(1)} %get-tuple-element.74, bf16[128,2816]{1,0:T(8,128)(2,1)S(1)} %pad_maximum_fusion.7, bf16[128,1024]{1,0:T(8,128)(2,1)S(1)} %fusion.102, bf16[128,1024]{1,0:T(8,128)(2,1)S(1)} %fusion.103, bf16[128,1024]{1,0:T(8,128)(2,1)S(1)} %fusion.100), kind=kOutput, calls=%fused_computation.15 | convolution fusion | flops 3858694144 | bytes 11730944 | tf_op jit(solution)/shard_map/dot_general | solution.py:37
  352.8 9.8 %all-to-all-start.3 = ((bf16[32,32,1024]{2,1,0:T(8,128)(2,1)}), bf16[32,32,1024]{2,1,0:T(8,128)(2,1)}, u32[]{:S(2)}, u32[]{:S(2)}) async-start(bf16[32,32,1024]{2,1,0:T(8,128)(2,1)} %bitcast.518), calls=%async_computation.3 | async-start | bytes 4194304 | tf_op jit(solution)/shard_map/all_to_all | solution.py:587
  362.6 5.4 select_convert_fusion
  368.0 4.6 convolution_convert_fusion.5
  376.2 6.0 fusion.26
  382.2 7.1 %collective-permute-done.54 = bf16[1002,256]{1,0:T(8,128)(2,1)S(1)} collective-permute-done((bf16[1002,256]{1,0:T(8,128)(2,1)S(1)}, bf16[1002,256]{1,0:T(8,128)(2,1)S(1)}, u32[]{:S(2)}, u32[]{:S(2)}) %collective-permute-start.54) | collective-permute-done | bytes 513056 | tf_op jit(solution)/shard_map/ppermute | solution.py:135
  390.9 6.3 multiply_convert_fusion.1
  397.3 4.3 fusion.82
  401.6 4.7 add_convert_fusion.2
  406.3 6.9 %all-to-all-start.4 = ((bf16[32,32,1024]{2,1,0:T(8,128)(2,1)}), bf16[32,32,1024]{2,1,0:T(8,128)(2,1)}, u32[]{:S(2)}, u32[]{:S(2)}) async-start(bf16[32,32,1024]{2,1,0:T(8,128)(2,1)} %bitcast.540), calls=%async_computation.4 | async-start | bytes 4194304 | tf_op jit(solution)/shard_map/all_to_all | solution.py:624
  413.2 3.9 convolution_convert_fusion.7
  417.1 3.4 convolution_convert_fusion.8
  433.3 14.0 %all-to-all-done.4 = bf16[32,32,1024]{2,1,0:T(8,128)(2,1)} async-done(((bf16[32,32,1024]{2,1,0:T(8,128)(2,1)}), bf16[32,32,1024]{2,1,0:T(8,128)(2,1)}, u32[]{:S(2)}, u32[]{:S(2)}) %all-to-all-start.4) | async-done | bytes 2097184 | tf_op jit(solution)/shard_map/all_to_all | solution.py:624
  460.1 5.2 multiply_reduce_fusion.5
  465.5 9.5 %all_to_all.66 = bf16[4,128,256]{2,1,0:T(8,128)(2,1)} all-to-all(bf16[4,128,256]{2,1,0:T(8,128)(2,1)S(1)} %bitcast.563), channel_id=1, replica_groups=mesh['dp'=4,'expert'=32] {'dp'}, dimensions={0} | all-to-all | bytes 524288 | tf_op jit(solution)/shard_map/all_to_all | solution.py:679
  505.8 7.0 %collective-permute-done.66 = bf16[8,32,1024]{2,1,0:T(8,128)(2,1)S(1)} collective-permute-done((bf16[8,32,1024]{2,1,0:T(8,128)(2,1)S(1)}, bf16[8,32,1024]{2,1,0:T(8,128)(2,1)S(1)}, u32[]{:S(2)}, u32[]{:S(2)}) %collective-permute-start.66) | collective-permute-done | bytes 524320 | tf_op jit(solution)/shard_map/ppermute | solution.py:131
  517.7 8.6 %collective-permute-done.68 = bf16[8,32,1152]{2,1,0:T(8,128)(2,1)S(1)} collective-permute-done((bf16[8,32,1152]{2,1,0:T(8,128)(2,1)S(1)}, bf16[8,32,1152]{2,1,0:T(8,128)(2,1)S(1)}, u32[]{:S(2)}, u32[]{:S(2)}) %collective-permute-start.68) | collective-permute-done | bytes 589856 | tf_op jit(solution)/shard_map/ppermute | solution.py:131
  526.5 5.5 collective-permute-done.61
  532.4 5.1 collective-permute-done.67
  537.6 5.3 collective-permute-done.64
  543.6 8.0 %collective-permute-done.70 = bf16[2,32,2176]{2,1,0:T(8,128)(2,1)S(1)} collective-permute-done((bf16[2,32,2176]{2,1,0:T(8,128)(2,1)S(1)}, bf16[2,32,2176]{2,1,0:T(8,128)(2,1)S(1)}, u32[]{:S(2)}, u32[]{:S(2)}) %collective-permute-start.70) | collective-permute-done | bytes 278560 | tf_op jit(solution)/shard_map/ppermute | solution.py:131
  551.7 13.9 %multiply_reduce_fusion.2 = (f32[256]{0:T(256)S(1)}, f32[1002,256]{1,0:T(8,128)}) fusion(bf16[16384,256]{1,0:T(8,128)(2,1)} %all-gather.11.cloned.1.call-done, s32[16384]{0:T(1024)S(1)} %bitcast.610), kind=kOutput, calls=%fused_computation.217 | convolution fusion | flops 8422315008 | bytes 9481216 | tf_op jit(solution)/shard_map/dot_general | solution.py:33
  575.0 4.2 all-to-all-start.6
  582.3 4.2 all-to-all-done.6
  589.1 13.8 %all-to-all-start.7 = ((f32[128,2,128]{2,1,0:T(2,128)}), f32[128,2,128]{2,1,0:T(2,128)}, u32[]{:S(2)}, u32[]{:S(2)}) async-start(f32[128,2,128]{2,1,0:T(2,128)} %broadcast_in_dim.249), calls=%async_computation.8 | async-start | bytes 262144 | tf_op jit(solution)/shard_map/all_to_all | solution.py:767
  627.8 8.1 %tables_update.1 = (f32[1002,2,256]{2,1,0:T(2,128)}, f32[1002,2,256]{2,1,0:T(2,128)}, f32[1002,2,256]{2,1,0:T(2,128)}) custom-call(f32[1,1]{1,0:T(1,128)} %bitcast.194.clip, f32[1002,2,256]{2,1,0:T(2,128)} %bitcast.526, f32[1002,2,256]{2,1,0:T(2,128)} %pad_maximum_fusion.3.grad, f32[1002,2,256]{2,1,0:T(2,128)} %bitcast.546, f32[1002,2,256]{2,1,0:T(2,128)} %bitcast.547), custom_call_target="tpu_custom_call" | custom-call | tf_op jit(solution)/shard_map/tables_update/pallas_call | solution.py:119
  (823 shorter events, 304.1 us)
Async XLA Ops:
  7.2 111.8 %all-gather.5.cloned.1.call-start = ((), (), s32[]{:S(2)}) async-start(), calls=%async_computation.9 | async-start | bytes 18757632 | tf_op jit(solution)/shard_map/all_gather | solution.py:375
  10.7 161.9 %all-gather.7.cloned.1.call-start = ((), (), s32[]{:S(2)}) async-start(), calls=%async_computation.10 | async-start | bytes 5406720 | tf_op jit(solution)/shard_map/all_gather | solution.py:421
  30.2 12.9 %collective-permute-start.3 = (bf16[4,2048,256]{2,1,0:T(8,128)(2,1)}, bf16[4,2048,256]{2,1,0:T(8,128)(2,1)}, u32[]{:S(2)}, u32[]{:S(2)}) collective-permute-start(bf16[4,2048,256]{2,1,0:T(8,128)(2,1)} %bitcast.30), channel_id=1, source_target_pairs={{0,1},{1,0},{2,3},{3,2},{4,5},{5,4},{6,7},{7,6},{8,9},{9,8},{10,11... | collective-permute-start | bytes 12582920 | tf_op jit(solution)/shard_map/ppermute | solution.py:131
  47.9 18.0 %collective-permute-start.4 = (bf16[8,128,256]{2,1,0:T(8,128)(2,1)}, bf16[8,128,256]{2,1,0:T(8,128)(2,1)}, u32[]{:S(2)}, u32[]{:S(2)}) collective-permute-start(bf16[8,128,256]{2,1,0:T(8,128)(2,1)} %bitcast.32), channel_id=1, source_target_pairs={{0,8},{1,9},{2,10},{3,11},{4,12},{5,13},{6,14},{7,15},{8,0},{9,1},... | collective-permute-start | bytes 1572872 | tf_op jit(solution)/shard_map/ppermute | solution.py:131
  51.0 18.4 %collective-permute-start.16 = (bf16[8,128,256]{2,1,0:T(8,128)(2,1)}, bf16[8,128,256]{2,1,0:T(8,128)(2,1)}, u32[]{:S(2)}, u32[]{:S(2)}) collective-permute-start(bf16[8,128,256]{2,1,0:T(8,128)(2,1)} %bitcast.570), channel_id=1, source_target_pairs={{0,6},{1,7},{2,4},{3,5},{4,2},{5,3},{6,0},{7,1},{8,14},{9,15},{10,... | collective-permute-start | bytes 1572872 | tf_op jit(solution)/shard_map/ppermute | solution.py:131
  53.7 19.5 %collective-permute-start.12 = (bf16[8,128,256]{2,1,0:T(8,128)(2,1)}, bf16[8,128,256]{2,1,0:T(8,128)(2,1)}, u32[]{:S(2)}, u32[]{:S(2)}) collective-permute-start(bf16[8,128,256]{2,1,0:T(8,128)(2,1)} %bitcast.569), channel_id=1, source_target_pairs={{0,2},{1,3},{2,0},{3,1},{4,6},{5,7},{6,4},{7,5},{8,10},{9,11},{10,... | collective-permute-start | bytes 1572872 | tf_op jit(solution)/shard_map/ppermute | solution.py:131
  53.7 27.5 %collective-permute-start.8 = (bf16[8,128,256]{2,1,0:T(8,128)(2,1)}, bf16[8,128,256]{2,1,0:T(8,128)(2,1)}, u32[]{:S(2)}, u32[]{:S(2)}) collective-permute-start(bf16[8,128,256]{2,1,0:T(8,128)(2,1)} %bitcast.568), channel_id=1, source_target_pairs={{0,24},{1,25},{2,26},{3,27},{4,28},{5,29},{6,30},{7,31},{8,16},{9,... | collective-permute-start | bytes 1572872 | tf_op jit(solution)/shard_map/ppermute | solution.py:131
  70.7 13.5 %collective-permute-start.17 = (bf16[4,128,256]{2,1,0:T(8,128)(2,1)S(1)}, bf16[4,128,256]{2,1,0:T(8,128)(2,1)S(1)}, u32[]{:S(2)}, u32[]{:S(2)}) collective-permute-start(bf16[4,128,256]{2,1,0:T(8,128)(2,1)S(1)} %slice.1004), channel_id=1, source_target_pairs={{0,2},{1,3},{2,0},{3,1},{4,6},{5,7},{6,4},{7,5},{8,10},{9,11},{10,... | collective-permute-start | bytes 786440 | tf_op jit(solution)/shard_map/ppermute | solution.py:131
  74.5 15.0 %collective-permute-start.5 = (bf16[4,128,256]{2,1,0:T(8,128)(2,1)}, bf16[4,128,256]{2,1,0:T(8,128)(2,1)}, u32[]{:S(2)}, u32[]{:S(2)}) collective-permute-start(bf16[4,128,256]{2,1,0:T(8,128)(2,1)} %slice.980), channel_id=1, source_target_pairs={{0,24},{1,25},{2,26},{3,27},{4,28},{5,29},{6,30},{7,31},{8,16},{9,... | collective-permute-start | bytes 786440 | tf_op jit(solution)/shard_map/ppermute | solution.py:131
  79.2 14.7 %collective-permute-start.13 = (bf16[4,128,256]{2,1,0:T(8,128)(2,1)S(1)}, bf16[4,128,256]{2,1,0:T(8,128)(2,1)S(1)}, u32[]{:S(2)}, u32[]{:S(2)}) collective-permute-start(bf16[4,128,256]{2,1,0:T(8,128)(2,1)S(1)} %slice.996), channel_id=1, source_target_pairs={{0,6},{1,7},{2,4},{3,5},{4,2},{5,3},{6,0},{7,1},{8,14},{9,15},{10,... | collective-permute-start | bytes 786440 | tf_op jit(solution)/shard_map/ppermute | solution.py:131
  82.4 13.3 %collective-permute-start.9 = (bf16[4,128,256]{2,1,0:T(8,128)(2,1)S(1)}, bf16[4,128,256]{2,1,0:T(8,128)(2,1)S(1)}, u32[]{:S(2)}, u32[]{:S(2)}) collective-permute-start(bf16[4,128,256]{2,1,0:T(8,128)(2,1)S(1)} %slice.988), channel_id=1, source_target_pairs={{0,8},{1,9},{2,10},{3,11},{4,12},{5,13},{6,14},{7,15},{8,0},{9,1},... | collective-permute-start | bytes 786440 | tf_op jit(solution)/shard_map/ppermute | solution.py:131
  84.3 12.0 %collective-permute-start.18 = (bf16[2,128,256]{2,1,0:T(8,128)(2,1)S(1)}, bf16[2,128,256]{2,1,0:T(8,128)(2,1)S(1)}, u32[]{:S(2)}, u32[]{:S(2)}) collective-permute-start(bf16[2,128,256]{2,1,0:T(8,128)(2,1)S(1)} %slice.1006), channel_id=1, source_target_pairs={{0,24},{1,25},{2,26},{3,27},{4,28},{5,29},{6,30},{7,31},{8,16},{9,... | collective-permute-start | bytes 393224 | tf_op jit(solution)/shard_map/ppermute | solution.py:131
  94.0 8.8 %collective-permute-start.14 = (bf16[2,128,256]{2,1,0:T(8,128)(2,1)S(1)}, bf16[2,128,256]{2,1,0:T(8,128)(2,1)S(1)}, u32[]{:S(2)}, u32[]{:S(2)}) collective-permute-start(bf16[2,128,256]{2,1,0:T(8,128)(2,1)S(1)} %slice.998), channel_id=1, source_target_pairs={{0,24},{1,25},{2,26},{3,27},{4,28},{5,29},{6,30},{7,31},{8,16},{9,... | collective-permute-start | bytes 393224 | tf_op jit(solution)/shard_map/ppermute | solution.py:131
  95.8 8.4 %collective-permute-start.10 = (bf16[2,128,256]{2,1,0:T(8,128)(2,1)S(1)}, bf16[2,128,256]{2,1,0:T(8,128)(2,1)S(1)}, u32[]{:S(2)}, u32[]{:S(2)}) collective-permute-start(bf16[2,128,256]{2,1,0:T(8,128)(2,1)S(1)} %slice.990), channel_id=1, source_target_pairs={{0,2},{1,3},{2,0},{3,1},{4,6},{5,7},{6,4},{7,5},{8,10},{9,11},{10,... | collective-permute-start | bytes 393224 | tf_op jit(solution)/shard_map/ppermute | solution.py:131
  96.4 9.2 %collective-permute-start.19 = (bf16[1,128,256]{2,1,0:T(8,128)(2,1)S(1)}, bf16[1,128,256]{2,1,0:T(8,128)(2,1)S(1)}, u32[]{:S(2)}, u32[]{:S(2)}) collective-permute-start(bf16[1,128,256]{2,1,0:T(8,128)(2,1)S(1)} %slice.1008), channel_id=1, source_target_pairs={{0,8},{1,9},{2,10},{3,11},{4,12},{5,13},{6,14},{7,15},{8,0},{9,1},... | collective-permute-start | bytes 196616 | tf_op jit(solution)/shard_map/ppermute | solution.py:131
  109.8 8.9 %all-to-all-start = ((bf16[4,128,256]{2,1,0:T(8,128)(2,1)}), bf16[4,128,256]{2,1,0:T(8,128)(2,1)S(1)}, u32[]{:S(2)}, u32[]{:S(2)}) async-start(bf16[4,128,256]{2,1,0:T(8,128)(2,1)} %pad_maximum_fusion.12), calls=%async_computation | async-start | bytes 524288 | tf_op jit(solution)/shard_map/all_to_all | solution.py:415
  136.0 38.5 %all-to-all-start.1 = ((bf16[32,32,1024]{2,1,0:T(8,128)(2,1)}), bf16[32,32,1024]{2,1,0:T(8,128)(2,1)}, u32[]{:S(2)}, u32[]{:S(2)}) async-start(bf16[32,32,1024]{2,1,0:T(8,128)(2,1)} %bitcast.63), calls=%async_computation.1 | async-start | bytes 4194304 | tf_op jit(solution)/shard_map/all_to_all | solution.py:487
  146.2 56.8 %all-gather.9.cloned.1.call-start = ((), (), s32[]{:S(2)}) async-start(), calls=%async_computation.11 | async-start | bytes 2580480 | tf_op jit(solution)/shard_map/all_gather | solution.py:482
  187.8 34.0 %all-to-all-start.2 = ((bf16[32,32,1024]{2,1,0:T(8,128)(2,1)}), bf16[32,32,1024]{2,1,0:T(8,128)(2,1)}, u32[]{:S(2)}, u32[]{:S(2)}) async-start(bf16[32,32,1024]{2,1,0:T(8,128)(2,1)} %bitcast.541), calls=%async_computation.2 | async-start | bytes 4194304 | tf_op jit(solution)/shard_map/all_to_all | solution.py:550
  193.5 304.3 %reduce-scatter.2.cloned.1.call-start = ((), (), s32[]{:S(2)}) async-start(), calls=%async_computation.12 | async-start | bytes 10272768 | tf_op jit(solution)/shard_map/reduce_scatter | solution.py:616
  249.1 10.8 %collective-permute-start.32 = (bf16[16,64,1024]{2,1,0:T(8,128)(2,1)S(1)}, bf16[16,64,1024]{2,1,0:T(8,128)(2,1)}, u32[]{:S(2)}, u32[]{:S(2)}) collective-permute-start(bf16[16,64,1024]{2,1,0:T(8,128)(2,1)S(1)} %bitcast.524), channel_id=1, source_target_pairs={{0,1},{1,0},{2,3},{3,2},{4,5},{5,4},{6,7},{7,6},{8,9},{9,8},{10,11... | collective-permute-start | bytes 6291464 | tf_op jit(solution)/shard_map/ppermute | solution.py:131
  268.9 10.4 %collective-permute-start.35 = (f32[3,2048]{1,0:T(4,128)S(1)}, f32[3,2048]{1,0:T(4,128)S(1)}, u32[]{:S(2)}, u32[]{:S(2)}) collective-permute-start(f32[3,2048]{1,0:T(4,128)S(1)} %pad_maximum_fusion.44.stats), channel_id=1, source_target_pairs={{0,24},{1,25},{2,26},{3,27},{4,28},{5,29},{6,30},{7,31},{8,16},{9,... | collective-permute-start | bytes 73736 | tf_op jit(solution)/shard_map/ppermute | solution.py:131
  269.7 9.6 %collective-permute-start.34 = (f32[3,2048]{1,0:T(4,128)S(1)}, f32[3,2048]{1,0:T(4,128)S(1)}, u32[]{:S(2)}, u32[]{:S(2)}) collective-permute-start(f32[3,2048]{1,0:T(4,128)S(1)} %pad_maximum_fusion.44.stats), channel_id=1, source_target_pairs={{0,16},{1,17},{2,18},{3,19},{4,20},{5,21},{6,22},{7,23},{8,24},{9,... | collective-permute-start | bytes 73736 | tf_op jit(solution)/shard_map/ppermute | solution.py:131
  310.1 8.5 %collective-permute-start.43 = (bf16[2,4,16,1024]{3,2,1,0:T(8,128)(2,1)S(1)}, bf16[2,4,16,1024]{3,2,1,0:T(8,128)(2,1)S(1)}, u32[]{:S(2)}, u32[]{:S(2)}) collective-permute-start(bf16[2,4,16,1024]{3,2,1,0:T(8,128)(2,1)S(1)} %pad_maximum_fusion.21), channel_id=1, source_target_pairs={{0,24},{1,25},{2,26},{3,27},{4,28},{5,29},{6,30},{7,31},{8,16},{9,... | collective-permute-start | bytes 786440 | tf_op jit(solution)/shard_map/ppermute | solution.py:131
  352.8 38.1 %all-to-all-start.3 = ((bf16[32,32,1024]{2,1,0:T(8,128)(2,1)}), bf16[32,32,1024]{2,1,0:T(8,128)(2,1)}, u32[]{:S(2)}, u32[]{:S(2)}) async-start(bf16[32,32,1024]{2,1,0:T(8,128)(2,1)} %bitcast.518), calls=%async_computation.3 | async-start | bytes 4194304 | tf_op jit(solution)/shard_map/all_to_all | solution.py:587
  375.0 14.3 %collective-permute-start.54 = (bf16[1002,256]{1,0:T(8,128)(2,1)S(1)}, bf16[1002,256]{1,0:T(8,128)(2,1)S(1)}, u32[]{:S(2)}, u32[]{:S(2)}) collective-permute-start(bf16[1002,256]{1,0:T(8,128)(2,1)S(1)} %get-tuple-element.336), channel_id=1, source_target_pairs={{0,96},{32,64},{64,32},{96,0},{1,97},{33,65},{65,33},{97,1},{2,98}... | collective-permute-start | bytes 1539080 | tf_op jit(solution)/shard_map/ppermute | solution.py:135
  376.0 13.3 %collective-permute-start.53 = (bf16[1002,256]{1,0:T(8,128)(2,1)S(1)}, bf16[1002,256]{1,0:T(8,128)(2,1)S(1)}, u32[]{:S(2)}, u32[]{:S(2)}) collective-permute-start(bf16[1002,256]{1,0:T(8,128)(2,1)S(1)} %get-tuple-element.337), channel_id=1, source_target_pairs={{0,32},{32,0},{64,96},{96,64},{1,33},{33,1},{65,97},{97,65},{2,34}... | collective-permute-start | bytes 1539080 | tf_op jit(solution)/shard_map/ppermute | solution.py:135
  406.3 41.0 %all-to-all-start.4 = ((bf16[32,32,1024]{2,1,0:T(8,128)(2,1)}), bf16[32,32,1024]{2,1,0:T(8,128)(2,1)}, u32[]{:S(2)}, u32[]{:S(2)}) async-start(bf16[32,32,1024]{2,1,0:T(8,128)(2,1)} %bitcast.540), calls=%async_computation.4 | async-start | bytes 4194304 | tf_op jit(solution)/shard_map/all_to_all | solution.py:624
  413.2 138.5 %all-gather.11.cloned.1.call-start = ((), (), s32[]{:S(2)}) async-start(), calls=%async_computation.13 | async-start | bytes 8650752 | tf_op jit(solution)/shard_map/all_gather | solution.py:680
  427.3 26.7 %collective-permute-start.56 = (bf16[3,176,1024]{2,1,0:T(8,128)(2,1)}, bf16[3,176,1024]{2,1,0:T(8,128)(2,1)}, u32[]{:S(2)}, u32[]{:S(2)}) collective-permute-start(bf16[3,176,1024]{2,1,0:T(8,128)(2,1)} %get-tuple-element.312), channel_id=1, source_target_pairs={{0,96},{32,64},{64,32},{96,0},{1,97},{33,65},{65,33},{97,1},{2,98}... | collective-permute-start | bytes 3244040 | tf_op jit(solution)/shard_map/ppermute | solution.py:135
  428.8 25.2 %collective-permute-start.55 = (bf16[3,176,1024]{2,1,0:T(8,128)(2,1)}, bf16[3,176,1024]{2,1,0:T(8,128)(2,1)}, u32[]{:S(2)}, u32[]{:S(2)}) collective-permute-start(bf16[3,176,1024]{2,1,0:T(8,128)(2,1)} %get-tuple-element.313), channel_id=1, source_target_pairs={{0,32},{32,0},{64,96},{96,64},{1,33},{33,1},{65,97},{97,65},{2,34}... | collective-permute-start | bytes 3244040 | tf_op jit(solution)/shard_map/ppermute | solution.py:135
  475.7 12.6 %collective-permute-start.59 = (bf16[512,1024]{1,0:T(8,128)(2,1)S(1)}, bf16[512,1024]{1,0:T(8,128)(2,1)S(1)}, u32[]{:S(2)}, u32[]{:S(2)}) collective-permute-start(bf16[512,1024]{1,0:T(8,128)(2,1)S(1)} %convolution_convert_fusion.9), channel_id=1, source_target_pairs={{0,1},{1,0},{2,3},{3,2},{4,5},{5,4},{6,7},{7,6},{8,9},{9,8},{10,11... | collective-permute-start | bytes 3145736 | tf_op jit(solution)/shard_map/ppermute | solution.py:131
  480.7 9.0 %collective-permute-start.58 = (bf16[512,1024]{1,0:T(8,128)(2,1)}, bf16[512,1024]{1,0:T(8,128)(2,1)}, u32[]{:S(2)}, u32[]{:S(2)}) collective-permute-start(bf16[512,1024]{1,0:T(8,128)(2,1)} %convolution_convert_fusion.10), channel_id=1, source_target_pairs={{0,1},{1,0},{2,3},{3,2},{4,5},{5,4},{6,7},{7,6},{8,9},{9,8},{10,11... | collective-permute-start | bytes 3145736 | tf_op jit(solution)/shard_map/ppermute | solution.py:131
  486.2 8.5 %collective-permute-start.57 = (bf16[512,1152]{1,0:T(8,128)(2,1)}, bf16[512,1152]{1,0:T(8,128)(2,1)}, u32[]{:S(2)}, u32[]{:S(2)}) collective-permute-start(bf16[512,1152]{1,0:T(8,128)(2,1)} %convolution_convert_fusion.1), channel_id=1, source_target_pairs={{0,1},{1,0},{2,3},{3,2},{4,5},{5,4},{6,7},{7,6},{8,9},{9,8},{10,11... | collective-permute-start | bytes 3538952 | tf_op jit(solution)/shard_map/ppermute | solution.py:131
  497.8 15.0 %collective-permute-start.66 = (bf16[8,32,1024]{2,1,0:T(8,128)(2,1)S(1)}, bf16[8,32,1024]{2,1,0:T(8,128)(2,1)S(1)}, u32[]{:S(2)}, u32[]{:S(2)}) collective-permute-start(bf16[8,32,1024]{2,1,0:T(8,128)(2,1)S(1)} %slice.926), channel_id=1, source_target_pairs={{0,2},{1,3},{2,0},{3,1},{4,6},{5,7},{6,4},{7,5},{8,10},{9,11},{10,... | collective-permute-start | bytes 1572872 | tf_op jit(solution)/shard_map/ppermute | solution.py:131
  499.1 18.2 %collective-permute-start.63 = (bf16[8,32,1024]{2,1,0:T(8,128)(2,1)S(1)}, bf16[8,32,1024]{2,1,0:T(8,128)(2,1)S(1)}, u32[]{:S(2)}, u32[]{:S(2)}) collective-permute-start(bf16[8,32,1024]{2,1,0:T(8,128)(2,1)S(1)} %slice.920), channel_id=1, source_target_pairs={{0,24},{1,25},{2,26},{3,27},{4,28},{5,29},{6,30},{7,31},{8,16},{9,... | collective-permute-start | bytes 1572872 | tf_op jit(solution)/shard_map/ppermute | solution.py:131
  503.1 23.2 %collective-permute-start.68 = (bf16[8,32,1152]{2,1,0:T(8,128)(2,1)S(1)}, bf16[8,32,1152]{2,1,0:T(8,128)(2,1)S(1)}, u32[]{:S(2)}, u32[]{:S(2)}) collective-permute-start(bf16[8,32,1152]{2,1,0:T(8,128)(2,1)S(1)} %slice.930), channel_id=1, source_target_pairs={{0,6},{1,7},{2,4},{3,5},{4,2},{5,3},{6,0},{7,1},{8,14},{9,15},{10,... | collective-permute-start | bytes 1769480 | tf_op jit(solution)/shard_map/ppermute | solution.py:131
  505.7 26.3 %collective-permute-start.61 = (bf16[8,32,1152]{2,1,0:T(8,128)(2,1)S(1)}, bf16[8,32,1152]{2,1,0:T(8,128)(2,1)S(1)}, u32[]{:S(2)}, u32[]{:S(2)}) collective-permute-start(bf16[8,32,1152]{2,1,0:T(8,128)(2,1)S(1)} %slice.916), channel_id=1, source_target_pairs={{0,8},{1,9},{2,10},{3,11},{4,12},{5,13},{6,14},{7,15},{8,0},{9,1},... | collective-permute-start | bytes 1769480 | tf_op jit(solution)/shard_map/ppermute | solution.py:131
  513.0 24.5 %collective-permute-start.67 = (bf16[4,32,1024]{2,1,0:T(8,128)(2,1)S(1)}, bf16[4,32,1024]{2,1,0:T(8,128)(2,1)S(1)}, u32[]{:S(2)}, u32[]{:S(2)}) collective-permute-start(bf16[4,32,1024]{2,1,0:T(8,128)(2,1)S(1)} %slice.1106), channel_id=1, source_target_pairs={{0,6},{1,7},{2,4},{3,5},{4,2},{5,3},{6,0},{7,1},{8,14},{9,15},{10,... | collective-permute-start | bytes 786440 | tf_op jit(solution)/shard_map/ppermute | solution.py:131
  517.6 25.3 %collective-permute-start.64 = (bf16[4,32,1024]{2,1,0:T(8,128)(2,1)S(1)}, bf16[4,32,1024]{2,1,0:T(8,128)(2,1)S(1)}, u32[]{:S(2)}, u32[]{:S(2)}) collective-permute-start(bf16[4,32,1024]{2,1,0:T(8,128)(2,1)S(1)} %slice.1102), channel_id=1, source_target_pairs={{0,8},{1,9},{2,10},{3,11},{4,12},{5,13},{6,14},{7,15},{8,0},{9,1},... | collective-permute-start | bytes 786440 | tf_op jit(solution)/shard_map/ppermute | solution.py:131
  526.4 16.5 %collective-permute-start.69 = (bf16[4,32,1152]{2,1,0:T(8,128)(2,1)S(1)}, bf16[4,32,1152]{2,1,0:T(8,128)(2,1)S(1)}, u32[]{:S(2)}, u32[]{:S(2)}) collective-permute-start(bf16[4,32,1152]{2,1,0:T(8,128)(2,1)S(1)} %slice.1108), channel_id=1, source_target_pairs={{0,2},{1,3},{2,0},{3,1},{4,6},{5,7},{6,4},{7,5},{8,10},{9,11},{10,... | collective-permute-start | bytes 884744 | tf_op jit(solution)/shard_map/ppermute | solution.py:131
  532.2 11.0 %collective-permute-start.62 = (bf16[4,32,1152]{2,1,0:T(8,128)(2,1)S(1)}, bf16[4,32,1152]{2,1,0:T(8,128)(2,1)S(1)}, u32[]{:S(2)}, u32[]{:S(2)}) collective-permute-start(bf16[4,32,1152]{2,1,0:T(8,128)(2,1)S(1)} %slice.1100), channel_id=1, source_target_pairs={{0,24},{1,25},{2,26},{3,27},{4,28},{5,29},{6,30},{7,31},{8,16},{9,... | collective-permute-start | bytes 884744 | tf_op jit(solution)/shard_map/ppermute | solution.py:131
  532.3 33.3 %collective-permute-start.71 = (bf16[1002,256]{1,0:T(8,128)(2,1)S(1)}, bf16[1002,256]{1,0:T(8,128)(2,1)}, u32[]{:S(2)}, u32[]{:S(2)}) collective-permute-start(bf16[1002,256]{1,0:T(8,128)(2,1)S(1)} %copy-done.48), channel_id=1, source_target_pairs={{0,64},{32,96},{64,0},{96,32},{1,65},{33,97},{65,1},{97,33},{2,66}... | collective-permute-start | bytes 1539080 | tf_op jit(solution)/shard_map/ppermute | solution.py:135
  537.5 28.7 %collective-permute-start.72 = (bf16[3,176,1024]{2,1,0:T(8,128)(2,1)S(1)}, bf16[3,176,1024]{2,1,0:T(8,128)(2,1)S(1)}, u32[]{:S(2)}, u32[]{:S(2)}) collective-permute-start(bf16[3,176,1024]{2,1,0:T(8,128)(2,1)S(1)} %copy-done.21), channel_id=1, source_target_pairs={{0,64},{32,96},{64,0},{96,32},{1,65},{33,97},{65,1},{97,33},{2,66}... | collective-permute-start | bytes 3244040 | tf_op jit(solution)/shard_map/ppermute | solution.py:135
  543.1 8.4 %collective-permute-start.70 = (bf16[2,32,2176]{2,1,0:T(8,128)(2,1)S(1)}, bf16[2,32,2176]{2,1,0:T(8,128)(2,1)S(1)}, u32[]{:S(2)}, u32[]{:S(2)}) collective-permute-start(bf16[2,32,2176]{2,1,0:T(8,128)(2,1)S(1)} %pad_maximum_fusion.10), channel_id=1, source_target_pairs={{0,24},{1,25},{2,26},{3,27},{4,28},{5,29},{6,30},{7,31},{8,16},{9,... | collective-permute-start | bytes 835592 | tf_op jit(solution)/shard_map/ppermute | solution.py:131
  543.3 8.3 %collective-permute-start.65 = (bf16[2,32,2176]{2,1,0:T(8,128)(2,1)S(1)}, bf16[2,32,2176]{2,1,0:T(8,128)(2,1)S(1)}, u32[]{:S(2)}, u32[]{:S(2)}) collective-permute-start(bf16[2,32,2176]{2,1,0:T(8,128)(2,1)S(1)} %pad_maximum_fusion.11), channel_id=1, source_target_pairs={{0,2},{1,3},{2,0},{3,1},{4,6},{5,7},{6,4},{7,5},{8,10},{9,11},{10,... | collective-permute-start | bytes 835592 | tf_op jit(solution)/shard_map/ppermute | solution.py:131
  575.0 11.5 %all-to-all-start.6 = ((bf16[4,8,9216]{2,1,0:T(8,128)(2,1)}), bf16[4,8,9216]{2,1,0:T(8,128)(2,1)}, u32[]{:S(2)}, u32[]{:S(2)}) async-start(bf16[4,8,9216]{2,1,0:T(8,128)(2,1)} %pad_maximum_fusion.9), calls=%async_computation.7 | async-start | bytes 1179648 | tf_op jit(solution)/shard_map/all_to_all | solution.py:733
  589.1 23.6 %all-to-all-start.7 = ((f32[128,2,128]{2,1,0:T(2,128)}), f32[128,2,128]{2,1,0:T(2,128)}, u32[]{:S(2)}, u32[]{:S(2)}) async-start(f32[128,2,128]{2,1,0:T(2,128)} %broadcast_in_dim.249), calls=%async_computation.8 | async-start | bytes 262144 | tf_op jit(solution)/shard_map/all_to_all | solution.py:767
  (196 other events, 1506.5 us)
Sparse Core Ops, SparseCore 0:
  11.7 99.6 all-gather.4
  113.6 48.6 all-gather.6
  164.5 33.8 all-gather.8
  347.6 119.2 reduce-scatter.1
  475.1 69.0 all-gather.10

commit v4 on v3

--- a/solution.py
+++ b/solution.py
@@ -27,6 +27,7 @@
 LOW = jnp.bfloat16
 BOTH = ("dp", "expert")
 STREAMS = 4
+ROUND_ROWS = 24
 
 
 def product(left, right):
@@ -386,32 +387,64 @@
     ids_all = by_distance(
         jnp.concatenate([ids] + [swap_group(ids, k) for k in range(1, groups)], axis=0), group_index
     ).reshape(groups, axis_width, rows_dev)
-    ids_near = by_distance(ids_all.swapaxes(0, 1), expert_index) - vocab_start
-    ids_near = ids_near.reshape(4, 4, 2, groups, rows_dev)
-    ids_near = jnp.stack([in_order(ids_near[:, :, :, s], s) for s in range(groups)])
     table_words = tables[0].astype(LOW)
-    looked_up = []
-    for core in (1, 0):
-        found = product(hot(ids_near[:, :, :, core].reshape(-1), vocab_part), table_words)
-        looked_up.append(found.astype(LOW).reshape(groups, 16 * rows_dev, part_width))
-    looked_up = add_low(looked_up[1], swap(looked_up[0], 1))
-    summed = []
-
-    def note(step, streams):
-        if step == 1:
-            summed.append(streams[0])
-        return streams
-
-    x_first = jnp.stack(
-        streams_sum(
-            (looked_up[s].reshape(16, rows_dev, part_width) for s in range(groups)),
-            note,
-            joined=False,
+    token_shards = ids_all // vocab_part
+    tokens_range = jnp.arange(rows_dev, dtype=jnp.int32)
+    before = tokens_range[:, None] < tokens_range[None, :]
+    held = token_shards == expert_index
+    held_place = product(held.reshape(-1, rows_dev).astype(LOW), before.astype(LOW)).astype(jnp.int32)
+    held_place = jnp.where(held, held_place.reshape(held.shape), -1).swapaxes(0, 1)
+    held_words = (ids_all - vocab_start).swapaxes(0, 1)
+    own_shards = lax.dynamic_index_in_dim(token_shards, expert_index, 1, False)
+    same = own_shards[:, :, None] == own_shards[:, None, :]
+    own_place = jnp.sum(jnp.where(same & before[None], 1, 0), axis=1)
+    places = jnp.arange(ROUND_ROWS, dtype=jnp.int32)
+    round_width = axis_width * ROUND_ROWS
+
+    def words_of(start):
+        wanted = jnp.where(
+            held_place[:, :, None, :] == (start + places)[:, None], held_words[:, :, None, :] + 1, 0
         )
-    )
-    routes, loss_rows, domains, targets, documents = after(
-        (routes, loss_rows, domains, targets, documents), summed
-    )
+        return jnp.sum(wanted, axis=-1).reshape(-1) - 1
+
+    def spots_of(start):
+        spot = own_place - start
+        return hot(
+            jnp.where((spot >= 0) & (spot < ROUND_ROWS), own_shards * ROUND_ROWS + spot, -1),
+            round_width,
+        )
+
+    def fetch_round(start):
+        sent = product(hot(words_of(start), vocab_part), table_words).astype(LOW)
+        got = lax.all_to_all(
+            sent.reshape(axis_width, groups * ROUND_ROWS, part_width),
+            "expert",
+            split_axis=0,
+            concat_axis=0,
+            tiled=True,
+        )
+        got = got.reshape(axis_width, groups, ROUND_ROWS, part_width).swapaxes(0, 1)
+        return jnp.einsum(
+            "gtr,grd->gtd",
+            spots_of(start),
+            got.reshape(groups, round_width, part_width),
+            preferred_element_type=f32,
+        ), sent
+
+    def further_rounds(turn, first):
+        return lax.while_loop(
+            lambda carry: carry[0] < most,
+            lambda carry: (carry[0] + ROUND_ROWS, carry[1] + turn(carry[0])),
+            (jnp.full((), ROUND_ROWS, jnp.int32), first),
+        )[1]
+
+    x_first, sent_first = fetch_round(0)
+    routes, loss_rows, domains, targets, documents, token_shards = after(
+        (routes, loss_rows, domains, targets, documents, token_shards), sent_first
+    )
+    shards = jnp.arange(axis_width, dtype=jnp.int32)
+    most = jnp.max(jnp.sum((token_shards[..., None] == shards).astype(jnp.int32), axis=2))
+    x_first = further_rounds(lambda start: fetch_round(start)[0], x_first).astype(LOW)
     x_first = lax.all_to_all(x_first, "dp", split_axis=0, concat_axis=0, tiled=True)
     x_first = x_first.swapaxes(0, 1).reshape(rows_dev, width_model).astype(f32)
 
@@ -521,16 +554,17 @@
     down_seconds = hot(
         jnp.where(down_row < own_rows, -1, down_turned + down_row - own_rows), width_model
     )
+    lefts = after((h_low, shared_hidden, attended, h_first_low), expert_rows)
     early_left = jnp.concatenate(
         [
-            product(h_low, turn_choice).astype(LOW),
-            product(shared_hidden, down_firsts).astype(LOW),
-            product(shared_hidden, down_seconds).astype(LOW),
+            product(lefts[0], turn_choice).astype(LOW),
+            product(lefts[1], down_firsts).astype(LOW),
+            product(lefts[1], down_seconds).astype(LOW),
         ],
         axis=0,
     )
     late_left, late_choice = [], []
-    for stream, left in enumerate((attended, h_first_low, h_first_low, h_first_low)):
+    for stream, left in enumerate((lefts[2], lefts[3], lefts[3], lefts[3])):
         distance = (owner % axis_width) ^ expert_index
         axes = [distance >> 3, (distance >> 1) & 3]
         first_axis, second_axis = axes if stream < 2 else axes[::-1]
@@ -539,7 +573,7 @@
         spot = ((distance & 1) * 16 + first_axis * 4 + second_axis) * groups + owner // axis_width
         choice = hot(spot * own_rows + row, width_model)
         if stream == 0:
-            left = jnp.concatenate([left, h_low, h_low], axis=0)
+            left = jnp.concatenate([left, lefts[0], lefts[0]], axis=0)
         late_left.append(product(left, choice).astype(LOW))
         late_choice.append(choice)
 

time: 655 us -> 634 us (0.968)
  matrix products: 200 us -> 174 us
  waiting for transfers between devices: 152 us -> 173 us
  starting transfers between devices: 134 us -> 120 us
    ppermute x66 -> x49, waiting for transfers between devices: 103 us -> 66.8 us  [swap(): return lax.ppermute(value, 'expert', [(i, i ^ number) for i in range(32)])]
    all_to_all x0 -> x1, waiting for transfers between devices: none -> 26.4 us  [fetch_round(): lax.all_to_all(sent.reshape(axis_width, groups * ROUND_ROWS, part_width),...]
    all_gather x1, waiting for transfers between devices: 0.02 us -> 25.3 us  [body(): packed_all = lax.all_gather(packed, BOTH, axis=0, tiled=True)]
    ppermute x66 -> x49, starting transfers between devices: 71.1 us -> 52.9 us  [swap(): return lax.ppermute(value, 'expert', [(i, i ^ number) for i in range(32)])]
    dot_general x40, matrix products: 113 us -> 97.7 us  [product(): return jnp.dot(left, right, preferred_element_type=jnp.float32)]
    dot_general x13, matrix products: 39 us -> 29.3 us  [inner_rows(): lax.dot_general(left, right, (((0,), (0,)), ((), ())), precision=precisio...]
    convert_element_type x40 -> x23, other arithmetic: 12.2 us -> 3.61 us  [add_low(): return (left.astype(jnp.float32) + right.astype(jnp.float32)).astype(LOW)]
    all_to_all x0 -> x1, starting transfers between devices: none -> 8.32 us  [fetch_round(): lax.all_to_all(sent.reshape(axis_width, groups * ROUND_ROWS, part_width),...]
  transfers between devices with their start and end apart: 87 -> 71, of which waited for: 52 -> 46; matrix products, arithmetic and copies ran while one was open for 39% -> 36% of each run, Pallas kernels for 0% -> 0%
where the time goes in v4:
time: 634 us; the launch traced here: 624 us
  matrix products  174 us (27%)
  waiting for transfers between devices  173 us (27%)
  starting transfers between devices  120 us (19%)
  other arithmetic  75.6 us (12%)
  local copies, waits for them, and re-layouts  38.1 us (6%)
  between operations  20.1 us (3%)
  Pallas kernels  12.7 us (2%)
  blocking collectives  9.37 us (1%)
    dot_general x40, matrix products, product(): return jnp.dot(left, right, preferred_element_type=jnp.float32)  97.7 us
    ppermute x49, waiting for transfers between devices, swap(): return lax.ppermute(value, 'expert', [(i, i ^ number) for i in range(32)])  66.8 us
    ppermute x49, starting transfers between devices, swap(): return lax.ppermute(value, 'expert', [(i, i ^ number) for i in range(32)])  52.9 us
    dot_general x13, matrix products, inner_cols(): lax.dot_general(left, right, (((1,), (1,)), ((), ())), precision=precisio...  39 us
    dot_general x13, matrix products, inner_rows(): lax.dot_general(left, right, (((0,), (0,)), ((), ())), precision=precisio...  29.3 us
    all_to_all x1, waiting for transfers between devices, fetch_round(): lax.all_to_all(sent.reshape(axis_width, groups * ROUND_ROWS, part_width),...  26.4 us
    all_gather x1, waiting for transfers between devices, body(): packed_all = lax.all_gather(packed, BOTH, axis=0, tiled=True)  25.3 us
    unnamed x334, local copies, waits for them, and re-layouts  19.4 us
  transfers between devices with their start and end apart: 71, of which 46 were waited for; matrix products, arithmetic and copies ran while one was open for 36% of the time, Pallas kernels for 0%

profile of v4, /device:TPU:1, one launch (start us, length us, event | category | flops | bytes accessed | tf_op | source)
XLA Modules:
  0.0 623.9 jit_solution(13135763696439804153)
XLA Ops:
  10.8 4.5 collective-permute-start.1
  26.9 3.7 fusion.41
  36.2 8.3 %all-to-all-start.1 = ((bf16[32,96,256]{2,1,0:T(8,128)(2,1)}), bf16[32,96,256]{2,1,0:T(8,128)(2,1)S(1)}, u32[]{:S(2)}, u32[]{:S(2)}) async-start(bf16[32,96,256]{2,1,0:T(8,128)(2,1)} %bitcast.500), calls=%async_computation.1 | async-start | bytes 3145728 | tf_op jit(solution)/shard_map/all_to_all | solution.py:419
  45.3 26.4 %all-to-all-done.1 = bf16[32,96,256]{2,1,0:T(8,128)(2,1)S(1)} async-done(((bf16[32,96,256]{2,1,0:T(8,128)(2,1)}), bf16[32,96,256]{2,1,0:T(8,128)(2,1)S(1)}, u32[]{:S(2)}, u32[]{:S(2)}) %all-to-all-start.1) | async-done | bytes 1572896 | tf_op jit(solution)/shard_map/all_to_all | solution.py:419
  74.4 4.8 all-to-all-start.2
  79.7 8.6 %all-to-all-done.2 = bf16[4,128,256]{2,1,0:T(8,128)(2,1)S(1)} async-done(((bf16[4,128,256]{2,1,0:T(8,128)(2,1)}), bf16[4,128,256]{2,1,0:T(8,128)(2,1)S(1)}, u32[]{:S(2)}, u32[]{:S(2)}) %all-to-all-start.2) | async-done | bytes 262176 | tf_op jit(solution)/shard_map/all_to_all | solution.py:448
  88.6 25.3 %all-gather.5.cloned.1.call-done = bf16[1024,9088]{1,0:T(8,128)(2,1)} async-done(((bf16[8,9088]{1,0:T(8,128)(2,1)}), bf16[1024,9088]{1,0:T(8,128)(2,1)}) %all-gather.5.cloned.1.call-update) | async-done | bytes 18612240 | tf_op jit(solution)/shard_map/all_gather | solution.py:376
  115.9 3.9 fusion.27
  129.8 5.0 all-to-all-start.3
  136.5 3.7 fusion.31
  145.4 5.3 fusion.19
  150.8 6.6 %add_convert_fusion.1 = bf16[1408,1024]{1,0:T(8,128)(2,1)} fusion(f32[1408,1024]{1,0:T(8,128)S(1)} %fusion.19, pred[1408,2048]{1,0:T(32,128)(4,1)S(1)} %iota_compare_fusion.12, bf16[1024,9088]{1,0:T(8,128)(2,1)} %all-gather.5.cloned.1.call-done), kind=kOutput, calls=%fused_computation.41 | convolution fusion | flops 2955673600 | bytes 12189696 | tf_op jit(solution)/shard_map/dot_general | solution.py:34
  158.4 4.0 all-gather.7.cloned.1.call-done
  163.1 3.8 fusion.88
  167.0 6.1 multiply_convert_fusion.2
  176.3 6.9 %all-to-all-start.4 = ((bf16[32,32,1024]{2,1,0:T(8,128)(2,1)}), bf16[32,32,1024]{2,1,0:T(8,128)(2,1)S(1)}, u32[]{:S(2)}, u32[]{:S(2)}) async-start(bf16[32,32,1024]{2,1,0:T(8,128)(2,1)} %bitcast.493), calls=%async_computation.4 | async-start | bytes 4194304 | tf_op jit(solution)/shard_map/all_to_all | solution.py:584
  193.2 5.2 all-gather.9.cloned.1.call-done
  198.4 7.9 %fusion.42 = bf16[2048,1024]{1,0:T(8,128)(2,1)} fusion(bf16[1002,1024]{1,0:T(8,128)(2,1)} %all-gather.9.cloned.1.call-done, s32[2048]{0:T(1024)S(1)} %sub.287), kind=kOutput, calls=%fused_computation.78 | convolution fusion | flops 4206841856 | bytes 6254592 | tf_op jit(solution)/shard_map/dot_general | solution.py:34
  206.4 5.2 all-to-all-done.4
  239.5 6.2 collective-permute-start.15
  245.8 4.1 select_reduce_fusion.2
  254.7 4.5 fusion.370
  264.9 6.9 %fusion.226 = f32[2048,1024]{1,0:T(8,128)} fusion(bf16[1002,1024]{1,0:T(8,128)(2,1)S(1)} %copy-done.147, f32[2048,1002]{0,1:T(8,128)S(1)} %get-tuple-element.622, f32[2048]{0:T(1024)S(1)} %get-tuple-element.621, s32[2048]{0:T(1024)S(1)} %copy-done.80), kind=kOutput, calls=%fused_computation.463 | convolution fusion | flops 4210900992 | bytes 18665472 | tf_op jit(solution)/shard_map/dot_general | solution.py:34
  289.0 5.3 add_convert_fusion
  330.9 8.2 %convolution_convert_fusion = bf16[1024,4864]{1,0:T(8,128)(2,1)} fusion(bf16[128,1024]{1,0:T(8,128)(2,1)S(1)} %get-tuple-element.201, bf16[128,2816]{1,0:T(8,128)(2,1)S(1)} %pad_maximum_fusion.7, bf16[128,1024]{1,0:T(8,128)(2,1)S(1)} %fusion.107, bf16[128,1024]{1,0:T(8,128)(2,1)S(1)} %fusion.108, bf16[128,1024]{1,0:T(8,128)(2,1)S(1)} %fusion.105), kind=kOutput, calls=%fused_computation.23 | convolution fusion | flops 3858694144 | bytes 11730944 | tf_op jit(solution)/shard_map/dot_general | solution.py:38
  344.6 9.4 %all-to-all-start.5 = ((bf16[32,32,1024]{2,1,0:T(8,128)(2,1)}), bf16[32,32,1024]{2,1,0:T(8,128)(2,1)}, u32[]{:S(2)}, u32[]{:S(2)}) async-start(bf16[32,32,1024]{2,1,0:T(8,128)(2,1)} %bitcast.470), calls=%async_computation.5 | async-start | bytes 4194304 | tf_op jit(solution)/shard_map/all_to_all | solution.py:621
  354.0 5.4 select_convert_fusion
  359.4 4.6 convolution_convert_fusion.5
  368.3 6.0 fusion.29
  374.3 6.3 %collective-permute-done.37 = bf16[1002,256]{1,0:T(8,128)(2,1)S(1)} collective-permute-done((bf16[1002,256]{1,0:T(8,128)(2,1)S(1)}, bf16[1002,256]{1,0:T(8,128)(2,1)S(1)}, u32[]{:S(2)}, u32[]{:S(2)}) %collective-permute-start.37) | collective-permute-done | bytes 513056 | tf_op jit(solution)/shard_map/ppermute | solution.py:136
  382.4 6.3 %multiply_convert_fusion.1 = (bf16[1024,704]{0,1:T(8,128)(2,1)S(1)}, bf16[1024,704]{0,1:T(8,128)(2,1)S(1)}) fusion(f32[1024,704]{0,1:T(8,128)} %copy-done.153, f32[1024,704]{0,1:T(8,128)} %get-tuple-element.616, bf16[1024,1024]{1,0:T(8,128)(2,1)} %bitcast.123, bf16[3,704,1024]{2,1,0:T(8,128)(2,1)} %all-gather.7.cloned.1.call-done), kind=kOutput, calls=%fused_computation.91 | convolution fusion | flops 1486487552 | bytes 12189696 | tf_op jit(solution)/shard_map/dot_general | solution.py:48
  388.7 4.3 fusion.87
  393.0 4.7 add_convert_fusion.2
  397.7 7.0 %all-to-all-start.6 = ((bf16[32,32,1024]{2,1,0:T(8,128)(2,1)}), bf16[32,32,1024]{2,1,0:T(8,128)(2,1)}, u32[]{:S(2)}, u32[]{:S(2)}) async-start(bf16[32,32,1024]{2,1,0:T(8,128)(2,1)} %bitcast.492), calls=%async_computation.6 | async-start | bytes 4194304 | tf_op jit(solution)/shard_map/all_to_all | solution.py:658
  404.8 3.8 convolution_convert_fusion.7
  408.6 3.4 convolution_convert_fusion.8
  412.0 3.3 convolution_convert_fusion.6
  424.1 15.3 %all-to-all-done.6 = bf16[32,32,1024]{2,1,0:T(8,128)(2,1)} async-done(((bf16[32,32,1024]{2,1,0:T(8,128)(2,1)}), bf16[32,32,1024]{2,1,0:T(8,128)(2,1)}, u32[]{:S(2)}, u32[]{:S(2)}) %all-to-all-start.6) | async-done | bytes 2097184 | tf_op jit(solution)/shard_map/all_to_all | solution.py:658
  452.4 5.2 multiply_reduce_fusion.5
  457.9 9.4 %all_to_all.81 = bf16[4,128,256]{2,1,0:T(8,128)(2,1)} all-to-all(bf16[4,128,256]{2,1,0:T(8,128)(2,1)S(1)} %bitcast.514), channel_id=1, replica_groups=mesh['dp'=4,'expert'=32] {'dp'}, dimensions={0} | all-to-all | bytes 524288 | tf_op jit(solution)/shard_map/all_to_all | solution.py:713
  490.7 5.7 collective-permute-done.49
  507.0 7.6 %collective-permute-done.50 = bf16[4,32,1024]{2,1,0:T(8,128)(2,1)S(1)} collective-permute-done((bf16[4,32,1024]{2,1,0:T(8,128)(2,1)S(1)}, bf16[4,32,1024]{2,1,0:T(8,128)(2,1)S(1)}, u32[]{:S(2)}, u32[]{:S(2)}) %collective-permute-start.50) | collective-permute-done | bytes 262176 | tf_op jit(solution)/shard_map/ppermute | solution.py:132
  521.3 11.8 %collective-permute-done.53 = bf16[2,32,2176]{2,1,0:T(8,128)(2,1)S(1)} collective-permute-done((bf16[2,32,2176]{2,1,0:T(8,128)(2,1)S(1)}, bf16[2,32,2176]{2,1,0:T(8,128)(2,1)S(1)}, u32[]{:S(2)}, u32[]{:S(2)}) %collective-permute-start.53) | collective-permute-done | bytes 278560 | tf_op jit(solution)/shard_map/ppermute | solution.py:132
  534.1 13.9 %multiply_reduce_fusion.2 = (f32[256]{0:T(256)S(1)}, f32[1002,256]{1,0:T(8,128)}) fusion(bf16[16384,256]{1,0:T(8,128)(2,1)} %all-gather.11.cloned.1.call-done, s32[16384]{0:T(1024)S(1)} %bitcast.489), kind=kOutput, calls=%fused_computation.224 | convolution fusion | flops 8422315008 | bytes 9481216 | tf_op jit(solution)/shard_map/dot_general | solution.py:34
  556.9 6.1 all-to-all-start.8
  566.1 5.4 all-to-all-done.8
  574.2 8.7 %all-to-all-start.9 = ((f32[128,2,128]{2,1,0:T(2,128)}), f32[128,2,128]{2,1,0:T(2,128)}, u32[]{:S(2)}, u32[]{:S(2)}) async-start(f32[128,2,128]{2,1,0:T(2,128)} %broadcast_in_dim.321), calls=%async_computation.10 | async-start | bytes 262144 | tf_op jit(solution)/shard_map/all_to_all | solution.py:801
  607.6 8.1 %tables_update.1 = (f32[1002,2,256]{2,1,0:T(2,128)}, f32[1002,2,256]{2,1,0:T(2,128)}, f32[1002,2,256]{2,1,0:T(2,128)}) custom-call(f32[1,1]{1,0:T(1,128)} %bitcast.165.clip, f32[1002,2,256]{2,1,0:T(2,128)} %bitcast.478, f32[1002,2,256]{2,1,0:T(2,128)} %pad_maximum_fusion.3.grad, f32[1002,2,256]{2,1,0:T(2,128)} %bitcast.498, f32[1002,2,256]{2,1,0:T(2,128)} %bitcast.499), custom_call_target="tpu_custom_call" | custom-call | tf_op jit(solution)/shard_map/tables_update/pallas_call | solution.py:120
  (754 shorter events, 261.7 us)
Async XLA Ops:
  7.2 106.6 %all-gather.5.cloned.1.call-start = ((), (), s32[]{:S(2)}) async-start(), calls=%async_computation.11 | async-start | bytes 18757632 | tf_op jit(solution)/shard_map/all_gather | solution.py:376
  10.8 151.6 %all-gather.7.cloned.1.call-start = ((), (), s32[]{:S(2)}) async-start(), calls=%async_computation.12 | async-start | bytes 5406720 | tf_op jit(solution)/shard_map/all_gather | solution.py:454
  10.8 11.7 %collective-permute-start.1 = (s32[1,4096]{1,0:T(1,128)}, s32[1,4096]{1,0:T(1,128)S(1)}, u32[]{:S(2)}, u32[]{:S(2)}) collective-permute-start(s32[1,4096]{1,0:T(1,128)} %param.27), channel_id=1, source_target_pairs={{0,64},{32,96},{64,0},{96,32},{1,65},{33,97},{65,1},{97,33},{2,66}... | collective-permute-start | bytes 49160 | tf_op jit(solution)/shard_map/ppermute | solution.py:136
  15.3 7.2 %collective-permute-start = (s32[1,4096]{1,0:T(1,128)}, s32[1,4096]{1,0:T(1,128)S(1)}, u32[]{:S(2)}, u32[]{:S(2)}) collective-permute-start(s32[1,4096]{1,0:T(1,128)} %param.27), channel_id=1, source_target_pairs={{0,32},{32,0},{64,96},{96,64},{1,33},{33,1},{65,97},{97,65},{2,34}... | collective-permute-start | bytes 49160 | tf_op jit(solution)/shard_map/ppermute | solution.py:136
  16.0 6.4 %collective-permute-start.2 = (s32[1,4096]{1,0:T(1,128)}, s32[1,4096]{1,0:T(1,128)S(1)}, u32[]{:S(2)}, u32[]{:S(2)}) collective-permute-start(s32[1,4096]{1,0:T(1,128)} %param.27), channel_id=1, source_target_pairs={{0,96},{32,64},{64,32},{96,0},{1,97},{33,65},{65,33},{97,1},{2,98}... | collective-permute-start | bytes 49160 | tf_op jit(solution)/shard_map/ppermute | solution.py:136
  36.2 35.6 %all-to-all-start.1 = ((bf16[32,96,256]{2,1,0:T(8,128)(2,1)}), bf16[32,96,256]{2,1,0:T(8,128)(2,1)S(1)}, u32[]{:S(2)}, u32[]{:S(2)}) async-start(bf16[32,96,256]{2,1,0:T(8,128)(2,1)} %bitcast.500), calls=%async_computation.1 | async-start | bytes 3145728 | tf_op jit(solution)/shard_map/all_to_all | solution.py:419
  74.4 13.9 %all-to-all-start.2 = ((bf16[4,128,256]{2,1,0:T(8,128)(2,1)}), bf16[4,128,256]{2,1,0:T(8,128)(2,1)S(1)}, u32[]{:S(2)}, u32[]{:S(2)}) async-start(bf16[4,128,256]{2,1,0:T(8,128)(2,1)} %convert_element_type.660), calls=%async_computation.2 | async-start | bytes 524288 | tf_op jit(solution)/shard_map/all_to_all | solution.py:448
  129.8 33.3 %all-to-all-start.3 = ((bf16[32,32,1024]{2,1,0:T(8,128)(2,1)}), bf16[32,32,1024]{2,1,0:T(8,128)(2,1)}, u32[]{:S(2)}, u32[]{:S(2)}) async-start(bf16[32,32,1024]{2,1,0:T(8,128)(2,1)} %bitcast.17), calls=%async_computation.3 | async-start | bytes 4194304 | tf_op jit(solution)/shard_map/all_to_all | solution.py:520
  134.8 63.7 %all-gather.9.cloned.1.call-start = ((), (), s32[]{:S(2)}) async-start(), calls=%async_computation.13 | async-start | bytes 2580480 | tf_op jit(solution)/shard_map/all_gather | solution.py:515
  176.3 35.3 %all-to-all-start.4 = ((bf16[32,32,1024]{2,1,0:T(8,128)(2,1)}), bf16[32,32,1024]{2,1,0:T(8,128)(2,1)S(1)}, u32[]{:S(2)}, u32[]{:S(2)}) async-start(bf16[32,32,1024]{2,1,0:T(8,128)(2,1)} %bitcast.493), calls=%async_computation.4 | async-start | bytes 4194304 | tf_op jit(solution)/shard_map/all_to_all | solution.py:584
  183.3 295.5 %reduce-scatter.2.cloned.1.call-start = ((), (), s32[]{:S(2)}) async-start(), calls=%async_computation.14 | async-start | bytes 10272768 | tf_op jit(solution)/shard_map/reduce_scatter | solution.py:650
  220.7 5.4 collective-permute-start.10
  224.6 6.7 %collective-permute-start.5 = (bf16[4,16,1024]{2,1,0:T(8,128)(2,1)S(1)}, bf16[4,16,1024]{2,1,0:T(8,128)(2,1)S(1)}, u32[]{:S(2)}, u32[]{:S(2)}) collective-permute-start(bf16[4,16,1024]{2,1,0:T(8,128)(2,1)S(1)} %get-tuple-element.575), channel_id=1, source_target_pairs={{0,24},{1,25},{2,26},{3,27},{4,28},{5,29},{6,30},{7,31},{8,16},{9,... | collective-permute-start | bytes 393224 | tf_op jit(solution)/shard_map/ppermute | solution.py:132
  226.2 7.0 %collective-permute-start.11 = (bf16[4,16,1024]{2,1,0:T(8,128)(2,1)S(1)}, bf16[4,16,1024]{2,1,0:T(8,128)(2,1)S(1)}, u32[]{:S(2)}, u32[]{:S(2)}) collective-permute-start(bf16[4,16,1024]{2,1,0:T(8,128)(2,1)S(1)} %get-tuple-element.581), channel_id=1, source_target_pairs={{0,6},{1,7},{2,4},{3,5},{4,2},{5,3},{6,0},{7,1},{8,14},{9,15},{10,... | collective-permute-start | bytes 393224 | tf_op jit(solution)/shard_map/ppermute | solution.py:132
  229.1 7.0 %collective-permute-start.8 = (bf16[2,4,16,1024]{3,2,1,0:T(8,128)(2,1)S(1)}, bf16[2,4,16,1024]{3,2,1,0:T(8,128)(2,1)S(1)}, u32[]{:S(2)}, u32[]{:S(2)}) collective-permute-start(bf16[2,4,16,1024]{3,2,1,0:T(8,128)(2,1)S(1)} %pad_maximum_fusion.16), channel_id=1, source_target_pairs={{0,24},{1,25},{2,26},{3,27},{4,28},{5,29},{6,30},{7,31},{8,16},{9,... | collective-permute-start | bytes 786440 | tf_op jit(solution)/shard_map/ppermute | solution.py:132
  231.3 7.5 %collective-permute-start.6 = (bf16[2,4,16,1024]{3,2,1,0:T(8,128)(2,1)S(1)}, bf16[2,4,16,1024]{3,2,1,0:T(8,128)(2,1)S(1)}, u32[]{:S(2)}, u32[]{:S(2)}) collective-permute-start(bf16[2,4,16,1024]{3,2,1,0:T(8,128)(2,1)S(1)} %pad_maximum_fusion.15), channel_id=1, source_target_pairs={{0,8},{1,9},{2,10},{3,11},{4,12},{5,13},{6,14},{7,15},{8,0},{9,1},... | collective-permute-start | bytes 786440 | tf_op jit(solution)/shard_map/ppermute | solution.py:132
  231.8 6.8 %collective-permute-start.14 = (bf16[2,4,16,1024]{3,2,0,1:T(8,128)(2,1)S(1)}, bf16[2,4,16,1024]{3,2,0,1:T(8,128)(2,1)S(1)}, u32[]{:S(2)}, u32[]{:S(2)}) collective-permute-start(bf16[2,4,16,1024]{3,2,0,1:T(8,128)(2,1)S(1)} %pad_maximum_fusion.19), channel_id=1, source_target_pairs={{0,6},{1,7},{2,4},{3,5},{4,2},{5,3},{6,0},{7,1},{8,14},{9,15},{10,... | collective-permute-start | bytes 786440 | tf_op jit(solution)/shard_map/ppermute | solution.py:132
  233.2 6.1 collective-permute-start.12
  239.5 12.9 %collective-permute-start.15 = (bf16[16,64,1024]{2,1,0:T(8,128)(2,1)S(1)}, bf16[16,64,1024]{2,1,0:T(8,128)(2,1)}, u32[]{:S(2)}, u32[]{:S(2)}) collective-permute-start(bf16[16,64,1024]{2,1,0:T(8,128)(2,1)S(1)} %bitcast.476), channel_id=1, source_target_pairs={{0,1},{1,0},{2,3},{3,2},{4,5},{5,4},{6,7},{7,6},{8,9},{9,8},{10,11... | collective-permute-start | bytes 6291464 | tf_op jit(solution)/shard_map/ppermute | solution.py:132
  261.5 10.3 %collective-permute-start.18 = (f32[3,2048]{1,0:T(4,128)S(1)}, f32[3,2048]{1,0:T(4,128)S(1)}, u32[]{:S(2)}, u32[]{:S(2)}) collective-permute-start(f32[3,2048]{1,0:T(4,128)S(1)} %pad_maximum_fusion.43.stats), channel_id=1, source_target_pairs={{0,24},{1,25},{2,26},{3,27},{4,28},{5,29},{6,30},{7,31},{8,16},{9,... | collective-permute-start | bytes 73736 | tf_op jit(solution)/shard_map/ppermute | solution.py:132
  262.3 9.5 %collective-permute-start.17 = (f32[3,2048]{1,0:T(4,128)S(1)}, f32[3,2048]{1,0:T(4,128)S(1)}, u32[]{:S(2)}, u32[]{:S(2)}) collective-permute-start(f32[3,2048]{1,0:T(4,128)S(1)} %pad_maximum_fusion.43.stats), channel_id=1, source_target_pairs={{0,16},{1,17},{2,18},{3,19},{4,20},{5,21},{6,22},{7,23},{8,24},{9,... | collective-permute-start | bytes 73736 | tf_op jit(solution)/shard_map/ppermute | solution.py:132
  264.7 7.2 %collective-permute-start.16 = (f32[3,2048]{1,0:T(4,128)S(1)}, f32[3,2048]{1,0:T(4,128)S(1)}, u32[]{:S(2)}, u32[]{:S(2)}) collective-permute-start(f32[3,2048]{1,0:T(4,128)S(1)} %pad_maximum_fusion.43.stats), channel_id=1, source_target_pairs={{0,8},{1,9},{2,10},{3,11},{4,12},{5,13},{6,14},{7,15},{8,0},{9,1},... | collective-permute-start | bytes 73736 | tf_op jit(solution)/shard_map/ppermute | solution.py:132
  300.5 7.6 %collective-permute-start.24 = (bf16[2,4,16,1024]{3,2,1,0:T(8,128)(2,1)S(1)}, bf16[2,4,16,1024]{3,2,1,0:T(8,128)(2,1)S(1)}, u32[]{:S(2)}, u32[]{:S(2)}) collective-permute-start(bf16[2,4,16,1024]{3,2,1,0:T(8,128)(2,1)S(1)} %slice_bitcast_fusion.15), channel_id=1, source_target_pairs={{0,8},{1,9},{2,10},{3,11},{4,12},{5,13},{6,14},{7,15},{8,0},{9,1},... | collective-permute-start | bytes 786440 | tf_op jit(solution)/shard_map/ppermute | solution.py:132
  301.8 8.5 %collective-permute-start.26 = (bf16[2,4,16,1024]{3,2,1,0:T(8,128)(2,1)S(1)}, bf16[2,4,16,1024]{3,2,1,0:T(8,128)(2,1)S(1)}, u32[]{:S(2)}, u32[]{:S(2)}) collective-permute-start(bf16[2,4,16,1024]{3,2,1,0:T(8,128)(2,1)S(1)} %pad_maximum_fusion.20), channel_id=1, source_target_pairs={{0,24},{1,25},{2,26},{3,27},{4,28},{5,29},{6,30},{7,31},{8,16},{9,... | collective-permute-start | bytes 786440 | tf_op jit(solution)/shard_map/ppermute | solution.py:132
  303.6 8.2 %collective-permute-start.32 = (bf16[2,4,16,1024]{3,2,0,1:T(8,128)(2,1)S(1)}, bf16[2,4,16,1024]{3,2,0,1:T(8,128)(2,1)S(1)}, u32[]{:S(2)}, u32[]{:S(2)}) collective-permute-start(bf16[2,4,16,1024]{3,2,0,1:T(8,128)(2,1)S(1)} %pad_maximum_fusion.21), channel_id=1, source_target_pairs={{0,6},{1,7},{2,4},{3,5},{4,2},{5,3},{6,0},{7,1},{8,14},{9,15},{10,... | collective-permute-start | bytes 786440 | tf_op jit(solution)/shard_map/ppermute | solution.py:132
  304.7 7.3 %collective-permute-start.30 = (bf16[2,4,16,1024]{3,2,1,0:T(8,128)(2,1)S(1)}, bf16[2,4,16,1024]{3,2,1,0:T(8,128)(2,1)S(1)}, u32[]{:S(2)}, u32[]{:S(2)}) collective-permute-start(bf16[2,4,16,1024]{3,2,1,0:T(8,128)(2,1)S(1)} %slice.687), channel_id=1, source_target_pairs={{0,2},{1,3},{2,0},{3,1},{4,6},{5,7},{6,4},{7,5},{8,10},{9,11},{10,... | collective-permute-start | bytes 786440 | tf_op jit(solution)/shard_map/ppermute | solution.py:132
  344.6 37.8 %all-to-all-start.5 = ((bf16[32,32,1024]{2,1,0:T(8,128)(2,1)}), bf16[32,32,1024]{2,1,0:T(8,128)(2,1)}, u32[]{:S(2)}, u32[]{:S(2)}) async-start(bf16[32,32,1024]{2,1,0:T(8,128)(2,1)} %bitcast.470), calls=%async_computation.5 | async-start | bytes 4194304 | tf_op jit(solution)/shard_map/all_to_all | solution.py:621
  366.4 14.2 %collective-permute-start.37 = (bf16[1002,256]{1,0:T(8,128)(2,1)S(1)}, bf16[1002,256]{1,0:T(8,128)(2,1)S(1)}, u32[]{:S(2)}, u32[]{:S(2)}) collective-permute-start(bf16[1002,256]{1,0:T(8,128)(2,1)S(1)} %get-tuple-element.548), channel_id=1, source_target_pairs={{0,96},{32,64},{64,32},{96,0},{1,97},{33,65},{65,33},{97,1},{2,98}... | collective-permute-start | bytes 1539080 | tf_op jit(solution)/shard_map/ppermute | solution.py:136
  367.0 13.6 %collective-permute-start.36 = (bf16[1002,256]{1,0:T(8,128)(2,1)S(1)}, bf16[1002,256]{1,0:T(8,128)(2,1)S(1)}, u32[]{:S(2)}, u32[]{:S(2)}) collective-permute-start(bf16[1002,256]{1,0:T(8,128)(2,1)S(1)} %get-tuple-element.549), channel_id=1, source_target_pairs={{0,32},{32,0},{64,96},{96,64},{1,33},{33,1},{65,97},{97,65},{2,34}... | collective-permute-start | bytes 1539080 | tf_op jit(solution)/shard_map/ppermute | solution.py:136
  397.7 41.7 %all-to-all-start.6 = ((bf16[32,32,1024]{2,1,0:T(8,128)(2,1)}), bf16[32,32,1024]{2,1,0:T(8,128)(2,1)}, u32[]{:S(2)}, u32[]{:S(2)}) async-start(bf16[32,32,1024]{2,1,0:T(8,128)(2,1)} %bitcast.492), calls=%async_computation.6 | async-start | bytes 4194304 | tf_op jit(solution)/shard_map/all_to_all | solution.py:658
  404.7 129.4 %all-gather.11.cloned.1.call-start = ((), (), s32[]{:S(2)}) async-start(), calls=%async_computation.15 | async-start | bytes 8650752 | tf_op jit(solution)/shard_map/all_gather | solution.py:714
  419.2 26.7 %collective-permute-start.39 = (bf16[3,176,1024]{2,1,0:T(8,128)(2,1)}, bf16[3,176,1024]{2,1,0:T(8,128)(2,1)}, u32[]{:S(2)}, u32[]{:S(2)}) collective-permute-start(bf16[3,176,1024]{2,1,0:T(8,128)(2,1)} %get-tuple-element.532), channel_id=1, source_target_pairs={{0,96},{32,64},{64,32},{96,0},{1,97},{33,65},{65,33},{97,1},{2,98}... | collective-permute-start | bytes 3244040 | tf_op jit(solution)/shard_map/ppermute | solution.py:136
  421.3 25.1 %collective-permute-start.38 = (bf16[3,176,1024]{2,1,0:T(8,128)(2,1)}, bf16[3,176,1024]{2,1,0:T(8,128)(2,1)}, u32[]{:S(2)}, u32[]{:S(2)}) collective-permute-start(bf16[3,176,1024]{2,1,0:T(8,128)(2,1)} %get-tuple-element.533), channel_id=1, source_target_pairs={{0,32},{32,0},{64,96},{96,64},{1,33},{33,1},{65,97},{97,65},{2,34}... | collective-permute-start | bytes 3244040 | tf_op jit(solution)/shard_map/ppermute | solution.py:136
  468.0 6.6 %collective-permute-start.42 = (bf16[512,1024]{1,0:T(8,128)(2,1)S(1)}, bf16[512,1024]{1,0:T(8,128)(2,1)S(1)}, u32[]{:S(2)}, u32[]{:S(2)}) collective-permute-start(bf16[512,1024]{1,0:T(8,128)(2,1)S(1)} %convolution_convert_fusion.9), channel_id=1, source_target_pairs={{0,1},{1,0},{2,3},{3,2},{4,5},{5,4},{6,7},{7,6},{8,9},{9,8},{10,11... | collective-permute-start | bytes 3145736 | tf_op jit(solution)/shard_map/ppermute | solution.py:132
  479.7 16.7 %collective-permute-start.49 = (bf16[8,32,1024]{2,1,0:T(8,128)(2,1)}, bf16[8,32,1024]{2,1,0:T(8,128)(2,1)}, u32[]{:S(2)}, u32[]{:S(2)}) collective-permute-start(bf16[8,32,1024]{2,1,0:T(8,128)(2,1)} %slice.592), channel_id=1, source_target_pairs={{0,2},{1,3},{2,0},{3,1},{4,6},{5,7},{6,4},{7,5},{8,10},{9,11},{10,... | collective-permute-start | bytes 1572872 | tf_op jit(solution)/shard_map/ppermute | solution.py:132
  482.8 16.8 %collective-permute-start.46 = (bf16[8,32,1024]{2,1,0:T(8,128)(2,1)S(1)}, bf16[8,32,1024]{2,1,0:T(8,128)(2,1)S(1)}, u32[]{:S(2)}, u32[]{:S(2)}) collective-permute-start(bf16[8,32,1024]{2,1,0:T(8,128)(2,1)S(1)} %slice.586), channel_id=1, source_target_pairs={{0,24},{1,25},{2,26},{3,27},{4,28},{5,29},{6,30},{7,31},{8,16},{9,... | collective-permute-start | bytes 1572872 | tf_op jit(solution)/shard_map/ppermute | solution.py:132
  488.0 16.0 %collective-permute-start.51 = (bf16[8,32,1152]{2,1,0:T(8,128)(2,1)S(1)}, bf16[8,32,1152]{2,1,0:T(8,128)(2,1)S(1)}, u32[]{:S(2)}, u32[]{:S(2)}) collective-permute-start(bf16[8,32,1152]{2,1,0:T(8,128)(2,1)S(1)} %slice.596), channel_id=1, source_target_pairs={{0,6},{1,7},{2,4},{3,5},{4,2},{5,3},{6,0},{7,1},{8,14},{9,15},{10,... | collective-permute-start | bytes 1769480 | tf_op jit(solution)/shard_map/ppermute | solution.py:132
  490.6 14.7 %collective-permute-start.44 = (bf16[8,32,1152]{2,1,0:T(8,128)(2,1)S(1)}, bf16[8,32,1152]{2,1,0:T(8,128)(2,1)S(1)}, u32[]{:S(2)}, u32[]{:S(2)}) collective-permute-start(bf16[8,32,1152]{2,1,0:T(8,128)(2,1)S(1)} %slice.582), channel_id=1, source_target_pairs={{0,8},{1,9},{2,10},{3,11},{4,12},{5,13},{6,14},{7,15},{8,0},{9,1},... | collective-permute-start | bytes 1769480 | tf_op jit(solution)/shard_map/ppermute | solution.py:132
  497.6 16.9 %collective-permute-start.50 = (bf16[4,32,1024]{2,1,0:T(8,128)(2,1)S(1)}, bf16[4,32,1024]{2,1,0:T(8,128)(2,1)S(1)}, u32[]{:S(2)}, u32[]{:S(2)}) collective-permute-start(bf16[4,32,1024]{2,1,0:T(8,128)(2,1)S(1)} %slice.720), channel_id=1, source_target_pairs={{0,6},{1,7},{2,4},{3,5},{4,2},{5,3},{6,0},{7,1},{8,14},{9,15},{10,... | collective-permute-start | bytes 786440 | tf_op jit(solution)/shard_map/ppermute | solution.py:132
  499.9 16.6 %collective-permute-start.47 = (bf16[4,32,1024]{2,1,0:T(8,128)(2,1)S(1)}, bf16[4,32,1024]{2,1,0:T(8,128)(2,1)S(1)}, u32[]{:S(2)}, u32[]{:S(2)}) collective-permute-start(bf16[4,32,1024]{2,1,0:T(8,128)(2,1)S(1)} %slice.716), channel_id=1, source_target_pairs={{0,8},{1,9},{2,10},{3,11},{4,12},{5,13},{6,14},{7,15},{8,0},{9,1},... | collective-permute-start | bytes 786440 | tf_op jit(solution)/shard_map/ppermute | solution.py:132
  504.1 14.0 %collective-permute-start.52 = (bf16[4,32,1152]{2,1,0:T(8,128)(2,1)S(1)}, bf16[4,32,1152]{2,1,0:T(8,128)(2,1)S(1)}, u32[]{:S(2)}, u32[]{:S(2)}) collective-permute-start(bf16[4,32,1152]{2,1,0:T(8,128)(2,1)S(1)} %slice.722), channel_id=1, source_target_pairs={{0,2},{1,3},{2,0},{3,1},{4,6},{5,7},{6,4},{7,5},{8,10},{9,11},{10,... | collective-permute-start | bytes 884744 | tf_op jit(solution)/shard_map/ppermute | solution.py:132
  505.4 15.4 %collective-permute-start.45 = (bf16[4,32,1152]{2,1,0:T(8,128)(2,1)S(1)}, bf16[4,32,1152]{2,1,0:T(8,128)(2,1)S(1)}, u32[]{:S(2)}, u32[]{:S(2)}) collective-permute-start(bf16[4,32,1152]{2,1,0:T(8,128)(2,1)S(1)} %slice.714), channel_id=1, source_target_pairs={{0,24},{1,25},{2,26},{3,27},{4,28},{5,29},{6,30},{7,31},{8,16},{9,... | collective-permute-start | bytes 884744 | tf_op jit(solution)/shard_map/ppermute | solution.py:132
  506.0 42.0 %collective-permute-start.54 = (bf16[1002,256]{1,0:T(8,128)(2,1)}, bf16[1002,256]{1,0:T(8,128)(2,1)S(1)}, u32[]{:S(2)}, u32[]{:S(2)}) collective-permute-start(bf16[1002,256]{1,0:T(8,128)(2,1)} %get-tuple-element.215), channel_id=1, source_target_pairs={{0,64},{32,96},{64,0},{96,32},{1,65},{33,97},{65,1},{97,33},{2,66}... | collective-permute-start | bytes 1539080 | tf_op jit(solution)/shard_map/ppermute | solution.py:136
  514.6 33.5 %collective-permute-start.55 = (bf16[3,176,1024]{2,1,0:T(8,128)(2,1)S(1)}, bf16[3,176,1024]{2,1,0:T(8,128)(2,1)S(1)}, u32[]{:S(2)}, u32[]{:S(2)}) collective-permute-start(bf16[3,176,1024]{2,1,0:T(8,128)(2,1)S(1)} %copy-done.24), channel_id=1, source_target_pairs={{0,64},{32,96},{64,0},{96,32},{1,65},{33,97},{65,1},{97,33},{2,66}... | collective-permute-start | bytes 3244040 | tf_op jit(solution)/shard_map/ppermute | solution.py:136
  518.3 14.9 %collective-permute-start.53 = (bf16[2,32,2176]{2,1,0:T(8,128)(2,1)S(1)}, bf16[2,32,2176]{2,1,0:T(8,128)(2,1)S(1)}, u32[]{:S(2)}, u32[]{:S(2)}) collective-permute-start(bf16[2,32,2176]{2,1,0:T(8,128)(2,1)S(1)} %pad_maximum_fusion.10), channel_id=1, source_target_pairs={{0,24},{1,25},{2,26},{3,27},{4,28},{5,29},{6,30},{7,31},{8,16},{9,... | collective-permute-start | bytes 835592 | tf_op jit(solution)/shard_map/ppermute | solution.py:132
  520.9 12.4 %collective-permute-start.48 = (bf16[2,32,2176]{2,1,0:T(8,128)(2,1)S(1)}, bf16[2,32,2176]{2,1,0:T(8,128)(2,1)S(1)}, u32[]{:S(2)}, u32[]{:S(2)}) collective-permute-start(bf16[2,32,2176]{2,1,0:T(8,128)(2,1)S(1)} %pad_maximum_fusion.11), channel_id=1, source_target_pairs={{0,2},{1,3},{2,0},{3,1},{4,6},{5,7},{6,4},{7,5},{8,10},{9,11},{10,... | collective-permute-start | bytes 835592 | tf_op jit(solution)/shard_map/ppermute | solution.py:132
  556.9 14.6 %all-to-all-start.8 = ((bf16[4,8,9216]{2,1,0:T(8,128)(2,1)}), bf16[4,8,9216]{2,1,0:T(8,128)(2,1)}, u32[]{:S(2)}, u32[]{:S(2)}) async-start(bf16[4,8,9216]{2,1,0:T(8,128)(2,1)} %pad_maximum_fusion.9), calls=%async_computation.9 | async-start | bytes 1179648 | tf_op jit(solution)/shard_map/all_to_all | solution.py:767
  574.2 18.4 %all-to-all-start.9 = ((f32[128,2,128]{2,1,0:T(2,128)}), f32[128,2,128]{2,1,0:T(2,128)}, u32[]{:S(2)}, u32[]{:S(2)}) async-start(f32[128,2,128]{2,1,0:T(2,128)} %broadcast_in_dim.321), calls=%async_computation.10 | async-start | bytes 262144 | tf_op jit(solution)/shard_map/all_to_all | solution.py:801
  (181 other events, 1328.0 us)
Sparse Core Ops, SparseCore 0:
  11.7 102.0 all-gather.4
  116.1 46.2 all-gather.6
  164.6 33.8 all-gather.8
  339.3 119.3 reduce-scatter.1
  467.4 66.6 all-gather.10

commit v5 on v4

--- a/solution.py
+++ b/solution.py
@@ -596,7 +596,7 @@
     row_total = jnp.sum(expos, axis=1)
     row_target = jnp.sum(jnp.where(is_target, logits, 0.0), axis=1)
     rest_low = jnp.where(is_target, 0.0, expos).astype(LOW)
-    d_rest = product(rest_low, head)
+    d_rest = product(rest_low, head).astype(LOW)
     stats = meet_stats(jnp.stack([row_top, row_total, row_target]), d_rest)
     log_norm = stats[0] + jnp.log(stats[1])
     entropy = log_norm[:per_device] - stats[2, :per_device]
@@ -605,7 +605,8 @@
     terms = jnp.concatenate([own_loss[None], counts, jnp.zeros((127 - experts,), f32)])
     rest_scale = jnp.exp(row_top - log_norm) * grad_weights
     target_grad = (jnp.exp(stats[2] - log_norm) - 1.0) * grad_weights
-    d_rows_all = d_rest * rest_scale[:, None] + target_grad[:, None] * target_head.astype(f32)
+    d_rows_all = d_rest.astype(f32) * rest_scale[:, None]
+    d_rows_all = d_rows_all + target_grad[:, None] * target_head.astype(f32)
     d_rows_all = d_rows_all.astype(LOW)
     d_logits = jnp.where(
         is_target, target_grad[:, None], rest_low.astype(f32) * rest_scale[:, None]
@@ -755,10 +756,9 @@
     def between(step, streams):
         if step == 0:
             streams = after(streams, early)
-        if step == 1:
             parts = after((head_block(2), experts_block(2)), streams)
             far.extend(swap_group(part, 2) for part in parts)
-        return after(streams, (far, d_embed)) if step == 3 else streams
+        return after(streams, far) if step == 3 else streams
 
     late = streams_sum(late, between)
     d_head_part = sum(part.astype(f32) for part in head_parts + far[:1])
@@ -767,6 +767,7 @@
     parts = lax.all_to_all(
         jnp.concatenate(late + [early], axis=1), "dp", split_axis=0, concat_axis=0, tiled=True
     )
+    parts = after(parts, d_embed)
     parts = jnp.sum(parts.reshape(groups, own_rows, -1).astype(f32), axis=0)
     late, early = parts[:, :late_width], parts[:, late_width:]
     behind = width_model + 128

time: 634 us -> 623 us (0.983)
  transfers between devices with their start and end apart: 71 -> 71, of which waited for: 46 -> 43; matrix products, arithmetic and copies ran while one was open for 36% -> 36% of each run, Pallas kernels for 0% -> 0%
where the time goes in v5:
time: 623 us; the launch traced here: 613 us
  matrix products  173 us (28%)
  waiting for transfers between devices  168 us (27%)
  starting transfers between devices  121 us (19%)
  other arithmetic  73.1 us (12%)
  local copies, waits for them, and re-layouts  35.1 us (6%)
  between operations  20.2 us (3%)
  Pallas kernels  12.7 us (2%)
  blocking collectives  9.39 us (2%)
    dot_general x40, matrix products, product(): return jnp.dot(left, right, preferred_element_type=jnp.float32)  97.1 us
    ppermute x49, waiting for transfers between devices, swap(): return lax.ppermute(value, 'expert', [(i, i ^ number) for i in range(32)])  63.3 us
    ppermute x49, starting transfers between devices, swap(): return lax.ppermute(value, 'expert', [(i, i ^ number) for i in range(32)])  52.1 us
    dot_general x13, matrix products, inner_cols(): lax.dot_general(left, right, (((1,), (1,)), ((), ())), precision=precisio...  39 us
    dot_general x13, matrix products, inner_rows(): lax.dot_general(left, right, (((0,), (0,)), ((), ())), precision=precisio...  29.2 us
    all_to_all x1, waiting for transfers between devices, fetch_round(): lax.all_to_all(sent.reshape(axis_width, groups * ROUND_ROWS, part_width),...  26.4 us
    all_gather x1, waiting for transfers between devices, body(): packed_all = lax.all_gather(packed, BOTH, axis=0, tiled=True)  25.2 us
    unnamed x334, local copies, waits for them, and re-layouts  18.3 us
  transfers between devices with their start and end apart: 71, of which 43 were waited for; matrix products, arithmetic and copies ran while one was open for 36% of the time, Pallas kernels for 0%

profile of v5, /device:TPU:1, one launch (start us, length us, event | category | flops | bytes accessed | tf_op | source)
XLA Modules:
  0.0 613.1 jit_solution(16756481833824141656)
XLA Ops:
  10.8 4.5 collective-permute-start.1
  26.9 3.7 fusion.41
  36.2 8.3 %all-to-all-start.1 = ((bf16[32,96,256]{2,1,0:T(8,128)(2,1)}), bf16[32,96,256]{2,1,0:T(8,128)(2,1)S(1)}, u32[]{:S(2)}, u32[]{:S(2)}) async-start(bf16[32,96,256]{2,1,0:T(8,128)(2,1)} %bitcast.504), calls=%async_computation.1 | async-start | bytes 3145728 | tf_op jit(solution)/shard_map/all_to_all | solution.py:419
  45.3 26.4 %all-to-all-done.1 = bf16[32,96,256]{2,1,0:T(8,128)(2,1)S(1)} async-done(((bf16[32,96,256]{2,1,0:T(8,128)(2,1)}), bf16[32,96,256]{2,1,0:T(8,128)(2,1)S(1)}, u32[]{:S(2)}, u32[]{:S(2)}) %all-to-all-start.1) | async-done | bytes 1572896 | tf_op jit(solution)/shard_map/all_to_all | solution.py:419
  74.4 4.8 all-to-all-start.2
  79.7 8.7 %all-to-all-done.2 = bf16[4,128,256]{2,1,0:T(8,128)(2,1)S(1)} async-done(((bf16[4,128,256]{2,1,0:T(8,128)(2,1)}), bf16[4,128,256]{2,1,0:T(8,128)(2,1)S(1)}, u32[]{:S(2)}, u32[]{:S(2)}) %all-to-all-start.2) | async-done | bytes 262176 | tf_op jit(solution)/shard_map/all_to_all | solution.py:448
  88.6 25.2 %all-gather.5.cloned.1.call-done = bf16[1024,9088]{1,0:T(8,128)(2,1)} async-done(((bf16[8,9088]{1,0:T(8,128)(2,1)}), bf16[1024,9088]{1,0:T(8,128)(2,1)}) %all-gather.5.cloned.1.call-update) | async-done | bytes 18612240 | tf_op jit(solution)/shard_map/all_gather | solution.py:376
  115.9 3.9 fusion.27
  129.8 5.0 all-to-all-start.3
  136.5 3.7 fusion.31
  145.4 5.3 fusion.19
  150.8 6.6 %add_convert_fusion.1 = bf16[1408,1024]{1,0:T(8,128)(2,1)} fusion(f32[1408,1024]{1,0:T(8,128)S(1)} %fusion.19, pred[1408,2048]{1,0:T(32,128)(4,1)S(1)} %iota_compare_fusion.12, bf16[1024,9088]{1,0:T(8,128)(2,1)} %all-gather.5.cloned.1.call-done), kind=kOutput, calls=%fused_computation.41 | convolution fusion | flops 2955673600 | bytes 12189696 | tf_op jit(solution)/shard_map/dot_general | solution.py:34
  158.3 4.0 all-gather.7.cloned.1.call-done
  163.1 3.8 fusion.88
  167.0 6.1 %multiply_convert_fusion.2 = (bf16[1024,704]{0,1:T(8,128)(2,1)S(1)}, f32[1024,704]{0,1:T(8,128)}) fusion(f32[1024,704]{0,1:T(8,128)S(1)} %fusion.88, bf16[1024,1024]{1,0:T(8,128)(2,1)} %bitcast.18, bf16[3,704,1024]{2,1,0:T(8,128)(2,1)S(1)} %copy-done.146), kind=kOutput, calls=%fused_computation.95 | convolution fusion | flops 1480720384 | bytes 10747904 | tf_op jit(solution)/shard_map/dot_general | solution.py:48
  176.3 6.9 %all-to-all-start.4 = ((bf16[32,32,1024]{2,1,0:T(8,128)(2,1)}), bf16[32,32,1024]{2,1,0:T(8,128)(2,1)S(1)}, u32[]{:S(2)}, u32[]{:S(2)}) async-start(bf16[32,32,1024]{2,1,0:T(8,128)(2,1)} %bitcast.497), calls=%async_computation.4 | async-start | bytes 4194304 | tf_op jit(solution)/shard_map/all_to_all | solution.py:584
  193.2 5.3 all-gather.9.cloned.1.call-done
  198.4 8.0 %fusion.42 = bf16[2048,1024]{1,0:T(8,128)(2,1)} fusion(bf16[1002,1024]{1,0:T(8,128)(2,1)} %all-gather.9.cloned.1.call-done, s32[2048]{0:T(1024)S(1)} %sub.287), kind=kOutput, calls=%fused_computation.78 | convolution fusion | flops 4206841856 | bytes 6254592 | tf_op jit(solution)/shard_map/dot_general | solution.py:34
  206.4 5.1 all-to-all-done.4
  239.5 6.2 %collective-permute-start.15 = (bf16[16,64,1024]{2,1,0:T(8,128)(2,1)S(1)}, bf16[16,64,1024]{2,1,0:T(8,128)(2,1)}, u32[]{:S(2)}, u32[]{:S(2)}) collective-permute-start(bf16[16,64,1024]{2,1,0:T(8,128)(2,1)S(1)} %bitcast.480), channel_id=1, source_target_pairs={{0,1},{1,0},{2,3},{3,2},{4,5},{5,4},{6,7},{7,6},{8,9},{9,8},{10,11... | collective-permute-start | bytes 6291464 | tf_op jit(solution)/shard_map/ppermute | solution.py:132
  245.7 4.1 select_reduce_fusion.2
  254.7 4.5 fusion.369
  264.9 6.3 %convolution_convert_fusion.1 = bf16[2048,1024]{1,0:T(8,128)(2,1)} fusion(bf16[1002,1024]{1,0:T(8,128)(2,1)S(1)} %copy-done.147, f32[2048,1002]{0,1:T(8,128)S(1)} %get-tuple-element.624, f32[2048]{0:T(1024)S(1)} %get-tuple-element.623, s32[2048]{0:T(1024)S(1)} %copy-done.80), kind=kOutput, calls=%fused_computation.79 | convolution fusion | flops 4212998144 | bytes 14471168 | tf_op jit(solution)/shard_map/dot_general | solution.py:34
  288.4 4.3 add_convert_fusion
  303.1 3.3 collective-permute-done.24
  329.3 8.2 %convolution_convert_fusion = bf16[1024,4864]{1,0:T(8,128)(2,1)} fusion(bf16[128,1024]{1,0:T(8,128)(2,1)S(1)} %get-tuple-element.202, bf16[128,2816]{1,0:T(8,128)(2,1)S(1)} %pad_maximum_fusion.7, bf16[128,1024]{1,0:T(8,128)(2,1)S(1)} %fusion.107, bf16[128,1024]{1,0:T(8,128)(2,1)S(1)} %fusion.108, bf16[128,1024]{1,0:T(8,128)(2,1)S(1)} %fusion.105), kind=kOutput, calls=%fused_computation.23 | convolution fusion | flops 3858694144 | bytes 11730944 | tf_op jit(solution)/shard_map/dot_general | solution.py:38
  342.9 9.4 %all-to-all-start.5 = ((bf16[32,32,1024]{2,1,0:T(8,128)(2,1)}), bf16[32,32,1024]{2,1,0:T(8,128)(2,1)}, u32[]{:S(2)}, u32[]{:S(2)}) async-start(bf16[32,32,1024]{2,1,0:T(8,128)(2,1)} %bitcast.474), calls=%async_computation.5 | async-start | bytes 4194304 | tf_op jit(solution)/shard_map/all_to_all | solution.py:622
  352.3 5.4 select_convert_fusion
  357.7 4.6 convolution_convert_fusion.6
  366.6 6.0 fusion.29
  372.6 6.3 %collective-permute-done.37 = bf16[1002,256]{1,0:T(8,128)(2,1)S(1)} collective-permute-done((bf16[1002,256]{1,0:T(8,128)(2,1)S(1)}, bf16[1002,256]{1,0:T(8,128)(2,1)S(1)}, u32[]{:S(2)}, u32[]{:S(2)}) %collective-permute-start.37) | collective-permute-done | bytes 513056 | tf_op jit(solution)/shard_map/ppermute | solution.py:136
  380.7 6.3 %multiply_convert_fusion.1 = (bf16[1024,704]{0,1:T(8,128)(2,1)S(1)}, bf16[1024,704]{0,1:T(8,128)(2,1)S(1)}) fusion(f32[1024,704]{0,1:T(8,128)} %copy-done.153, f32[1024,704]{0,1:T(8,128)} %get-tuple-element.618, bf16[1024,1024]{1,0:T(8,128)(2,1)} %bitcast.123, bf16[3,704,1024]{2,1,0:T(8,128)(2,1)} %all-gather.7.cloned.1.call-done), kind=kOutput, calls=%fused_computation.92 | convolution fusion | flops 1486487552 | bytes 12189696 | tf_op jit(solution)/shard_map/dot_general | solution.py:48
  387.0 4.3 fusion.87
  391.3 4.7 add_convert_fusion.2
  396.0 7.0 %all-to-all-start.6 = ((bf16[32,32,1024]{2,1,0:T(8,128)(2,1)}), bf16[32,32,1024]{2,1,0:T(8,128)(2,1)}, u32[]{:S(2)}, u32[]{:S(2)}) async-start(bf16[32,32,1024]{2,1,0:T(8,128)(2,1)} %bitcast.496), calls=%async_computation.6 | async-start | bytes 4194304 | tf_op jit(solution)/shard_map/all_to_all | solution.py:659
  403.1 3.8 convolution_convert_fusion.8
  406.9 3.4 convolution_convert_fusion.9
  422.4 15.3 %all-to-all-done.6 = bf16[32,32,1024]{2,1,0:T(8,128)(2,1)} async-done(((bf16[32,32,1024]{2,1,0:T(8,128)(2,1)}), bf16[32,32,1024]{2,1,0:T(8,128)(2,1)}, u32[]{:S(2)}, u32[]{:S(2)}) %all-to-all-start.6) | async-done | bytes 2097184 | tf_op jit(solution)/shard_map/all_to_all | solution.py:659
  450.8 5.2 multiply_reduce_fusion.5
  456.3 9.4 %all_to_all.84 = bf16[4,128,256]{2,1,0:T(8,128)(2,1)} all-to-all(bf16[4,128,256]{2,1,0:T(8,128)(2,1)S(1)} %bitcast.518), channel_id=1, replica_groups=mesh['dp'=4,'expert'=32] {'dp'}, dimensions={0} | all-to-all | bytes 524288 | tf_op jit(solution)/shard_map/all_to_all | solution.py:714
  487.9 4.1 collective-permute-done.54
  503.4 9.2 %collective-permute-done.50 = bf16[4,32,1024]{2,1,0:T(8,128)(2,1)S(1)} collective-permute-done((bf16[4,32,1024]{2,1,0:T(8,128)(2,1)S(1)}, bf16[4,32,1024]{2,1,0:T(8,128)(2,1)S(1)}, u32[]{:S(2)}, u32[]{:S(2)}) %collective-permute-start.50) | collective-permute-done | bytes 262176 | tf_op jit(solution)/shard_map/ppermute | solution.py:132
  518.5 11.6 %collective-permute-done.53 = bf16[2,32,2176]{2,1,0:T(8,128)(2,1)S(1)} collective-permute-done((bf16[2,32,2176]{2,1,0:T(8,128)(2,1)S(1)}, bf16[2,32,2176]{2,1,0:T(8,128)(2,1)S(1)}, u32[]{:S(2)}, u32[]{:S(2)}) %collective-permute-start.53) | collective-permute-done | bytes 278560 | tf_op jit(solution)/shard_map/ppermute | solution.py:132
  535.1 3.4 collective-permute-done.56
  539.4 4.7 all-to-all-start.7
  544.2 13.8 %multiply_reduce_fusion.2 = (f32[256]{0:T(256)S(1)}, f32[1002,256]{1,0:T(8,128)}) fusion(bf16[16384,256]{1,0:T(8,128)(2,1)} %all-gather.11.cloned.1.call-done, s32[16384]{0:T(1024)S(1)} %bitcast.493), kind=kOutput, calls=%fused_computation.225 | convolution fusion | flops 8422315008 | bytes 9481216 | tf_op jit(solution)/shard_map/dot_general | solution.py:34
  560.7 11.4 %all-to-all-start.9 = ((f32[128,2,128]{2,1,0:T(2,128)}), f32[128,2,128]{2,1,0:T(2,128)}, u32[]{:S(2)}, u32[]{:S(2)}) async-start(f32[128,2,128]{2,1,0:T(2,128)} %broadcast_in_dim.321), calls=%async_computation.10 | async-start | bytes 262144 | tf_op jit(solution)/shard_map/all_to_all | solution.py:802
  596.9 8.1 %tables_update.1 = (f32[1002,2,256]{2,1,0:T(2,128)}, f32[1002,2,256]{2,1,0:T(2,128)}, f32[1002,2,256]{2,1,0:T(2,128)}) custom-call(f32[1,1]{1,0:T(1,128)} %bitcast.167.clip, f32[1002,2,256]{2,1,0:T(2,128)} %bitcast.482, f32[1002,2,256]{2,1,0:T(2,128)} %pad_maximum_fusion.3.grad, f32[1002,2,256]{2,1,0:T(2,128)} %bitcast.502, f32[1002,2,256]{2,1,0:T(2,128)} %bitcast.503), custom_call_target="tpu_custom_call" | custom-call | tf_op jit(solution)/shard_map/tables_update/pallas_call | solution.py:120
  (754 shorter events, 253.2 us)
Async XLA Ops:
  7.2 106.6 %all-gather.5.cloned.1.call-start = ((), (), s32[]{:S(2)}) async-start(), calls=%async_computation.11 | async-start | bytes 18757632 | tf_op jit(solution)/shard_map/all_gather | solution.py:376
  10.8 151.6 %all-gather.7.cloned.1.call-start = ((), (), s32[]{:S(2)}) async-start(), calls=%async_computation.12 | async-start | bytes 5406720 | tf_op jit(solution)/shard_map/all_gather | solution.py:454
  10.8 11.7 %collective-permute-start.1 = (s32[1,4096]{1,0:T(1,128)}, s32[1,4096]{1,0:T(1,128)S(1)}, u32[]{:S(2)}, u32[]{:S(2)}) collective-permute-start(s32[1,4096]{1,0:T(1,128)} %param.27), channel_id=1, source_target_pairs={{0,64},{32,96},{64,0},{96,32},{1,65},{33,97},{65,1},{97,33},{2,66}... | collective-permute-start | bytes 49160 | tf_op jit(solution)/shard_map/ppermute | solution.py:136
  15.3 7.2 %collective-permute-start = (s32[1,4096]{1,0:T(1,128)}, s32[1,4096]{1,0:T(1,128)S(1)}, u32[]{:S(2)}, u32[]{:S(2)}) collective-permute-start(s32[1,4096]{1,0:T(1,128)} %param.27), channel_id=1, source_target_pairs={{0,32},{32,0},{64,96},{96,64},{1,33},{33,1},{65,97},{97,65},{2,34}... | collective-permute-start | bytes 49160 | tf_op jit(solution)/shard_map/ppermute | solution.py:136
  16.0 6.4 %collective-permute-start.2 = (s32[1,4096]{1,0:T(1,128)}, s32[1,4096]{1,0:T(1,128)S(1)}, u32[]{:S(2)}, u32[]{:S(2)}) collective-permute-start(s32[1,4096]{1,0:T(1,128)} %param.27), channel_id=1, source_target_pairs={{0,96},{32,64},{64,32},{96,0},{1,97},{33,65},{65,33},{97,1},{2,98}... | collective-permute-start | bytes 49160 | tf_op jit(solution)/shard_map/ppermute | solution.py:136
  36.2 35.6 %all-to-all-start.1 = ((bf16[32,96,256]{2,1,0:T(8,128)(2,1)}), bf16[32,96,256]{2,1,0:T(8,128)(2,1)S(1)}, u32[]{:S(2)}, u32[]{:S(2)}) async-start(bf16[32,96,256]{2,1,0:T(8,128)(2,1)} %bitcast.504), calls=%async_computation.1 | async-start | bytes 3145728 | tf_op jit(solution)/shard_map/all_to_all | solution.py:419
  74.4 14.0 %all-to-all-start.2 = ((bf16[4,128,256]{2,1,0:T(8,128)(2,1)}), bf16[4,128,256]{2,1,0:T(8,128)(2,1)S(1)}, u32[]{:S(2)}, u32[]{:S(2)}) async-start(bf16[4,128,256]{2,1,0:T(8,128)(2,1)} %convert_element_type.669), calls=%async_computation.2 | async-start | bytes 524288 | tf_op jit(solution)/shard_map/all_to_all | solution.py:448
  129.8 33.3 %all-to-all-start.3 = ((bf16[32,32,1024]{2,1,0:T(8,128)(2,1)}), bf16[32,32,1024]{2,1,0:T(8,128)(2,1)}, u32[]{:S(2)}, u32[]{:S(2)}) async-start(bf16[32,32,1024]{2,1,0:T(8,128)(2,1)} %bitcast.17), calls=%async_computation.3 | async-start | bytes 4194304 | tf_op jit(solution)/shard_map/all_to_all | solution.py:520
  134.8 63.7 %all-gather.9.cloned.1.call-start = ((), (), s32[]{:S(2)}) async-start(), calls=%async_computation.13 | async-start | bytes 2580480 | tf_op jit(solution)/shard_map/all_gather | solution.py:515
  176.3 35.2 %all-to-all-start.4 = ((bf16[32,32,1024]{2,1,0:T(8,128)(2,1)}), bf16[32,32,1024]{2,1,0:T(8,128)(2,1)S(1)}, u32[]{:S(2)}, u32[]{:S(2)}) async-start(bf16[32,32,1024]{2,1,0:T(8,128)(2,1)} %bitcast.497), calls=%async_computation.4 | async-start | bytes 4194304 | tf_op jit(solution)/shard_map/all_to_all | solution.py:584
  183.3 293.9 %reduce-scatter.2.cloned.1.call-start = ((), (), s32[]{:S(2)}) async-start(), calls=%async_computation.14 | async-start | bytes 10272768 | tf_op jit(solution)/shard_map/reduce_scatter | solution.py:651
  220.7 5.3 collective-permute-start.10
  224.6 6.7 %collective-permute-start.5 = (bf16[4,16,1024]{2,1,0:T(8,128)(2,1)S(1)}, bf16[4,16,1024]{2,1,0:T(8,128)(2,1)S(1)}, u32[]{:S(2)}, u32[]{:S(2)}) collective-permute-start(bf16[4,16,1024]{2,1,0:T(8,128)(2,1)S(1)} %get-tuple-element.577), channel_id=1, source_target_pairs={{0,24},{1,25},{2,26},{3,27},{4,28},{5,29},{6,30},{7,31},{8,16},{9,... | collective-permute-start | bytes 393224 | tf_op jit(solution)/shard_map/ppermute | solution.py:132
  226.2 7.0 %collective-permute-start.11 = (bf16[4,16,1024]{2,1,0:T(8,128)(2,1)S(1)}, bf16[4,16,1024]{2,1,0:T(8,128)(2,1)S(1)}, u32[]{:S(2)}, u32[]{:S(2)}) collective-permute-start(bf16[4,16,1024]{2,1,0:T(8,128)(2,1)S(1)} %get-tuple-element.583), channel_id=1, source_target_pairs={{0,6},{1,7},{2,4},{3,5},{4,2},{5,3},{6,0},{7,1},{8,14},{9,15},{10,... | collective-permute-start | bytes 393224 | tf_op jit(solution)/shard_map/ppermute | solution.py:132
  229.1 7.0 %collective-permute-start.8 = (bf16[2,4,16,1024]{3,2,1,0:T(8,128)(2,1)S(1)}, bf16[2,4,16,1024]{3,2,1,0:T(8,128)(2,1)S(1)}, u32[]{:S(2)}, u32[]{:S(2)}) collective-permute-start(bf16[2,4,16,1024]{3,2,1,0:T(8,128)(2,1)S(1)} %pad_maximum_fusion.16), channel_id=1, source_target_pairs={{0,24},{1,25},{2,26},{3,27},{4,28},{5,29},{6,30},{7,31},{8,16},{9,... | collective-permute-start | bytes 786440 | tf_op jit(solution)/shard_map/ppermute | solution.py:132
  231.3 7.5 %collective-permute-start.6 = (bf16[2,4,16,1024]{3,2,1,0:T(8,128)(2,1)S(1)}, bf16[2,4,16,1024]{3,2,1,0:T(8,128)(2,1)S(1)}, u32[]{:S(2)}, u32[]{:S(2)}) collective-permute-start(bf16[2,4,16,1024]{3,2,1,0:T(8,128)(2,1)S(1)} %pad_maximum_fusion.15), channel_id=1, source_target_pairs={{0,8},{1,9},{2,10},{3,11},{4,12},{5,13},{6,14},{7,15},{8,0},{9,1},... | collective-permute-start | bytes 786440 | tf_op jit(solution)/shard_map/ppermute | solution.py:132
  231.8 6.8 %collective-permute-start.14 = (bf16[2,4,16,1024]{3,2,0,1:T(8,128)(2,1)S(1)}, bf16[2,4,16,1024]{3,2,0,1:T(8,128)(2,1)S(1)}, u32[]{:S(2)}, u32[]{:S(2)}) collective-permute-start(bf16[2,4,16,1024]{3,2,0,1:T(8,128)(2,1)S(1)} %pad_maximum_fusion.19), channel_id=1, source_target_pairs={{0,6},{1,7},{2,4},{3,5},{4,2},{5,3},{6,0},{7,1},{8,14},{9,15},{10,... | collective-permute-start | bytes 786440 | tf_op jit(solution)/shard_map/ppermute | solution.py:132
  233.2 6.1 %collective-permute-start.12 = (bf16[2,4,16,1024]{3,2,1,0:T(8,128)(2,1)S(1)}, bf16[2,4,16,1024]{3,2,1,0:T(8,128)(2,1)S(1)}, u32[]{:S(2)}, u32[]{:S(2)}) collective-permute-start(bf16[2,4,16,1024]{3,2,1,0:T(8,128)(2,1)S(1)} %pad_maximum_fusion.18), channel_id=1, source_target_pairs={{0,2},{1,3},{2,0},{3,1},{4,6},{5,7},{6,4},{7,5},{8,10},{9,11},{10,... | collective-permute-start | bytes 786440 | tf_op jit(solution)/shard_map/ppermute | solution.py:132
  239.5 13.0 %collective-permute-start.15 = (bf16[16,64,1024]{2,1,0:T(8,128)(2,1)S(1)}, bf16[16,64,1024]{2,1,0:T(8,128)(2,1)}, u32[]{:S(2)}, u32[]{:S(2)}) collective-permute-start(bf16[16,64,1024]{2,1,0:T(8,128)(2,1)S(1)} %bitcast.480), channel_id=1, source_target_pairs={{0,1},{1,0},{2,3},{3,2},{4,5},{5,4},{6,7},{7,6},{8,9},{9,8},{10,11... | collective-permute-start | bytes 6291464 | tf_op jit(solution)/shard_map/ppermute | solution.py:132
  261.5 9.7 %collective-permute-start.18 = (f32[3,2048]{1,0:T(4,128)S(1)}, f32[3,2048]{1,0:T(4,128)S(1)}, u32[]{:S(2)}, u32[]{:S(2)}) collective-permute-start(f32[3,2048]{1,0:T(4,128)S(1)} %pad_maximum_fusion.43.stats), channel_id=1, source_target_pairs={{0,24},{1,25},{2,26},{3,27},{4,28},{5,29},{6,30},{7,31},{8,16},{9,... | collective-permute-start | bytes 73736 | tf_op jit(solution)/shard_map/ppermute | solution.py:132
  262.3 8.9 %collective-permute-start.17 = (f32[3,2048]{1,0:T(4,128)S(1)}, f32[3,2048]{1,0:T(4,128)S(1)}, u32[]{:S(2)}, u32[]{:S(2)}) collective-permute-start(f32[3,2048]{1,0:T(4,128)S(1)} %pad_maximum_fusion.43.stats), channel_id=1, source_target_pairs={{0,16},{1,17},{2,18},{3,19},{4,20},{5,21},{6,22},{7,23},{8,24},{9,... | collective-permute-start | bytes 73736 | tf_op jit(solution)/shard_map/ppermute | solution.py:132
  264.6 6.6 %collective-permute-start.16 = (f32[3,2048]{1,0:T(4,128)S(1)}, f32[3,2048]{1,0:T(4,128)S(1)}, u32[]{:S(2)}, u32[]{:S(2)}) collective-permute-start(f32[3,2048]{1,0:T(4,128)S(1)} %pad_maximum_fusion.43.stats), channel_id=1, source_target_pairs={{0,8},{1,9},{2,10},{3,11},{4,12},{5,13},{6,14},{7,15},{8,0},{9,1},... | collective-permute-start | bytes 73736 | tf_op jit(solution)/shard_map/ppermute | solution.py:132
  298.8 7.6 %collective-permute-start.24 = (bf16[2,4,16,1024]{3,2,1,0:T(8,128)(2,1)S(1)}, bf16[2,4,16,1024]{3,2,1,0:T(8,128)(2,1)S(1)}, u32[]{:S(2)}, u32[]{:S(2)}) collective-permute-start(bf16[2,4,16,1024]{3,2,1,0:T(8,128)(2,1)S(1)} %slice_bitcast_fusion.15), channel_id=1, source_target_pairs={{0,8},{1,9},{2,10},{3,11},{4,12},{5,13},{6,14},{7,15},{8,0},{9,1},... | collective-permute-start | bytes 786440 | tf_op jit(solution)/shard_map/ppermute | solution.py:132
  300.1 8.5 %collective-permute-start.26 = (bf16[2,4,16,1024]{3,2,1,0:T(8,128)(2,1)S(1)}, bf16[2,4,16,1024]{3,2,1,0:T(8,128)(2,1)S(1)}, u32[]{:S(2)}, u32[]{:S(2)}) collective-permute-start(bf16[2,4,16,1024]{3,2,1,0:T(8,128)(2,1)S(1)} %pad_maximum_fusion.20), channel_id=1, source_target_pairs={{0,24},{1,25},{2,26},{3,27},{4,28},{5,29},{6,30},{7,31},{8,16},{9,... | collective-permute-start | bytes 786440 | tf_op jit(solution)/shard_map/ppermute | solution.py:132
  302.0 8.2 %collective-permute-start.32 = (bf16[2,4,16,1024]{3,2,0,1:T(8,128)(2,1)S(1)}, bf16[2,4,16,1024]{3,2,0,1:T(8,128)(2,1)S(1)}, u32[]{:S(2)}, u32[]{:S(2)}) collective-permute-start(bf16[2,4,16,1024]{3,2,0,1:T(8,128)(2,1)S(1)} %pad_maximum_fusion.21), channel_id=1, source_target_pairs={{0,6},{1,7},{2,4},{3,5},{4,2},{5,3},{6,0},{7,1},{8,14},{9,15},{10,... | collective-permute-start | bytes 786440 | tf_op jit(solution)/shard_map/ppermute | solution.py:132
  303.1 7.2 %collective-permute-start.30 = (bf16[2,4,16,1024]{3,2,1,0:T(8,128)(2,1)S(1)}, bf16[2,4,16,1024]{3,2,1,0:T(8,128)(2,1)S(1)}, u32[]{:S(2)}, u32[]{:S(2)}) collective-permute-start(bf16[2,4,16,1024]{3,2,1,0:T(8,128)(2,1)S(1)} %slice.687), channel_id=1, source_target_pairs={{0,2},{1,3},{2,0},{3,1},{4,6},{5,7},{6,4},{7,5},{8,10},{9,11},{10,... | collective-permute-start | bytes 786440 | tf_op jit(solution)/shard_map/ppermute | solution.py:132
  342.9 37.8 %all-to-all-start.5 = ((bf16[32,32,1024]{2,1,0:T(8,128)(2,1)}), bf16[32,32,1024]{2,1,0:T(8,128)(2,1)}, u32[]{:S(2)}, u32[]{:S(2)}) async-start(bf16[32,32,1024]{2,1,0:T(8,128)(2,1)} %bitcast.474), calls=%async_computation.5 | async-start | bytes 4194304 | tf_op jit(solution)/shard_map/all_to_all | solution.py:622
  364.7 14.3 %collective-permute-start.37 = (bf16[1002,256]{1,0:T(8,128)(2,1)S(1)}, bf16[1002,256]{1,0:T(8,128)(2,1)S(1)}, u32[]{:S(2)}, u32[]{:S(2)}) collective-permute-start(bf16[1002,256]{1,0:T(8,128)(2,1)S(1)} %get-tuple-element.550), channel_id=1, source_target_pairs={{0,96},{32,64},{64,32},{96,0},{1,97},{33,65},{65,33},{97,1},{2,98}... | collective-permute-start | bytes 1539080 | tf_op jit(solution)/shard_map/ppermute | solution.py:136
  365.3 13.6 %collective-permute-start.36 = (bf16[1002,256]{1,0:T(8,128)(2,1)S(1)}, bf16[1002,256]{1,0:T(8,128)(2,1)S(1)}, u32[]{:S(2)}, u32[]{:S(2)}) collective-permute-start(bf16[1002,256]{1,0:T(8,128)(2,1)S(1)} %get-tuple-element.551), channel_id=1, source_target_pairs={{0,32},{32,0},{64,96},{96,64},{1,33},{33,1},{65,97},{97,65},{2,34}... | collective-permute-start | bytes 1539080 | tf_op jit(solution)/shard_map/ppermute | solution.py:136
  396.0 41.7 %all-to-all-start.6 = ((bf16[32,32,1024]{2,1,0:T(8,128)(2,1)}), bf16[32,32,1024]{2,1,0:T(8,128)(2,1)}, u32[]{:S(2)}, u32[]{:S(2)}) async-start(bf16[32,32,1024]{2,1,0:T(8,128)(2,1)} %bitcast.496), calls=%async_computation.6 | async-start | bytes 4194304 | tf_op jit(solution)/shard_map/all_to_all | solution.py:659
  403.0 141.1 %all-gather.11.cloned.1.call-start = ((), (), s32[]{:S(2)}) async-start(), calls=%async_computation.15 | async-start | bytes 8650752 | tf_op jit(solution)/shard_map/all_gather | solution.py:715
  417.5 26.8 %collective-permute-start.39 = (bf16[3,176,1024]{2,1,0:T(8,128)(2,1)}, bf16[3,176,1024]{2,1,0:T(8,128)(2,1)}, u32[]{:S(2)}, u32[]{:S(2)}) collective-permute-start(bf16[3,176,1024]{2,1,0:T(8,128)(2,1)} %get-tuple-element.534), channel_id=1, source_target_pairs={{0,96},{32,64},{64,32},{96,0},{1,97},{33,65},{65,33},{97,1},{2,98}... | collective-permute-start | bytes 3244040 | tf_op jit(solution)/shard_map/ppermute | solution.py:136
  419.6 25.2 %collective-permute-start.38 = (bf16[3,176,1024]{2,1,0:T(8,128)(2,1)}, bf16[3,176,1024]{2,1,0:T(8,128)(2,1)}, u32[]{:S(2)}, u32[]{:S(2)}) collective-permute-start(bf16[3,176,1024]{2,1,0:T(8,128)(2,1)} %get-tuple-element.535), channel_id=1, source_target_pairs={{0,32},{32,0},{64,96},{96,64},{1,33},{33,1},{65,97},{97,65},{2,34}... | collective-permute-start | bytes 3244040 | tf_op jit(solution)/shard_map/ppermute | solution.py:136
  466.3 6.6 %collective-permute-start.42 = (bf16[512,1024]{1,0:T(8,128)(2,1)S(1)}, bf16[512,1024]{1,0:T(8,128)(2,1)S(1)}, u32[]{:S(2)}, u32[]{:S(2)}) collective-permute-start(bf16[512,1024]{1,0:T(8,128)(2,1)S(1)} %convolution_convert_fusion.10), channel_id=1, source_target_pairs={{0,1},{1,0},{2,3},{3,2},{4,5},{5,4},{6,7},{7,6},{8,9},{9,8},{10,11... | collective-permute-start | bytes 3145736 | tf_op jit(solution)/shard_map/ppermute | solution.py:132
  477.2 14.9 %collective-permute-start.54 = (bf16[1002,256]{1,0:T(8,128)(2,1)}, bf16[1002,256]{1,0:T(8,128)(2,1)}, u32[]{:S(2)}, u32[]{:S(2)}) collective-permute-start(bf16[1002,256]{1,0:T(8,128)(2,1)} %get-tuple-element.216), channel_id=1, source_target_pairs={{0,64},{32,96},{64,0},{96,32},{1,65},{33,97},{65,1},{97,33},{2,66}... | collective-permute-start | bytes 1539080 | tf_op jit(solution)/shard_map/ppermute | solution.py:136
  480.0 16.2 %collective-permute-start.49 = (bf16[8,32,1024]{2,1,0:T(8,128)(2,1)S(1)}, bf16[8,32,1024]{2,1,0:T(8,128)(2,1)S(1)}, u32[]{:S(2)}, u32[]{:S(2)}) collective-permute-start(bf16[8,32,1024]{2,1,0:T(8,128)(2,1)S(1)} %slice.592), channel_id=1, source_target_pairs={{0,2},{1,3},{2,0},{3,1},{4,6},{5,7},{6,4},{7,5},{8,10},{9,11},{10,... | collective-permute-start | bytes 1572872 | tf_op jit(solution)/shard_map/ppermute | solution.py:132
  483.4 15.6 %collective-permute-start.46 = (bf16[8,32,1024]{2,1,0:T(8,128)(2,1)S(1)}, bf16[8,32,1024]{2,1,0:T(8,128)(2,1)S(1)}, u32[]{:S(2)}, u32[]{:S(2)}) collective-permute-start(bf16[8,32,1024]{2,1,0:T(8,128)(2,1)S(1)} %slice.586), channel_id=1, source_target_pairs={{0,24},{1,25},{2,26},{3,27},{4,28},{5,29},{6,30},{7,31},{8,16},{9,... | collective-permute-start | bytes 1572872 | tf_op jit(solution)/shard_map/ppermute | solution.py:132
  486.0 15.9 %collective-permute-start.51 = (bf16[8,32,1152]{2,1,0:T(8,128)(2,1)S(1)}, bf16[8,32,1152]{2,1,0:T(8,128)(2,1)S(1)}, u32[]{:S(2)}, u32[]{:S(2)}) collective-permute-start(bf16[8,32,1152]{2,1,0:T(8,128)(2,1)S(1)} %slice.596), channel_id=1, source_target_pairs={{0,6},{1,7},{2,4},{3,5},{4,2},{5,3},{6,0},{7,1},{8,14},{9,15},{10,... | collective-permute-start | bytes 1769480 | tf_op jit(solution)/shard_map/ppermute | solution.py:132
  487.9 14.2 %collective-permute-start.44 = (bf16[8,32,1152]{2,1,0:T(8,128)(2,1)S(1)}, bf16[8,32,1152]{2,1,0:T(8,128)(2,1)S(1)}, u32[]{:S(2)}, u32[]{:S(2)}) collective-permute-start(bf16[8,32,1152]{2,1,0:T(8,128)(2,1)S(1)} %slice.582), channel_id=1, source_target_pairs={{0,8},{1,9},{2,10},{3,11},{4,12},{5,13},{6,14},{7,15},{8,0},{9,1},... | collective-permute-start | bytes 1769480 | tf_op jit(solution)/shard_map/ppermute | solution.py:132
  492.1 38.2 %collective-permute-start.55 = (bf16[3,176,1024]{2,1,0:T(8,128)(2,1)S(1)}, bf16[3,176,1024]{2,1,0:T(8,128)(2,1)S(1)}, u32[]{:S(2)}, u32[]{:S(2)}) collective-permute-start(bf16[3,176,1024]{2,1,0:T(8,128)(2,1)S(1)} %copy-done.26), channel_id=1, source_target_pairs={{0,64},{32,96},{64,0},{96,32},{1,65},{33,97},{65,1},{97,33},{2,66}... | collective-permute-start | bytes 3244040 | tf_op jit(solution)/shard_map/ppermute | solution.py:136
  496.4 16.2 %collective-permute-start.50 = (bf16[4,32,1024]{2,1,0:T(8,128)(2,1)S(1)}, bf16[4,32,1024]{2,1,0:T(8,128)(2,1)S(1)}, u32[]{:S(2)}, u32[]{:S(2)}) collective-permute-start(bf16[4,32,1024]{2,1,0:T(8,128)(2,1)S(1)} %slice.720), channel_id=1, source_target_pairs={{0,6},{1,7},{2,4},{3,5},{4,2},{5,3},{6,0},{7,1},{8,14},{9,15},{10,... | collective-permute-start | bytes 786440 | tf_op jit(solution)/shard_map/ppermute | solution.py:132
  499.2 13.6 %collective-permute-start.47 = (bf16[4,32,1024]{2,1,0:T(8,128)(2,1)S(1)}, bf16[4,32,1024]{2,1,0:T(8,128)(2,1)S(1)}, u32[]{:S(2)}, u32[]{:S(2)}) collective-permute-start(bf16[4,32,1024]{2,1,0:T(8,128)(2,1)S(1)} %slice.716), channel_id=1, source_target_pairs={{0,8},{1,9},{2,10},{3,11},{4,12},{5,13},{6,14},{7,15},{8,0},{9,1},... | collective-permute-start | bytes 786440 | tf_op jit(solution)/shard_map/ppermute | solution.py:132
  502.0 13.8 %collective-permute-start.52 = (bf16[4,32,1152]{2,1,0:T(8,128)(2,1)S(1)}, bf16[4,32,1152]{2,1,0:T(8,128)(2,1)S(1)}, u32[]{:S(2)}, u32[]{:S(2)}) collective-permute-start(bf16[4,32,1152]{2,1,0:T(8,128)(2,1)S(1)} %slice.722), channel_id=1, source_target_pairs={{0,2},{1,3},{2,0},{3,1},{4,6},{5,7},{6,4},{7,5},{8,10},{9,11},{10,... | collective-permute-start | bytes 884744 | tf_op jit(solution)/shard_map/ppermute | solution.py:132
  502.3 15.7 %collective-permute-start.45 = (bf16[4,32,1152]{2,1,0:T(8,128)(2,1)S(1)}, bf16[4,32,1152]{2,1,0:T(8,128)(2,1)S(1)}, u32[]{:S(2)}, u32[]{:S(2)}) collective-permute-start(bf16[4,32,1152]{2,1,0:T(8,128)(2,1)S(1)} %slice.714), channel_id=1, source_target_pairs={{0,24},{1,25},{2,26},{3,27},{4,28},{5,29},{6,30},{7,31},{8,16},{9,... | collective-permute-start | bytes 884744 | tf_op jit(solution)/shard_map/ppermute | solution.py:132
  515.9 14.2 %collective-permute-start.53 = (bf16[2,32,2176]{2,1,0:T(8,128)(2,1)S(1)}, bf16[2,32,2176]{2,1,0:T(8,128)(2,1)S(1)}, u32[]{:S(2)}, u32[]{:S(2)}) collective-permute-start(bf16[2,32,2176]{2,1,0:T(8,128)(2,1)S(1)} %pad_maximum_fusion.10), channel_id=1, source_target_pairs={{0,24},{1,25},{2,26},{3,27},{4,28},{5,29},{6,30},{7,31},{8,16},{9,... | collective-permute-start | bytes 835592 | tf_op jit(solution)/shard_map/ppermute | solution.py:132
  518.1 12.1 %collective-permute-start.48 = (bf16[2,32,2176]{2,1,0:T(8,128)(2,1)S(1)}, bf16[2,32,2176]{2,1,0:T(8,128)(2,1)S(1)}, u32[]{:S(2)}, u32[]{:S(2)}) collective-permute-start(bf16[2,32,2176]{2,1,0:T(8,128)(2,1)S(1)} %pad_maximum_fusion.11), channel_id=1, source_target_pairs={{0,2},{1,3},{2,0},{3,1},{4,6},{5,7},{6,4},{7,5},{8,10},{9,11},{10,... | collective-permute-start | bytes 835592 | tf_op jit(solution)/shard_map/ppermute | solution.py:132
  539.4 18.6 %all-to-all-start.7 = ((bf16[4,8,9216]{2,1,0:T(8,128)(2,1)}), bf16[4,8,9216]{2,1,0:T(8,128)(2,1)}, u32[]{:S(2)}, u32[]{:S(2)}) async-start(bf16[4,8,9216]{2,1,0:T(8,128)(2,1)} %pad_maximum_fusion.9), calls=%async_computation.8 | async-start | bytes 1179648 | tf_op jit(solution)/shard_map/all_to_all | solution.py:767
  560.7 21.2 %all-to-all-start.9 = ((f32[128,2,128]{2,1,0:T(2,128)}), f32[128,2,128]{2,1,0:T(2,128)}, u32[]{:S(2)}, u32[]{:S(2)}) async-start(f32[128,2,128]{2,1,0:T(2,128)} %broadcast_in_dim.321), calls=%async_computation.10 | async-start | bytes 262144 | tf_op jit(solution)/shard_map/all_to_all | solution.py:802
  (181 other events, 1308.4 us)
Sparse Core Ops, SparseCore 0:
  11.7 102.0 all-gather.4
  116.1 46.2 all-gather.6
  164.6 33.8 all-gather.8
  337.7 119.4 reduce-scatter.1
  465.8 65.1 all-gather.10

commit v6 on v5

--- a/solution.py
+++ b/solution.py
@@ -791,14 +791,16 @@
         axis=0,
     )
     start = 3 * width_model + behind
-    gains_part = late[:, start : start + gains.shape[0]].T
+    gains_part = inner_rows(
+        late[:, start : start + gains.shape[0]], jnp.eye(own_rows, dtype=f32), HIGH
+    )
     up_part = experts_part[:2]
     down_part = experts_part[2:]
 
     grads = (parts, d_embed, d_head_part, experts_part)
     squares = sum(lane_squares(grad) for grad in grads)
     sums = jnp.stack([squares, terms])
-    d_embed, d_head_part, gains_part = after((d_embed, d_head_part, gains_part), sums)
+    d_embed = after(d_embed, sums)
     sums = lax.all_to_all(
         jnp.broadcast_to(sums[None], (devices, 2, 128)), BOTH, split_axis=0, concat_axis=0, tiled=True
     )

time: 623 us -> 625 us (level)
    unnamed x334 -> x320, local copies, waits for them, and re-layouts: 18.3 us -> 14.3 us
    dot_general x13 -> x14, matrix products: 29.2 us -> 29.9 us  [inner_rows(): lax.dot_general(left, right, (((0,), (0,)), ((), ())), precision=precisio...]
  transfers between devices with their start and end apart: 71 -> 71, of which waited for: 43 -> 44; matrix products, arithmetic and copies ran while one was open for 36% -> 35% of each run, Pallas kernels for 0% -> 0%
where the time goes in v6:
time: 625 us; the launch traced here: 615 us
  matrix products  174 us (28%)
  waiting for transfers between devices  172 us (28%)
  starting transfers between devices  119 us (19%)
  other arithmetic  74.6 us (12%)
  local copies, waits for them, and re-layouts  32.1 us (5%)
  between operations  20.1 us (3%)
  Pallas kernels  12.7 us (2%)
  blocking collectives  9.34 us (1%)
    dot_general x40, matrix products, product(): return jnp.dot(left, right, preferred_element_type=jnp.float32)  97 us
    ppermute x49, waiting for transfers between devices, swap(): return lax.ppermute(value, 'expert', [(i, i ^ number) for i in range(32)])  63.9 us
    ppermute x49, starting transfers between devices, swap(): return lax.ppermute(value, 'expert', [(i, i ^ number) for i in range(32)])  50.5 us
    dot_general x13, matrix products, inner_cols(): lax.dot_general(left, right, (((1,), (1,)), ((), ())), precision=precisio...  39 us
    dot_general x14, matrix products, inner_rows(): lax.dot_general(left, right, (((0,), (0,)), ((), ())), precision=precisio...  29.9 us
    all_to_all x1, waiting for transfers between devices, fetch_round(): lax.all_to_all(sent.reshape(axis_width, groups * ROUND_ROWS, part_width),...  26.4 us
    all_gather x1, waiting for transfers between devices, body(): packed_all = lax.all_gather(packed, BOTH, axis=0, tiled=True)  25.2 us
    all_to_all x1, waiting for transfers between devices, body(): lax.all_to_all(d_sent, 'expert', split_axis=0, concat_axis=0, tiled=True)  15.3 us
  transfers between devices with their start and end apart: 71, of which 44 were waited for; matrix products, arithmetic and copies ran while one was open for 35% of the time, Pallas kernels for 0%

profile of v6, /device:TPU:1, one launch (start us, length us, event | category | flops | bytes accessed | tf_op | source)
XLA Modules:
  0.0 614.9 jit_solution(7579007455789127179)
XLA Ops:
  10.8 4.5 collective-permute-start.1
  26.9 3.7 fusion.41
  36.2 8.3 %all-to-all-start.1 = ((bf16[32,96,256]{2,1,0:T(8,128)(2,1)}), bf16[32,96,256]{2,1,0:T(8,128)(2,1)S(1)}, u32[]{:S(2)}, u32[]{:S(2)}) async-start(bf16[32,96,256]{2,1,0:T(8,128)(2,1)} %bitcast.502), calls=%async_computation.1 | async-start | bytes 3145728 | tf_op jit(solution)/shard_map/all_to_all | solution.py:419
  45.3 26.4 %all-to-all-done.1 = bf16[32,96,256]{2,1,0:T(8,128)(2,1)S(1)} async-done(((bf16[32,96,256]{2,1,0:T(8,128)(2,1)}), bf16[32,96,256]{2,1,0:T(8,128)(2,1)S(1)}, u32[]{:S(2)}, u32[]{:S(2)}) %all-to-all-start.1) | async-done | bytes 1572896 | tf_op jit(solution)/shard_map/all_to_all | solution.py:419
  74.4 4.8 all-to-all-start.2
  79.7 8.7 %all-to-all-done.2 = bf16[4,128,256]{2,1,0:T(8,128)(2,1)S(1)} async-done(((bf16[4,128,256]{2,1,0:T(8,128)(2,1)}), bf16[4,128,256]{2,1,0:T(8,128)(2,1)S(1)}, u32[]{:S(2)}, u32[]{:S(2)}) %all-to-all-start.2) | async-done | bytes 262176 | tf_op jit(solution)/shard_map/all_to_all | solution.py:448
  88.6 25.2 %all-gather.5.cloned.1.call-done = bf16[1024,9088]{1,0:T(8,128)(2,1)} async-done(((bf16[8,9088]{1,0:T(8,128)(2,1)}), bf16[1024,9088]{1,0:T(8,128)(2,1)}) %all-gather.5.cloned.1.call-update) | async-done | bytes 18612240 | tf_op jit(solution)/shard_map/all_gather | solution.py:376
  115.9 3.9 fusion.27
  129.8 5.0 all-to-all-start.3
  136.4 3.6 fusion.31
  145.4 5.3 fusion.19
  150.7 6.6 %add_convert_fusion.1 = bf16[1408,1024]{1,0:T(8,128)(2,1)} fusion(f32[1408,1024]{1,0:T(8,128)S(1)} %fusion.19, pred[1408,2048]{1,0:T(32,128)(4,1)S(1)} %iota_compare_fusion.12, bf16[1024,9088]{1,0:T(8,128)(2,1)} %all-gather.5.cloned.1.call-done), kind=kOutput, calls=%fused_computation.41 | convolution fusion | flops 2955673600 | bytes 12189696 | tf_op jit(solution)/shard_map/dot_general | solution.py:34
  158.3 4.0 all-gather.7.cloned.1.call-done
  163.1 3.8 fusion.88
  167.0 6.1 multiply_convert_fusion.2
  176.3 7.0 %all-to-all-start.4 = ((bf16[32,32,1024]{2,1,0:T(8,128)(2,1)}), bf16[32,32,1024]{2,1,0:T(8,128)(2,1)S(1)}, u32[]{:S(2)}, u32[]{:S(2)}) async-start(bf16[32,32,1024]{2,1,0:T(8,128)(2,1)} %bitcast.495), calls=%async_computation.4 | async-start | bytes 4194304 | tf_op jit(solution)/shard_map/all_to_all | solution.py:584
  193.2 5.3 all-gather.9.cloned.1.call-done
  198.4 8.0 %fusion.42 = bf16[2048,1024]{1,0:T(8,128)(2,1)} fusion(bf16[1002,1024]{1,0:T(8,128)(2,1)} %all-gather.9.cloned.1.call-done, s32[2048]{0:T(1024)S(1)} %sub.287), kind=kOutput, calls=%fused_computation.78 | convolution fusion | flops 4206841856 | bytes 6254592 | tf_op jit(solution)/shard_map/dot_general | solution.py:34
  206.4 5.1 all-to-all-done.4
  239.5 6.3 %collective-permute-start.15 = (bf16[16,64,1024]{2,1,0:T(8,128)(2,1)S(1)}, bf16[16,64,1024]{2,1,0:T(8,128)(2,1)}, u32[]{:S(2)}, u32[]{:S(2)}) collective-permute-start(bf16[16,64,1024]{2,1,0:T(8,128)(2,1)S(1)} %bitcast.478), channel_id=1, source_target_pairs={{0,1},{1,0},{2,3},{3,2},{4,5},{5,4},{6,7},{7,6},{8,9},{9,8},{10,11... | collective-permute-start | bytes 6291464 | tf_op jit(solution)/shard_map/ppermute | solution.py:132
  245.8 4.1 select_reduce_fusion.2
  254.7 4.5 fusion.370
  264.9 6.3 %convolution_convert_fusion.1 = bf16[2048,1024]{1,0:T(8,128)(2,1)} fusion(bf16[1002,1024]{1,0:T(8,128)(2,1)S(1)} %copy-done.141, f32[2048,1002]{0,1:T(8,128)S(1)} %get-tuple-element.436, f32[2048]{0:T(1024)S(1)} %get-tuple-element.435, s32[2048]{0:T(1024)S(1)} %copy-done.79), kind=kOutput, calls=%fused_computation.79 | convolution fusion | flops 4212998144 | bytes 14471168 | tf_op jit(solution)/shard_map/dot_general | solution.py:34
  288.5 4.3 add_convert_fusion
  303.1 3.4 collective-permute-done.24
  329.3 8.2 %convolution_convert_fusion = bf16[1024,4864]{1,0:T(8,128)(2,1)} fusion(bf16[128,1024]{1,0:T(8,128)(2,1)S(1)} %get-tuple-element.200, bf16[128,2816]{1,0:T(8,128)(2,1)S(1)} %pad_maximum_fusion.7, bf16[128,1024]{1,0:T(8,128)(2,1)S(1)} %fusion.107, bf16[128,1024]{1,0:T(8,128)(2,1)S(1)} %fusion.108, bf16[128,1024]{1,0:T(8,128)(2,1)S(1)} %fusion.105), kind=kOutput, calls=%fused_computation.23 | convolution fusion | flops 3858694144 | bytes 11730944 | tf_op jit(solution)/shard_map/dot_general | solution.py:38
  342.8 9.4 %all-to-all-start.5 = ((bf16[32,32,1024]{2,1,0:T(8,128)(2,1)}), bf16[32,32,1024]{2,1,0:T(8,128)(2,1)}, u32[]{:S(2)}, u32[]{:S(2)}) async-start(bf16[32,32,1024]{2,1,0:T(8,128)(2,1)} %bitcast.472), calls=%async_computation.5 | async-start | bytes 4194304 | tf_op jit(solution)/shard_map/all_to_all | solution.py:622
  352.2 5.4 select_convert_fusion
  357.6 4.6 convolution_convert_fusion.6
  366.5 6.0 fusion.29
  372.5 6.4 %collective-permute-done.37 = bf16[1002,256]{1,0:T(8,128)(2,1)S(1)} collective-permute-done((bf16[1002,256]{1,0:T(8,128)(2,1)S(1)}, bf16[1002,256]{1,0:T(8,128)(2,1)S(1)}, u32[]{:S(2)}, u32[]{:S(2)}) %collective-permute-start.37) | collective-permute-done | bytes 513056 | tf_op jit(solution)/shard_map/ppermute | solution.py:136
  380.6 6.3 %multiply_convert_fusion.1 = (bf16[1024,704]{0,1:T(8,128)(2,1)S(1)}, bf16[1024,704]{0,1:T(8,128)(2,1)S(1)}) fusion(f32[1024,704]{0,1:T(8,128)} %copy-done.149, f32[1024,704]{0,1:T(8,128)} %get-tuple-element.430, bf16[1024,1024]{1,0:T(8,128)(2,1)} %bitcast.123, bf16[3,704,1024]{2,1,0:T(8,128)(2,1)} %all-gather.7.cloned.1.call-done), kind=kOutput, calls=%fused_computation.92 | convolution fusion | flops 1486487552 | bytes 12189696 | tf_op jit(solution)/shard_map/dot_general | solution.py:48
  386.9 4.3 fusion.87
  391.2 4.7 add_convert_fusion.2
  395.9 7.0 %all-to-all-start.6 = ((bf16[32,32,1024]{2,1,0:T(8,128)(2,1)}), bf16[32,32,1024]{2,1,0:T(8,128)(2,1)}, u32[]{:S(2)}, u32[]{:S(2)}) async-start(bf16[32,32,1024]{2,1,0:T(8,128)(2,1)} %bitcast.494), calls=%async_computation.6 | async-start | bytes 4194304 | tf_op jit(solution)/shard_map/all_to_all | solution.py:659
  403.0 3.8 convolution_convert_fusion.8
  422.4 15.3 %all-to-all-done.6 = bf16[32,32,1024]{2,1,0:T(8,128)(2,1)} async-done(((bf16[32,32,1024]{2,1,0:T(8,128)(2,1)}), bf16[32,32,1024]{2,1,0:T(8,128)(2,1)}, u32[]{:S(2)}, u32[]{:S(2)}) %all-to-all-start.6) | async-done | bytes 2097184 | tf_op jit(solution)/shard_map/all_to_all | solution.py:659
  450.8 5.2 multiply_reduce_fusion.5
  456.3 9.3 %all_to_all.84 = bf16[4,128,256]{2,1,0:T(8,128)(2,1)} all-to-all(bf16[4,128,256]{2,1,0:T(8,128)(2,1)S(1)} %bitcast.516), channel_id=1, replica_groups=mesh['dp'=4,'expert'=32] {'dp'}, dimensions={0} | all-to-all | bytes 524288 | tf_op jit(solution)/shard_map/all_to_all | solution.py:714
  485.7 6.3 %collective-permute-done.54 = bf16[1002,256]{1,0:T(8,128)(2,1)} collective-permute-done((bf16[1002,256]{1,0:T(8,128)(2,1)}, bf16[1002,256]{1,0:T(8,128)(2,1)}, u32[]{:S(2)}, u32[]{:S(2)}) %collective-permute-start.54) | collective-permute-done | bytes 513056 | tf_op jit(solution)/shard_map/ppermute | solution.py:136
  501.3 9.0 %collective-permute-done.50 = bf16[4,32,1024]{2,1,0:T(8,128)(2,1)S(1)} collective-permute-done((bf16[4,32,1024]{2,1,0:T(8,128)(2,1)S(1)}, bf16[4,32,1024]{2,1,0:T(8,128)(2,1)S(1)}, u32[]{:S(2)}, u32[]{:S(2)}) %collective-permute-start.50) | collective-permute-done | bytes 262176 | tf_op jit(solution)/shard_map/ppermute | solution.py:132
  517.8 12.0 %collective-permute-done.53 = bf16[2,32,2176]{2,1,0:T(8,128)(2,1)S(1)} collective-permute-done((bf16[2,32,2176]{2,1,0:T(8,128)(2,1)S(1)}, bf16[2,32,2176]{2,1,0:T(8,128)(2,1)S(1)}, u32[]{:S(2)}, u32[]{:S(2)}) %collective-permute-start.53) | collective-permute-done | bytes 278560 | tf_op jit(solution)/shard_map/ppermute | solution.py:132
  539.2 4.4 all-to-all-start.7
  543.6 13.8 %multiply_reduce_fusion.2 = (f32[256]{0:T(256)S(1)}, f32[1002,256]{1,0:T(8,128)}) fusion(bf16[16384,256]{1,0:T(8,128)(2,1)} %all-gather.11.cloned.1.call-done, s32[16384]{0:T(1024)S(1)} %bitcast.491), kind=kOutput, calls=%fused_computation.226 | convolution fusion | flops 8422315008 | bytes 9481216 | tf_op jit(solution)/shard_map/dot_general | solution.py:34
  563.0 11.9 %all-to-all-start.9 = ((f32[128,2,128]{2,1,0:T(2,128)}), f32[128,2,128]{2,1,0:T(2,128)}, u32[]{:S(2)}, u32[]{:S(2)}) async-start(f32[128,2,128]{2,1,0:T(2,128)} %broadcast_in_dim.321), calls=%async_computation.10 | async-start | bytes 262144 | tf_op jit(solution)/shard_map/all_to_all | solution.py:804
  578.0 4.4 pad_maximum_fusion.3.grad
  590.3 3.4 multiply_subtract_fusion
  598.7 8.1 %tables_update.1 = (f32[1002,2,256]{2,1,0:T(2,128)}, f32[1002,2,256]{2,1,0:T(2,128)}, f32[1002,2,256]{2,1,0:T(2,128)}) custom-call(f32[1,1]{1,0:T(1,128)} %bitcast.166.clip, f32[1002,2,256]{2,1,0:T(2,128)} %bitcast.480, f32[1002,2,256]{2,1,0:T(2,128)} %pad_maximum_fusion.3.grad, f32[1002,2,256]{2,1,0:T(2,128)} %bitcast.500, f32[1002,2,256]{2,1,0:T(2,128)} %bitcast.501), custom_call_target="tpu_custom_call" | custom-call | tf_op jit(solution)/shard_map/tables_update/pallas_call | solution.py:120
  (739 shorter events, 251.4 us)
Async XLA Ops:
  7.2 106.6 %all-gather.5.cloned.1.call-start = ((), (), s32[]{:S(2)}) async-start(), calls=%async_computation.11 | async-start | bytes 18757632 | tf_op jit(solution)/shard_map/all_gather | solution.py:376
  10.8 151.6 %all-gather.7.cloned.1.call-start = ((), (), s32[]{:S(2)}) async-start(), calls=%async_computation.12 | async-start | bytes 5406720 | tf_op jit(solution)/shard_map/all_gather | solution.py:454
  10.8 11.7 %collective-permute-start.1 = (s32[1,4096]{1,0:T(1,128)}, s32[1,4096]{1,0:T(1,128)S(1)}, u32[]{:S(2)}, u32[]{:S(2)}) collective-permute-start(s32[1,4096]{1,0:T(1,128)} %param.27), channel_id=1, source_target_pairs={{0,64},{32,96},{64,0},{96,32},{1,65},{33,97},{65,1},{97,33},{2,66}... | collective-permute-start | bytes 49160 | tf_op jit(solution)/shard_map/ppermute | solution.py:136
  15.3 7.2 %collective-permute-start = (s32[1,4096]{1,0:T(1,128)}, s32[1,4096]{1,0:T(1,128)S(1)}, u32[]{:S(2)}, u32[]{:S(2)}) collective-permute-start(s32[1,4096]{1,0:T(1,128)} %param.27), channel_id=1, source_target_pairs={{0,32},{32,0},{64,96},{96,64},{1,33},{33,1},{65,97},{97,65},{2,34}... | collective-permute-start | bytes 49160 | tf_op jit(solution)/shard_map/ppermute | solution.py:136
  16.0 6.4 %collective-permute-start.2 = (s32[1,4096]{1,0:T(1,128)}, s32[1,4096]{1,0:T(1,128)S(1)}, u32[]{:S(2)}, u32[]{:S(2)}) collective-permute-start(s32[1,4096]{1,0:T(1,128)} %param.27), channel_id=1, source_target_pairs={{0,96},{32,64},{64,32},{96,0},{1,97},{33,65},{65,33},{97,1},{2,98}... | collective-permute-start | bytes 49160 | tf_op jit(solution)/shard_map/ppermute | solution.py:136
  36.2 35.6 %all-to-all-start.1 = ((bf16[32,96,256]{2,1,0:T(8,128)(2,1)}), bf16[32,96,256]{2,1,0:T(8,128)(2,1)S(1)}, u32[]{:S(2)}, u32[]{:S(2)}) async-start(bf16[32,96,256]{2,1,0:T(8,128)(2,1)} %bitcast.502), calls=%async_computation.1 | async-start | bytes 3145728 | tf_op jit(solution)/shard_map/all_to_all | solution.py:419
  74.4 13.9 %all-to-all-start.2 = ((bf16[4,128,256]{2,1,0:T(8,128)(2,1)}), bf16[4,128,256]{2,1,0:T(8,128)(2,1)S(1)}, u32[]{:S(2)}, u32[]{:S(2)}) async-start(bf16[4,128,256]{2,1,0:T(8,128)(2,1)} %convert_element_type.670), calls=%async_computation.2 | async-start | bytes 524288 | tf_op jit(solution)/shard_map/all_to_all | solution.py:448
  129.8 33.3 %all-to-all-start.3 = ((bf16[32,32,1024]{2,1,0:T(8,128)(2,1)}), bf16[32,32,1024]{2,1,0:T(8,128)(2,1)}, u32[]{:S(2)}, u32[]{:S(2)}) async-start(bf16[32,32,1024]{2,1,0:T(8,128)(2,1)} %bitcast.17), calls=%async_computation.3 | async-start | bytes 4194304 | tf_op jit(solution)/shard_map/all_to_all | solution.py:520
  134.8 63.7 %all-gather.9.cloned.1.call-start = ((), (), s32[]{:S(2)}) async-start(), calls=%async_computation.13 | async-start | bytes 2580480 | tf_op jit(solution)/shard_map/all_gather | solution.py:515
  176.3 35.3 %all-to-all-start.4 = ((bf16[32,32,1024]{2,1,0:T(8,128)(2,1)}), bf16[32,32,1024]{2,1,0:T(8,128)(2,1)S(1)}, u32[]{:S(2)}, u32[]{:S(2)}) async-start(bf16[32,32,1024]{2,1,0:T(8,128)(2,1)} %bitcast.495), calls=%async_computation.4 | async-start | bytes 4194304 | tf_op jit(solution)/shard_map/all_to_all | solution.py:584
  183.2 293.9 %reduce-scatter.2.cloned.1.call-start = ((), (), s32[]{:S(2)}) async-start(), calls=%async_computation.14 | async-start | bytes 10272768 | tf_op jit(solution)/shard_map/reduce_scatter | solution.py:651
  220.7 5.3 collective-permute-start.10
  224.5 6.7 %collective-permute-start.5 = (bf16[4,16,1024]{2,1,0:T(8,128)(2,1)S(1)}, bf16[4,16,1024]{2,1,0:T(8,128)(2,1)S(1)}, u32[]{:S(2)}, u32[]{:S(2)}) collective-permute-start(bf16[4,16,1024]{2,1,0:T(8,128)(2,1)S(1)} %get-tuple-element.389), channel_id=1, source_target_pairs={{0,24},{1,25},{2,26},{3,27},{4,28},{5,29},{6,30},{7,31},{8,16},{9,... | collective-permute-start | bytes 393224 | tf_op jit(solution)/shard_map/ppermute | solution.py:132
  226.1 7.0 %collective-permute-start.11 = (bf16[4,16,1024]{2,1,0:T(8,128)(2,1)S(1)}, bf16[4,16,1024]{2,1,0:T(8,128)(2,1)S(1)}, u32[]{:S(2)}, u32[]{:S(2)}) collective-permute-start(bf16[4,16,1024]{2,1,0:T(8,128)(2,1)S(1)} %get-tuple-element.395), channel_id=1, source_target_pairs={{0,6},{1,7},{2,4},{3,5},{4,2},{5,3},{6,0},{7,1},{8,14},{9,15},{10,... | collective-permute-start | bytes 393224 | tf_op jit(solution)/shard_map/ppermute | solution.py:132
  229.0 7.0 %collective-permute-start.8 = (bf16[2,4,16,1024]{3,2,1,0:T(8,128)(2,1)S(1)}, bf16[2,4,16,1024]{3,2,1,0:T(8,128)(2,1)S(1)}, u32[]{:S(2)}, u32[]{:S(2)}) collective-permute-start(bf16[2,4,16,1024]{3,2,1,0:T(8,128)(2,1)S(1)} %pad_maximum_fusion.16), channel_id=1, source_target_pairs={{0,24},{1,25},{2,26},{3,27},{4,28},{5,29},{6,30},{7,31},{8,16},{9,... | collective-permute-start | bytes 786440 | tf_op jit(solution)/shard_map/ppermute | solution.py:132
  231.2 7.5 %collective-permute-start.6 = (bf16[2,4,16,1024]{3,2,1,0:T(8,128)(2,1)S(1)}, bf16[2,4,16,1024]{3,2,1,0:T(8,128)(2,1)S(1)}, u32[]{:S(2)}, u32[]{:S(2)}) collective-permute-start(bf16[2,4,16,1024]{3,2,1,0:T(8,128)(2,1)S(1)} %pad_maximum_fusion.15), channel_id=1, source_target_pairs={{0,8},{1,9},{2,10},{3,11},{4,12},{5,13},{6,14},{7,15},{8,0},{9,1},... | collective-permute-start | bytes 786440 | tf_op jit(solution)/shard_map/ppermute | solution.py:132
  231.8 6.8 %collective-permute-start.14 = (bf16[2,4,16,1024]{3,2,0,1:T(8,128)(2,1)S(1)}, bf16[2,4,16,1024]{3,2,0,1:T(8,128)(2,1)S(1)}, u32[]{:S(2)}, u32[]{:S(2)}) collective-permute-start(bf16[2,4,16,1024]{3,2,0,1:T(8,128)(2,1)S(1)} %pad_maximum_fusion.19), channel_id=1, source_target_pairs={{0,6},{1,7},{2,4},{3,5},{4,2},{5,3},{6,0},{7,1},{8,14},{9,15},{10,... | collective-permute-start | bytes 786440 | tf_op jit(solution)/shard_map/ppermute | solution.py:132
  233.1 6.2 %collective-permute-start.12 = (bf16[2,4,16,1024]{3,2,1,0:T(8,128)(2,1)S(1)}, bf16[2,4,16,1024]{3,2,1,0:T(8,128)(2,1)S(1)}, u32[]{:S(2)}, u32[]{:S(2)}) collective-permute-start(bf16[2,4,16,1024]{3,2,1,0:T(8,128)(2,1)S(1)} %pad_maximum_fusion.18), channel_id=1, source_target_pairs={{0,2},{1,3},{2,0},{3,1},{4,6},{5,7},{6,4},{7,5},{8,10},{9,11},{10,... | collective-permute-start | bytes 786440 | tf_op jit(solution)/shard_map/ppermute | solution.py:132
  239.5 13.0 %collective-permute-start.15 = (bf16[16,64,1024]{2,1,0:T(8,128)(2,1)S(1)}, bf16[16,64,1024]{2,1,0:T(8,128)(2,1)}, u32[]{:S(2)}, u32[]{:S(2)}) collective-permute-start(bf16[16,64,1024]{2,1,0:T(8,128)(2,1)S(1)} %bitcast.478), channel_id=1, source_target_pairs={{0,1},{1,0},{2,3},{3,2},{4,5},{5,4},{6,7},{7,6},{8,9},{9,8},{10,11... | collective-permute-start | bytes 6291464 | tf_op jit(solution)/shard_map/ppermute | solution.py:132
  261.6 9.7 %collective-permute-start.18 = (f32[3,2048]{1,0:T(4,128)S(1)}, f32[3,2048]{1,0:T(4,128)S(1)}, u32[]{:S(2)}, u32[]{:S(2)}) collective-permute-start(f32[3,2048]{1,0:T(4,128)S(1)} %pad_maximum_fusion.43.stats), channel_id=1, source_target_pairs={{0,24},{1,25},{2,26},{3,27},{4,28},{5,29},{6,30},{7,31},{8,16},{9,... | collective-permute-start | bytes 73736 | tf_op jit(solution)/shard_map/ppermute | solution.py:132
  262.3 9.0 %collective-permute-start.17 = (f32[3,2048]{1,0:T(4,128)S(1)}, f32[3,2048]{1,0:T(4,128)S(1)}, u32[]{:S(2)}, u32[]{:S(2)}) collective-permute-start(f32[3,2048]{1,0:T(4,128)S(1)} %pad_maximum_fusion.43.stats), channel_id=1, source_target_pairs={{0,16},{1,17},{2,18},{3,19},{4,20},{5,21},{6,22},{7,23},{8,24},{9,... | collective-permute-start | bytes 73736 | tf_op jit(solution)/shard_map/ppermute | solution.py:132
  264.6 6.7 %collective-permute-start.16 = (f32[3,2048]{1,0:T(4,128)S(1)}, f32[3,2048]{1,0:T(4,128)S(1)}, u32[]{:S(2)}, u32[]{:S(2)}) collective-permute-start(f32[3,2048]{1,0:T(4,128)S(1)} %pad_maximum_fusion.43.stats), channel_id=1, source_target_pairs={{0,8},{1,9},{2,10},{3,11},{4,12},{5,13},{6,14},{7,15},{8,0},{9,1},... | collective-permute-start | bytes 73736 | tf_op jit(solution)/shard_map/ppermute | solution.py:132
  298.9 7.6 %collective-permute-start.24 = (bf16[2,4,16,1024]{3,2,1,0:T(8,128)(2,1)S(1)}, bf16[2,4,16,1024]{3,2,1,0:T(8,128)(2,1)S(1)}, u32[]{:S(2)}, u32[]{:S(2)}) collective-permute-start(bf16[2,4,16,1024]{3,2,1,0:T(8,128)(2,1)S(1)} %slice_bitcast_fusion.15), channel_id=1, source_target_pairs={{0,8},{1,9},{2,10},{3,11},{4,12},{5,13},{6,14},{7,15},{8,0},{9,1},... | collective-permute-start | bytes 786440 | tf_op jit(solution)/shard_map/ppermute | solution.py:132
  300.1 8.5 %collective-permute-start.26 = (bf16[2,4,16,1024]{3,2,1,0:T(8,128)(2,1)S(1)}, bf16[2,4,16,1024]{3,2,1,0:T(8,128)(2,1)S(1)}, u32[]{:S(2)}, u32[]{:S(2)}) collective-permute-start(bf16[2,4,16,1024]{3,2,1,0:T(8,128)(2,1)S(1)} %pad_maximum_fusion.20), channel_id=1, source_target_pairs={{0,24},{1,25},{2,26},{3,27},{4,28},{5,29},{6,30},{7,31},{8,16},{9,... | collective-permute-start | bytes 786440 | tf_op jit(solution)/shard_map/ppermute | solution.py:132
  301.9 8.2 %collective-permute-start.32 = (bf16[2,4,16,1024]{3,2,0,1:T(8,128)(2,1)S(1)}, bf16[2,4,16,1024]{3,2,0,1:T(8,128)(2,1)S(1)}, u32[]{:S(2)}, u32[]{:S(2)}) collective-permute-start(bf16[2,4,16,1024]{3,2,0,1:T(8,128)(2,1)S(1)} %pad_maximum_fusion.21), channel_id=1, source_target_pairs={{0,6},{1,7},{2,4},{3,5},{4,2},{5,3},{6,0},{7,1},{8,14},{9,15},{10,... | collective-permute-start | bytes 786440 | tf_op jit(solution)/shard_map/ppermute | solution.py:132
  303.1 7.3 %collective-permute-start.30 = (bf16[2,4,16,1024]{3,2,1,0:T(8,128)(2,1)S(1)}, bf16[2,4,16,1024]{3,2,1,0:T(8,128)(2,1)S(1)}, u32[]{:S(2)}, u32[]{:S(2)}) collective-permute-start(bf16[2,4,16,1024]{3,2,1,0:T(8,128)(2,1)S(1)} %slice.687), channel_id=1, source_target_pairs={{0,2},{1,3},{2,0},{3,1},{4,6},{5,7},{6,4},{7,5},{8,10},{9,11},{10,... | collective-permute-start | bytes 786440 | tf_op jit(solution)/shard_map/ppermute | solution.py:132
  342.8 37.8 %all-to-all-start.5 = ((bf16[32,32,1024]{2,1,0:T(8,128)(2,1)}), bf16[32,32,1024]{2,1,0:T(8,128)(2,1)}, u32[]{:S(2)}, u32[]{:S(2)}) async-start(bf16[32,32,1024]{2,1,0:T(8,128)(2,1)} %bitcast.472), calls=%async_computation.5 | async-start | bytes 4194304 | tf_op jit(solution)/shard_map/all_to_all | solution.py:622
  364.6 14.3 %collective-permute-start.37 = (bf16[1002,256]{1,0:T(8,128)(2,1)S(1)}, bf16[1002,256]{1,0:T(8,128)(2,1)S(1)}, u32[]{:S(2)}, u32[]{:S(2)}) collective-permute-start(bf16[1002,256]{1,0:T(8,128)(2,1)S(1)} %get-tuple-element.362), channel_id=1, source_target_pairs={{0,96},{32,64},{64,32},{96,0},{1,97},{33,65},{65,33},{97,1},{2,98}... | collective-permute-start | bytes 1539080 | tf_op jit(solution)/shard_map/ppermute | solution.py:136
  365.3 13.6 %collective-permute-start.36 = (bf16[1002,256]{1,0:T(8,128)(2,1)S(1)}, bf16[1002,256]{1,0:T(8,128)(2,1)S(1)}, u32[]{:S(2)}, u32[]{:S(2)}) collective-permute-start(bf16[1002,256]{1,0:T(8,128)(2,1)S(1)} %get-tuple-element.363), channel_id=1, source_target_pairs={{0,32},{32,0},{64,96},{96,64},{1,33},{33,1},{65,97},{97,65},{2,34}... | collective-permute-start | bytes 1539080 | tf_op jit(solution)/shard_map/ppermute | solution.py:136
  395.9 41.7 %all-to-all-start.6 = ((bf16[32,32,1024]{2,1,0:T(8,128)(2,1)}), bf16[32,32,1024]{2,1,0:T(8,128)(2,1)}, u32[]{:S(2)}, u32[]{:S(2)}) async-start(bf16[32,32,1024]{2,1,0:T(8,128)(2,1)} %bitcast.494), calls=%async_computation.6 | async-start | bytes 4194304 | tf_op jit(solution)/shard_map/all_to_all | solution.py:659
  402.9 140.7 %all-gather.11.cloned.1.call-start = ((), (), s32[]{:S(2)}) async-start(), calls=%async_computation.15 | async-start | bytes 8650752 | tf_op jit(solution)/shard_map/all_gather | solution.py:715
  417.4 26.8 %collective-permute-start.39 = (bf16[3,176,1024]{2,1,0:T(8,128)(2,1)}, bf16[3,176,1024]{2,1,0:T(8,128)(2,1)}, u32[]{:S(2)}, u32[]{:S(2)}) collective-permute-start(bf16[3,176,1024]{2,1,0:T(8,128)(2,1)} %get-tuple-element.346), channel_id=1, source_target_pairs={{0,96},{32,64},{64,32},{96,0},{1,97},{33,65},{65,33},{97,1},{2,98}... | collective-permute-start | bytes 3244040 | tf_op jit(solution)/shard_map/ppermute | solution.py:136
  419.5 25.2 %collective-permute-start.38 = (bf16[3,176,1024]{2,1,0:T(8,128)(2,1)}, bf16[3,176,1024]{2,1,0:T(8,128)(2,1)}, u32[]{:S(2)}, u32[]{:S(2)}) collective-permute-start(bf16[3,176,1024]{2,1,0:T(8,128)(2,1)} %get-tuple-element.347), channel_id=1, source_target_pairs={{0,32},{32,0},{64,96},{96,64},{1,33},{33,1},{65,97},{97,65},{2,34}... | collective-permute-start | bytes 3244040 | tf_op jit(solution)/shard_map/ppermute | solution.py:136
  466.3 6.6 %collective-permute-start.42 = (bf16[512,1024]{1,0:T(8,128)(2,1)S(1)}, bf16[512,1024]{1,0:T(8,128)(2,1)S(1)}, u32[]{:S(2)}, u32[]{:S(2)}) collective-permute-start(bf16[512,1024]{1,0:T(8,128)(2,1)S(1)} %convolution_convert_fusion.10), channel_id=1, source_target_pairs={{0,1},{1,0},{2,3},{3,2},{4,5},{5,4},{6,7},{7,6},{8,9},{9,8},{10,11... | collective-permute-start | bytes 3145736 | tf_op jit(solution)/shard_map/ppermute | solution.py:132
  477.1 14.9 %collective-permute-start.54 = (bf16[1002,256]{1,0:T(8,128)(2,1)}, bf16[1002,256]{1,0:T(8,128)(2,1)}, u32[]{:S(2)}, u32[]{:S(2)}) collective-permute-start(bf16[1002,256]{1,0:T(8,128)(2,1)} %get-tuple-element.214), channel_id=1, source_target_pairs={{0,64},{32,96},{64,0},{96,32},{1,65},{33,97},{65,1},{97,33},{2,66}... | collective-permute-start | bytes 1539080 | tf_op jit(solution)/shard_map/ppermute | solution.py:136
  477.9 16.8 %collective-permute-start.49 = (bf16[8,32,1024]{2,1,0:T(8,128)(2,1)S(1)}, bf16[8,32,1024]{2,1,0:T(8,128)(2,1)S(1)}, u32[]{:S(2)}, u32[]{:S(2)}) collective-permute-start(bf16[8,32,1024]{2,1,0:T(8,128)(2,1)S(1)} %slice.592), channel_id=1, source_target_pairs={{0,2},{1,3},{2,0},{3,1},{4,6},{5,7},{6,4},{7,5},{8,10},{9,11},{10,... | collective-permute-start | bytes 1572872 | tf_op jit(solution)/shard_map/ppermute | solution.py:132
  481.2 16.7 %collective-permute-start.46 = (bf16[8,32,1024]{2,1,0:T(8,128)(2,1)S(1)}, bf16[8,32,1024]{2,1,0:T(8,128)(2,1)S(1)}, u32[]{:S(2)}, u32[]{:S(2)}) collective-permute-start(bf16[8,32,1024]{2,1,0:T(8,128)(2,1)S(1)} %slice.586), channel_id=1, source_target_pairs={{0,24},{1,25},{2,26},{3,27},{4,28},{5,29},{6,30},{7,31},{8,16},{9,... | collective-permute-start | bytes 1572872 | tf_op jit(solution)/shard_map/ppermute | solution.py:132
  483.8 16.5 %collective-permute-start.51 = (bf16[8,32,1152]{2,1,0:T(8,128)(2,1)S(1)}, bf16[8,32,1152]{2,1,0:T(8,128)(2,1)S(1)}, u32[]{:S(2)}, u32[]{:S(2)}) collective-permute-start(bf16[8,32,1152]{2,1,0:T(8,128)(2,1)S(1)} %slice.596), channel_id=1, source_target_pairs={{0,6},{1,7},{2,4},{3,5},{4,2},{5,3},{6,0},{7,1},{8,14},{9,15},{10,... | collective-permute-start | bytes 1769480 | tf_op jit(solution)/shard_map/ppermute | solution.py:132
  485.7 14.9 %collective-permute-start.44 = (bf16[8,32,1152]{2,1,0:T(8,128)(2,1)S(1)}, bf16[8,32,1152]{2,1,0:T(8,128)(2,1)S(1)}, u32[]{:S(2)}, u32[]{:S(2)}) collective-permute-start(bf16[8,32,1152]{2,1,0:T(8,128)(2,1)S(1)} %slice.582), channel_id=1, source_target_pairs={{0,8},{1,9},{2,10},{3,11},{4,12},{5,13},{6,14},{7,15},{8,0},{9,1},... | collective-permute-start | bytes 1769480 | tf_op jit(solution)/shard_map/ppermute | solution.py:132
  492.0 38.0 %collective-permute-start.55 = (bf16[3,176,1024]{2,1,0:T(8,128)(2,1)S(1)}, bf16[3,176,1024]{2,1,0:T(8,128)(2,1)S(1)}, u32[]{:S(2)}, u32[]{:S(2)}) collective-permute-start(bf16[3,176,1024]{2,1,0:T(8,128)(2,1)S(1)} %copy-done.25), channel_id=1, source_target_pairs={{0,64},{32,96},{64,0},{96,32},{1,65},{33,97},{65,1},{97,33},{2,66}... | collective-permute-start | bytes 3244040 | tf_op jit(solution)/shard_map/ppermute | solution.py:136
  495.0 15.3 %collective-permute-start.50 = (bf16[4,32,1024]{2,1,0:T(8,128)(2,1)S(1)}, bf16[4,32,1024]{2,1,0:T(8,128)(2,1)S(1)}, u32[]{:S(2)}, u32[]{:S(2)}) collective-permute-start(bf16[4,32,1024]{2,1,0:T(8,128)(2,1)S(1)} %slice.720), channel_id=1, source_target_pairs={{0,6},{1,7},{2,4},{3,5},{4,2},{5,3},{6,0},{7,1},{8,14},{9,15},{10,... | collective-permute-start | bytes 786440 | tf_op jit(solution)/shard_map/ppermute | solution.py:132
  498.2 14.2 %collective-permute-start.47 = (bf16[4,32,1024]{2,1,0:T(8,128)(2,1)S(1)}, bf16[4,32,1024]{2,1,0:T(8,128)(2,1)S(1)}, u32[]{:S(2)}, u32[]{:S(2)}) collective-permute-start(bf16[4,32,1024]{2,1,0:T(8,128)(2,1)S(1)} %slice.716), channel_id=1, source_target_pairs={{0,8},{1,9},{2,10},{3,11},{4,12},{5,13},{6,14},{7,15},{8,0},{9,1},... | collective-permute-start | bytes 786440 | tf_op jit(solution)/shard_map/ppermute | solution.py:132
  500.6 14.2 %collective-permute-start.52 = (bf16[4,32,1152]{2,1,0:T(8,128)(2,1)S(1)}, bf16[4,32,1152]{2,1,0:T(8,128)(2,1)S(1)}, u32[]{:S(2)}, u32[]{:S(2)}) collective-permute-start(bf16[4,32,1152]{2,1,0:T(8,128)(2,1)S(1)} %slice.722), channel_id=1, source_target_pairs={{0,2},{1,3},{2,0},{3,1},{4,6},{5,7},{6,4},{7,5},{8,10},{9,11},{10,... | collective-permute-start | bytes 884744 | tf_op jit(solution)/shard_map/ppermute | solution.py:132
  500.9 15.4 %collective-permute-start.45 = (bf16[4,32,1152]{2,1,0:T(8,128)(2,1)S(1)}, bf16[4,32,1152]{2,1,0:T(8,128)(2,1)S(1)}, u32[]{:S(2)}, u32[]{:S(2)}) collective-permute-start(bf16[4,32,1152]{2,1,0:T(8,128)(2,1)S(1)} %slice.714), channel_id=1, source_target_pairs={{0,24},{1,25},{2,26},{3,27},{4,28},{5,29},{6,30},{7,31},{8,16},{9,... | collective-permute-start | bytes 884744 | tf_op jit(solution)/shard_map/ppermute | solution.py:132
  514.9 15.0 %collective-permute-start.53 = (bf16[2,32,2176]{2,1,0:T(8,128)(2,1)S(1)}, bf16[2,32,2176]{2,1,0:T(8,128)(2,1)S(1)}, u32[]{:S(2)}, u32[]{:S(2)}) collective-permute-start(bf16[2,32,2176]{2,1,0:T(8,128)(2,1)S(1)} %pad_maximum_fusion.10), channel_id=1, source_target_pairs={{0,24},{1,25},{2,26},{3,27},{4,28},{5,29},{6,30},{7,31},{8,16},{9,... | collective-permute-start | bytes 835592 | tf_op jit(solution)/shard_map/ppermute | solution.py:132
  516.4 13.5 %collective-permute-start.48 = (bf16[2,32,2176]{2,1,0:T(8,128)(2,1)S(1)}, bf16[2,32,2176]{2,1,0:T(8,128)(2,1)S(1)}, u32[]{:S(2)}, u32[]{:S(2)}) collective-permute-start(bf16[2,32,2176]{2,1,0:T(8,128)(2,1)S(1)} %pad_maximum_fusion.11), channel_id=1, source_target_pairs={{0,2},{1,3},{2,0},{3,1},{4,6},{5,7},{6,4},{7,5},{8,10},{9,11},{10,... | collective-permute-start | bytes 835592 | tf_op jit(solution)/shard_map/ppermute | solution.py:132
  539.2 18.3 %all-to-all-start.7 = ((bf16[4,8,9216]{2,1,0:T(8,128)(2,1)}), bf16[4,8,9216]{2,1,0:T(8,128)(2,1)}, u32[]{:S(2)}, u32[]{:S(2)}) async-start(bf16[4,8,9216]{2,1,0:T(8,128)(2,1)} %pad_maximum_fusion.9), calls=%async_computation.8 | async-start | bytes 1179648 | tf_op jit(solution)/shard_map/all_to_all | solution.py:767
  563.0 21.7 %all-to-all-start.9 = ((f32[128,2,128]{2,1,0:T(2,128)}), f32[128,2,128]{2,1,0:T(2,128)}, u32[]{:S(2)}, u32[]{:S(2)}) async-start(f32[128,2,128]{2,1,0:T(2,128)} %broadcast_in_dim.321), calls=%async_computation.10 | async-start | bytes 262144 | tf_op jit(solution)/shard_map/all_to_all | solution.py:804
  (177 other events, 1305.9 us)
Sparse Core Ops, SparseCore 0:
  11.7 102.0 all-gather.4
  116.1 46.2 all-gather.6
  164.6 33.8 all-gather.8
  337.6 119.4 reduce-scatter.1
  465.7 66.2 all-gather.10
